TPU v7x, 32 devices: a whole 2x2x4 slice. The times are simulated.
32 devices in a mesh: pipe: 8 (over z, x), expert: 4 (over y, core).
Axes of the slice: x: 2, y: 2, z: 4, core: 2. Of those that a mesh axis runs over, the one named last changes fastest.
Arguments:
- upstream: bfloat16 [8, 1024, 7168], P('pipe', None, 'expert'), may hold values from -6 to 6
- shared_down: bfloat16 [8, 1024, 7168], P('pipe', None, 'expert'), may hold values from -0.0625 to 0.0625
- shared_gate: bfloat16 [8, 7168, 1024], P('pipe', 'expert'), may hold values from -0.1875 to 0.1875
- shared_up: bfloat16 [8, 7168, 1024], P('pipe', 'expert'), may hold values from -0.1875 to 0.1875
- router_weight: bfloat16 [8, 7168, 256], P('pipe', 'expert'), may hold values from -2 to 2
- gate_pre: bfloat16 [8, 1024, 1024], P('pipe', 'expert'), may hold values from -6 to 6
- up_pre: bfloat16 [8, 1024, 1024], P('pipe', 'expert'), may hold values from -6 to 6
- gate_grad: float32 [8, 1024, 8], P('pipe'), may hold values from -6 to 6
- gate_scores: float32 [8, 1024, 8], P('pipe'), may hold values from 0.05 to 0.95
- expert_ids: int32 [8, 1024, 8], P('pipe'), may hold values from 0 to 255, all different within a row
Outputs:
- down_grad: bfloat16 [8, 1024, 7168], P('pipe', None, 'expert')
Inputs may be any that keep to these rules, and one draw needn't show every extreme that they name: `expert_ids`: each token names 8 different experts.
All inputs are finite; a program needn't handle non-finite values.
Results may differ from a plain program's by a relative error of at most 0.02.
Values may be sent and summed in bfloat16 or wider, within the bound.
No kernel may reach another device: no remote copies, remote signals or barrier semaphores. Data moves between devices by JAX's collectives and lax.ppermute only.
A program may use at most 64 MiB of HBM per device.

v0:
```python
import jax
import jax.numpy as jnp
from jax import lax
from jax.sharding import PartitionSpec as P


def passed_along(x, axis, by):
    length = lax.axis_size(axis)
    return lax.ppermute(x, axis, [(i, (i + by) % length) for i in range(length)])


def contract_last(left, right):
    return lax.dot_general(
        left, right, (((1,), (1,)), ((), ())), preferred_element_type=jnp.float32
    )


def section_backward(
    incoming, w_down, w_gate, w_up, w_router, pre_gate, pre_up, grad_gate, scores, chosen
):
    hid_width = w_down.shape[0]
    hidden_grad = lax.psum_scatter(
        contract_last(incoming, w_down)
        .astype(jnp.bfloat16)
        .astype(jnp.float32)
        .astype(jnp.bfloat16),
        "expert",
        scatter_dimension=0,
        tiled=True,
    ).astype(jnp.float32)
    act_a = pre_gate.astype(jnp.float32)
    act_b = pre_up.astype(jnp.float32)
    sigma = jax.nn.sigmoid(act_a)
    gate_part = (hidden_grad * act_b * sigma * (1.0 + act_a * (1.0 - sigma))).astype(jnp.bfloat16)
    up_part = (hidden_grad * act_a * sigma).astype(jnp.bfloat16)
    stacked = jnp.concatenate([gate_part, up_part], axis=1)
    piece = lax.all_gather(stacked, "expert", axis=0, tiled=True)
    shared_term = contract_last(piece[:, :hid_width], w_gate) + contract_last(
        piece[:, hid_width:], w_up
    )
    total = jnp.sum(scores, axis=-1, keepdims=True)
    mixed = jnp.sum(grad_gate * scores, axis=-1, keepdims=True)
    logit_grad = 2.5 * (grad_gate - mixed / total) / total * scores * (1.0 - scores)
    n_experts = w_router.shape[1]
    columns = lax.broadcasted_iota(jnp.int32, (1, n_experts), 1)
    dense = jnp.zeros((grad_gate.shape[0], n_experts), jnp.float32)
    for slot in range(grad_gate.shape[1]):
        dense = dense + jnp.where(
            chosen[:, slot : slot + 1] == columns, logit_grad[:, slot : slot + 1], 0.0
        )
    dense_grad = dense.astype(jnp.bfloat16)
    router_term = contract_last(dense_grad, w_router)
    return (shared_term + router_term).astype(jnp.bfloat16)


def shards(
    upstream,
    shared_down,
    shared_gate,
    shared_up,
    router_weight,
    gate_pre,
    up_pre,
    gate_grad,
    gate_scores,
    expert_ids,
):
    incoming = passed_along(upstream, "pipe", -1)
    local_grad = section_backward(
        incoming[0],
        shared_down[0],
        shared_gate[0],
        shared_up[0],
        router_weight[0],
        gate_pre[0],
        up_pre[0],
        gate_grad[0],
        gate_scores[0],
        expert_ids[0],
    )
    return passed_along(local_grad[None], "pipe", -1)


def solution(mesh):
    in_specs = (
        P("pipe", None, "expert"),
        P("pipe", None, "expert"),
        P("pipe", "expert", None),
        P("pipe", "expert", None),
        P("pipe", "expert", None),
        P("pipe", "expert", None),
        P("pipe", "expert", None),
        P("pipe", None, None),
        P("pipe", None, None),
        P("pipe", None, None),
    )
    out_specs = P("pipe", None, "expert")
    return jax.shard_map(shards, mesh=mesh, in_specs=in_specs, out_specs=out_specs, check_vma=False)
```

profile of v0, /device:TPU:0, one launch (start us, length us, event | category | flops | bytes accessed | tf_op | source)
XLA Modules:
  0.0 277.7 jit_solution(1923212618700606469)
XLA Ops:
  6.5 0.0 copy-start
  6.5 0.0 copy-start.1
  6.5 0.0 copy-start.2
  6.5 0.0 reduce-scatter.2.cloned.1.call-start
  6.5 6.0 %collective-permute-start = (bf16[1,1024,1792]{2,1,0:T(8,128)(2,1)}, bf16[1,1024,1792]{2,1,0:T(8,128)(2,1)S(1)}, u32[]{:S(2)}, u32[]{:S(2)}) collective-permute-start(bf16[1,1024,1792]{2,1,0:T(8,128)(2,1)} %param.10), channel_id=1, source_target_pairs={{0,28},{4,0},{8,4},{12,8},{16,12},{20,16},{24,20},{28,24},{1,29},{... | collective-permute-start | bytes 11010056 | tf_op jit(solution)/shard_map/ppermute | solution.py:9
  12.6 78.9 %collective-permute-done = bf16[1,1024,1792]{2,1,0:T(8,128)(2,1)S(1)} collective-permute-done((bf16[1,1024,1792]{2,1,0:T(8,128)(2,1)}, bf16[1,1024,1792]{2,1,0:T(8,128)(2,1)S(1)}, u32[]{:S(2)}, u32[]{:S(2)}) %collective-permute-start) | collective-permute-done | bytes 3670048 | tf_op jit(solution)/shard_map/ppermute | solution.py:9
  91.5 7.2 %fusion.10 = bf16[1024,1024]{1,0:T(8,128)(2,1)} fusion(bf16[1,1024,1792]{2,1,0:T(8,128)(2,1)} %param.11, bf16[1,1024,1792]{2,1,0:T(8,128)(2,1)S(1)} %collective-permute-done), kind=kOutput, calls=%fused_computation.11 | convolution fusion | flops 3759144960 | bytes 9437184 | tf_op jit(solution)/shard_map/dot_general | solution.py:13
  98.7 0.0 copy-start.3
  98.7 0.0 copy-start.4
  98.7 0.0 copy-start.5
  98.7 0.0 reduce-scatter.2.cloned.1.call-update
  98.7 0.0 all-gather.2.cloned.1.call-start
  98.8 33.3 %reduce-scatter.2.cloned.1.call-done = bf16[256,1024]{1,0:T(8,128)(2,1)} async-done(((bf16[1024,1024]{1,0:T(8,128)(2,1)}), bf16[256,1024]{1,0:T(8,128)(2,1)}) %reduce-scatter.2.cloned.1.call-update) | async-done | bytes 524304 | tf_op jit(solution)/shard_map/reduce_scatter | solution.py:22
  132.1 0.0 copy-done.1
  132.1 0.0 copy-done.2
  132.1 1.6 fusion.17
  133.7 1.1 pad_maximum_fusion
  134.8 0.0 all-gather.2.cloned.1.call-update
  134.8 0.0 copy-done.3
  134.8 0.0 copy-done.4
  134.9 0.0 copy-done.5
  135.0 34.5 %all-gather.2.cloned.1.call-done = bf16[1024,2048]{1,0:T(8,128)(2,1)} async-done(((bf16[256,2048]{1,0:T(8,128)(2,1)}), bf16[1024,2048]{1,0:T(8,128)(2,1)}) %all-gather.2.cloned.1.call-update) | async-done | bytes 4194320 | tf_op jit(solution)/shard_map/all_gather | solution.py:37
  169.4 0.0 copy-start.6
  169.5 6.8 %fusion.2 = f32[1024,1792]{1,0:T(8,128)S(1)} fusion(bf16[1,1792,1024]{2,1,0:T(8,128)(2,1)} %param.12, bf16[1024,2048]{1,0:T(8,128)(2,1)} %all-gather.2.cloned.1.call-done), kind=kOutput, calls=%fused_computation.3 | convolution fusion | flops 3758096384 | bytes 13107200 | tf_op jit(solution)/shard_map/dot_general | solution.py:13
  176.3 0.0 copy-done.6
  176.3 0.0 copy-done.7
  176.3 4.0 %fusion = f32[1024,1792]{1,0:T(8,128)S(1)} fusion(bf16[1,1792,1024]{2,1,0:T(8,128)(2,1)S(1)} %copy-done.7, bf16[1024,2048]{1,0:T(8,128)(2,1)S(1)} %copy-done.6), kind=kOutput, calls=%fused_computation.1 | convolution fusion | flops 3758096384 | bytes 13107200 | tf_op jit(solution)/shard_map/dot_general | solution.py:13
  180.3 0.0 copy-done
  180.3 5.4 %fusion.7 = bf16[1,1024,1792]{2,1,0:T(8,128)(2,1)S(1)} fusion(f32[1024,1792]{1,0:T(8,128)S(1)} %fusion.2, f32[1024,1792]{1,0:T(8,128)S(1)} %fusion, bf16[1,1792,256]{2,1,0:T(8,128)(2,1)S(1)} %copy-done, f32[1024]{0:T(1024)S(1)} %bitcast.65, s32[1024]{0:T(1024)S(1)} %bitcast.73, f32[1024]{0:T(1024)S(1)} %bitcast.66, s32[1024]{0:T(1024)S(1)} %bitcast.74, ...), kind=kOutput, calls=%fused_computation.8 | convolution fusion | flops 951320576 | bytes 19333120 | tf_op jit(solution)/shard_map/dot_general | solution.py:13
  185.7 4.3 %collective-permute-start.1 = (bf16[1,1024,1792]{2,1,0:T(8,128)(2,1)S(1)}, bf16[1,1024,1792]{2,1,0:T(8,128)(2,1)S(1)}, u32[]{:S(2)}, u32[]{:S(2)}) collective-permute-start(bf16[1,1024,1792]{2,1,0:T(8,128)(2,1)S(1)} %fusion.7), channel_id=1, source_target_pairs={{0,28},{4,0},{8,4},{12,8},{16,12},{20,16},{24,20},{28,24},{1,29},{... | collective-permute-start | bytes 11010056 | tf_op jit(solution)/shard_map/ppermute | solution.py:9
  190.0 79.0 %collective-permute-done.1 = bf16[1,1024,1792]{2,1,0:T(8,128)(2,1)S(1)} collective-permute-done((bf16[1,1024,1792]{2,1,0:T(8,128)(2,1)S(1)}, bf16[1,1024,1792]{2,1,0:T(8,128)(2,1)S(1)}, u32[]{:S(2)}, u32[]{:S(2)}) %collective-permute-start.1) | collective-permute-done | bytes 3670048 | tf_op jit(solution)/shard_map/ppermute | solution.py:9
  269.0 1.8 copy.12
  (7 shorter events, 0.1 us)
Async XLA Ops:
  6.5 173.8 %copy-start = (bf16[1,1792,256]{2,1,0:T(8,128)(2,1)S(1)}, bf16[1,1792,256]{2,1,0:T(8,128)(2,1)}, u32[]{:S(2)}) copy-start(bf16[1,1792,256]{2,1,0:T(8,128)(2,1)} %param.14) | copy-start | bytes 2752516
  6.5 125.6 %copy-start.1 = (bf16[1,256,1024]{2,1,0:T(8,128)(2,1)S(1)}, bf16[1,256,1024]{2,1,0:T(8,128)(2,1)}, u32[]{:S(2)}) copy-start(bf16[1,256,1024]{2,1,0:T(8,128)(2,1)} %param.16) | copy-start | bytes 1572868
  6.5 125.6 %copy-start.2 = (bf16[1,256,1024]{2,1,0:T(8,128)(2,1)S(1)}, bf16[1,256,1024]{2,1,0:T(8,128)(2,1)}, u32[]{:S(2)}) copy-start(bf16[1,256,1024]{2,1,0:T(8,128)(2,1)} %param.15) | copy-start | bytes 1572868
  6.5 125.6 %reduce-scatter.2.cloned.1.call-start = ((), (), s32[]{:S(2)}) async-start(), calls=%async_computation.1 | async-start | bytes 2621440 | tf_op jit(solution)/shard_map/reduce_scatter | solution.py:22
  6.5 84.9 %collective-permute-start = (bf16[1,1024,1792]{2,1,0:T(8,128)(2,1)}, bf16[1,1024,1792]{2,1,0:T(8,128)(2,1)S(1)}, u32[]{:S(2)}, u32[]{:S(2)}) collective-permute-start(bf16[1,1024,1792]{2,1,0:T(8,128)(2,1)} %param.10), channel_id=1, source_target_pairs={{0,28},{4,0},{8,4},{12,8},{16,12},{20,16},{24,20},{28,24},{1,29},{... | collective-permute-start | bytes 11010056 | tf_op jit(solution)/shard_map/ppermute | solution.py:9
  98.7 36.1 %copy-start.3 = (f32[1,1024,8]{1,2,0:T(8,128)S(1)}, f32[1,1024,8]{1,2,0:T(8,128)}, u32[]{:S(2)}) copy-start(f32[1,1024,8]{1,2,0:T(8,128)} %param.18) | copy-start | bytes 98308
  98.7 36.2 %copy-start.4 = (f32[1,1024,8]{1,2,0:T(8,128)S(1)}, f32[1,1024,8]{1,2,0:T(8,128)}, u32[]{:S(2)}) copy-start(f32[1,1024,8]{1,2,0:T(8,128)} %param.17) | copy-start | bytes 98308
  98.7 36.3 %copy-start.5 = (s32[1,1024,8]{1,2,0:T(8,128)S(1)}, s32[1,1024,8]{1,2,0:T(8,128)}, u32[]{:S(2)}) copy-start(s32[1,1024,8]{1,2,0:T(8,128)} %param.19) | copy-start | bytes 98308
  98.7 70.7 %all-gather.2.cloned.1.call-start = ((), (), s32[]{:S(2)}) async-start(), calls=%async_computation.2 | async-start | bytes 5242880 | tf_op jit(solution)/shard_map/all_gather | solution.py:37
  169.4 6.8 %copy-start.6 = (bf16[1024,2048]{1,0:T(8,128)(2,1)S(1)}, bf16[1024,2048]{1,0:T(8,128)(2,1)}, u32[]{:S(2)}) copy-start(bf16[1024,2048]{1,0:T(8,128)(2,1)} %all-gather.2.cloned.1.call-done) | copy-start | bytes 12582916
  169.4 6.8 %copy-start.7 = (bf16[1,1792,1024]{2,1,0:T(8,128)(2,1)S(1)}, bf16[1,1792,1024]{2,1,0:T(8,128)(2,1)}, u32[]{:S(2)}) copy-start(bf16[1,1792,1024]{2,1,0:T(8,128)(2,1)} %param.13) | copy-start | bytes 11010052
  185.7 83.3 %collective-permute-start.1 = (bf16[1,1024,1792]{2,1,0:T(8,128)(2,1)S(1)}, bf16[1,1024,1792]{2,1,0:T(8,128)(2,1)S(1)}, u32[]{:S(2)}, u32[]{:S(2)}) collective-permute-start(bf16[1,1024,1792]{2,1,0:T(8,128)(2,1)S(1)} %fusion.7), channel_id=1, source_target_pairs={{0,28},{4,0},{8,4},{12,8},{16,12},{20,16},{24,20},{28,24},{1,29},{... | collective-permute-start | bytes 11010056 | tf_op jit(solution)/shard_map/ppermute | solution.py:9
Sparse Core Ops, SparseCore 0:
  98.8 33.2 reduce-scatter.1
  134.9 34.4 all-gather.1
where the time goes:
time: 278 us
  waiting for transfers between devices  226 us (81%)
  matrix products  23.4 us (8%)
  between operations  13.5 us (5%)
  starting transfers between devices  10.4 us (4%)
    ppermute x2, waiting for transfers between devices, passed_along(): lax.ppermute(x, axis, [(i, (i + by) % length) for i in range(length)])  158 us
    all_gather x1, waiting for transfers between devices, section_backward(): piece = lax.all_gather(stacked, 'expert', axis=0, tiled=True)  34.5 us
    reduce_scatter x1, waiting for transfers between devices, section_backward(): lax.psum_scatter(contract_last(incoming, w_down).astype(jnp.bfloat16).ast...  33.3 us
    dot_general x4, matrix products, contract_last(): lax.dot_general(left, right, (((1,), (1,)), ((), ())), preferred_element_...  23.4 us
    ppermute x2, starting transfers between devices, passed_along(): lax.ppermute(x, axis, [(i, (i + by) % length) for i in range(length)])  10.3 us
  transfers between devices with their start and end apart: 4, of which 4 were waited for; matrix products, arithmetic and copies ran while one was open for 0% of the time, Pallas kernels for 0%

commit v1 on v0

v1 whole, which is shorter than its diff:
```python
import jax
import jax.numpy as jnp
from jax import lax
from jax.sharding import PartitionSpec as P

CHUNKS = 4
IN_FLIGHT = 2


def back_one(x):
    length = lax.axis_size("pipe")
    return lax.ppermute(x, "pipe", [(i, (i - 1) % length) for i in range(length)])


def contract_last(left, right):
    return lax.dot_general(
        left, right, (((1,), (1,)), ((), ())), preferred_element_type=jnp.float32
    )


def sum_to_owners(blocks):
    n = lax.axis_size("expert")
    me = lax.axis_index("expert")
    total = lax.dynamic_index_in_dim(blocks, me, keepdims=False).astype(jnp.float32)
    for step in range(1, n):
        part = lax.dynamic_index_in_dim(blocks, (me + step) % n, keepdims=False)
        part = lax.ppermute(part, "expert", [(i, (i + step) % n) for i in range(n)])
        total = total + part.astype(jnp.float32)
    return total


def gather_chips(own):
    n = lax.axis_size("expert")
    chips, chip = n // 2, lax.axis_index("expert") // 2
    held = lax.dynamic_update_index_in_dim(
        jnp.zeros((chips,) + own.shape, own.dtype), own, chip, 0
    )
    for step in range(1, chips):
        part = lax.ppermute(own, "expert", [(i, (i + 2 * step) % n) for i in range(n)])
        held = lax.dynamic_update_index_in_dim(held, part, (chip - step) % chips, 0)
    return held


def gather_cores(held):
    n = lax.axis_size("expert")
    core = lax.axis_index("expert") % 2
    other = lax.ppermute(held, "expert", [(i, i ^ 1) for i in range(n)])
    first = jnp.where(core == 0, held, other)
    second = jnp.where(core == 0, other, held)
    return jnp.stack([first, second], axis=1).reshape(n, *held.shape[1:])


def in_order(later, earlier):
    return lax.optimization_barrier((later, earlier))


def routed_grad(grad_gate, scores, chosen, n_experts):
    total = jnp.sum(scores, axis=-1, keepdims=True)
    mixed = jnp.sum(grad_gate * scores, axis=-1, keepdims=True)
    logit_grad = 2.5 * (grad_gate - mixed / total) / total * scores * (1.0 - scores)
    columns = lax.broadcasted_iota(jnp.int32, (1, n_experts), 1)
    dense = jnp.zeros((grad_gate.shape[0], n_experts), jnp.float32)
    for slot in range(grad_gate.shape[1]):
        dense = dense + jnp.where(
            chosen[:, slot : slot + 1] == columns, logit_grad[:, slot : slot + 1], 0.0
        )
    return dense.astype(jnp.bfloat16)


def shards(
    upstream,
    shared_down,
    shared_gate,
    shared_up,
    router_weight,
    gate_pre,
    up_pre,
    gate_grad,
    gate_scores,
    expert_ids,
):
    n = lax.axis_size("expert")
    tokens, width = upstream.shape[1:]
    hidden = shared_down.shape[1]
    rows = tokens // n
    chunks = min(CHUNKS, rows // 16)
    part = rows // chunks
    w_down, w_gate, w_up, w_router = (
        shared_down[0],
        shared_gate[0],
        shared_up[0],
        router_weight[0],
    )
    dense = routed_grad(gate_grad[0], gate_scores[0], expert_ids[0], w_router.shape[1])
    dense = dense.reshape(n, rows, -1)
    grads = upstream.reshape(n, rows, width)
    arrived = []
    for c in range(chunks):
        piece = grads[:, c * part : (c + 1) * part].reshape(n * part, width)
        if c >= IN_FLIGHT:
            piece, arrived[c - IN_FLIGHT] = in_order(piece, arrived[c - IN_FLIGHT])
        arrived.append(back_one(piece))

    def first_product(c):
        partial = contract_last(arrived[c], w_down).astype(jnp.bfloat16)
        return partial.reshape(n, part, hidden)

    def activation(c, hidden_grad):
        here = slice(c * part, (c + 1) * part)
        act_a = gate_pre[0, here].astype(jnp.float32)
        act_b = up_pre[0, here].astype(jnp.float32)
        sigma = jax.nn.sigmoid(act_a)
        gate_part = hidden_grad * act_b * sigma * (1.0 + act_a * (1.0 - sigma))
        up_part = hidden_grad * act_a * sigma
        return jnp.concatenate([gate_part, up_part], axis=1).astype(jnp.bfloat16)

    def second_product(c, both):
        both = both.reshape(n * part, 2 * hidden)
        routed = dense[:, c * part : (c + 1) * part].reshape(n * part, -1)
        result = contract_last(both[:, :hidden], w_gate)
        result = result + contract_last(both[:, hidden:], w_up)
        result = result + contract_last(routed, w_router)
        return result.astype(jnp.bfloat16)

    out = jnp.zeros((n, rows, width), jnp.bfloat16)
    own = activation(0, sum_to_owners(first_product(0)))
    for c in range(chunks):
        by_chip = gather_chips(own)
        if c + 1 < chunks:
            arrived[c + 1], own = in_order(arrived[c + 1], own)
            partial = first_product(c + 1)
            partial, by_chip = in_order(partial, by_chip)
            hidden_grad = sum_to_owners(partial)
        result = second_product(c, gather_cores(by_chip))
        if c + 1 < chunks:
            hidden_grad, result = in_order(hidden_grad, result)
            own = activation(c + 1, hidden_grad)
        result = back_one(result).reshape(n, part, width)
        out = lax.dynamic_update_slice(out, result, (0, c * part, 0))
    return out.reshape(1, tokens, width)


def solution(mesh):
    in_specs = (
        P("pipe", None, "expert"),
        P("pipe", None, "expert"),
        P("pipe", "expert", None),
        P("pipe", "expert", None),
        P("pipe", "expert", None),
        P("pipe", "expert", None),
        P("pipe", "expert", None),
        P("pipe", None, None),
        P("pipe", None, None),
        P("pipe", None, None),
    )
    out_specs = P("pipe", None, "expert")
    return jax.shard_map(shards, mesh=mesh, in_specs=in_specs, out_specs=out_specs, check_vma=False)
```

time: 278 us -> 222 us (0.80)
  waiting for transfers between devices: 226 us -> 138 us
  starting transfers between devices: 10.4 us -> 38.8 us
  local copies, waits for them, and re-layouts: 1.92 us -> 16.2 us
  between operations: 13.5 us -> 0.76 us
  other arithmetic: 2.71 us -> 7.59 us
  matrix products: 23.4 us -> 20.2 us
    all_gather x1 -> x0, waiting for transfers between devices: 34.5 us -> none  [section_backward(): piece = lax.all_gather(stacked, 'expert', axis=0, tiled=True)]
    reduce_scatter x1 -> x0, waiting for transfers between devices: 33.3 us -> none  [section_backward(): lax.psum_scatter(contract_last(incoming, w_down).astype(jnp.bfloat16).ast...]
    ppermute x2 -> x28, starting transfers between devices: 10.3 us -> 38.8 us  [the longest x8 23.8 us: back_one(): lax.ppermute(x, 'pipe', [(i, (i - 1) % length) for i in range(length)])]
    ppermute x2 -> x28, waiting for transfers between devices: 158 us -> 138 us  [the longest x8 120 us: back_one(): lax.ppermute(x, 'pipe', [(i, (i - 1) % length) for i in range(length)])]
    slice x2 -> x4, local copies, waits for them, and re-layouts: 0.05 us -> 3.93 us  [the longest x1 3.71 us: shards(): piece = grads[:, c * part:(c + 1) * part].reshape(n * part, width)]
    broadcast_in_dim x0 -> x8, local copies, waits for them, and re-layouts: none -> 3.6 us  [routed_grad(): jnp.where(chosen[:, slot:slot + 1] == columns, logit_grad[:, slot:slot +...]
    eq x0 -> x8, local copies, waits for them, and re-layouts: none -> 3.59 us  [routed_grad(): chosen[:, slot:slot + 1] == columns]
    dot_general x4 -> x16, matrix products: 23.4 us -> 20.2 us  [contract_last(): lax.dot_general(left, right, (((1,), (1,)), ((), ())), preferred_element_...]
  transfers between devices with their start and end apart: 4 -> 28, of which waited for: 4 -> 14; matrix products, arithmetic and copies ran while one was open for 0% -> 15% of each run, Pallas kernels for 0% -> 0%
where the time goes in v1:
time: 222 us
  waiting for transfers between devices  138 us (62%)
  starting transfers between devices  38.8 us (17%)
  matrix products  20.2 us (9%)
  local copies, waits for them, and re-layouts  16.2 us (7%)
  other arithmetic  7.59 us (3%)
    ppermute x8, waiting for transfers between devices, back_one(): lax.ppermute(x, 'pipe', [(i, (i - 1) % length) for i in range(length)])  120 us
    ppermute x8, starting transfers between devices, back_one(): lax.ppermute(x, 'pipe', [(i, (i - 1) % length) for i in range(length)])  23.8 us
    dot_general x16, matrix products, contract_last(): lax.dot_general(left, right, (((1,), (1,)), ((), ())), preferred_element_...  20.2 us
    ppermute x12, waiting for transfers between devices, sum_to_owners(): part = lax.ppermute(part, 'expert', [(i, (i + step) % n) for i in range(n)])  10.6 us
    ppermute x4, waiting for transfers between devices, gather_chips(): lax.ppermute(own, 'expert', [(i, (i + 2 * step) % n) for i in range(n)])  7.42 us
    ppermute x12, starting transfers between devices, sum_to_owners(): part = lax.ppermute(part, 'expert', [(i, (i + step) % n) for i in range(n)])  7.35 us
    ppermute x4, starting transfers between devices, gather_chips(): lax.ppermute(own, 'expert', [(i, (i + 2 * step) % n) for i in range(n)])  5.57 us
    convert_element_type x1, other arithmetic, routed_grad(): return dense.astype(jnp.bfloat16)  4.62 us
  transfers between devices with their start and end apart: 28, of which 14 were waited for; matrix products, arithmetic and copies ran while one was open for 15% of the time, Pallas kernels for 0%

profile of v1, /device:TPU:0, one launch (start us, length us, event | category | flops | bytes accessed | tf_op | source)
XLA Modules:
  0.0 221.8 jit_solution(6739522810948293812)
XLA Ops:
  0.0 3.7 %fusion.112 = (bf16[4,64,1792]{2,1,0:T(8,128)(2,1)}, bf16[4,64,1792]{2,1,0:T(8,128)(2,1)S(1)}, bf16[4,64,1792]{2,1,0:T(8,128)(2,1)}, bf16[4,64,1792]{2,1,0:T(8,128)(2,1)S(1)}) fusion(bf16[4,256,1792]{2,1,0:T(8,128)(2,1)} %bitcast.204), kind=kLoop, calls=%fused_computation.188 | loop fusion | bytes 7340032 | tf_op jit(solution)/shard_map/slice | solution.py:99
  3.7 6.0 %collective-permute-start.1 = (bf16[256,1792]{1,0:T(8,128)(2,1)}, bf16[256,1792]{1,0:T(8,128)(2,1)}, u32[]{:S(2)}, u32[]{:S(2)}) collective-permute-start(bf16[256,1792]{1,0:T(8,128)(2,1)} %bitcast.4), channel_id=1, source_target_pairs={{0,28},{4,0},{8,4},{12,8},{16,12},{20,16},{24,20},{28,24},{1,29},{... | collective-permute-start | bytes 2752520 | tf_op jit(solution)/shard_map/ppermute | solution.py:12
  17.8 13.0 %collective-permute-done.1 = bf16[256,1792]{1,0:T(8,128)(2,1)} collective-permute-done((bf16[256,1792]{1,0:T(8,128)(2,1)}, bf16[256,1792]{1,0:T(8,128)(2,1)}, u32[]{:S(2)}, u32[]{:S(2)}) %collective-permute-start.1) | collective-permute-done | bytes 917536 | tf_op jit(solution)/shard_map/ppermute | solution.py:12
  30.8 3.5 %fusion.40 = bf16[256,1024]{1,0:T(8,128)(2,1)S(1)} fusion(bf16[256,1792]{1,0:T(8,128)(2,1)} %collective-permute-done.1, bf16[1,1024,1792]{2,1,0:T(8,128)(2,1)} %param.11), kind=kOutput, calls=%fused_computation.36 | convolution fusion | flops 939786240 | bytes 5111808 | tf_op jit(solution)/shard_map/dot_general | solution.py:16
  35.0 1.5 collective-permute-start.3
  36.8 4.6 %add_convert_fusion = bf16[4,256,256]{2,1,0:T(8,128)(2,1)S(1)} fusion(f32[4,256]{1,0:T(4,128)S(1)} %broadcast_in_dim.106, s32[4,256]{1,0:T(4,128)S(1)} %eq.188, f32[4,256]{1,0:T(4,128)S(1)} %broadcast_in_dim.104, s32[4,256]{1,0:T(4,128)S(1)} %eq.184, f32[4,256]{1,0:T(4,128)} %broadcast_in_dim.102, s32[4,256]{1,0:T(4,128)} %eq.180, ...), kind=kLoop, calls=%fused_computation.44 | loop fusion | flops 6291456 | bytes 589824 | tf_op jit(solution)/shard_map/convert_element_type | solution.py:67
  41.5 7.8 %collective-permute-done = bf16[256,1792]{1,0:T(8,128)(2,1)} collective-permute-done((bf16[256,1792]{1,0:T(8,128)(2,1)}, bf16[256,1792]{1,0:T(8,128)(2,1)}, u32[]{:S(2)}, u32[]{:S(2)}) %collective-permute-start) | collective-permute-done | bytes 917536 | tf_op jit(solution)/shard_map/ppermute | solution.py:12
  49.3 1.4 fusion.69
  50.7 1.6 collective-permute-start.5
  52.3 3.5 %fusion.43 = bf16[256,1024]{1,0:T(8,128)(2,1)S(1)} fusion(bf16[256,1792]{1,0:T(8,128)(2,1)} %collective-permute-done, bf16[1,1024,1792]{2,1,0:T(8,128)(2,1)} %param.11), kind=kOutput, calls=%fused_computation.37 | convolution fusion | flops 939786240 | bytes 5111808 | tf_op jit(solution)/shard_map/dot_general | solution.py:16
  55.9 2.1 collective-permute-done.5
  58.1 1.7 collective-permute-start.8
  60.3 5.2 %collective-permute-start.11 = (bf16[256,1792]{1,0:T(8,128)(2,1)S(1)}, bf16[256,1792]{1,0:T(8,128)(2,1)S(1)}, u32[]{:S(2)}, u32[]{:S(2)}) collective-permute-start(bf16[256,1792]{1,0:T(8,128)(2,1)S(1)} %bitcast.222), channel_id=1, source_target_pairs={{0,28},{4,0},{8,4},{12,8},{16,12},{20,16},{24,20},{28,24},{1,29},{... | collective-permute-start | bytes 2752520 | tf_op jit(solution)/shard_map/ppermute | solution.py:12
  65.6 1.4 collective-permute-done.7
  71.7 1.6 collective-permute-start.12
  73.3 12.4 %collective-permute-done.11 = bf16[256,1792]{1,0:T(8,128)(2,1)S(1)} collective-permute-done((bf16[256,1792]{1,0:T(8,128)(2,1)S(1)}, bf16[256,1792]{1,0:T(8,128)(2,1)S(1)}, u32[]{:S(2)}, u32[]{:S(2)}) %collective-permute-start.11) | collective-permute-done | bytes 917536 | tf_op jit(solution)/shard_map/ppermute | solution.py:12
  87.8 1.2 collective-permute-start.15
  89.5 4.9 %collective-permute-start.18 = (bf16[256,1792]{1,0:T(8,128)(2,1)S(1)}, bf16[256,1792]{1,0:T(8,128)(2,1)S(1)}, u32[]{:S(2)}, u32[]{:S(2)}) collective-permute-start(bf16[256,1792]{1,0:T(8,128)(2,1)S(1)} %bitcast.221), channel_id=1, source_target_pairs={{0,28},{4,0},{8,4},{12,8},{16,12},{20,16},{24,20},{28,24},{1,29},{... | collective-permute-start | bytes 2752520 | tf_op jit(solution)/shard_map/ppermute | solution.py:12
  94.5 2.1 collective-permute-done.14
  101.1 13.2 %collective-permute-done.18 = bf16[256,1792]{1,0:T(8,128)(2,1)S(1)} collective-permute-done((bf16[256,1792]{1,0:T(8,128)(2,1)S(1)}, bf16[256,1792]{1,0:T(8,128)(2,1)S(1)}, u32[]{:S(2)}, u32[]{:S(2)}) %collective-permute-start.18) | collective-permute-done | bytes 917536 | tf_op jit(solution)/shard_map/ppermute | solution.py:12
  116.7 1.2 collective-permute-start.22
  118.4 3.3 %collective-permute-done.22 = bf16[64,1024]{1,0:T(8,128)(2,1)S(1)} collective-permute-done((bf16[64,1024]{1,0:T(8,128)(2,1)S(1)}, bf16[64,1024]{1,0:T(8,128)(2,1)S(1)}, u32[]{:S(2)}, u32[]{:S(2)}) %collective-permute-start.22) | collective-permute-done | bytes 131104 | tf_op jit(solution)/shard_map/ppermute | solution.py:27
  121.7 3.7 %collective-permute-done.21 = bf16[64,1024]{1,0:T(8,128)(2,1)S(1)} collective-permute-done((bf16[64,1024]{1,0:T(8,128)(2,1)S(1)}, bf16[64,1024]{1,0:T(8,128)(2,1)S(1)}, u32[]{:S(2)}, u32[]{:S(2)}) %collective-permute-start.21) | collective-permute-done | bytes 131104 | tf_op jit(solution)/shard_map/ppermute | solution.py:27
  128.8 1.2 collective-permute-start.25
  130.1 5.3 %collective-permute-done.25 = bf16[64,2048]{1,0:T(8,128)(2,1)S(1)} collective-permute-done((bf16[64,2048]{1,0:T(8,128)(2,1)S(1)}, bf16[64,2048]{1,0:T(8,128)(2,1)S(1)}, u32[]{:S(2)}, u32[]{:S(2)}) %collective-permute-start.25) | collective-permute-done | bytes 262176 | tf_op jit(solution)/shard_map/ppermute | solution.py:39
  135.5 5.2 %collective-permute-start.10 = (bf16[256,1792]{1,0:T(8,128)(2,1)S(1)}, bf16[256,1792]{1,0:T(8,128)(2,1)S(1)}, u32[]{:S(2)}, u32[]{:S(2)}) collective-permute-start(bf16[256,1792]{1,0:T(8,128)(2,1)S(1)} %fusion.36), channel_id=1, source_target_pairs={{0,28},{4,0},{8,4},{12,8},{16,12},{20,16},{24,20},{28,24},{1,29},{... | collective-permute-start | bytes 2752520 | tf_op jit(solution)/shard_map/ppermute | solution.py:12
  143.9 1.7 collective-permute-start.27
  145.7 15.7 %collective-permute-done.10 = bf16[256,1792]{1,0:T(8,128)(2,1)S(1)} collective-permute-done((bf16[256,1792]{1,0:T(8,128)(2,1)S(1)}, bf16[256,1792]{1,0:T(8,128)(2,1)S(1)}, u32[]{:S(2)}, u32[]{:S(2)}) %collective-permute-start.10) | collective-permute-done | bytes 917536 | tf_op jit(solution)/shard_map/ppermute | solution.py:12
  161.6 19.4 %collective-permute-done.17 = bf16[256,1792]{1,0:T(8,128)(2,1)S(1)} collective-permute-done((bf16[256,1792]{1,0:T(8,128)(2,1)S(1)}, bf16[256,1792]{1,0:T(8,128)(2,1)S(1)}, u32[]{:S(2)}, u32[]{:S(2)}) %collective-permute-start.17) | collective-permute-done | bytes 917536 | tf_op jit(solution)/shard_map/ppermute | solution.py:12
  181.1 19.6 %collective-permute-done.24 = bf16[256,1792]{1,0:T(8,128)(2,1)S(1)} collective-permute-done((bf16[256,1792]{1,0:T(8,128)(2,1)S(1)}, bf16[256,1792]{1,0:T(8,128)(2,1)S(1)}, u32[]{:S(2)}, u32[]{:S(2)}) %collective-permute-start.24) | collective-permute-done | bytes 917536 | tf_op jit(solution)/shard_map/ppermute | solution.py:12
  200.8 19.1 %collective-permute-done.27 = bf16[256,1792]{1,0:T(8,128)(2,1)S(1)} collective-permute-done((bf16[256,1792]{1,0:T(8,128)(2,1)S(1)}, bf16[256,1792]{1,0:T(8,128)(2,1)S(1)}, u32[]{:S(2)}, u32[]{:S(2)}) %collective-permute-start.27) | collective-permute-done | bytes 917536 | tf_op jit(solution)/shard_map/ppermute | solution.py:12
  220.0 1.8 copy-done.2
  (145 shorter events, 31.2 us)
Async XLA Ops:
  0.0 70.4 %copy-start = (bf16[1,1792,256]{2,1,0:T(8,128)(2,1)S(1)}, bf16[1,1792,256]{2,1,0:T(8,128)(2,1)}, u32[]{:S(2)}) copy-start(bf16[1,1792,256]{2,1,0:T(8,128)(2,1)} %param.14) | copy-start | bytes 2752516
  3.7 27.1 %collective-permute-start.1 = (bf16[256,1792]{1,0:T(8,128)(2,1)}, bf16[256,1792]{1,0:T(8,128)(2,1)}, u32[]{:S(2)}, u32[]{:S(2)}) collective-permute-start(bf16[256,1792]{1,0:T(8,128)(2,1)} %bitcast.4), channel_id=1, source_target_pairs={{0,28},{4,0},{8,4},{12,8},{16,12},{20,16},{24,20},{28,24},{1,29},{... | collective-permute-start | bytes 2752520 | tf_op jit(solution)/shard_map/ppermute | solution.py:12
  9.7 39.6 %collective-permute-start = (bf16[256,1792]{1,0:T(8,128)(2,1)}, bf16[256,1792]{1,0:T(8,128)(2,1)}, u32[]{:S(2)}, u32[]{:S(2)}) collective-permute-start(bf16[256,1792]{1,0:T(8,128)(2,1)} %bitcast.2), channel_id=1, source_target_pairs={{0,28},{4,0},{8,4},{12,8},{16,12},{20,16},{24,20},{28,24},{1,29},{... | collective-permute-start | bytes 2752520 | tf_op jit(solution)/shard_map/ppermute | solution.py:12
  17.8 19.1 %copy-start.13 = (f32[4,256]{1,0:T(4,128)S(1)}, f32[4,256]{1,0:T(4,128)}, u32[]{:S(2)}) copy-start(f32[4,256]{1,0:T(4,128)} %broadcast_in_dim.94) | copy-start | bytes 12292
  17.8 19.1 %copy-start.14 = (s32[4,256]{1,0:T(4,128)S(1)}, s32[4,256]{1,0:T(4,128)}, u32[]{:S(2)}) copy-start(s32[4,256]{1,0:T(4,128)} %eq.164) | copy-start | bytes 12292
  17.8 19.1 %copy-start.15 = (f32[4,256]{1,0:T(4,128)S(1)}, f32[4,256]{1,0:T(4,128)}, u32[]{:S(2)}) copy-start(f32[4,256]{1,0:T(4,128)} %broadcast_in_dim.91) | copy-start | bytes 12292
  35.0 14.3 %collective-permute-start.4 = (bf16[64,1024]{1,0:T(8,128)(2,1)}, bf16[64,1024]{1,0:T(8,128)(2,1)}, u32[]{:S(2)}, u32[]{:S(2)}) collective-permute-start(bf16[64,1024]{1,0:T(8,128)(2,1)} %get-tuple-element.93), channel_id=1, source_target_pairs={{0,3},{1,0},{2,1},{3,2},{4,7},{5,4},{6,5},{7,6},{8,11},{9,8},{10,9... | collective-permute-start | bytes 393224 | tf_op jit(solution)/shard_map/ppermute | solution.py:27
  35.0 14.3 %collective-permute-start.3 = (bf16[64,1024]{1,0:T(8,128)(2,1)S(1)}, bf16[64,1024]{1,0:T(8,128)(2,1)}, u32[]{:S(2)}, u32[]{:S(2)}) collective-permute-start(bf16[64,1024]{1,0:T(8,128)(2,1)S(1)} %get-tuple-element.94), channel_id=1, source_target_pairs={{0,2},{1,3},{2,0},{3,1},{4,6},{5,7},{6,4},{7,5},{8,10},{9,11},{10,... | collective-permute-start | bytes 393224 | tf_op jit(solution)/shard_map/ppermute | solution.py:27
  36.6 12.7 %collective-permute-start.2 = (bf16[64,1024]{1,0:T(8,128)(2,1)S(1)}, bf16[64,1024]{1,0:T(8,128)(2,1)}, u32[]{:S(2)}, u32[]{:S(2)}) collective-permute-start(bf16[64,1024]{1,0:T(8,128)(2,1)S(1)} %get-tuple-element.92), channel_id=1, source_target_pairs={{0,1},{1,2},{2,3},{3,0},{4,5},{5,6},{6,7},{7,4},{8,9},{9,10},{10,1... | collective-permute-start | bytes 393224 | tf_op jit(solution)/shard_map/ppermute | solution.py:27
  50.7 7.2 %collective-permute-start.5 = (bf16[64,2048]{1,0:T(8,128)(2,1)S(1)}, bf16[64,2048]{1,0:T(8,128)(2,1)S(1)}, u32[]{:S(2)}, u32[]{:S(2)}) collective-permute-start(bf16[64,2048]{1,0:T(8,128)(2,1)S(1)} %pad_maximum_fusion.4), channel_id=1, source_target_pairs={{0,2},{1,3},{2,0},{3,1},{4,6},{5,7},{6,4},{7,5},{8,10},{9,11},{10,... | collective-permute-start | bytes 786440 | tf_op jit(solution)/shard_map/ppermute | solution.py:39
  58.0 9.0 %collective-permute-start.9 = (bf16[2,64,2048]{2,1,0:T(8,128)(2,1)S(1)}, bf16[2,64,2048]{2,1,0:T(8,128)(2,1)S(1)}, u32[]{:S(2)}, u32[]{:S(2)}) collective-permute-start(bf16[2,64,2048]{2,1,0:T(8,128)(2,1)S(1)} %bitcast_dynamic-update-slice_fusion.3), channel_id=1, source_target_pairs={{0,1},{1,0},{2,3},{3,2},{4,5},{5,4},{6,7},{7,6},{8,9},{9,8},{10,11... | collective-permute-start | bytes 1572872 | tf_op jit(solution)/shard_map/ppermute | solution.py:47
  58.1 7.4 %collective-permute-start.8 = (bf16[64,1024]{1,0:T(8,128)(2,1)S(1)}, bf16[64,1024]{1,0:T(8,128)(2,1)S(1)}, u32[]{:S(2)}, u32[]{:S(2)}) collective-permute-start(bf16[64,1024]{1,0:T(8,128)(2,1)S(1)} %get-tuple-element.90), channel_id=1, source_target_pairs={{0,3},{1,0},{2,1},{3,2},{4,7},{5,4},{6,5},{7,6},{8,11},{9,8},{10,9... | collective-permute-start | bytes 393224 | tf_op jit(solution)/shard_map/ppermute | solution.py:27
  59.8 7.2 %collective-permute-start.7 = (bf16[64,1024]{1,0:T(8,128)(2,1)S(1)}, bf16[64,1024]{1,0:T(8,128)(2,1)S(1)}, u32[]{:S(2)}, u32[]{:S(2)}) collective-permute-start(bf16[64,1024]{1,0:T(8,128)(2,1)S(1)} %get-tuple-element.91), channel_id=1, source_target_pairs={{0,2},{1,3},{2,0},{3,1},{4,6},{5,7},{6,4},{7,5},{8,10},{9,11},{10,... | collective-permute-start | bytes 393224 | tf_op jit(solution)/shard_map/ppermute | solution.py:27
  60.3 6.7 %collective-permute-start.6 = (bf16[64,1024]{1,0:T(8,128)(2,1)S(1)}, bf16[64,1024]{1,0:T(8,128)(2,1)S(1)}, u32[]{:S(2)}, u32[]{:S(2)}) collective-permute-start(bf16[64,1024]{1,0:T(8,128)(2,1)S(1)} %get-tuple-element.89), channel_id=1, source_target_pairs={{0,1},{1,2},{2,3},{3,0},{4,5},{5,6},{6,7},{7,4},{8,9},{9,10},{10,1... | collective-permute-start | bytes 393224 | tf_op jit(solution)/shard_map/ppermute | solution.py:27
  60.3 25.4 %collective-permute-start.11 = (bf16[256,1792]{1,0:T(8,128)(2,1)S(1)}, bf16[256,1792]{1,0:T(8,128)(2,1)S(1)}, u32[]{:S(2)}, u32[]{:S(2)}) collective-permute-start(bf16[256,1792]{1,0:T(8,128)(2,1)S(1)} %bitcast.222), channel_id=1, source_target_pairs={{0,28},{4,0},{8,4},{12,8},{16,12},{20,16},{24,20},{28,24},{1,29},{... | collective-permute-start | bytes 2752520 | tf_op jit(solution)/shard_map/ppermute | solution.py:12
  71.7 15.2 %collective-permute-start.12 = (bf16[64,2048]{1,0:T(8,128)(2,1)S(1)}, bf16[64,2048]{1,0:T(8,128)(2,1)S(1)}, u32[]{:S(2)}, u32[]{:S(2)}) collective-permute-start(bf16[64,2048]{1,0:T(8,128)(2,1)S(1)} %pad_maximum_fusion.5), channel_id=1, source_target_pairs={{0,2},{1,3},{2,0},{3,1},{4,6},{5,7},{6,4},{7,5},{8,10},{9,11},{10,... | collective-permute-start | bytes 786440 | tf_op jit(solution)/shard_map/ppermute | solution.py:39
  87.0 9.7 %collective-permute-start.16 = (bf16[2,64,2048]{2,1,0:T(8,128)(2,1)S(1)}, bf16[2,64,2048]{2,1,0:T(8,128)(2,1)S(1)}, u32[]{:S(2)}, u32[]{:S(2)}) collective-permute-start(bf16[2,64,2048]{2,1,0:T(8,128)(2,1)S(1)} %bitcast_dynamic-update-slice_fusion.2), channel_id=1, source_target_pairs={{0,1},{1,0},{2,3},{3,2},{4,5},{5,4},{6,7},{7,6},{8,9},{9,8},{10,11... | collective-permute-start | bytes 1572872 | tf_op jit(solution)/shard_map/ppermute | solution.py:47
  87.8 6.6 %collective-permute-start.15 = (bf16[64,1024]{1,0:T(8,128)(2,1)S(1)}, bf16[64,1024]{1,0:T(8,128)(2,1)S(1)}, u32[]{:S(2)}, u32[]{:S(2)}) collective-permute-start(bf16[64,1024]{1,0:T(8,128)(2,1)S(1)} %get-tuple-element.87), channel_id=1, source_target_pairs={{0,3},{1,0},{2,1},{3,2},{4,7},{5,4},{6,5},{7,6},{8,11},{9,8},{10,9... | collective-permute-start | bytes 393224 | tf_op jit(solution)/shard_map/ppermute | solution.py:27
  89.0 7.6 %collective-permute-start.14 = (bf16[64,1024]{1,0:T(8,128)(2,1)S(1)}, bf16[64,1024]{1,0:T(8,128)(2,1)S(1)}, u32[]{:S(2)}, u32[]{:S(2)}) collective-permute-start(bf16[64,1024]{1,0:T(8,128)(2,1)S(1)} %get-tuple-element.88), channel_id=1, source_target_pairs={{0,2},{1,3},{2,0},{3,1},{4,6},{5,7},{6,4},{7,5},{8,10},{9,11},{10,... | collective-permute-start | bytes 393224 | tf_op jit(solution)/shard_map/ppermute | solution.py:27
  89.5 7.1 %collective-permute-start.13 = (bf16[64,1024]{1,0:T(8,128)(2,1)S(1)}, bf16[64,1024]{1,0:T(8,128)(2,1)S(1)}, u32[]{:S(2)}, u32[]{:S(2)}) collective-permute-start(bf16[64,1024]{1,0:T(8,128)(2,1)S(1)} %get-tuple-element.86), channel_id=1, source_target_pairs={{0,1},{1,2},{2,3},{3,0},{4,5},{5,6},{6,7},{7,4},{8,9},{9,10},{10,1... | collective-permute-start | bytes 393224 | tf_op jit(solution)/shard_map/ppermute | solution.py:27
  89.5 24.8 %collective-permute-start.18 = (bf16[256,1792]{1,0:T(8,128)(2,1)S(1)}, bf16[256,1792]{1,0:T(8,128)(2,1)S(1)}, u32[]{:S(2)}, u32[]{:S(2)}) collective-permute-start(bf16[256,1792]{1,0:T(8,128)(2,1)S(1)} %bitcast.221), channel_id=1, source_target_pairs={{0,28},{4,0},{8,4},{12,8},{16,12},{20,16},{24,20},{28,24},{1,29},{... | collective-permute-start | bytes 2752520 | tf_op jit(solution)/shard_map/ppermute | solution.py:12
  99.9 15.6 %collective-permute-start.19 = (bf16[64,2048]{1,0:T(8,128)(2,1)S(1)}, bf16[64,2048]{1,0:T(8,128)(2,1)S(1)}, u32[]{:S(2)}, u32[]{:S(2)}) collective-permute-start(bf16[64,2048]{1,0:T(8,128)(2,1)S(1)} %pad_maximum_fusion.6), channel_id=1, source_target_pairs={{0,2},{1,3},{2,0},{3,1},{4,6},{5,7},{6,4},{7,5},{8,10},{9,11},{10,... | collective-permute-start | bytes 786440 | tf_op jit(solution)/shard_map/ppermute | solution.py:39
  115.6 10.0 %collective-permute-start.23 = (bf16[2,64,2048]{2,1,0:T(8,128)(2,1)S(1)}, bf16[2,64,2048]{2,1,0:T(8,128)(2,1)S(1)}, u32[]{:S(2)}, u32[]{:S(2)}) collective-permute-start(bf16[2,64,2048]{2,1,0:T(8,128)(2,1)S(1)} %bitcast_dynamic-update-slice_fusion.1), channel_id=1, source_target_pairs={{0,1},{1,0},{2,3},{3,2},{4,5},{5,4},{6,7},{7,6},{8,9},{9,8},{10,11... | collective-permute-start | bytes 1572872 | tf_op jit(solution)/shard_map/ppermute | solution.py:47
  116.7 5.0 %collective-permute-start.22 = (bf16[64,1024]{1,0:T(8,128)(2,1)S(1)}, bf16[64,1024]{1,0:T(8,128)(2,1)S(1)}, u32[]{:S(2)}, u32[]{:S(2)}) collective-permute-start(bf16[64,1024]{1,0:T(8,128)(2,1)S(1)} %get-tuple-element.84), channel_id=1, source_target_pairs={{0,3},{1,0},{2,1},{3,2},{4,7},{5,4},{6,5},{7,6},{8,11},{9,8},{10,9... | collective-permute-start | bytes 393224 | tf_op jit(solution)/shard_map/ppermute | solution.py:27
  117.9 7.6 %collective-permute-start.21 = (bf16[64,1024]{1,0:T(8,128)(2,1)S(1)}, bf16[64,1024]{1,0:T(8,128)(2,1)S(1)}, u32[]{:S(2)}, u32[]{:S(2)}) collective-permute-start(bf16[64,1024]{1,0:T(8,128)(2,1)S(1)} %get-tuple-element.85), channel_id=1, source_target_pairs={{0,2},{1,3},{2,0},{3,1},{4,6},{5,7},{6,4},{7,5},{8,10},{9,11},{10,... | collective-permute-start | bytes 393224 | tf_op jit(solution)/shard_map/ppermute | solution.py:27
  118.4 7.1 %collective-permute-start.20 = (bf16[64,1024]{1,0:T(8,128)(2,1)S(1)}, bf16[64,1024]{1,0:T(8,128)(2,1)S(1)}, u32[]{:S(2)}, u32[]{:S(2)}) collective-permute-start(bf16[64,1024]{1,0:T(8,128)(2,1)S(1)} %get-tuple-element.83), channel_id=1, source_target_pairs={{0,1},{1,2},{2,3},{3,0},{4,5},{5,6},{6,7},{7,4},{8,9},{9,10},{10,1... | collective-permute-start | bytes 393224 | tf_op jit(solution)/shard_map/ppermute | solution.py:27
  128.8 6.6 %collective-permute-start.25 = (bf16[64,2048]{1,0:T(8,128)(2,1)S(1)}, bf16[64,2048]{1,0:T(8,128)(2,1)S(1)}, u32[]{:S(2)}, u32[]{:S(2)}) collective-permute-start(bf16[64,2048]{1,0:T(8,128)(2,1)S(1)} %pad_maximum_fusion.7), channel_id=1, source_target_pairs={{0,2},{1,3},{2,0},{3,1},{4,6},{5,7},{6,4},{7,5},{8,10},{9,11},{10,... | collective-permute-start | bytes 786440 | tf_op jit(solution)/shard_map/ppermute | solution.py:39
  135.4 5.5 %collective-permute-start.26 = (bf16[2,64,2048]{2,1,0:T(8,128)(2,1)S(1)}, bf16[2,64,2048]{2,1,0:T(8,128)(2,1)S(1)}, u32[]{:S(2)}, u32[]{:S(2)}) collective-permute-start(bf16[2,64,2048]{2,1,0:T(8,128)(2,1)S(1)} %bitcast_dynamic-update-slice_fusion), channel_id=1, source_target_pairs={{0,1},{1,0},{2,3},{3,2},{4,5},{5,4},{6,7},{7,6},{8,9},{9,8},{10,11... | collective-permute-start | bytes 1572872 | tf_op jit(solution)/shard_map/ppermute | solution.py:47
  135.5 25.9 %collective-permute-start.10 = (bf16[256,1792]{1,0:T(8,128)(2,1)S(1)}, bf16[256,1792]{1,0:T(8,128)(2,1)S(1)}, u32[]{:S(2)}, u32[]{:S(2)}) collective-permute-start(bf16[256,1792]{1,0:T(8,128)(2,1)S(1)} %fusion.36), channel_id=1, source_target_pairs={{0,28},{4,0},{8,4},{12,8},{16,12},{20,16},{24,20},{28,24},{1,29},{... | collective-permute-start | bytes 2752520 | tf_op jit(solution)/shard_map/ppermute | solution.py:12
  140.7 40.3 %collective-permute-start.17 = (bf16[256,1792]{1,0:T(8,128)(2,1)S(1)}, bf16[256,1792]{1,0:T(8,128)(2,1)S(1)}, u32[]{:S(2)}, u32[]{:S(2)}) collective-permute-start(bf16[256,1792]{1,0:T(8,128)(2,1)S(1)} %fusion.37), channel_id=1, source_target_pairs={{0,28},{4,0},{8,4},{12,8},{16,12},{20,16},{24,20},{28,24},{1,29},{... | collective-permute-start | bytes 2752520 | tf_op jit(solution)/shard_map/ppermute | solution.py:12
  140.8 59.9 %collective-permute-start.24 = (bf16[256,1792]{1,0:T(8,128)(2,1)S(1)}, bf16[256,1792]{1,0:T(8,128)(2,1)S(1)}, u32[]{:S(2)}, u32[]{:S(2)}) collective-permute-start(bf16[256,1792]{1,0:T(8,128)(2,1)S(1)} %fusion.38), channel_id=1, source_target_pairs={{0,28},{4,0},{8,4},{12,8},{16,12},{20,16},{24,20},{28,24},{1,29},{... | collective-permute-start | bytes 2752520 | tf_op jit(solution)/shard_map/ppermute | solution.py:12
  143.9 76.0 %collective-permute-start.27 = (bf16[256,1792]{1,0:T(8,128)(2,1)S(1)}, bf16[256,1792]{1,0:T(8,128)(2,1)S(1)}, u32[]{:S(2)}, u32[]{:S(2)}) collective-permute-start(bf16[256,1792]{1,0:T(8,128)(2,1)S(1)} %fusion.39), channel_id=1, source_target_pairs={{0,28},{4,0},{8,4},{12,8},{16,12},{20,16},{24,20},{28,24},{1,29},{... | collective-permute-start | bytes 2752520 | tf_op jit(solution)/shard_map/ppermute | solution.py:12
  (15 other events, 161.3 us)

commit v2 on v0

v2 whole, which is shorter than its diff:
```python
import functools

import jax
import jax.numpy as jnp
from jax import lax
from jax.experimental import pallas as pl
from jax.experimental.pallas import tpu as pltpu
from jax.sharding import PartitionSpec as P

CHUNKS = 4
FREE = pl.CostEstimate(flops=0, bytes_accessed=0, transcendentals=0)
FAR = pl.BlockSpec(memory_space=pl.ANY)


def params(**kwargs):
    return pltpu.CompilerParams(vmem_limit_bytes=24 * 1024 * 1024, **kwargs)


def block_of(size, most):
    fits = [b for b in range(128, min(size, most) + 1, 128) if size % b == 0]
    return fits[-1] if fits else size


def back_one(x):
    length = lax.axis_size("pipe")
    return lax.ppermute(x, "pipe", [(i, (i - 1) % length) for i in range(length)])


def to_expert(x, by):
    n = lax.axis_size("expert")
    return lax.ppermute(x, "expert", [(i, (i + by) % n) for i in range(n)])


def to_other_core(x):
    n = lax.axis_size("expert")
    return lax.ppermute(x, "expert", [(i, i ^ 1) for i in range(n)])


def in_order(later, earlier):
    return lax.optimization_barrier((later, earlier))


def contract_last(left, right):
    return lax.dot_general(
        left, right, (((1,), (1,)), ((), ())), preferred_element_type=jnp.float32
    )


def take_kernel(source_ref, out_ref):
    out_ref[...] = source_ref[...]


def put_kernel(source_ref, *refs):
    refs[-1][...] = source_ref[...]


def take_rows(array, c, part):
    n, _, width = array.shape
    return pl.pallas_call(
        take_kernel,
        out_shape=jax.ShapeDtypeStruct((n, part, width), array.dtype),
        grid=(n,),
        in_specs=[pl.BlockSpec((1, part, width), lambda i: (i, c, 0))],
        out_specs=pl.BlockSpec((1, part, width), lambda i: (i, 0, 0)),
        cost_estimate=FREE,
        name="take_rows",
    )(array)


def put_rows(out, piece, c, rows):
    n, part, width = piece.shape
    spec = pl.BlockSpec((1, part, width), lambda i: (i, 0, 0))
    return pl.pallas_call(
        put_kernel,
        out_shape=jax.ShapeDtypeStruct((n, rows, width), piece.dtype),
        grid=(n,),
        in_specs=[spec] + ([] if out is None else [FAR]),
        out_specs=pl.BlockSpec((1, part, width), lambda i: (i, c, 0)),
        input_output_aliases={} if out is None else {1: 0},
        cost_estimate=FREE,
        name="put_rows",
    )(*((piece,) if out is None else (piece, out)))


def routed_kernel(grad_ref, score_ref, chosen_ref, out_ref):
    grad, scores, chosen = grad_ref[...], score_ref[...], chosen_ref[...]
    total = jnp.sum(scores, axis=-1, keepdims=True)
    mixed = jnp.sum(grad * scores, axis=-1, keepdims=True)
    logit_grad = 2.5 * (grad - mixed / total) / total * scores * (1.0 - scores)
    columns = lax.broadcasted_iota(jnp.int32, out_ref.shape, 1)
    dense = jnp.zeros(out_ref.shape, jnp.float32)
    for slot in range(grad.shape[1]):
        here = chosen[:, slot : slot + 1] == columns
        dense = dense + jnp.where(here, logit_grad[:, slot : slot + 1], 0.0)
    out_ref[...] = dense.astype(out_ref.dtype)


def routed_grad(grad, scores, chosen, n_experts):
    tokens, top = grad.shape
    block = min(tokens, 128)
    spec = pl.BlockSpec((block, top), lambda i: (i, 0))
    return pl.pallas_call(
        routed_kernel,
        out_shape=jax.ShapeDtypeStruct((tokens, n_experts), jnp.bfloat16),
        grid=(tokens // block,),
        in_specs=[spec, spec, spec],
        out_specs=pl.BlockSpec((block, n_experts), lambda i: (i, 0)),
        cost_estimate=FREE,
        name="routed_grad",
    )(grad, scores, chosen)


def first_kernel(n, me_ref, rows_ref, weight_ref, *out_refs):
    me = me_ref[0]
    part = rows_ref.shape[1]
    left = jnp.concatenate([rows_ref[lax.rem(me + j, n)] for j in range(n)], axis=0)
    product = contract_last(left, weight_ref[...]).astype(jnp.bfloat16)
    for j in range(n):
        out_refs[j][...] = product[j * part : (j + 1) * part]


def first_product(me, rows, weight):
    n, part, width = rows.shape
    hidden = weight.shape[0]
    block = block_of(hidden, 256)
    return pl.pallas_call(
        functools.partial(first_kernel, n),
        out_shape=[jax.ShapeDtypeStruct((part, hidden), jnp.bfloat16)] * n,
        grid_spec=pltpu.PrefetchScalarGridSpec(
            num_scalar_prefetch=1,
            grid=(hidden // block,),
            in_specs=[
                pl.BlockSpec((n, part, width), lambda i, me: (0, 0, 0)),
                pl.BlockSpec((block, width), lambda i, me: (i, 0)),
            ],
            out_specs=[pl.BlockSpec((part, block), lambda i, me: (0, i))] * n,
        ),
        compiler_params=params(),
        cost_estimate=FREE,
        name="first_product",
    )(me, rows, weight)


def activation_kernel(gate_ref, up_ref, *refs):
    *part_refs, out_ref = refs
    hidden = gate_ref.shape[1]
    hidden_grad = part_refs[0][...].astype(jnp.float32)
    for ref in part_refs[1:]:
        hidden_grad = hidden_grad + ref[...].astype(jnp.float32)
    act_a = gate_ref[...].astype(jnp.float32)
    act_b = up_ref[...].astype(jnp.float32)
    sigma = 1.0 / (1.0 + jnp.exp(-act_a))
    gate_part = hidden_grad * act_b * sigma * (1.0 + act_a * (1.0 - sigma))
    up_part = hidden_grad * act_a * sigma
    out_ref[:, :hidden] = gate_part.astype(out_ref.dtype)
    out_ref[:, hidden:] = up_part.astype(out_ref.dtype)


def activation(gate_pre, up_pre, c, partials):
    part, hidden = partials[0].shape
    saved = pl.BlockSpec((part, hidden), lambda i: (c, 0))
    return pl.pallas_call(
        activation_kernel,
        out_shape=jax.ShapeDtypeStruct((part, 2 * hidden), jnp.bfloat16),
        grid=(1,),
        in_specs=[saved, saved] + [pl.BlockSpec((part, hidden), lambda i: (0, 0))] * len(partials),
        out_specs=pl.BlockSpec((part, 2 * hidden), lambda i: (0, 0)),
        compiler_params=params(),
        cost_estimate=FREE,
        name="activation",
    )(gate_pre, up_pre, *partials)


def second_kernel(n, me_ref, dense_ref, gate_ref, up_ref, router_ref, *refs):
    *block_refs, out_ref, held = refs
    chips = n // 2
    hidden = gate_ref.shape[1]

    @pl.when(pl.program_id(0) == 0)
    def _():
        me = me_ref[0]
        chip, core = me // 2, lax.rem(me, 2)
        for step in range(chips):
            there = lax.rem(chip - step + chips, chips) * 2
            held[there + core] = block_refs[2 * step][...]
            held[there + 1 - core] = block_refs[2 * step + 1][...]

    both = held[...].reshape(-1, 2 * hidden)
    result = contract_last(both[:, :hidden], gate_ref[...])
    result = result + contract_last(both[:, hidden:], up_ref[...])
    dense = dense_ref[...].reshape(both.shape[0], -1)
    result = result + contract_last(dense, router_ref[...])
    out_ref[...] = result.astype(out_ref.dtype).reshape(out_ref.shape)


def second_product(me, blocks, c, dense, w_gate, w_up, w_router):
    n = len(blocks)
    part, both = blocks[0].shape
    width, hidden = w_gate.shape
    n_experts = w_router.shape[1]
    block = block_of(width, 256)
    return pl.pallas_call(
        functools.partial(second_kernel, n),
        out_shape=jax.ShapeDtypeStruct((n, part, width), jnp.bfloat16),
        grid_spec=pltpu.PrefetchScalarGridSpec(
            num_scalar_prefetch=1,
            grid=(width // block,),
            in_specs=[
                pl.BlockSpec((n, part, n_experts), lambda i, me: (0, c, 0)),
                pl.BlockSpec((block, hidden), lambda i, me: (i, 0)),
                pl.BlockSpec((block, hidden), lambda i, me: (i, 0)),
                pl.BlockSpec((block, n_experts), lambda i, me: (i, 0)),
            ]
            + [pl.BlockSpec((part, both), lambda i, me: (0, 0))] * n,
            out_specs=pl.BlockSpec((n, part, block), lambda i, me: (0, 0, i)),
            scratch_shapes=[pltpu.VMEM((n, part, both), jnp.bfloat16)],
        ),
        compiler_params=params(),
        cost_estimate=FREE,
        name="second_product",
    )(me, dense, w_gate, w_up, w_router, *blocks)


def shards(
    upstream,
    shared_down,
    shared_gate,
    shared_up,
    router_weight,
    gate_pre,
    up_pre,
    gate_grad,
    gate_scores,
    expert_ids,
):
    n = lax.axis_size("expert")
    chips = n // 2
    me = lax.axis_index("expert").astype(jnp.int32).reshape(1)
    tokens, width = upstream.shape[1:]
    rows = tokens // n
    chunks = min(CHUNKS, rows // 16)
    part = rows // chunks
    grads = upstream.reshape(n, rows, width)
    arrived = [back_one(take_rows(grads, c, part)) for c in range(chunks)]
    dense = routed_grad(gate_grad[0], gate_scores[0], expert_ids[0], router_weight.shape[2])
    dense = dense.reshape(n, rows, -1)

    def partial_sums(c):
        own, *others = first_product(me, arrived[c], shared_down[0])
        return [own] + [to_expert(x, j + 1) for j, x in enumerate(others)]

    arrived[0], dense = in_order(arrived[0], dense)
    own = activation(gate_pre[0], up_pre[0], 0, partial_sums(0))
    out, sent = None, []
    for c in range(chunks):
        near = [own] + [to_expert(own, 2 * step) for step in range(1, chips)]
        far = [to_other_core(own)]
        if c + 1 < chunks:
            arrived[c + 1], own = in_order(arrived[c + 1], own)
            partials = partial_sums(c + 1)
            partials[0], near[-1] = in_order(partials[0], near[-1])
        far += [to_other_core(x) for x in near[1:]]
        if c >= 2:
            far[-1], out = in_order(far[-1], out)
        blocks = [x for pair in zip(near, far) for x in pair]
        result = second_product(
            me, blocks, c, dense, shared_gate[0], shared_up[0], router_weight[0]
        )
        if c + 1 < chunks:
            partials[0], result = in_order(partials[0], result)
            own = activation(gate_pre[0], up_pre[0], c + 1, partials)
        sent.append(back_one(result))
        if c >= 1:
            out = put_rows(out, sent[c - 1], c - 1, rows)
    out = put_rows(out, sent[-1], chunks - 1, rows)
    return out.reshape(1, tokens, width)


def solution(mesh):
    in_specs = (
        P("pipe", None, "expert"),
        P("pipe", None, "expert"),
        P("pipe", "expert", None),
        P("pipe", "expert", None),
        P("pipe", "expert", None),
        P("pipe", "expert", None),
        P("pipe", "expert", None),
        P("pipe", None, None),
        P("pipe", None, None),
        P("pipe", None, None),
    )
    out_specs = P("pipe", None, "expert")
    return jax.shard_map(shards, mesh=mesh, in_specs=in_specs, out_specs=out_specs, check_vma=False)
```

time: 278 us -> 188 us (0.68)
  waiting for transfers between devices: 226 us -> 57.8 us
  Pallas kernels: 0 us -> 63.8 us
  starting transfers between devices: 10.4 us -> 41.4 us
  matrix products: 23.4 us -> 0 us
  local copies, waits for them, and re-layouts: 1.92 us -> 24 us
  between operations: 13.5 us -> 0.2 us
    ppermute x2 -> x32, waiting for transfers between devices: 158 us -> 57.8 us  [the longest x8 49.1 us: back_one(): lax.ppermute(x, 'pipe', [(i, (i - 1) % length) for i in range(length)])]
    pallas_call x0 -> x21, Pallas kernels: none -> 63.8 us  [the longest x4 17.2 us: second_product(): pl.pallas_call(functools.partial(second_kernel, n), out_shape=jax.ShapeDt...]
    all_gather x1 -> x0, waiting for transfers between devices: 34.5 us -> none  [section_backward(): piece = lax.all_gather(stacked, 'expert', axis=0, tiled=True)]
    reduce_scatter x1 -> x0, waiting for transfers between devices: 33.3 us -> none  [section_backward(): lax.psum_scatter(contract_last(incoming, w_down).astype(jnp.bfloat16).ast...]
    ppermute x2 -> x32, starting transfers between devices: 10.3 us -> 41.4 us  [the longest x8 26.5 us: back_one(): lax.ppermute(x, 'pipe', [(i, (i - 1) % length) for i in range(length)])]
    dot_general x4 -> x0, matrix products: 23.4 us -> none  [contract_last(): lax.dot_general(left, right, (((1,), (1,)), ((), ())), preferred_element_...]
    unnamed x17 -> x53, local copies, waits for them, and re-layouts: 1.87 us -> 24 us
  transfers between devices with their start and end apart: 4 -> 32, of which waited for: 4 -> 8; matrix products, arithmetic and copies ran while one was open for 0% -> 2% of each run, Pallas kernels for 0% -> 31%
where the time goes in v2:
time: 188 us; the launch traced here: 187 us
  Pallas kernels  63.8 us (34%)
  waiting for transfers between devices  57.8 us (31%)
  starting transfers between devices  41.4 us (22%)
  local copies, waits for them, and re-layouts  24 us (13%)
    ppermute x8, waiting for transfers between devices, back_one(): lax.ppermute(x, 'pipe', [(i, (i - 1) % length) for i in range(length)])  49.1 us
    ppermute x8, starting transfers between devices, back_one(): lax.ppermute(x, 'pipe', [(i, (i - 1) % length) for i in range(length)])  26.5 us
    unnamed x53, local copies, waits for them, and re-layouts  24 us
    pallas_call x4, Pallas kernels, second_product(): pl.pallas_call(functools.partial(second_kernel, n), out_shape=jax.ShapeDt...  17.2 us
    ppermute x16, starting transfers between devices, to_expert(): return lax.ppermute(x, 'expert', [(i, (i + by) % n) for i in range(n)])  13.6 us
    pallas_call x4, Pallas kernels, put_rows(): pl.pallas_call(put_kernel, out_shape=jax.ShapeDtypeStruct((n, rows, width...  13.2 us
    pallas_call x4, Pallas kernels, take_rows(): pl.pallas_call(take_kernel, out_shape=jax.ShapeDtypeStruct((n, part, widt...  13.2 us
    pallas_call x4, Pallas kernels, first_product(): pl.pallas_call(functools.partial(first_kernel, n), out_shape=[jax.ShapeDt...  10.4 us
  transfers between devices with their start and end apart: 32, of which 8 were waited for; matrix products, arithmetic and copies ran while one was open for 2% of the time, Pallas kernels for 31%

profile of v2, /device:TPU:0, one launch (start us, length us, event | category | flops | bytes accessed | tf_op | source)
XLA Modules:
  0.0 187.1 jit_solution(6415525340232125354)
XLA Ops:
  0.0 3.3 %take_rows.4 = bf16[4,64,1792]{2,1,0:T(8,128)(2,1)} custom-call(bf16[4,256,1792]{2,1,0:T(8,128)(2,1)} %bitcast.41), custom_call_target="tpu_custom_call" | custom-call | tf_op jit(solution)/shard_map/take_rows/pallas_call | solution.py:59
  3.3 6.0 %collective-permute-start = (bf16[4,64,1792]{2,1,0:T(8,128)(2,1)}, bf16[4,64,1792]{2,1,0:T(8,128)(2,1)S(1)}, u32[]{:S(2)}, u32[]{:S(2)}) collective-permute-start(bf16[4,64,1792]{2,1,0:T(8,128)(2,1)} %take_rows.4), channel_id=1, source_target_pairs={{0,28},{4,0},{8,4},{12,8},{16,12},{20,16},{24,20},{28,24},{1,29},{... | collective-permute-start | bytes 2752520 | tf_op jit(solution)/shard_map/ppermute | solution.py:26
  9.3 3.3 %take_rows.7 = bf16[4,64,1792]{2,1,0:T(8,128)(2,1)} custom-call(bf16[4,256,1792]{2,1,0:T(8,128)(2,1)} %bitcast.42), custom_call_target="tpu_custom_call" | custom-call | tf_op jit(solution)/shard_map/take_rows/pallas_call | solution.py:59
  16.2 6.9 %routed_grad.1 = bf16[1024,256]{1,0:T(8,128)(2,1)} custom-call(f32[1024,8]{1,0:T(8,128)} %bitcast.45, f32[1024,8]{1,0:T(8,128)} %bitcast.46, s32[1024,8]{1,0:T(8,128)} %bitcast.47), custom_call_target="tpu_custom_call" | custom-call | tf_op jit(solution)/shard_map/routed_grad/pallas_call | solution.py:102
  23.1 7.3 %collective-permute-done.rows_ref = bf16[4,64,1792]{2,1,0:T(8,128)(2,1)S(1)} collective-permute-done((bf16[4,64,1792]{2,1,0:T(8,128)(2,1)}, bf16[4,64,1792]{2,1,0:T(8,128)(2,1)S(1)}, u32[]{:S(2)}, u32[]{:S(2)}) %collective-permute-start) | collective-permute-done | bytes 917536 | tf_op jit(solution)/shard_map/ppermute | solution.py:26
  30.4 2.0 %copy-done = bf16[1,1024,1792]{2,1,0:T(8,128)(2,1)S(1)} copy-done((bf16[1,1024,1792]{2,1,0:T(8,128)(2,1)S(1)}, bf16[1,1024,1792]{2,1,0:T(8,128)(2,1)}, u32[]{:S(2)}) %copy-start) | copy-done | bytes 3670040
  32.4 2.7 %first_product.4 = (bf16[64,1024]{1,0:T(8,128)(2,1)S(1)}, bf16[64,1024]{1,0:T(8,128)(2,1)}, bf16[64,1024]{1,0:T(8,128)(2,1)}, bf16[64,1024]{1,0:T(8,128)(2,1)}) custom-call(s32[1]{0:T(128)} %bitcast.me_ref, bf16[4,64,1792]{2,1,0:T(8,128)(2,1)S(1)} %collective-permute-done.rows_ref, bf16[1024,1792]{1,0:T(8,128)(2,1)S(1)} %bitcast.13), custom_call_target="tpu_custom_call" | custom-call | tf_op jit(solution)/shard_map/first_product/pallas_call | solution.py:126
  38.1 3.3 %take_rows.6 = bf16[4,64,1792]{2,1,0:T(8,128)(2,1)} custom-call(bf16[4,256,1792]{2,1,0:T(8,128)(2,1)} %bitcast.43), custom_call_target="tpu_custom_call" | custom-call | tf_op jit(solution)/shard_map/take_rows/pallas_call | solution.py:59
  41.4 5.1 %collective-permute-start.2 = (bf16[4,64,1792]{2,1,0:T(8,128)(2,1)}, bf16[4,64,1792]{2,1,0:T(8,128)(2,1)}, u32[]{:S(2)}, u32[]{:S(2)}) collective-permute-start(bf16[4,64,1792]{2,1,0:T(8,128)(2,1)} %take_rows.6), channel_id=1, source_target_pairs={{0,28},{4,0},{8,4},{12,8},{16,12},{20,16},{24,20},{28,24},{1,29},{... | collective-permute-start | bytes 2752520 | tf_op jit(solution)/shard_map/ppermute | solution.py:26
  50.0 2.0 %copy-done.1 = bf16[1,1024,1792]{2,1,0:T(8,128)(2,1)S(1)} copy-done((bf16[1,1024,1792]{2,1,0:T(8,128)(2,1)S(1)}, bf16[1,1024,1792]{2,1,0:T(8,128)(2,1)}, u32[]{:S(2)}) %copy-start.1) | copy-done | bytes 3670040
  59.7 3.8 %second_product.4 = bf16[4,64,1792]{2,1,0:T(8,128)(2,1)S(1)} custom-call(s32[1]{0:T(128)} %bitcast.me_ref, bf16[4,256,256]{2,1,0:T(8,128)(2,1)S(1)} %bitcast.29, bf16[1792,1024]{1,0:T(8,128)(2,1)S(1)} %bitcast.17, bf16[1792,1024]{1,0:T(8,128)(2,1)S(1)} %bitcast.21, bf16[1792,256]{1,0:T(8,128)(2,1)S(1)} %bitcast.25, bf16[64,2048]{1,0:T(8,128)(2,1)S(1)} %activation.4.refs_0_, ...), custom_call_target="tpu_custom_call" | custom-call | tf_op jit(solution)/shard_map/second_product/pallas_call | solution.py:202
  65.4 3.3 %take_rows.5 = bf16[4,64,1792]{2,1,0:T(8,128)(2,1)} custom-call(bf16[4,256,1792]{2,1,0:T(8,128)(2,1)} %bitcast.44), custom_call_target="tpu_custom_call" | custom-call | tf_op jit(solution)/shard_map/take_rows/pallas_call | solution.py:59
  68.7 4.4 %collective-permute-start.1 = (bf16[4,64,1792]{2,1,0:T(8,128)(2,1)}, bf16[4,64,1792]{2,1,0:T(8,128)(2,1)S(1)}, u32[]{:S(2)}, u32[]{:S(2)}) collective-permute-start(bf16[4,64,1792]{2,1,0:T(8,128)(2,1)} %take_rows.5), channel_id=1, source_target_pairs={{0,28},{4,0},{8,4},{12,8},{16,12},{20,16},{24,20},{28,24},{1,29},{... | collective-permute-start | bytes 2752520 | tf_op jit(solution)/shard_map/ppermute | solution.py:26
  75.1 3.2 %first_product.6 = (bf16[64,1024]{1,0:T(8,128)(2,1)S(1)}, bf16[64,1024]{1,0:T(8,128)(2,1)S(1)}, bf16[64,1024]{1,0:T(8,128)(2,1)S(1)}, bf16[64,1024]{1,0:T(8,128)(2,1)S(1)}) custom-call(s32[1]{0:T(128)} %bitcast.me_ref, bf16[4,64,1792]{2,1,0:T(8,128)(2,1)} %collective-permute-done.2.rows_ref, bf16[1024,1792]{1,0:T(8,128)(2,1)S(1)} %bitcast.15), custom_call_target="tpu_custom_call" | custom-call | tf_op jit(solution)/shard_map/first_product/pallas_call | solution.py:126
  82.1 2.0 %copy-done.9 = bf16[1,1792,1024]{2,1,0:T(8,128)(2,1)S(1)} copy-done((bf16[1,1792,1024]{2,1,0:T(8,128)(2,1)S(1)}, bf16[1,1792,1024]{2,1,0:T(8,128)(2,1)}, u32[]{:S(2)}) %copy-start.9) | copy-done | bytes 3670040
  84.2 4.8 %second_product.5 = bf16[4,64,1792]{2,1,0:T(8,128)(2,1)} custom-call(s32[1]{0:T(128)} %bitcast.me_ref, bf16[4,256,256]{2,1,0:T(8,128)(2,1)S(1)} %bitcast.30, bf16[1792,1024]{1,0:T(8,128)(2,1)S(1)} %bitcast.18, bf16[1792,1024]{1,0:T(8,128)(2,1)S(1)} %bitcast.22, bf16[1792,256]{1,0:T(8,128)(2,1)S(1)} %bitcast.26, bf16[64,2048]{1,0:T(8,128)(2,1)S(1)} %activation.5.refs_0_, ...), custom_call_target="tpu_custom_call" | custom-call | tf_op jit(solution)/shard_map/second_product/pallas_call | solution.py:202
  89.8 4.3 %collective-permute-done.1.rows_ref = bf16[4,64,1792]{2,1,0:T(8,128)(2,1)S(1)} collective-permute-done((bf16[4,64,1792]{2,1,0:T(8,128)(2,1)}, bf16[4,64,1792]{2,1,0:T(8,128)(2,1)S(1)}, u32[]{:S(2)}, u32[]{:S(2)}) %collective-permute-start.1) | collective-permute-done | bytes 917536 | tf_op jit(solution)/shard_map/ppermute | solution.py:26
  94.2 2.7 %first_product.7 = (bf16[64,1024]{1,0:T(8,128)(2,1)S(1)}, bf16[64,1024]{1,0:T(8,128)(2,1)}, bf16[64,1024]{1,0:T(8,128)(2,1)}, bf16[64,1024]{1,0:T(8,128)(2,1)}) custom-call(s32[1]{0:T(128)} %bitcast.me_ref, bf16[4,64,1792]{2,1,0:T(8,128)(2,1)S(1)} %collective-permute-done.1.rows_ref, bf16[1024,1792]{1,0:T(8,128)(2,1)S(1)} %bitcast.16), custom_call_target="tpu_custom_call" | custom-call | tf_op jit(solution)/shard_map/first_product/pallas_call | solution.py:126
  97.5 5.1 %collective-permute-start.29 = (bf16[4,64,1792]{2,1,0:T(8,128)(2,1)}, bf16[4,64,1792]{2,1,0:T(8,128)(2,1)}, u32[]{:S(2)}, u32[]{:S(2)}) collective-permute-start(bf16[4,64,1792]{2,1,0:T(8,128)(2,1)} %second_product.5), channel_id=1, source_target_pairs={{0,28},{4,0},{8,4},{12,8},{16,12},{20,16},{24,20},{28,24},{1,29},{... | collective-permute-start | bytes 2752520 | tf_op jit(solution)/shard_map/ppermute | solution.py:26
  103.1 10.7 %collective-permute-done.22.source_ref = bf16[4,64,1792]{2,1,0:T(8,128)(2,1)S(1)} collective-permute-done((bf16[4,64,1792]{2,1,0:T(8,128)(2,1)S(1)}, bf16[4,64,1792]{2,1,0:T(8,128)(2,1)S(1)}, u32[]{:S(2)}, u32[]{:S(2)}) %collective-permute-start.22) | collective-permute-done | bytes 917536 | tf_op jit(solution)/shard_map/ppermute | solution.py:26
  115.3 3.3 %put_rows.4.refs_0_ = bf16[4,256,1792]{2,1,0:T(8,128)(2,1)} custom-call(bf16[4,64,1792]{2,1,0:T(8,128)(2,1)} %copy-done.20), custom_call_target="tpu_custom_call" | custom-call | tf_op jit(solution)/shard_map/put_rows/pallas_call | solution.py:73
  118.6 2.0 %copy-done.6 = bf16[1,1792,1024]{2,1,0:T(8,128)(2,1)S(1)} copy-done((bf16[1,1792,1024]{2,1,0:T(8,128)(2,1)S(1)}, bf16[1,1792,1024]{2,1,0:T(8,128)(2,1)}, u32[]{:S(2)}) %copy-start.6) | copy-done | bytes 3670040
  120.6 2.0 %copy-done.10 = bf16[1,1792,1024]{2,1,0:T(8,128)(2,1)S(1)} copy-done((bf16[1,1792,1024]{2,1,0:T(8,128)(2,1)S(1)}, bf16[1,1792,1024]{2,1,0:T(8,128)(2,1)}, u32[]{:S(2)}) %copy-start.10) | copy-done | bytes 3670040
  122.7 4.8 %second_product.6 = bf16[4,64,1792]{2,1,0:T(8,128)(2,1)} custom-call(s32[1]{0:T(128)} %bitcast.me_ref, bf16[4,256,256]{2,1,0:T(8,128)(2,1)S(1)} %bitcast.31, bf16[1792,1024]{1,0:T(8,128)(2,1)S(1)} %bitcast.19, bf16[1792,1024]{1,0:T(8,128)(2,1)S(1)} %bitcast.23, bf16[1792,256]{1,0:T(8,128)(2,1)S(1)} %bitcast.27, bf16[64,2048]{1,0:T(8,128)(2,1)S(1)} %activation.6.refs_0_, ...), custom_call_target="tpu_custom_call" | custom-call | tf_op jit(solution)/shard_map/second_product/pallas_call | solution.py:202
  129.7 7.8 %collective-permute-done.27.refs_2_ = bf16[64,2048]{1,0:T(8,128)(2,1)S(1)} collective-permute-done((bf16[64,2048]{1,0:T(8,128)(2,1)S(1)}, bf16[64,2048]{1,0:T(8,128)(2,1)S(1)}, u32[]{:S(2)}, u32[]{:S(2)}) %collective-permute-start.27) | collective-permute-done | bytes 262176 | tf_op jit(solution)/shard_map/ppermute | solution.py:31
  138.0 5.2 %collective-permute-start.31 = (bf16[4,64,1792]{2,1,0:T(8,128)(2,1)}, bf16[4,64,1792]{2,1,0:T(8,128)(2,1)}, u32[]{:S(2)}, u32[]{:S(2)}) collective-permute-start(bf16[4,64,1792]{2,1,0:T(8,128)(2,1)} %second_product.6), channel_id=1, source_target_pairs={{0,28},{4,0},{8,4},{12,8},{16,12},{20,16},{24,20},{28,24},{1,29},{... | collective-permute-start | bytes 2752520 | tf_op jit(solution)/shard_map/ppermute | solution.py:26
  143.2 3.3 %put_rows.5.refs_0_ = bf16[4,256,1792]{2,1,0:T(8,128)(2,1)} custom-call(bf16[4,64,1792]{2,1,0:T(8,128)(2,1)} %collective-permute-done.29.source_ref, bf16[4,256,1792]{2,1,0:T(8,128)(2,1)} %put_rows.4.refs_0_), custom_call_target="tpu_custom_call", output_to_operand_aliasing={{}: (1, {})} | custom-call | tf_op jit(solution)/shard_map/put_rows/pallas_call | solution.py:73
  150.6 3.8 %second_product.7 = bf16[4,64,1792]{2,1,0:T(8,128)(2,1)S(1)} custom-call(s32[1]{0:T(128)} %bitcast.me_ref, bf16[4,256,256]{2,1,0:T(8,128)(2,1)S(1)} %bitcast.32, bf16[1792,1024]{1,0:T(8,128)(2,1)S(1)} %bitcast.20, bf16[1792,1024]{1,0:T(8,128)(2,1)S(1)} %bitcast.24, bf16[1792,256]{1,0:T(8,128)(2,1)S(1)} %bitcast.28, bf16[64,2048]{1,0:T(8,128)(2,1)S(1)} %activation.7.refs_0_, ...), custom_call_target="tpu_custom_call" | custom-call | tf_op jit(solution)/shard_map/second_product/pallas_call | solution.py:202
  154.5 9.8 %collective-permute-done.31.source_ref = bf16[4,64,1792]{2,1,0:T(8,128)(2,1)} collective-permute-done((bf16[4,64,1792]{2,1,0:T(8,128)(2,1)}, bf16[4,64,1792]{2,1,0:T(8,128)(2,1)}, u32[]{:S(2)}, u32[]{:S(2)}) %collective-permute-start.31) | collective-permute-done | bytes 917536 | tf_op jit(solution)/shard_map/ppermute | solution.py:26
  164.2 3.3 %put_rows.6.refs_0_ = bf16[4,256,1792]{2,1,0:T(8,128)(2,1)} custom-call(bf16[4,64,1792]{2,1,0:T(8,128)(2,1)} %collective-permute-done.31.source_ref, bf16[4,256,1792]{2,1,0:T(8,128)(2,1)} %put_rows.5.refs_0_), custom_call_target="tpu_custom_call", output_to_operand_aliasing={{}: (1, {})} | custom-call | tf_op jit(solution)/shard_map/put_rows/pallas_call | solution.py:73
  167.5 15.3 %collective-permute-done.30.source_ref = bf16[4,64,1792]{2,1,0:T(8,128)(2,1)S(1)} collective-permute-done((bf16[4,64,1792]{2,1,0:T(8,128)(2,1)S(1)}, bf16[4,64,1792]{2,1,0:T(8,128)(2,1)S(1)}, u32[]{:S(2)}, u32[]{:S(2)}) %collective-permute-start.30) | collective-permute-done | bytes 917536 | tf_op jit(solution)/shard_map/ppermute | solution.py:26
  183.8 3.3 %put_rows.7 = bf16[4,256,1792]{2,1,0:T(8,128)(2,1)} custom-call(bf16[4,64,1792]{2,1,0:T(8,128)(2,1)} %copy-done.21, bf16[4,256,1792]{2,1,0:T(8,128)(2,1)} %put_rows.6.refs_0_), custom_call_target="tpu_custom_call", output_to_operand_aliasing={{}: (1, {})} | custom-call | tf_op jit(solution)/shard_map/put_rows/pallas_call | solution.py:73
  (106 shorter events, 36.9 us)
Async XLA Ops:
  3.3 27.0 %collective-permute-start = (bf16[4,64,1792]{2,1,0:T(8,128)(2,1)}, bf16[4,64,1792]{2,1,0:T(8,128)(2,1)S(1)}, u32[]{:S(2)}, u32[]{:S(2)}) collective-permute-start(bf16[4,64,1792]{2,1,0:T(8,128)(2,1)} %take_rows.4), channel_id=1, source_target_pairs={{0,28},{4,0},{8,4},{12,8},{16,12},{20,16},{24,20},{28,24},{1,29},{... | collective-permute-start | bytes 2752520 | tf_op jit(solution)/shard_map/ppermute | solution.py:26
  12.6 37.4 %collective-permute-start.3 = (bf16[4,64,1792]{2,1,0:T(8,128)(2,1)}, bf16[4,64,1792]{2,1,0:T(8,128)(2,1)S(1)}, u32[]{:S(2)}, u32[]{:S(2)}) collective-permute-start(bf16[4,64,1792]{2,1,0:T(8,128)(2,1)} %take_rows.7), channel_id=1, source_target_pairs={{0,28},{4,0},{8,4},{12,8},{16,12},{20,16},{24,20},{28,24},{1,29},{... | collective-permute-start | bytes 2752520 | tf_op jit(solution)/shard_map/ppermute | solution.py:26
  35.1 11.4 %collective-permute-start.4 = (bf16[64,1024]{1,0:T(8,128)(2,1)}, bf16[64,1024]{1,0:T(8,128)(2,1)}, u32[]{:S(2)}, u32[]{:S(2)}) collective-permute-start(bf16[64,1024]{1,0:T(8,128)(2,1)} %get-tuple-element.45), channel_id=1, source_target_pairs={{0,1},{1,2},{2,3},{3,0},{4,5},{5,6},{6,7},{7,4},{8,9},{9,10},{10,1... | collective-permute-start | bytes 393224 | tf_op jit(solution)/shard_map/ppermute | solution.py:31
  35.1 11.4 %collective-permute-start.5 = (bf16[64,1024]{1,0:T(8,128)(2,1)}, bf16[64,1024]{1,0:T(8,128)(2,1)}, u32[]{:S(2)}, u32[]{:S(2)}) collective-permute-start(bf16[64,1024]{1,0:T(8,128)(2,1)} %get-tuple-element.46), channel_id=1, source_target_pairs={{0,2},{1,3},{2,0},{3,1},{4,6},{5,7},{6,4},{7,5},{8,10},{9,11},{10,... | collective-permute-start | bytes 393224 | tf_op jit(solution)/shard_map/ppermute | solution.py:31
  36.6 9.8 %collective-permute-start.6 = (bf16[64,1024]{1,0:T(8,128)(2,1)}, bf16[64,1024]{1,0:T(8,128)(2,1)}, u32[]{:S(2)}, u32[]{:S(2)}) collective-permute-start(bf16[64,1024]{1,0:T(8,128)(2,1)} %get-tuple-element.47), channel_id=1, source_target_pairs={{0,3},{1,0},{2,1},{3,2},{4,7},{5,4},{6,5},{7,6},{8,11},{9,8},{10,9... | collective-permute-start | bytes 393224 | tf_op jit(solution)/shard_map/ppermute | solution.py:31
  41.4 31.7 %collective-permute-start.2 = (bf16[4,64,1792]{2,1,0:T(8,128)(2,1)}, bf16[4,64,1792]{2,1,0:T(8,128)(2,1)}, u32[]{:S(2)}, u32[]{:S(2)}) collective-permute-start(bf16[4,64,1792]{2,1,0:T(8,128)(2,1)} %take_rows.6), channel_id=1, source_target_pairs={{0,28},{4,0},{8,4},{12,8},{16,12},{20,16},{24,20},{28,24},{1,29},{... | collective-permute-start | bytes 2752520 | tf_op jit(solution)/shard_map/ppermute | solution.py:26
  47.7 7.1 %collective-permute-start.7 = (bf16[64,2048]{1,0:T(8,128)(2,1)S(1)}, bf16[64,2048]{1,0:T(8,128)(2,1)S(1)}, u32[]{:S(2)}, u32[]{:S(2)}) collective-permute-start(bf16[64,2048]{1,0:T(8,128)(2,1)S(1)} %activation.4.refs_0_), channel_id=1, source_target_pairs={{0,2},{1,3},{2,0},{3,1},{4,6},{5,7},{6,4},{7,5},{8,10},{9,11},{10,... | collective-permute-start | bytes 786440 | tf_op jit(solution)/shard_map/ppermute | solution.py:31
  48.3 8.3 %collective-permute-start.8 = (bf16[64,2048]{1,0:T(8,128)(2,1)S(1)}, bf16[64,2048]{1,0:T(8,128)(2,1)S(1)}, u32[]{:S(2)}, u32[]{:S(2)}) collective-permute-start(bf16[64,2048]{1,0:T(8,128)(2,1)S(1)} %activation.4.refs_0_), channel_id=1, source_target_pairs={{0,1},{1,0},{2,3},{3,2},{4,5},{5,4},{6,7},{7,6},{8,9},{9,8},{10,11... | collective-permute-start | bytes 786440 | tf_op jit(solution)/shard_map/ppermute | solution.py:36
  54.8 2.8 %collective-permute-start.9 = (bf16[64,2048]{1,0:T(8,128)(2,1)S(1)}, bf16[64,2048]{1,0:T(8,128)(2,1)S(1)}, u32[]{:S(2)}, u32[]{:S(2)}) collective-permute-start(bf16[64,2048]{1,0:T(8,128)(2,1)S(1)} %collective-permute-done.7.refs_2_), channel_id=1, source_target_pairs={{0,1},{1,0},{2,3},{3,2},{4,5},{5,4},{6,7},{7,6},{8,9},{9,8},{10,11... | collective-permute-start | bytes 786440 | tf_op jit(solution)/shard_map/ppermute | solution.py:36
  54.8 9.6 %collective-permute-start.10 = (bf16[64,1024]{1,0:T(8,128)(2,1)S(1)}, bf16[64,1024]{1,0:T(8,128)(2,1)S(1)}, u32[]{:S(2)}, u32[]{:S(2)}) collective-permute-start(bf16[64,1024]{1,0:T(8,128)(2,1)S(1)} %get-tuple-element.53), channel_id=1, source_target_pairs={{0,1},{1,2},{2,3},{3,0},{4,5},{5,6},{6,7},{7,4},{8,9},{9,10},{10,1... | collective-permute-start | bytes 393224 | tf_op jit(solution)/shard_map/ppermute | solution.py:31
  55.3 9.1 %collective-permute-start.11 = (bf16[64,1024]{1,0:T(8,128)(2,1)S(1)}, bf16[64,1024]{1,0:T(8,128)(2,1)S(1)}, u32[]{:S(2)}, u32[]{:S(2)}) collective-permute-start(bf16[64,1024]{1,0:T(8,128)(2,1)S(1)} %get-tuple-element.54), channel_id=1, source_target_pairs={{0,2},{1,3},{2,0},{3,1},{4,6},{5,7},{6,4},{7,5},{8,10},{9,11},{10,... | collective-permute-start | bytes 393224 | tf_op jit(solution)/shard_map/ppermute | solution.py:31
  56.6 7.8 %collective-permute-start.12 = (bf16[64,1024]{1,0:T(8,128)(2,1)S(1)}, bf16[64,1024]{1,0:T(8,128)(2,1)S(1)}, u32[]{:S(2)}, u32[]{:S(2)}) collective-permute-start(bf16[64,1024]{1,0:T(8,128)(2,1)S(1)} %get-tuple-element.55), channel_id=1, source_target_pairs={{0,3},{1,0},{2,1},{3,2},{4,7},{5,4},{6,5},{7,6},{8,11},{9,8},{10,9... | collective-permute-start | bytes 393224 | tf_op jit(solution)/shard_map/ppermute | solution.py:31
  64.6 13.7 %collective-permute-start.13 = (bf16[64,2048]{1,0:T(8,128)(2,1)S(1)}, bf16[64,2048]{1,0:T(8,128)(2,1)S(1)}, u32[]{:S(2)}, u32[]{:S(2)}) collective-permute-start(bf16[64,2048]{1,0:T(8,128)(2,1)S(1)} %activation.5.refs_0_), channel_id=1, source_target_pairs={{0,2},{1,3},{2,0},{3,1},{4,6},{5,7},{6,4},{7,5},{8,10},{9,11},{10,... | collective-permute-start | bytes 786440 | tf_op jit(solution)/shard_map/ppermute | solution.py:31
  68.7 25.4 %collective-permute-start.1 = (bf16[4,64,1792]{2,1,0:T(8,128)(2,1)}, bf16[4,64,1792]{2,1,0:T(8,128)(2,1)S(1)}, u32[]{:S(2)}, u32[]{:S(2)}) collective-permute-start(bf16[4,64,1792]{2,1,0:T(8,128)(2,1)} %take_rows.5), channel_id=1, source_target_pairs={{0,28},{4,0},{8,4},{12,8},{16,12},{20,16},{24,20},{28,24},{1,29},{... | collective-permute-start | bytes 2752520 | tf_op jit(solution)/shard_map/ppermute | solution.py:26
  73.1 6.2 %collective-permute-start.14 = (bf16[64,2048]{1,0:T(8,128)(2,1)S(1)}, bf16[64,2048]{1,0:T(8,128)(2,1)S(1)}, u32[]{:S(2)}, u32[]{:S(2)}) collective-permute-start(bf16[64,2048]{1,0:T(8,128)(2,1)S(1)} %activation.5.refs_0_), channel_id=1, source_target_pairs={{0,1},{1,0},{2,3},{3,2},{4,5},{5,4},{6,7},{7,6},{8,9},{9,8},{10,11... | collective-permute-start | bytes 786440 | tf_op jit(solution)/shard_map/ppermute | solution.py:36
  78.3 2.5 %collective-permute-start.15 = (bf16[64,2048]{1,0:T(8,128)(2,1)S(1)}, bf16[64,2048]{1,0:T(8,128)(2,1)S(1)}, u32[]{:S(2)}, u32[]{:S(2)}) collective-permute-start(bf16[64,2048]{1,0:T(8,128)(2,1)S(1)} %collective-permute-done.13.refs_2_), channel_id=1, source_target_pairs={{0,1},{1,0},{2,3},{3,2},{4,5},{5,4},{6,7},{7,6},{8,9},{9,8},{10,11... | collective-permute-start | bytes 786440 | tf_op jit(solution)/shard_map/ppermute | solution.py:36
  78.9 34.8 %collective-permute-start.22 = (bf16[4,64,1792]{2,1,0:T(8,128)(2,1)S(1)}, bf16[4,64,1792]{2,1,0:T(8,128)(2,1)S(1)}, u32[]{:S(2)}, u32[]{:S(2)}) collective-permute-start(bf16[4,64,1792]{2,1,0:T(8,128)(2,1)S(1)} %copy-done.17), channel_id=1, source_target_pairs={{0,28},{4,0},{8,4},{12,8},{16,12},{20,16},{24,20},{28,24},{1,29},{... | collective-permute-start | bytes 2752520 | tf_op jit(solution)/shard_map/ppermute | solution.py:26
  79.1 9.8 %collective-permute-start.16 = (bf16[64,1024]{1,0:T(8,128)(2,1)S(1)}, bf16[64,1024]{1,0:T(8,128)(2,1)S(1)}, u32[]{:S(2)}, u32[]{:S(2)}) collective-permute-start(bf16[64,1024]{1,0:T(8,128)(2,1)S(1)} %get-tuple-element.61), channel_id=1, source_target_pairs={{0,1},{1,2},{2,3},{3,0},{4,5},{5,6},{6,7},{7,4},{8,9},{9,10},{10,1... | collective-permute-start | bytes 393224 | tf_op jit(solution)/shard_map/ppermute | solution.py:31
  79.3 9.7 %collective-permute-start.17 = (bf16[64,1024]{1,0:T(8,128)(2,1)S(1)}, bf16[64,1024]{1,0:T(8,128)(2,1)S(1)}, u32[]{:S(2)}, u32[]{:S(2)}) collective-permute-start(bf16[64,1024]{1,0:T(8,128)(2,1)S(1)} %get-tuple-element.62), channel_id=1, source_target_pairs={{0,2},{1,3},{2,0},{3,1},{4,6},{5,7},{6,4},{7,5},{8,10},{9,11},{10,... | collective-permute-start | bytes 393224 | tf_op jit(solution)/shard_map/ppermute | solution.py:31
  80.8 8.1 %collective-permute-start.18 = (bf16[64,1024]{1,0:T(8,128)(2,1)S(1)}, bf16[64,1024]{1,0:T(8,128)(2,1)S(1)}, u32[]{:S(2)}, u32[]{:S(2)}) collective-permute-start(bf16[64,1024]{1,0:T(8,128)(2,1)S(1)} %get-tuple-element.63), channel_id=1, source_target_pairs={{0,3},{1,0},{2,1},{3,2},{4,7},{5,4},{6,5},{7,6},{8,11},{9,8},{10,9... | collective-permute-start | bytes 393224 | tf_op jit(solution)/shard_map/ppermute | solution.py:31
  89.2 8.3 %collective-permute-start.19 = (bf16[64,2048]{1,0:T(8,128)(2,1)S(1)}, bf16[64,2048]{1,0:T(8,128)(2,1)S(1)}, u32[]{:S(2)}, u32[]{:S(2)}) collective-permute-start(bf16[64,2048]{1,0:T(8,128)(2,1)S(1)} %activation.6.refs_0_), channel_id=1, source_target_pairs={{0,2},{1,3},{2,0},{3,1},{4,6},{5,7},{6,4},{7,5},{8,10},{9,11},{10,... | collective-permute-start | bytes 786440 | tf_op jit(solution)/shard_map/ppermute | solution.py:31
  97.5 17.8 %collective-permute-start.21 = (bf16[64,2048]{1,0:T(8,128)(2,1)S(1)}, bf16[64,2048]{1,0:T(8,128)(2,1)S(1)}, u32[]{:S(2)}, u32[]{:S(2)}) collective-permute-start(bf16[64,2048]{1,0:T(8,128)(2,1)S(1)} %collective-permute-done.19.refs_2_), channel_id=1, source_target_pairs={{0,1},{1,0},{2,3},{3,2},{4,5},{5,4},{6,7},{7,6},{8,9},{9,8},{10,11... | collective-permute-start | bytes 786440 | tf_op jit(solution)/shard_map/ppermute | solution.py:36
  97.5 45.7 %collective-permute-start.29 = (bf16[4,64,1792]{2,1,0:T(8,128)(2,1)}, bf16[4,64,1792]{2,1,0:T(8,128)(2,1)}, u32[]{:S(2)}, u32[]{:S(2)}) collective-permute-start(bf16[4,64,1792]{2,1,0:T(8,128)(2,1)} %second_product.5), channel_id=1, source_target_pairs={{0,28},{4,0},{8,4},{12,8},{16,12},{20,16},{24,20},{28,24},{1,29},{... | collective-permute-start | bytes 2752520 | tf_op jit(solution)/shard_map/ppermute | solution.py:26
  102.5 16.1 %collective-permute-start.20 = (bf16[64,2048]{1,0:T(8,128)(2,1)S(1)}, bf16[64,2048]{1,0:T(8,128)(2,1)S(1)}, u32[]{:S(2)}, u32[]{:S(2)}) collective-permute-start(bf16[64,2048]{1,0:T(8,128)(2,1)S(1)} %activation.6.refs_0_), channel_id=1, source_target_pairs={{0,1},{1,0},{2,3},{3,2},{4,5},{5,4},{6,7},{7,6},{8,9},{9,8},{10,11... | collective-permute-start | bytes 786440 | tf_op jit(solution)/shard_map/ppermute | solution.py:36
  102.8 24.7 %collective-permute-start.23 = (bf16[64,1024]{1,0:T(8,128)(2,1)}, bf16[64,1024]{1,0:T(8,128)(2,1)}, u32[]{:S(2)}, u32[]{:S(2)}) collective-permute-start(bf16[64,1024]{1,0:T(8,128)(2,1)} %get-tuple-element.71), channel_id=1, source_target_pairs={{0,1},{1,2},{2,3},{3,0},{4,5},{5,6},{6,7},{7,4},{8,9},{9,10},{10,1... | collective-permute-start | bytes 393224 | tf_op jit(solution)/shard_map/ppermute | solution.py:31
  113.7 13.8 %collective-permute-start.24 = (bf16[64,1024]{1,0:T(8,128)(2,1)}, bf16[64,1024]{1,0:T(8,128)(2,1)}, u32[]{:S(2)}, u32[]{:S(2)}) collective-permute-start(bf16[64,1024]{1,0:T(8,128)(2,1)} %get-tuple-element.72), channel_id=1, source_target_pairs={{0,2},{1,3},{2,0},{3,1},{4,6},{5,7},{6,4},{7,5},{8,10},{9,11},{10,... | collective-permute-start | bytes 393224 | tf_op jit(solution)/shard_map/ppermute | solution.py:31
  115.3 12.2 %collective-permute-start.25 = (bf16[64,1024]{1,0:T(8,128)(2,1)}, bf16[64,1024]{1,0:T(8,128)(2,1)}, u32[]{:S(2)}, u32[]{:S(2)}) collective-permute-start(bf16[64,1024]{1,0:T(8,128)(2,1)} %get-tuple-element.73), channel_id=1, source_target_pairs={{0,3},{1,0},{2,1},{3,2},{4,7},{5,4},{6,5},{7,6},{8,11},{9,8},{10,9... | collective-permute-start | bytes 393224 | tf_op jit(solution)/shard_map/ppermute | solution.py:31
  128.7 8.8 %collective-permute-start.27 = (bf16[64,2048]{1,0:T(8,128)(2,1)S(1)}, bf16[64,2048]{1,0:T(8,128)(2,1)S(1)}, u32[]{:S(2)}, u32[]{:S(2)}) collective-permute-start(bf16[64,2048]{1,0:T(8,128)(2,1)S(1)} %activation.7.refs_0_), channel_id=1, source_target_pairs={{0,2},{1,3},{2,0},{3,1},{4,6},{5,7},{6,4},{7,5},{8,10},{9,11},{10,... | collective-permute-start | bytes 786440 | tf_op jit(solution)/shard_map/ppermute | solution.py:31
  137.5 9.0 %collective-permute-start.28 = (bf16[64,2048]{1,0:T(8,128)(2,1)S(1)}, bf16[64,2048]{1,0:T(8,128)(2,1)S(1)}, u32[]{:S(2)}, u32[]{:S(2)}) collective-permute-start(bf16[64,2048]{1,0:T(8,128)(2,1)S(1)} %collective-permute-done.27.refs_2_), channel_id=1, source_target_pairs={{0,1},{1,0},{2,3},{3,2},{4,5},{5,4},{6,7},{7,6},{8,9},{9,8},{10,11... | collective-permute-start | bytes 786440 | tf_op jit(solution)/shard_map/ppermute | solution.py:36
  137.5 9.0 %collective-permute-start.26 = (bf16[64,2048]{1,0:T(8,128)(2,1)S(1)}, bf16[64,2048]{1,0:T(8,128)(2,1)S(1)}, u32[]{:S(2)}, u32[]{:S(2)}) collective-permute-start(bf16[64,2048]{1,0:T(8,128)(2,1)S(1)} %activation.7.refs_0_), channel_id=1, source_target_pairs={{0,1},{1,0},{2,3},{3,2},{4,5},{5,4},{6,7},{7,6},{8,9},{9,8},{10,11... | collective-permute-start | bytes 786440 | tf_op jit(solution)/shard_map/ppermute | solution.py:36
  138.0 26.2 %collective-permute-start.31 = (bf16[4,64,1792]{2,1,0:T(8,128)(2,1)}, bf16[4,64,1792]{2,1,0:T(8,128)(2,1)}, u32[]{:S(2)}, u32[]{:S(2)}) collective-permute-start(bf16[4,64,1792]{2,1,0:T(8,128)(2,1)} %second_product.6), channel_id=1, source_target_pairs={{0,28},{4,0},{8,4},{12,8},{16,12},{20,16},{24,20},{28,24},{1,29},{... | collective-permute-start | bytes 2752520 | tf_op jit(solution)/shard_map/ppermute | solution.py:26
  154.4 28.4 %collective-permute-start.30 = (bf16[4,64,1792]{2,1,0:T(8,128)(2,1)S(1)}, bf16[4,64,1792]{2,1,0:T(8,128)(2,1)S(1)}, u32[]{:S(2)}, u32[]{:S(2)}) collective-permute-start(bf16[4,64,1792]{2,1,0:T(8,128)(2,1)S(1)} %second_product.7), channel_id=1, source_target_pairs={{0,28},{4,0},{8,4},{12,8},{16,12},{20,16},{24,20},{28,24},{1,29},{... | collective-permute-start | bytes 2752520 | tf_op jit(solution)/shard_map/ppermute | solution.py:26
  (25 other events, 153.4 us)

commit v3 on v2

--- a/solution.py
+++ b/solution.py
@@ -8,12 +8,13 @@
 from jax.sharding import PartitionSpec as P
 
 CHUNKS = 4
+START = {2: 0, 3: 1}
+WAIT = {("act", 3): (0,), ("mm2", 3): (1,), ("out", 2): (0,), ("out", 3): (1,)}
 FREE = pl.CostEstimate(flops=0, bytes_accessed=0, transcendentals=0)
-FAR = pl.BlockSpec(memory_space=pl.ANY)
 
 
 def params(**kwargs):
-    return pltpu.CompilerParams(vmem_limit_bytes=24 * 1024 * 1024, **kwargs)
+    return pltpu.CompilerParams(vmem_limit_bytes=48 * 1024 * 1024, **kwargs)
 
 
 def block_of(size, most):
@@ -44,42 +45,6 @@
     return lax.dot_general(
         left, right, (((1,), (1,)), ((), ())), preferred_element_type=jnp.float32
     )
-
-
-def take_kernel(source_ref, out_ref):
-    out_ref[...] = source_ref[...]
-
-
-def put_kernel(source_ref, *refs):
-    refs[-1][...] = source_ref[...]
-
-
-def take_rows(array, c, part):
-    n, _, width = array.shape
-    return pl.pallas_call(
-        take_kernel,
-        out_shape=jax.ShapeDtypeStruct((n, part, width), array.dtype),
-        grid=(n,),
-        in_specs=[pl.BlockSpec((1, part, width), lambda i: (i, c, 0))],
-        out_specs=pl.BlockSpec((1, part, width), lambda i: (i, 0, 0)),
-        cost_estimate=FREE,
-        name="take_rows",
-    )(array)
-
-
-def put_rows(out, piece, c, rows):
-    n, part, width = piece.shape
-    spec = pl.BlockSpec((1, part, width), lambda i: (i, 0, 0))
-    return pl.pallas_call(
-        put_kernel,
-        out_shape=jax.ShapeDtypeStruct((n, rows, width), piece.dtype),
-        grid=(n,),
-        in_specs=[spec] + ([] if out is None else [FAR]),
-        out_specs=pl.BlockSpec((1, part, width), lambda i: (i, c, 0)),
-        input_output_aliases={} if out is None else {1: 0},
-        cost_estimate=FREE,
-        name="put_rows",
-    )(*((piece,) if out is None else (piece, out)))
 
 
 def routed_kernel(grad_ref, score_ref, chosen_ref, out_ref):
@@ -241,38 +206,53 @@
     chunks = min(CHUNKS, rows // 16)
     part = rows // chunks
     grads = upstream.reshape(n, rows, width)
-    arrived = [back_one(take_rows(grads, c, part)) for c in range(chunks)]
+    arrived, sent = [], []
     dense = routed_grad(gate_grad[0], gate_scores[0], expert_ids[0], router_weight.shape[2])
+    for c in range(chunks):
+        source = grads
+        if c in START and START[c] < c:
+            source, arrived[START[c]] = in_order(source, arrived[START[c]])
+        elif c > 0:
+            source, dense = in_order(source, dense)
+        arrived.append(back_one(source[:, c * part : (c + 1) * part]))
     dense = dense.reshape(n, rows, -1)
+
+    def at(point, c, x):
+        for p in WAIT.get((point, c), ()):
+            x, sent[p] = in_order(x, sent[p])
+        return x
 
     def partial_sums(c):
         own, *others = first_product(me, arrived[c], shared_down[0])
+        others[0] = at("rs", c, others[0])
         return [own] + [to_expert(x, j + 1) for j, x in enumerate(others)]
 
     arrived[0], dense = in_order(arrived[0], dense)
     own = activation(gate_pre[0], up_pre[0], 0, partial_sums(0))
-    out, sent = None, []
     for c in range(chunks):
+        own = at("agy", c, own)
         near = [own] + [to_expert(own, 2 * step) for step in range(1, chips)]
         far = [to_other_core(own)]
         if c + 1 < chunks:
             arrived[c + 1], own = in_order(arrived[c + 1], own)
             partials = partial_sums(c + 1)
             partials[0], near[-1] = in_order(partials[0], near[-1])
+        near[-1] = at("agc", c, near[-1])
         far += [to_other_core(x) for x in near[1:]]
-        if c >= 2:
-            far[-1], out = in_order(far[-1], out)
+        far[-1] = at("mm2", c, far[-1])
         blocks = [x for pair in zip(near, far) for x in pair]
         result = second_product(
             me, blocks, c, dense, shared_gate[0], shared_up[0], router_weight[0]
         )
         if c + 1 < chunks:
             partials[0], result = in_order(partials[0], result)
+            partials[0] = at("act", c + 1, partials[0])
             own = activation(gate_pre[0], up_pre[0], c + 1, partials)
+        result = at("out", c, result)
         sent.append(back_one(result))
-        if c >= 1:
-            out = put_rows(out, sent[c - 1], c - 1, rows)
-    out = put_rows(out, sent[-1], chunks - 1, rows)
+    out = jnp.zeros((n, rows, width), jnp.bfloat16)
+    for c in range(chunks):
+        out = lax.dynamic_update_slice(out, sent[c], (0, c * part, 0))
     return out.reshape(1, tokens, width)
 
 

time: 188 us -> 169 us (0.90)
  Pallas kernels: 63.8 us -> 43.4 us
  starting transfers between devices: 41.4 us -> 51.4 us
  local copies, waits for them, and re-layouts: 24 us -> 16.6 us
    pallas_call x8 -> x0, Pallas kernels: 26.5 us -> none  [the longest x4 13.2 us: put_rows(): pl.pallas_call(put_kernel, out_shape=jax.ShapeDtypeStruct((n, rows, width...]
    unnamed x53 -> x17, local copies, waits for them, and re-layouts: 24 us -> 9.22 us
    pallas_call x4, Pallas kernels: 17.2 us -> 28.3 us  [second_product(): pl.pallas_call(functools.partial(second_kernel, n), out_shape=jax.ShapeDt...]
    ppermute x8, starting transfers between devices: 26.5 us -> 34.9 us  [back_one(): lax.ppermute(x, 'pipe', [(i, (i - 1) % length) for i in range(length)])]
    slice x0 -> x4, local copies, waits for them, and re-layouts: none -> 6.93 us  [shards(): arrived.append(back_one(source[:, c * part:(c + 1) * part]))]
    pallas_call x4, Pallas kernels: 10.4 us -> 7.42 us  [first_product(): pl.pallas_call(functools.partial(first_kernel, n), out_shape=[jax.ShapeDt...]
    ppermute x16, waiting for transfers between devices: 8.69 us -> 6.32 us  [to_expert(): return lax.ppermute(x, 'expert', [(i, (i + by) % n) for i in range(n)])]
    pallas_call x4, Pallas kernels: 2.88 us -> 0.81 us  [activation(): pl.pallas_call(activation_kernel, out_shape=jax.ShapeDtypeStruct((part, 2...]
  transfers between devices with their start and end apart: 32 -> 32, of which waited for: 8 -> 9; matrix products, arithmetic and copies ran while one was open for 2% -> 6% of each run, Pallas kernels for 31% -> 26%
where the time goes in v3:
time: 169 us; the launch traced here: 168 us
  waiting for transfers between devices  56.4 us (33%)
  starting transfers between devices  51.4 us (30%)
  Pallas kernels  43.4 us (26%)
  local copies, waits for them, and re-layouts  16.6 us (10%)
    ppermute x8, waiting for transfers between devices, back_one(): lax.ppermute(x, 'pipe', [(i, (i - 1) % length) for i in range(length)])  50.1 us
    ppermute x8, starting transfers between devices, back_one(): lax.ppermute(x, 'pipe', [(i, (i - 1) % length) for i in range(length)])  34.9 us
    pallas_call x4, Pallas kernels, second_product(): pl.pallas_call(functools.partial(second_kernel, n), out_shape=jax.ShapeDt...  28.3 us
    ppermute x16, starting transfers between devices, to_expert(): return lax.ppermute(x, 'expert', [(i, (i + by) % n) for i in range(n)])  15.4 us
    unnamed x17, local copies, waits for them, and re-layouts  9.22 us
    pallas_call x4, Pallas kernels, first_product(): pl.pallas_call(functools.partial(first_kernel, n), out_shape=[jax.ShapeDt...  7.42 us
    slice x4, local copies, waits for them, and re-layouts, shards(): arrived.append(back_one(source[:, c * part:(c + 1) * part]))  6.93 us
    pallas_call x1, Pallas kernels, routed_grad(): pl.pallas_call(routed_kernel, out_shape=jax.ShapeDtypeStruct((tokens, n_e...  6.85 us
  transfers between devices with their start and end apart: 32, of which 9 were waited for; matrix products, arithmetic and copies ran while one was open for 6% of the time, Pallas kernels for 26%

profile of v3, /device:TPU:0, one launch (start us, length us, event | category | flops | bytes accessed | tf_op | source)
XLA Modules:
  0.0 168.1 jit_solution(7879693078935955878)
XLA Ops:
  0.0 2.2 %slice.16 = bf16[4,64,1792]{2,1,0:T(8,128)(2,1)} slice(bf16[4,256,1792]{2,1,0:T(8,128)(2,1)} %bitcast.41), slice={[0:4], [0:64], [0:1792]} | slice | bytes 1835008 | tf_op jit(solution)/shard_map/slice | solution.py:217
  2.2 6.0 %collective-permute-start.2 = (bf16[4,64,1792]{2,1,0:T(8,128)(2,1)}, bf16[4,64,1792]{2,1,0:T(8,128)(2,1)S(1)}, u32[]{:S(2)}, u32[]{:S(2)}) collective-permute-start(bf16[4,64,1792]{2,1,0:T(8,128)(2,1)} %slice.16), channel_id=1, source_target_pairs={{0,28},{4,0},{8,4},{12,8},{16,12},{20,16},{24,20},{28,24},{1,29},{... | collective-permute-start | bytes 2752520 | tf_op jit(solution)/shard_map/ppermute | solution.py:27
  8.1 1.8 %copy.11 = f32[1,1024,8]{2,1,0:T(8,128)} copy(f32[1,1024,8]{1,2,0:T(8,128)} %param.17) | data formatting | bytes 65536 | tf_op args[7]
  9.9 1.8 %copy.12 = f32[1,1024,8]{2,1,0:T(8,128)} copy(f32[1,1024,8]{1,2,0:T(8,128)} %param.18) | data formatting | bytes 65536 | tf_op args[8]
  11.7 1.8 %copy.13 = s32[1,1024,8]{2,1,0:T(8,128)} copy(s32[1,1024,8]{1,2,0:T(8,128)} %param.19) | data formatting | bytes 65536 | tf_op args[9]
  13.5 6.8 %routed_grad.1 = bf16[1024,256]{1,0:T(8,128)(2,1)} custom-call(f32[1024,8]{1,0:T(8,128)} %bitcast.45, f32[1024,8]{1,0:T(8,128)} %bitcast.46, s32[1024,8]{1,0:T(8,128)} %bitcast.47), custom_call_target="tpu_custom_call" | custom-call | tf_op jit(solution)/shard_map/routed_grad/pallas_call | solution.py:67
  20.3 2.3 %slice.12 = bf16[4,64,1792]{2,1,0:T(8,128)(2,1)} slice(bf16[4,256,1792]{2,1,0:T(8,128)(2,1)} %bitcast.42), slice={[0:4], [64:128], [0:1792]} | slice | bytes 1835008 | tf_op jit(solution)/shard_map/slice | solution.py:217
  23.1 6.1 %collective-permute-done.2.rows_ref = bf16[4,64,1792]{2,1,0:T(8,128)(2,1)S(1)} collective-permute-done((bf16[4,64,1792]{2,1,0:T(8,128)(2,1)}, bf16[4,64,1792]{2,1,0:T(8,128)(2,1)S(1)}, u32[]{:S(2)}, u32[]{:S(2)}) %collective-permute-start.2) | collective-permute-done | bytes 917536 | tf_op jit(solution)/shard_map/ppermute | solution.py:27
  29.2 2.0 %copy-done = bf16[1,1024,1792]{2,1,0:T(8,128)(2,1)S(1)} copy-done((bf16[1,1024,1792]{2,1,0:T(8,128)(2,1)S(1)}, bf16[1,1024,1792]{2,1,0:T(8,128)(2,1)}, u32[]{:S(2)}) %copy-start) | copy-done | bytes 3670040
  31.3 1.9 %first_product.4 = (bf16[64,1024]{1,0:T(8,128)(2,1)S(1)}, bf16[64,1024]{1,0:T(8,128)(2,1)S(1)}, bf16[64,1024]{1,0:T(8,128)(2,1)S(1)}, bf16[64,1024]{1,0:T(8,128)(2,1)S(1)}) custom-call(s32[1]{0:T(128)} %bitcast.me_ref, bf16[4,64,1792]{2,1,0:T(8,128)(2,1)S(1)} %collective-permute-done.2.rows_ref, bf16[1024,1792]{1,0:T(8,128)(2,1)S(1)} %bitcast.13), custom_call_target="tpu_custom_call" | custom-call | tf_op jit(solution)/shard_map/first_product/pallas_call | solution.py:91
  37.4 5.1 %collective-permute-start.3 = (bf16[4,64,1792]{2,1,0:T(8,128)(2,1)S(1)}, bf16[4,64,1792]{2,1,0:T(8,128)(2,1)S(1)}, u32[]{:S(2)}, u32[]{:S(2)}) collective-permute-start(bf16[4,64,1792]{2,1,0:T(8,128)(2,1)S(1)} %slice.15), channel_id=1, source_target_pairs={{0,28},{4,0},{8,4},{12,8},{16,12},{20,16},{24,20},{28,24},{1,29},{... | collective-permute-start | bytes 2752520 | tf_op jit(solution)/shard_map/ppermute | solution.py:27
  43.4 5.5 %collective-permute-done.rows_ref = bf16[4,64,1792]{2,1,0:T(8,128)(2,1)S(1)} collective-permute-done((bf16[4,64,1792]{2,1,0:T(8,128)(2,1)}, bf16[4,64,1792]{2,1,0:T(8,128)(2,1)S(1)}, u32[]{:S(2)}, u32[]{:S(2)}) %collective-permute-start) | collective-permute-done | bytes 917536 | tf_op jit(solution)/shard_map/ppermute | solution.py:27
  48.9 1.9 %first_product.5 = (bf16[64,1024]{1,0:T(8,128)(2,1)S(1)}, bf16[64,1024]{1,0:T(8,128)(2,1)S(1)}, bf16[64,1024]{1,0:T(8,128)(2,1)S(1)}, bf16[64,1024]{1,0:T(8,128)(2,1)S(1)}) custom-call(s32[1]{0:T(128)} %bitcast.me_ref, bf16[4,64,1792]{2,1,0:T(8,128)(2,1)S(1)} %collective-permute-done.rows_ref, bf16[1024,1792]{1,0:T(8,128)(2,1)S(1)} %bitcast.14), custom_call_target="tpu_custom_call" | custom-call | tf_op jit(solution)/shard_map/first_product/pallas_call | solution.py:91
  53.9 7.1 %second_product.4 = bf16[4,64,1792]{2,1,0:T(8,128)(2,1)S(1)} custom-call(s32[1]{0:T(128)} %bitcast.me_ref, bf16[4,256,256]{2,1,0:T(8,128)(2,1)S(1)} %bitcast.21, bf16[1792,1024]{1,0:T(8,128)(2,1)} %bitcast.33, bf16[1792,1024]{1,0:T(8,128)(2,1)} %bitcast.37, bf16[1792,256]{1,0:T(8,128)(2,1)S(1)} %bitcast.17, bf16[64,2048]{1,0:T(8,128)(2,1)S(1)} %activation.4.refs_0_, ...), custom_call_target="tpu_custom_call" | custom-call | tf_op jit(solution)/shard_map/second_product/pallas_call | solution.py:167
  63.1 5.1 %collective-permute-start.1 = (bf16[4,64,1792]{2,1,0:T(8,128)(2,1)S(1)}, bf16[4,64,1792]{2,1,0:T(8,128)(2,1)S(1)}, u32[]{:S(2)}, u32[]{:S(2)}) collective-permute-start(bf16[4,64,1792]{2,1,0:T(8,128)(2,1)S(1)} %slice.13), channel_id=1, source_target_pairs={{0,28},{4,0},{8,4},{12,8},{16,12},{20,16},{24,20},{28,24},{1,29},{... | collective-permute-start | bytes 2752520 | tf_op jit(solution)/shard_map/ppermute | solution.py:27
  68.2 1.8 %first_product.6 = (bf16[64,1024]{1,0:T(8,128)(2,1)S(1)}, bf16[64,1024]{1,0:T(8,128)(2,1)S(1)}, bf16[64,1024]{1,0:T(8,128)(2,1)S(1)}, bf16[64,1024]{1,0:T(8,128)(2,1)S(1)}) custom-call(s32[1]{0:T(128)} %bitcast.me_ref, bf16[4,64,1792]{2,1,0:T(8,128)(2,1)S(1)} %collective-permute-done.3.rows_ref, bf16[1024,1792]{1,0:T(8,128)(2,1)S(1)} %bitcast.15), custom_call_target="tpu_custom_call" | custom-call | tf_op jit(solution)/shard_map/first_product/pallas_call | solution.py:91
  70.6 3.8 %collective-permute-start.22 = (bf16[4,64,1792]{2,1,0:T(8,128)(2,1)S(1)}, bf16[4,64,1792]{2,1,0:T(8,128)(2,1)S(1)}, u32[]{:S(2)}, u32[]{:S(2)}) collective-permute-start(bf16[4,64,1792]{2,1,0:T(8,128)(2,1)S(1)} %second_product.4), channel_id=1, source_target_pairs={{0,28},{4,0},{8,4},{12,8},{16,12},{20,16},{24,20},{28,24},{1,29},{... | collective-permute-start | bytes 2752520 | tf_op jit(solution)/shard_map/ppermute | solution.py:27
  77.4 7.1 %second_product.5 = bf16[4,64,1792]{2,1,0:T(8,128)(2,1)S(1)} custom-call(s32[1]{0:T(128)} %bitcast.me_ref, bf16[4,256,256]{2,1,0:T(8,128)(2,1)S(1)} %bitcast.22, bf16[1792,1024]{1,0:T(8,128)(2,1)} %bitcast.34, bf16[1792,1024]{1,0:T(8,128)(2,1)} %bitcast.38, bf16[1792,256]{1,0:T(8,128)(2,1)S(1)} %bitcast.18, bf16[64,2048]{1,0:T(8,128)(2,1)S(1)} %activation.5.refs_0_, ...), custom_call_target="tpu_custom_call" | custom-call | tf_op jit(solution)/shard_map/second_product/pallas_call | solution.py:167
  85.3 3.6 %collective-permute-done.1.rows_ref = bf16[4,64,1792]{2,1,0:T(8,128)(2,1)S(1)} collective-permute-done((bf16[4,64,1792]{2,1,0:T(8,128)(2,1)S(1)}, bf16[4,64,1792]{2,1,0:T(8,128)(2,1)S(1)}, u32[]{:S(2)}, u32[]{:S(2)}) %collective-permute-start.1) | collective-permute-done | bytes 917536 | tf_op jit(solution)/shard_map/ppermute | solution.py:27
  89.0 1.8 %first_product.7 = (bf16[64,1024]{1,0:T(8,128)(2,1)S(1)}, bf16[64,1024]{1,0:T(8,128)(2,1)S(1)}, bf16[64,1024]{1,0:T(8,128)(2,1)S(1)}, bf16[64,1024]{1,0:T(8,128)(2,1)S(1)}) custom-call(s32[1]{0:T(128)} %bitcast.me_ref, bf16[4,64,1792]{2,1,0:T(8,128)(2,1)S(1)} %collective-permute-done.1.rows_ref, bf16[1024,1792]{1,0:T(8,128)(2,1)S(1)} %bitcast.16), custom_call_target="tpu_custom_call" | custom-call | tf_op jit(solution)/shard_map/first_product/pallas_call | solution.py:91
  92.3 3.9 %collective-permute-start.29 = (bf16[4,64,1792]{2,1,0:T(8,128)(2,1)S(1)}, bf16[4,64,1792]{2,1,0:T(8,128)(2,1)S(1)}, u32[]{:S(2)}, u32[]{:S(2)}) collective-permute-start(bf16[4,64,1792]{2,1,0:T(8,128)(2,1)S(1)} %second_product.5), channel_id=1, source_target_pairs={{0,28},{4,0},{8,4},{12,8},{16,12},{20,16},{24,20},{28,24},{1,29},{... | collective-permute-start | bytes 2752520 | tf_op jit(solution)/shard_map/ppermute | solution.py:27
  99.1 7.1 %second_product.6 = bf16[4,64,1792]{2,1,0:T(8,128)(2,1)S(1)} custom-call(s32[1]{0:T(128)} %bitcast.me_ref, bf16[4,256,256]{2,1,0:T(8,128)(2,1)S(1)} %bitcast.23, bf16[1792,1024]{1,0:T(8,128)(2,1)} %bitcast.35, bf16[1792,1024]{1,0:T(8,128)(2,1)} %bitcast.39, bf16[1792,256]{1,0:T(8,128)(2,1)S(1)} %bitcast.19, bf16[64,2048]{1,0:T(8,128)(2,1)S(1)} %activation.6.refs_0_, ...), custom_call_target="tpu_custom_call" | custom-call | tf_op jit(solution)/shard_map/second_product/pallas_call | solution.py:167
  106.2 2.4 %collective-permute-done.22 = bf16[4,64,1792]{2,1,0:T(8,128)(2,1)S(1)} collective-permute-done((bf16[4,64,1792]{2,1,0:T(8,128)(2,1)S(1)}, bf16[4,64,1792]{2,1,0:T(8,128)(2,1)S(1)}, u32[]{:S(2)}, u32[]{:S(2)}) %collective-permute-start.22) | collective-permute-done | bytes 917536 | tf_op jit(solution)/shard_map/ppermute | solution.py:27
  108.9 1.6 collective-permute-start.27
  110.4 4.8 %collective-permute-done.27.refs_2_ = bf16[64,2048]{1,0:T(8,128)(2,1)S(1)} collective-permute-done((bf16[64,2048]{1,0:T(8,128)(2,1)S(1)}, bf16[64,2048]{1,0:T(8,128)(2,1)S(1)}, u32[]{:S(2)}, u32[]{:S(2)}) %collective-permute-start.27) | collective-permute-done | bytes 262176 | tf_op jit(solution)/shard_map/ppermute | solution.py:32
  115.8 5.2 %collective-permute-start.30 = (bf16[4,64,1792]{2,1,0:T(8,128)(2,1)S(1)}, bf16[4,64,1792]{2,1,0:T(8,128)(2,1)S(1)}, u32[]{:S(2)}, u32[]{:S(2)}) collective-permute-start(bf16[4,64,1792]{2,1,0:T(8,128)(2,1)S(1)} %second_product.6), channel_id=1, source_target_pairs={{0,28},{4,0},{8,4},{12,8},{16,12},{20,16},{24,20},{28,24},{1,29},{... | collective-permute-start | bytes 2752520 | tf_op jit(solution)/shard_map/ppermute | solution.py:27
  121.0 7.3 %collective-permute-done.29 = bf16[4,64,1792]{2,1,0:T(8,128)(2,1)S(1)} collective-permute-done((bf16[4,64,1792]{2,1,0:T(8,128)(2,1)S(1)}, bf16[4,64,1792]{2,1,0:T(8,128)(2,1)S(1)}, u32[]{:S(2)}, u32[]{:S(2)}) %collective-permute-start.29) | collective-permute-done | bytes 917536 | tf_op jit(solution)/shard_map/ppermute | solution.py:27
  128.3 7.1 %second_product.7 = bf16[4,64,1792]{2,1,0:T(8,128)(2,1)S(1)} custom-call(s32[1]{0:T(128)} %bitcast.me_ref, bf16[4,256,256]{2,1,0:T(8,128)(2,1)S(1)} %bitcast.24, bf16[1792,1024]{1,0:T(8,128)(2,1)} %bitcast.36, bf16[1792,1024]{1,0:T(8,128)(2,1)} %bitcast.40, bf16[1792,256]{1,0:T(8,128)(2,1)S(1)} %bitcast.20, bf16[64,2048]{1,0:T(8,128)(2,1)S(1)} %activation.7.refs_0_, ...), custom_call_target="tpu_custom_call" | custom-call | tf_op jit(solution)/shard_map/second_product/pallas_call | solution.py:167
  135.4 5.2 %collective-permute-start.31 = (bf16[4,64,1792]{2,1,0:T(8,128)(2,1)S(1)}, bf16[4,64,1792]{2,1,0:T(8,128)(2,1)S(1)}, u32[]{:S(2)}, u32[]{:S(2)}) collective-permute-start(bf16[4,64,1792]{2,1,0:T(8,128)(2,1)S(1)} %second_product.7), channel_id=1, source_target_pairs={{0,28},{4,0},{8,4},{12,8},{16,12},{20,16},{24,20},{28,24},{1,29},{... | collective-permute-start | bytes 2752520 | tf_op jit(solution)/shard_map/ppermute | solution.py:27
  140.9 7.0 %collective-permute-done.30 = bf16[4,64,1792]{2,1,0:T(8,128)(2,1)S(1)} collective-permute-done((bf16[4,64,1792]{2,1,0:T(8,128)(2,1)S(1)}, bf16[4,64,1792]{2,1,0:T(8,128)(2,1)S(1)}, u32[]{:S(2)}, u32[]{:S(2)}) %collective-permute-start.30) | collective-permute-done | bytes 917536 | tf_op jit(solution)/shard_map/ppermute | solution.py:27
  148.0 18.2 %collective-permute-done.31 = bf16[4,64,1792]{2,1,0:T(8,128)(2,1)S(1)} collective-permute-done((bf16[4,64,1792]{2,1,0:T(8,128)(2,1)S(1)}, bf16[4,64,1792]{2,1,0:T(8,128)(2,1)S(1)}, u32[]{:S(2)}, u32[]{:S(2)}) %collective-permute-start.31) | collective-permute-done | bytes 917536 | tf_op jit(solution)/shard_map/ppermute | solution.py:27
  166.3 1.8 %copy-done.6 = bf16[4,256,1792]{2,1,0:T(8,128)(2,1)} copy-done((bf16[4,256,1792]{2,1,0:T(8,128)(2,1)}, bf16[4,256,1792]{2,1,0:T(8,128)(2,1)S(1)}, u32[]{:S(2)}) %copy-start.6) | copy-done | bytes 3670040
  (70 shorter events, 20.7 us)
Async XLA Ops:
  2.2 27.0 %collective-permute-start.2 = (bf16[4,64,1792]{2,1,0:T(8,128)(2,1)}, bf16[4,64,1792]{2,1,0:T(8,128)(2,1)S(1)}, u32[]{:S(2)}, u32[]{:S(2)}) collective-permute-start(bf16[4,64,1792]{2,1,0:T(8,128)(2,1)} %slice.16), channel_id=1, source_target_pairs={{0,28},{4,0},{8,4},{12,8},{16,12},{20,16},{24,20},{28,24},{1,29},{... | collective-permute-start | bytes 2752520 | tf_op jit(solution)/shard_map/ppermute | solution.py:27
  22.6 26.3 %collective-permute-start = (bf16[4,64,1792]{2,1,0:T(8,128)(2,1)}, bf16[4,64,1792]{2,1,0:T(8,128)(2,1)S(1)}, u32[]{:S(2)}, u32[]{:S(2)}) collective-permute-start(bf16[4,64,1792]{2,1,0:T(8,128)(2,1)} %slice.12), channel_id=1, source_target_pairs={{0,28},{4,0},{8,4},{12,8},{16,12},{20,16},{24,20},{28,24},{1,29},{... | collective-permute-start | bytes 2752520 | tf_op jit(solution)/shard_map/ppermute | solution.py:27
  33.1 9.4 %collective-permute-start.4 = (bf16[64,1024]{1,0:T(8,128)(2,1)S(1)}, bf16[64,1024]{1,0:T(8,128)(2,1)S(1)}, u32[]{:S(2)}, u32[]{:S(2)}) collective-permute-start(bf16[64,1024]{1,0:T(8,128)(2,1)S(1)} %get-tuple-element.60), channel_id=1, source_target_pairs={{0,1},{1,2},{2,3},{3,0},{4,5},{5,6},{6,7},{7,4},{8,9},{9,10},{10,1... | collective-permute-start | bytes 393224 | tf_op jit(solution)/shard_map/ppermute | solution.py:32
  33.2 9.4 %collective-permute-start.5 = (bf16[64,1024]{1,0:T(8,128)(2,1)S(1)}, bf16[64,1024]{1,0:T(8,128)(2,1)S(1)}, u32[]{:S(2)}, u32[]{:S(2)}) collective-permute-start(bf16[64,1024]{1,0:T(8,128)(2,1)S(1)} %get-tuple-element.61), channel_id=1, source_target_pairs={{0,2},{1,3},{2,0},{3,1},{4,6},{5,7},{6,4},{7,5},{8,10},{9,11},{10,... | collective-permute-start | bytes 393224 | tf_op jit(solution)/shard_map/ppermute | solution.py:32
  34.8 7.8 %collective-permute-start.6 = (bf16[64,1024]{1,0:T(8,128)(2,1)S(1)}, bf16[64,1024]{1,0:T(8,128)(2,1)S(1)}, u32[]{:S(2)}, u32[]{:S(2)}) collective-permute-start(bf16[64,1024]{1,0:T(8,128)(2,1)S(1)} %get-tuple-element.62), channel_id=1, source_target_pairs={{0,3},{1,0},{2,1},{3,2},{4,7},{5,4},{6,5},{7,6},{8,11},{9,8},{10,9... | collective-permute-start | bytes 393224 | tf_op jit(solution)/shard_map/ppermute | solution.py:32
  37.4 30.8 %collective-permute-start.3 = (bf16[4,64,1792]{2,1,0:T(8,128)(2,1)S(1)}, bf16[4,64,1792]{2,1,0:T(8,128)(2,1)S(1)}, u32[]{:S(2)}, u32[]{:S(2)}) collective-permute-start(bf16[4,64,1792]{2,1,0:T(8,128)(2,1)S(1)} %slice.15), channel_id=1, source_target_pairs={{0,28},{4,0},{8,4},{12,8},{16,12},{20,16},{24,20},{28,24},{1,29},{... | collective-permute-start | bytes 2752520 | tf_op jit(solution)/shard_map/ppermute | solution.py:27
  42.8 8.0 %collective-permute-start.7 = (bf16[64,2048]{1,0:T(8,128)(2,1)S(1)}, bf16[64,2048]{1,0:T(8,128)(2,1)S(1)}, u32[]{:S(2)}, u32[]{:S(2)}) collective-permute-start(bf16[64,2048]{1,0:T(8,128)(2,1)S(1)} %activation.4.refs_0_), channel_id=1, source_target_pairs={{0,2},{1,3},{2,0},{3,1},{4,6},{5,7},{6,4},{7,5},{8,10},{9,11},{10,... | collective-permute-start | bytes 786440 | tf_op jit(solution)/shard_map/ppermute | solution.py:32
  43.4 9.5 %collective-permute-start.8 = (bf16[64,2048]{1,0:T(8,128)(2,1)S(1)}, bf16[64,2048]{1,0:T(8,128)(2,1)S(1)}, u32[]{:S(2)}, u32[]{:S(2)}) collective-permute-start(bf16[64,2048]{1,0:T(8,128)(2,1)S(1)} %activation.4.refs_0_), channel_id=1, source_target_pairs={{0,1},{1,0},{2,3},{3,2},{4,5},{5,4},{6,7},{7,6},{8,9},{9,8},{10,11... | collective-permute-start | bytes 786440 | tf_op jit(solution)/shard_map/ppermute | solution.py:37
  50.8 3.1 %collective-permute-start.9 = (bf16[64,2048]{1,0:T(8,128)(2,1)S(1)}, bf16[64,2048]{1,0:T(8,128)(2,1)S(1)}, u32[]{:S(2)}, u32[]{:S(2)}) collective-permute-start(bf16[64,2048]{1,0:T(8,128)(2,1)S(1)} %collective-permute-done.7.refs_2_), channel_id=1, source_target_pairs={{0,1},{1,0},{2,3},{3,2},{4,5},{5,4},{6,7},{7,6},{8,9},{9,8},{10,11... | collective-permute-start | bytes 786440 | tf_op jit(solution)/shard_map/ppermute | solution.py:37
  50.8 10.2 %collective-permute-start.10 = (bf16[64,1024]{1,0:T(8,128)(2,1)S(1)}, bf16[64,1024]{1,0:T(8,128)(2,1)S(1)}, u32[]{:S(2)}, u32[]{:S(2)}) collective-permute-start(bf16[64,1024]{1,0:T(8,128)(2,1)S(1)} %get-tuple-element.69), channel_id=1, source_target_pairs={{0,1},{1,2},{2,3},{3,0},{4,5},{5,6},{6,7},{7,4},{8,9},{9,10},{10,1... | collective-permute-start | bytes 393224 | tf_op jit(solution)/shard_map/ppermute | solution.py:32
  51.3 9.7 %collective-permute-start.11 = (bf16[64,1024]{1,0:T(8,128)(2,1)S(1)}, bf16[64,1024]{1,0:T(8,128)(2,1)S(1)}, u32[]{:S(2)}, u32[]{:S(2)}) collective-permute-start(bf16[64,1024]{1,0:T(8,128)(2,1)S(1)} %get-tuple-element.70), channel_id=1, source_target_pairs={{0,2},{1,3},{2,0},{3,1},{4,6},{5,7},{6,4},{7,5},{8,10},{9,11},{10,... | collective-permute-start | bytes 393224 | tf_op jit(solution)/shard_map/ppermute | solution.py:32
  52.9 8.2 %collective-permute-start.12 = (bf16[64,1024]{1,0:T(8,128)(2,1)S(1)}, bf16[64,1024]{1,0:T(8,128)(2,1)S(1)}, u32[]{:S(2)}, u32[]{:S(2)}) collective-permute-start(bf16[64,1024]{1,0:T(8,128)(2,1)S(1)} %get-tuple-element.71), channel_id=1, source_target_pairs={{0,3},{1,0},{2,1},{3,2},{4,7},{5,4},{6,5},{7,6},{8,11},{9,8},{10,9... | collective-permute-start | bytes 393224 | tf_op jit(solution)/shard_map/ppermute | solution.py:32
  61.2 8.8 %collective-permute-start.13 = (bf16[64,2048]{1,0:T(8,128)(2,1)S(1)}, bf16[64,2048]{1,0:T(8,128)(2,1)S(1)}, u32[]{:S(2)}, u32[]{:S(2)}) collective-permute-start(bf16[64,2048]{1,0:T(8,128)(2,1)S(1)} %activation.5.refs_0_), channel_id=1, source_target_pairs={{0,2},{1,3},{2,0},{3,1},{4,6},{5,7},{6,4},{7,5},{8,10},{9,11},{10,... | collective-permute-start | bytes 786440 | tf_op jit(solution)/shard_map/ppermute | solution.py:32
  63.1 25.9 %collective-permute-start.1 = (bf16[4,64,1792]{2,1,0:T(8,128)(2,1)S(1)}, bf16[4,64,1792]{2,1,0:T(8,128)(2,1)S(1)}, u32[]{:S(2)}, u32[]{:S(2)}) collective-permute-start(bf16[4,64,1792]{2,1,0:T(8,128)(2,1)S(1)} %slice.13), channel_id=1, source_target_pairs={{0,28},{4,0},{8,4},{12,8},{16,12},{20,16},{24,20},{28,24},{1,29},{... | collective-permute-start | bytes 2752520 | tf_op jit(solution)/shard_map/ppermute | solution.py:27
  68.2 6.4 %collective-permute-start.14 = (bf16[64,2048]{1,0:T(8,128)(2,1)S(1)}, bf16[64,2048]{1,0:T(8,128)(2,1)S(1)}, u32[]{:S(2)}, u32[]{:S(2)}) collective-permute-start(bf16[64,2048]{1,0:T(8,128)(2,1)S(1)} %activation.5.refs_0_), channel_id=1, source_target_pairs={{0,1},{1,0},{2,3},{3,2},{4,5},{5,4},{6,7},{7,6},{8,9},{9,8},{10,11... | collective-permute-start | bytes 786440 | tf_op jit(solution)/shard_map/ppermute | solution.py:37
  70.0 6.1 %collective-permute-start.15 = (bf16[64,2048]{1,0:T(8,128)(2,1)S(1)}, bf16[64,2048]{1,0:T(8,128)(2,1)S(1)}, u32[]{:S(2)}, u32[]{:S(2)}) collective-permute-start(bf16[64,2048]{1,0:T(8,128)(2,1)S(1)} %collective-permute-done.13.refs_2_), channel_id=1, source_target_pairs={{0,1},{1,0},{2,3},{3,2},{4,5},{5,4},{6,7},{7,6},{8,9},{9,8},{10,11... | collective-permute-start | bytes 786440 | tf_op jit(solution)/shard_map/ppermute | solution.py:37
  70.6 38.0 %collective-permute-start.22 = (bf16[4,64,1792]{2,1,0:T(8,128)(2,1)S(1)}, bf16[4,64,1792]{2,1,0:T(8,128)(2,1)S(1)}, u32[]{:S(2)}, u32[]{:S(2)}) collective-permute-start(bf16[4,64,1792]{2,1,0:T(8,128)(2,1)S(1)} %second_product.4), channel_id=1, source_target_pairs={{0,28},{4,0},{8,4},{12,8},{16,12},{20,16},{24,20},{28,24},{1,29},{... | collective-permute-start | bytes 2752520 | tf_op jit(solution)/shard_map/ppermute | solution.py:27
  74.4 10.1 %collective-permute-start.16 = (bf16[64,1024]{1,0:T(8,128)(2,1)S(1)}, bf16[64,1024]{1,0:T(8,128)(2,1)S(1)}, u32[]{:S(2)}, u32[]{:S(2)}) collective-permute-start(bf16[64,1024]{1,0:T(8,128)(2,1)S(1)} %get-tuple-element.77), channel_id=1, source_target_pairs={{0,1},{1,2},{2,3},{3,0},{4,5},{5,6},{6,7},{7,4},{8,9},{9,10},{10,1... | collective-permute-start | bytes 393224 | tf_op jit(solution)/shard_map/ppermute | solution.py:32
  74.6 9.9 %collective-permute-start.17 = (bf16[64,1024]{1,0:T(8,128)(2,1)S(1)}, bf16[64,1024]{1,0:T(8,128)(2,1)S(1)}, u32[]{:S(2)}, u32[]{:S(2)}) collective-permute-start(bf16[64,1024]{1,0:T(8,128)(2,1)S(1)} %get-tuple-element.78), channel_id=1, source_target_pairs={{0,2},{1,3},{2,0},{3,1},{4,6},{5,7},{6,4},{7,5},{8,10},{9,11},{10,... | collective-permute-start | bytes 393224 | tf_op jit(solution)/shard_map/ppermute | solution.py:32
  76.1 8.4 %collective-permute-start.18 = (bf16[64,1024]{1,0:T(8,128)(2,1)S(1)}, bf16[64,1024]{1,0:T(8,128)(2,1)S(1)}, u32[]{:S(2)}, u32[]{:S(2)}) collective-permute-start(bf16[64,1024]{1,0:T(8,128)(2,1)S(1)} %get-tuple-element.79), channel_id=1, source_target_pairs={{0,3},{1,0},{2,1},{3,2},{4,7},{5,4},{6,5},{7,6},{8,11},{9,8},{10,9... | collective-permute-start | bytes 393224 | tf_op jit(solution)/shard_map/ppermute | solution.py:32
  84.8 7.5 %collective-permute-start.19 = (bf16[64,2048]{1,0:T(8,128)(2,1)S(1)}, bf16[64,2048]{1,0:T(8,128)(2,1)S(1)}, u32[]{:S(2)}, u32[]{:S(2)}) collective-permute-start(bf16[64,2048]{1,0:T(8,128)(2,1)S(1)} %activation.6.refs_0_), channel_id=1, source_target_pairs={{0,2},{1,3},{2,0},{3,1},{4,6},{5,7},{6,4},{7,5},{8,10},{9,11},{10,... | collective-permute-start | bytes 786440 | tf_op jit(solution)/shard_map/ppermute | solution.py:32
  85.3 11.0 %collective-permute-start.20 = (bf16[64,2048]{1,0:T(8,128)(2,1)S(1)}, bf16[64,2048]{1,0:T(8,128)(2,1)S(1)}, u32[]{:S(2)}, u32[]{:S(2)}) collective-permute-start(bf16[64,2048]{1,0:T(8,128)(2,1)S(1)} %activation.6.refs_0_), channel_id=1, source_target_pairs={{0,1},{1,0},{2,3},{3,2},{4,5},{5,4},{6,7},{7,6},{8,9},{9,8},{10,11... | collective-permute-start | bytes 786440 | tf_op jit(solution)/shard_map/ppermute | solution.py:37
  92.3 5.6 %collective-permute-start.21 = (bf16[64,2048]{1,0:T(8,128)(2,1)S(1)}, bf16[64,2048]{1,0:T(8,128)(2,1)S(1)}, u32[]{:S(2)}, u32[]{:S(2)}) collective-permute-start(bf16[64,2048]{1,0:T(8,128)(2,1)S(1)} %collective-permute-done.19.refs_2_), channel_id=1, source_target_pairs={{0,1},{1,0},{2,3},{3,2},{4,5},{5,4},{6,7},{7,6},{8,9},{9,8},{10,11... | collective-permute-start | bytes 786440 | tf_op jit(solution)/shard_map/ppermute | solution.py:37
  92.3 36.0 %collective-permute-start.29 = (bf16[4,64,1792]{2,1,0:T(8,128)(2,1)S(1)}, bf16[4,64,1792]{2,1,0:T(8,128)(2,1)S(1)}, u32[]{:S(2)}, u32[]{:S(2)}) collective-permute-start(bf16[4,64,1792]{2,1,0:T(8,128)(2,1)S(1)} %second_product.5), channel_id=1, source_target_pairs={{0,28},{4,0},{8,4},{12,8},{16,12},{20,16},{24,20},{28,24},{1,29},{... | collective-permute-start | bytes 2752520 | tf_op jit(solution)/shard_map/ppermute | solution.py:27
  96.1 12.5 %collective-permute-start.23 = (bf16[64,1024]{1,0:T(8,128)(2,1)S(1)}, bf16[64,1024]{1,0:T(8,128)(2,1)S(1)}, u32[]{:S(2)}, u32[]{:S(2)}) collective-permute-start(bf16[64,1024]{1,0:T(8,128)(2,1)S(1)} %get-tuple-element.90), channel_id=1, source_target_pairs={{0,1},{1,2},{2,3},{3,0},{4,5},{5,6},{6,7},{7,4},{8,9},{9,10},{10,1... | collective-permute-start | bytes 393224 | tf_op jit(solution)/shard_map/ppermute | solution.py:32
  96.3 12.3 %collective-permute-start.24 = (bf16[64,1024]{1,0:T(8,128)(2,1)S(1)}, bf16[64,1024]{1,0:T(8,128)(2,1)S(1)}, u32[]{:S(2)}, u32[]{:S(2)}) collective-permute-start(bf16[64,1024]{1,0:T(8,128)(2,1)S(1)} %get-tuple-element.91), channel_id=1, source_target_pairs={{0,2},{1,3},{2,0},{3,1},{4,6},{5,7},{6,4},{7,5},{8,10},{9,11},{10,... | collective-permute-start | bytes 393224 | tf_op jit(solution)/shard_map/ppermute | solution.py:32
  97.8 10.8 %collective-permute-start.25 = (bf16[64,1024]{1,0:T(8,128)(2,1)S(1)}, bf16[64,1024]{1,0:T(8,128)(2,1)S(1)}, u32[]{:S(2)}, u32[]{:S(2)}) collective-permute-start(bf16[64,1024]{1,0:T(8,128)(2,1)S(1)} %get-tuple-element.92), channel_id=1, source_target_pairs={{0,3},{1,0},{2,1},{3,2},{4,7},{5,4},{6,5},{7,6},{8,11},{9,8},{10,9... | collective-permute-start | bytes 393224 | tf_op jit(solution)/shard_map/ppermute | solution.py:32
  108.9 6.4 %collective-permute-start.27 = (bf16[64,2048]{1,0:T(8,128)(2,1)S(1)}, bf16[64,2048]{1,0:T(8,128)(2,1)S(1)}, u32[]{:S(2)}, u32[]{:S(2)}) collective-permute-start(bf16[64,2048]{1,0:T(8,128)(2,1)S(1)} %activation.7.refs_0_), channel_id=1, source_target_pairs={{0,2},{1,3},{2,0},{3,1},{4,6},{5,7},{6,4},{7,5},{8,10},{9,11},{10,... | collective-permute-start | bytes 786440 | tf_op jit(solution)/shard_map/ppermute | solution.py:32
  115.3 13.0 %collective-permute-start.28 = (bf16[64,2048]{1,0:T(8,128)(2,1)S(1)}, bf16[64,2048]{1,0:T(8,128)(2,1)S(1)}, u32[]{:S(2)}, u32[]{:S(2)}) collective-permute-start(bf16[64,2048]{1,0:T(8,128)(2,1)S(1)} %collective-permute-done.27.refs_2_), channel_id=1, source_target_pairs={{0,1},{1,0},{2,3},{3,2},{4,5},{5,4},{6,7},{7,6},{8,9},{9,8},{10,11... | collective-permute-start | bytes 786440 | tf_op jit(solution)/shard_map/ppermute | solution.py:37
  115.3 13.0 %collective-permute-start.26 = (bf16[64,2048]{1,0:T(8,128)(2,1)S(1)}, bf16[64,2048]{1,0:T(8,128)(2,1)S(1)}, u32[]{:S(2)}, u32[]{:S(2)}) collective-permute-start(bf16[64,2048]{1,0:T(8,128)(2,1)S(1)} %activation.7.refs_0_), channel_id=1, source_target_pairs={{0,1},{1,0},{2,3},{3,2},{4,5},{5,4},{6,7},{7,6},{8,9},{9,8},{10,11... | collective-permute-start | bytes 786440 | tf_op jit(solution)/shard_map/ppermute | solution.py:37
  115.8 32.2 %collective-permute-start.30 = (bf16[4,64,1792]{2,1,0:T(8,128)(2,1)S(1)}, bf16[4,64,1792]{2,1,0:T(8,128)(2,1)S(1)}, u32[]{:S(2)}, u32[]{:S(2)}) collective-permute-start(bf16[4,64,1792]{2,1,0:T(8,128)(2,1)S(1)} %second_product.6), channel_id=1, source_target_pairs={{0,28},{4,0},{8,4},{12,8},{16,12},{20,16},{24,20},{28,24},{1,29},{... | collective-permute-start | bytes 2752520 | tf_op jit(solution)/shard_map/ppermute | solution.py:27
  135.4 30.8 %collective-permute-start.31 = (bf16[4,64,1792]{2,1,0:T(8,128)(2,1)S(1)}, bf16[4,64,1792]{2,1,0:T(8,128)(2,1)S(1)}, u32[]{:S(2)}, u32[]{:S(2)}) collective-permute-start(bf16[4,64,1792]{2,1,0:T(8,128)(2,1)S(1)} %second_product.7), channel_id=1, source_target_pairs={{0,28},{4,0},{8,4},{12,8},{16,12},{20,16},{24,20},{28,24},{1,29},{... | collective-permute-start | bytes 2752520 | tf_op jit(solution)/shard_map/ppermute | solution.py:27
  (7 other events, 99.0 us)

commit v4 on v3

--- a/solution.py
+++ b/solution.py
@@ -8,7 +8,8 @@
 from jax.sharding import PartitionSpec as P
 
 CHUNKS = 4
-START = {2: 0, 3: 1}
+IN_FLIGHT = 2
+NEED = {("act", 1): (2,), ("act", 2): (3,)}
 WAIT = {("act", 3): (0,), ("mm2", 3): (1,), ("out", 2): (0,), ("out", 3): (1,)}
 FREE = pl.CostEstimate(flops=0, bytes_accessed=0, transcendentals=0)
 
@@ -35,6 +36,10 @@
 def to_other_core(x):
     n = lax.axis_size("expert")
     return lax.ppermute(x, "expert", [(i, i ^ 1) for i in range(n)])
+
+
+def in_hbm(x):
+    return pltpu.with_memory_space_constraint(x, pltpu.HBM)
 
 
 def in_order(later, earlier):
@@ -47,23 +52,91 @@
     )
 
 
+def take_kernel(c, pieces, source, target, sems):
+    n, part, _ = target.shape
+    step = part // pieces
+    copies = []
+    for i in range(n):
+        for k in range(pieces):
+            copy = pltpu.make_async_copy(
+                source.at[i, pl.ds(c * part + k * step, step)],
+                target.at[i, pl.ds(k * step, step)],
+                sems.at[i, k],
+            )
+            copy.start()
+            copies.append(copy)
+    for copy in copies:
+        copy.wait()
+
+
+def put_kernel(c, pieces, source, old, target, sems):
+    del old
+    n, part, _ = source.shape
+    step = part // pieces
+    copies = []
+    for i in range(n):
+        for k in range(pieces):
+            copy = pltpu.make_async_copy(
+                source.at[i, pl.ds(k * step, step)],
+                target.at[i, pl.ds(c * part + k * step, step)],
+                sems.at[i, k],
+            )
+            copy.start()
+            copies.append(copy)
+    for copy in copies:
+        copy.wait()
+
+
+def pieces_of(part):
+    return 2 if part % 32 == 0 else 1
+
+
+def take_rows(array, c, part):
+    n, _, width = array.shape
+    pieces = pieces_of(part)
+    return pl.pallas_call(
+        functools.partial(take_kernel, c, pieces),
+        out_shape=pltpu.VMEM((n, part, width), array.dtype),
+        in_specs=[pl.BlockSpec(memory_space=pltpu.HBM)],
+        out_specs=pl.BlockSpec(memory_space=pltpu.VMEM),
+        scratch_shapes=[pltpu.SemaphoreType.DMA((n, pieces))],
+        cost_estimate=FREE,
+        name="take_rows",
+    )(in_hbm(array))
+
+
+def put_rows(out, piece, c):
+    n, part, _ = piece.shape
+    pieces = pieces_of(part)
+    return pl.pallas_call(
+        functools.partial(put_kernel, c, pieces),
+        out_shape=jax.ShapeDtypeStruct(out.shape, out.dtype),
+        in_specs=[pl.BlockSpec(memory_space=pltpu.VMEM), pl.BlockSpec(memory_space=pltpu.HBM)],
+        out_specs=pl.BlockSpec(memory_space=pltpu.HBM),
+        scratch_shapes=[pltpu.SemaphoreType.DMA((n, pieces))],
+        input_output_aliases={1: 0},
+        cost_estimate=FREE,
+        name="put_rows",
+    )(pltpu.with_memory_space_constraint(piece, pltpu.VMEM), out)
+
+
 def routed_kernel(grad_ref, score_ref, chosen_ref, out_ref):
     grad, scores, chosen = grad_ref[...], score_ref[...], chosen_ref[...]
-    total = jnp.sum(scores, axis=-1, keepdims=True)
-    mixed = jnp.sum(grad * scores, axis=-1, keepdims=True)
+    total = jnp.sum(scores, axis=0, keepdims=True)
+    mixed = jnp.sum(grad * scores, axis=0, keepdims=True)
     logit_grad = 2.5 * (grad - mixed / total) / total * scores * (1.0 - scores)
-    columns = lax.broadcasted_iota(jnp.int32, out_ref.shape, 1)
-    dense = jnp.zeros(out_ref.shape, jnp.float32)
-    for slot in range(grad.shape[1]):
-        here = chosen[:, slot : slot + 1] == columns
-        dense = dense + jnp.where(here, logit_grad[:, slot : slot + 1], 0.0)
-    out_ref[...] = dense.astype(out_ref.dtype)
+    experts = lax.broadcasted_iota(jnp.int32, out_ref.shape[::-1], 0)
+    dense = jnp.zeros(experts.shape, jnp.float32)
+    for slot in range(grad.shape[0]):
+        here = chosen[slot : slot + 1] == experts
+        dense = dense + jnp.where(here, logit_grad[slot : slot + 1], 0.0)
+    out_ref[...] = dense.T.astype(out_ref.dtype)
 
 
 def routed_grad(grad, scores, chosen, n_experts):
     tokens, top = grad.shape
-    block = min(tokens, 128)
-    spec = pl.BlockSpec((block, top), lambda i: (i, 0))
+    block = block_of(tokens, 128)
+    spec = pl.BlockSpec((top, block), lambda i: (0, i))
     return pl.pallas_call(
         routed_kernel,
         out_shape=jax.ShapeDtypeStruct((tokens, n_experts), jnp.bfloat16),
@@ -72,7 +145,7 @@
         out_specs=pl.BlockSpec((block, n_experts), lambda i: (i, 0)),
         cost_estimate=FREE,
         name="routed_grad",
-    )(grad, scores, chosen)
+    )(in_hbm(grad.T), in_hbm(scores.T), in_hbm(chosen.T))
 
 
 def first_kernel(n, me_ref, rows_ref, weight_ref, *out_refs):
@@ -84,7 +157,7 @@
         out_refs[j][...] = product[j * part : (j + 1) * part]
 
 
-def first_product(me, rows, weight):
+def first_product(me, rows, weight, late):
     n, part, width = rows.shape
     hidden = weight.shape[0]
     block = block_of(hidden, 256)
@@ -103,7 +176,7 @@
         compiler_params=params(),
         cost_estimate=FREE,
         name="first_product",
-    )(me, rows, weight)
+    )(me, rows, weight if late else in_hbm(weight))
 
 
 def activation_kernel(gate_ref, up_ref, *refs):
@@ -133,7 +206,7 @@
         compiler_params=params(),
         cost_estimate=FREE,
         name="activation",
-    )(gate_pre, up_pre, *partials)
+    )(in_hbm(gate_pre), in_hbm(up_pre), *partials)
 
 
 def second_kernel(n, me_ref, dense_ref, gate_ref, up_ref, router_ref, *refs):
@@ -209,21 +282,25 @@
     arrived, sent = [], []
     dense = routed_grad(gate_grad[0], gate_scores[0], expert_ids[0], router_weight.shape[2])
     for c in range(chunks):
-        source = grads
-        if c in START and START[c] < c:
-            source, arrived[START[c]] = in_order(source, arrived[START[c]])
-        elif c > 0:
-            source, dense = in_order(source, dense)
-        arrived.append(back_one(source[:, c * part : (c + 1) * part]))
+        if c == 0:
+            piece = take_rows(grads, c, part)
+            grads, dense = in_order(grads, dense)
+        else:
+            piece = grads[:, c * part : (c + 1) * part]
+        if c >= IN_FLIGHT:
+            piece, arrived[c - IN_FLIGHT] = in_order(piece, arrived[c - IN_FLIGHT])
+        arrived.append(back_one(piece))
     dense = dense.reshape(n, rows, -1)
 
     def at(point, c, x):
+        for p in NEED.get((point, c), ()):
+            x, arrived[p] = in_order(x, arrived[p])
         for p in WAIT.get((point, c), ()):
             x, sent[p] = in_order(x, sent[p])
         return x
 
     def partial_sums(c):
-        own, *others = first_product(me, arrived[c], shared_down[0])
+        own, *others = first_product(me, arrived[c], shared_down[0], c > 0)
         others[0] = at("rs", c, others[0])
         return [own] + [to_expert(x, j + 1) for j, x in enumerate(others)]
 
@@ -251,8 +328,9 @@
         result = at("out", c, result)
         sent.append(back_one(result))
     out = jnp.zeros((n, rows, width), jnp.bfloat16)
-    for c in range(chunks):
+    for c in range(chunks - 1):
         out = lax.dynamic_update_slice(out, sent[c], (0, c * part, 0))
+    out = put_rows(out, sent[-1], chunks - 1)
     return out.reshape(1, tokens, width)
 
 

time: 169 us -> 167 us (0.988)
  waiting for transfers between devices: 56.4 us -> 67.9 us
  starting transfers between devices: 51.4 us -> 40.2 us
  local copies, waits for them, and re-layouts: 16.6 us -> 7.4 us
  Pallas kernels: 43.4 us -> 49.8 us
    ppermute x16, waiting for transfers between devices: 6.32 us -> 24.7 us  [to_expert(): return lax.ppermute(x, 'expert', [(i, (i + by) % n) for i in range(n)])]
    ppermute x8, starting transfers between devices: 34.9 us -> 23.6 us  [back_one(): lax.ppermute(x, 'pipe', [(i, (i - 1) % length) for i in range(length)])]
    unnamed x17 -> x8, local copies, waits for them, and re-layouts: 9.22 us -> 0.02 us
    ppermute x8, waiting for transfers between devices: 50.1 us -> 43.2 us  [back_one(): lax.ppermute(x, 'pipe', [(i, (i - 1) % length) for i in range(length)])]
    pallas_call x4, Pallas kernels: 0.81 us -> 4.69 us  [activation(): pl.pallas_call(activation_kernel, out_shape=jax.ShapeDtypeStruct((part, 2...]
    dynamic_update_slice x4 -> x3, local copies, waits for them, and re-layouts: 0.42 us -> 4.04 us  [shards(): out = lax.dynamic_update_slice(out, sent[c], (0, c * part, 0))]
    slice x4 -> x1, local copies, waits for them, and re-layouts: 6.93 us -> 3.33 us  [shards(): piece = grads[:, c * part:(c + 1) * part]]
    pallas_call x0 -> x2, Pallas kernels: none -> 2.29 us  [the longest x1 1.32 us: take_rows(): pl.pallas_call(functools.partial(take_kernel, c, pieces), out_shape=pltpu...]
  transfers between devices with their start and end apart: 32 -> 32, of which waited for: 9 -> 13; matrix products, arithmetic and copies ran while one was open for 6% -> 4% of each run, Pallas kernels for 26% -> 29%
where the time goes in v4:
time: 167 us; the launch traced here: 166 us
  waiting for transfers between devices  67.9 us (41%)
  Pallas kernels  49.8 us (30%)
  starting transfers between devices  40.2 us (24%)
  local copies, waits for them, and re-layouts  7.4 us (4%)
    ppermute x8, waiting for transfers between devices, back_one(): lax.ppermute(x, 'pipe', [(i, (i - 1) % length) for i in range(length)])  43.2 us
    pallas_call x4, Pallas kernels, second_product(): pl.pallas_call(functools.partial(second_kernel, n), out_shape=jax.ShapeDt...  28.3 us
    ppermute x16, waiting for transfers between devices, to_expert(): return lax.ppermute(x, 'expert', [(i, (i + by) % n) for i in range(n)])  24.7 us
    ppermute x8, starting transfers between devices, back_one(): lax.ppermute(x, 'pipe', [(i, (i - 1) % length) for i in range(length)])  23.6 us
    ppermute x16, starting transfers between devices, to_expert(): return lax.ppermute(x, 'expert', [(i, (i + by) % n) for i in range(n)])  15.2 us
    pallas_call x4, Pallas kernels, first_product(): pl.pallas_call(functools.partial(first_kernel, n), out_shape=[jax.ShapeDt...  9.54 us
    pallas_call x1, Pallas kernels, routed_grad(): pl.pallas_call(routed_kernel, out_shape=jax.ShapeDtypeStruct((tokens, n_e...  5.05 us
    pallas_call x4, Pallas kernels, activation(): pl.pallas_call(activation_kernel, out_shape=jax.ShapeDtypeStruct((part, 2...  4.69 us
  transfers between devices with their start and end apart: 32, of which 13 were waited for; matrix products, arithmetic and copies ran while one was open for 4% of the time, Pallas kernels for 29%

profile of v4, /device:TPU:0, one launch (start us, length us, event | category | flops | bytes accessed | tf_op | source)
XLA Modules:
  0.0 165.6 jit_solution(8427186038064087913)
XLA Ops:
  0.0 1.3 take_rows.1
  1.3 6.0 %collective-permute-start = (bf16[4,64,1792]{2,1,0:T(8,128)(2,1)S(1)}, bf16[4,64,1792]{2,1,0:T(8,128)(2,1)S(1)}, u32[]{:S(2)}, u32[]{:S(2)}) collective-permute-start(bf16[4,64,1792]{2,1,0:T(8,128)(2,1)S(1)} %take_rows.1), channel_id=1, source_target_pairs={{0,28},{4,0},{8,4},{12,8},{16,12},{20,16},{24,20},{28,24},{1,29},{... | collective-permute-start | bytes 2752520 | tf_op jit(solution)/shard_map/ppermute | solution.py:28
  7.4 5.0 %routed_grad.1 = bf16[1024,256]{1,0:T(8,128)(2,1)} custom-call(f32[8,1024]{1,0:T(8,128)} %bitcast.49, f32[8,1024]{1,0:T(8,128)} %bitcast.50, s32[8,1024]{1,0:T(8,128)} %bitcast.51), custom_call_target="tpu_custom_call" | custom-call | tf_op jit(solution)/shard_map/routed_grad/pallas_call | solution.py:140
  12.4 3.3 %fusion = (bf16[4,64,1792]{2,1,0:T(8,128)(2,1)}, bf16[4,64,1792]{2,1,0:T(8,128)(2,1)}, bf16[4,64,1792]{2,1,0:T(8,128)(2,1)}) fusion(bf16[4,256,1792]{2,1,0:T(8,128)(2,1)} %bitcast.40), kind=kLoop, calls=%fused_computation.2 | loop fusion | bytes 5505024 | tf_op jit(solution)/shard_map/slice | solution.py:289
  16.3 11.8 %collective-permute-done.rows_ref = bf16[4,64,1792]{2,1,0:T(8,128)(2,1)S(1)} collective-permute-done((bf16[4,64,1792]{2,1,0:T(8,128)(2,1)S(1)}, bf16[4,64,1792]{2,1,0:T(8,128)(2,1)S(1)}, u32[]{:S(2)}, u32[]{:S(2)}) %collective-permute-start) | collective-permute-done | bytes 917536 | tf_op jit(solution)/shard_map/ppermute | solution.py:28
  28.1 5.2 %collective-permute-start.8 = (bf16[4,64,1792]{2,1,0:T(8,128)(2,1)}, bf16[4,64,1792]{2,1,0:T(8,128)(2,1)S(1)}, u32[]{:S(2)}, u32[]{:S(2)}) collective-permute-start(bf16[4,64,1792]{2,1,0:T(8,128)(2,1)} %get-tuple-element.71), channel_id=1, source_target_pairs={{0,28},{4,0},{8,4},{12,8},{16,12},{20,16},{24,20},{28,24},{1,29},{... | collective-permute-start | bytes 2752520 | tf_op jit(solution)/shard_map/ppermute | solution.py:28
  33.3 4.0 %first_product.4 = (bf16[64,1024]{1,0:T(8,128)(2,1)S(1)}, bf16[64,1024]{1,0:T(8,128)(2,1)S(1)}, bf16[64,1024]{1,0:T(8,128)(2,1)S(1)}, bf16[64,1024]{1,0:T(8,128)(2,1)S(1)}) custom-call(s32[1]{0:T(128)} %bitcast.me_ref, bf16[4,64,1792]{2,1,0:T(8,128)(2,1)S(1)} %collective-permute-done.rows_ref, bf16[1024,1792]{1,0:T(8,128)(2,1)} %bitcast.19), custom_call_target="tpu_custom_call" | custom-call | tf_op jit(solution)/shard_map/first_product/pallas_call | solution.py:164
  37.4 1.6 collective-permute-start.3
  38.9 1.4 collective-permute-start.4
  40.3 2.2 %collective-permute-done.2.refs_1_ = bf16[64,1024]{1,0:T(8,128)(2,1)S(1)} collective-permute-done((bf16[64,1024]{1,0:T(8,128)(2,1)S(1)}, bf16[64,1024]{1,0:T(8,128)(2,1)S(1)}, u32[]{:S(2)}, u32[]{:S(2)}) %collective-permute-start.2) | collective-permute-done | bytes 131104 | tf_op jit(solution)/shard_map/ppermute | solution.py:33
  48.5 1.9 %first_product.5 = (bf16[64,1024]{1,0:T(8,128)(2,1)S(1)}, bf16[64,1024]{1,0:T(8,128)(2,1)S(1)}, bf16[64,1024]{1,0:T(8,128)(2,1)S(1)}, bf16[64,1024]{1,0:T(8,128)(2,1)S(1)}) custom-call(s32[1]{0:T(128)} %bitcast.me_ref, bf16[4,64,1792]{2,1,0:T(8,128)(2,1)S(1)} %collective-permute-done.1.rows_ref, bf16[1024,1792]{1,0:T(8,128)(2,1)S(1)} %bitcast.20), custom_call_target="tpu_custom_call" | custom-call | tf_op jit(solution)/shard_map/first_product/pallas_call | solution.py:164
  50.4 4.9 %collective-permute-done.5.refs_2_ = bf16[64,2048]{1,0:T(8,128)(2,1)S(1)} collective-permute-done((bf16[64,2048]{1,0:T(8,128)(2,1)S(1)}, bf16[64,2048]{1,0:T(8,128)(2,1)S(1)}, u32[]{:S(2)}, u32[]{:S(2)}) %collective-permute-start.5) | collective-permute-done | bytes 262176 | tf_op jit(solution)/shard_map/ppermute | solution.py:33
  57.0 1.4 collective-permute-start.11
  58.4 7.1 %second_product.4 = bf16[4,64,1792]{2,1,0:T(8,128)(2,1)S(1)} custom-call(s32[1]{0:T(128)} %bitcast.me_ref, bf16[4,256,256]{2,1,0:T(8,128)(2,1)S(1)} %bitcast.27, bf16[1792,1024]{1,0:T(8,128)(2,1)} %bitcast.31, bf16[1792,1024]{1,0:T(8,128)(2,1)} %bitcast.35, bf16[1792,256]{1,0:T(8,128)(2,1)S(1)} %bitcast.23, bf16[64,2048]{1,0:T(8,128)(2,1)S(1)} %activation.4.refs_0_, ...), custom_call_target="tpu_custom_call" | custom-call | tf_op jit(solution)/shard_map/second_product/pallas_call | solution.py:240
  65.5 2.0 %collective-permute-done.8.rows_ref = bf16[4,64,1792]{2,1,0:T(8,128)(2,1)S(1)} collective-permute-done((bf16[4,64,1792]{2,1,0:T(8,128)(2,1)}, bf16[4,64,1792]{2,1,0:T(8,128)(2,1)S(1)}, u32[]{:S(2)}, u32[]{:S(2)}) %collective-permute-start.8) | collective-permute-done | bytes 917536 | tf_op jit(solution)/shard_map/ppermute | solution.py:28
  68.7 1.6 collective-permute-start.12
  70.3 1.9 %first_product.6 = (bf16[64,1024]{1,0:T(8,128)(2,1)S(1)}, bf16[64,1024]{1,0:T(8,128)(2,1)S(1)}, bf16[64,1024]{1,0:T(8,128)(2,1)S(1)}, bf16[64,1024]{1,0:T(8,128)(2,1)S(1)}) custom-call(s32[1]{0:T(128)} %bitcast.me_ref, bf16[4,64,1792]{2,1,0:T(8,128)(2,1)S(1)} %collective-permute-done.8.rows_ref, bf16[1024,1792]{1,0:T(8,128)(2,1)S(1)} %bitcast.21), custom_call_target="tpu_custom_call" | custom-call | tf_op jit(solution)/shard_map/first_product/pallas_call | solution.py:164
  72.2 3.0 %collective-permute-done.12.refs_2_ = bf16[64,2048]{1,0:T(8,128)(2,1)S(1)} collective-permute-done((bf16[64,2048]{1,0:T(8,128)(2,1)S(1)}, bf16[64,2048]{1,0:T(8,128)(2,1)S(1)}, u32[]{:S(2)}, u32[]{:S(2)}) %collective-permute-start.12) | collective-permute-done | bytes 262176 | tf_op jit(solution)/shard_map/ppermute | solution.py:33
  75.2 5.1 %collective-permute-start.22 = (bf16[4,64,1792]{2,1,0:T(8,128)(2,1)S(1)}, bf16[4,64,1792]{2,1,0:T(8,128)(2,1)S(1)}, u32[]{:S(2)}, u32[]{:S(2)}) collective-permute-start(bf16[4,64,1792]{2,1,0:T(8,128)(2,1)S(1)} %second_product.4), channel_id=1, source_target_pairs={{0,28},{4,0},{8,4},{12,8},{16,12},{20,16},{24,20},{28,24},{1,29},{... | collective-permute-start | bytes 2752520 | tf_op jit(solution)/shard_map/ppermute | solution.py:28
  80.5 1.6 collective-permute-start.17
  83.2 7.1 %second_product.5 = bf16[4,64,1792]{2,1,0:T(8,128)(2,1)S(1)} custom-call(s32[1]{0:T(128)} %bitcast.me_ref, bf16[4,256,256]{2,1,0:T(8,128)(2,1)S(1)} %bitcast.28, bf16[1792,1024]{1,0:T(8,128)(2,1)} %bitcast.32, bf16[1792,1024]{1,0:T(8,128)(2,1)} %bitcast.36, bf16[1792,256]{1,0:T(8,128)(2,1)S(1)} %bitcast.24, bf16[64,2048]{1,0:T(8,128)(2,1)S(1)} %activation.5.refs_0_, ...), custom_call_target="tpu_custom_call" | custom-call | tf_op jit(solution)/shard_map/second_product/pallas_call | solution.py:240
  92.1 1.8 %first_product.7 = (bf16[64,1024]{1,0:T(8,128)(2,1)S(1)}, bf16[64,1024]{1,0:T(8,128)(2,1)S(1)}, bf16[64,1024]{1,0:T(8,128)(2,1)S(1)}, bf16[64,1024]{1,0:T(8,128)(2,1)S(1)}) custom-call(s32[1]{0:T(128)} %bitcast.me_ref, bf16[4,64,1792]{2,1,0:T(8,128)(2,1)S(1)} %collective-permute-done.15.rows_ref, bf16[1024,1792]{1,0:T(8,128)(2,1)S(1)} %bitcast.22), custom_call_target="tpu_custom_call" | custom-call | tf_op jit(solution)/shard_map/first_product/pallas_call | solution.py:164
  94.0 5.2 %collective-permute-done.19.refs_2_ = bf16[64,2048]{1,0:T(8,128)(2,1)S(1)} collective-permute-done((bf16[64,2048]{1,0:T(8,128)(2,1)S(1)}, bf16[64,2048]{1,0:T(8,128)(2,1)S(1)}, u32[]{:S(2)}, u32[]{:S(2)}) %collective-permute-start.19) | collective-permute-done | bytes 262176 | tf_op jit(solution)/shard_map/ppermute | solution.py:33
  100.1 1.6 collective-permute-start.24
  102.9 7.1 %second_product.6 = bf16[4,64,1792]{2,1,0:T(8,128)(2,1)S(1)} custom-call(s32[1]{0:T(128)} %bitcast.me_ref, bf16[4,256,256]{2,1,0:T(8,128)(2,1)S(1)} %bitcast.29, bf16[1792,1024]{1,0:T(8,128)(2,1)} %bitcast.33, bf16[1792,1024]{1,0:T(8,128)(2,1)} %bitcast.37, bf16[1792,256]{1,0:T(8,128)(2,1)S(1)} %bitcast.25, bf16[64,2048]{1,0:T(8,128)(2,1)S(1)} %activation.6.refs_0_, ...), custom_call_target="tpu_custom_call" | custom-call | tf_op jit(solution)/shard_map/second_product/pallas_call | solution.py:240
  111.8 7.0 %collective-permute-done.27.refs_2_ = bf16[64,2048]{1,0:T(8,128)(2,1)S(1)} collective-permute-done((bf16[64,2048]{1,0:T(8,128)(2,1)S(1)}, bf16[64,2048]{1,0:T(8,128)(2,1)S(1)}, u32[]{:S(2)}, u32[]{:S(2)}) %collective-permute-start.27) | collective-permute-done | bytes 262176 | tf_op jit(solution)/shard_map/ppermute | solution.py:33
  120.1 6.3 %collective-permute-done.29 = bf16[4,64,1792]{2,1,0:T(8,128)(2,1)S(1)} collective-permute-done((bf16[4,64,1792]{2,1,0:T(8,128)(2,1)S(1)}, bf16[4,64,1792]{2,1,0:T(8,128)(2,1)S(1)}, u32[]{:S(2)}, u32[]{:S(2)}) %collective-permute-start.29) | collective-permute-done | bytes 917536 | tf_op jit(solution)/shard_map/ppermute | solution.py:28
  126.4 7.1 %second_product.7 = bf16[4,64,1792]{2,1,0:T(8,128)(2,1)S(1)} custom-call(s32[1]{0:T(128)} %bitcast.me_ref, bf16[4,256,256]{2,1,0:T(8,128)(2,1)S(1)} %bitcast.30, bf16[1792,1024]{1,0:T(8,128)(2,1)} %bitcast.34, bf16[1792,1024]{1,0:T(8,128)(2,1)} %bitcast.38, bf16[1792,256]{1,0:T(8,128)(2,1)S(1)} %bitcast.26, bf16[64,2048]{1,0:T(8,128)(2,1)S(1)} %activation.7.refs_0_, ...), custom_call_target="tpu_custom_call" | custom-call | tf_op jit(solution)/shard_map/second_product/pallas_call | solution.py:240
  133.5 5.2 %collective-permute-start.30 = (bf16[4,64,1792]{2,1,0:T(8,128)(2,1)S(1)}, bf16[4,64,1792]{2,1,0:T(8,128)(2,1)S(1)}, u32[]{:S(2)}, u32[]{:S(2)}) collective-permute-start(bf16[4,64,1792]{2,1,0:T(8,128)(2,1)S(1)} %second_product.7), channel_id=1, source_target_pairs={{0,28},{4,0},{8,4},{12,8},{16,12},{20,16},{24,20},{28,24},{1,29},{... | collective-permute-start | bytes 2752520 | tf_op jit(solution)/shard_map/ppermute | solution.py:28
  138.7 2.1 %dynamic_update_slice.9 = bf16[4,256,1792]{2,1,0:T(8,128)(2,1)} pad(bf16[4,64,1792]{2,1,0:T(8,128)(2,1)S(1)} %collective-permute-done.22, bf16[]{:T(256)} %constant.1.clone.1), padding=0_0x0_192x0_0 | pad | bytes 4587522 | tf_op jit(solution)/shard_map/dynamic_update_slice | solution.py:332
  141.8 4.3 %collective-permute-done.31 = bf16[4,64,1792]{2,1,0:T(8,128)(2,1)S(1)} collective-permute-done((bf16[4,64,1792]{2,1,0:T(8,128)(2,1)S(1)}, bf16[4,64,1792]{2,1,0:T(8,128)(2,1)S(1)}, u32[]{:S(2)}, u32[]{:S(2)}) %collective-permute-start.31) | collective-permute-done | bytes 917536 | tf_op jit(solution)/shard_map/ppermute | solution.py:28
  147.1 17.5 %collective-permute-done.30.source = bf16[4,64,1792]{2,1,0:T(8,128)(2,1)S(1)} collective-permute-done((bf16[4,64,1792]{2,1,0:T(8,128)(2,1)S(1)}, bf16[4,64,1792]{2,1,0:T(8,128)(2,1)S(1)}, u32[]{:S(2)}, u32[]{:S(2)}) %collective-permute-start.30) | collective-permute-done | bytes 917536 | tf_op jit(solution)/shard_map/ppermute | solution.py:28
  (59 shorter events, 20.9 us)
Async XLA Ops:
  1.3 26.8 %collective-permute-start = (bf16[4,64,1792]{2,1,0:T(8,128)(2,1)S(1)}, bf16[4,64,1792]{2,1,0:T(8,128)(2,1)S(1)}, u32[]{:S(2)}, u32[]{:S(2)}) collective-permute-start(bf16[4,64,1792]{2,1,0:T(8,128)(2,1)S(1)} %take_rows.1), channel_id=1, source_target_pairs={{0,28},{4,0},{8,4},{12,8},{16,12},{20,16},{24,20},{28,24},{1,29},{... | collective-permute-start | bytes 2752520 | tf_op jit(solution)/shard_map/ppermute | solution.py:28
  15.7 32.1 %collective-permute-start.1 = (bf16[4,64,1792]{2,1,0:T(8,128)(2,1)}, bf16[4,64,1792]{2,1,0:T(8,128)(2,1)S(1)}, u32[]{:S(2)}, u32[]{:S(2)}) collective-permute-start(bf16[4,64,1792]{2,1,0:T(8,128)(2,1)} %get-tuple-element.107), channel_id=1, source_target_pairs={{0,28},{4,0},{8,4},{12,8},{16,12},{20,16},{24,20},{28,24},{1,29},{... | collective-permute-start | bytes 2752520 | tf_op jit(solution)/shard_map/ppermute | solution.py:28
  28.1 39.4 %collective-permute-start.8 = (bf16[4,64,1792]{2,1,0:T(8,128)(2,1)}, bf16[4,64,1792]{2,1,0:T(8,128)(2,1)S(1)}, u32[]{:S(2)}, u32[]{:S(2)}) collective-permute-start(bf16[4,64,1792]{2,1,0:T(8,128)(2,1)} %get-tuple-element.71), channel_id=1, source_target_pairs={{0,28},{4,0},{8,4},{12,8},{16,12},{20,16},{24,20},{28,24},{1,29},{... | collective-permute-start | bytes 2752520 | tf_op jit(solution)/shard_map/ppermute | solution.py:28
  37.3 5.2 %collective-permute-start.2 = (bf16[64,1024]{1,0:T(8,128)(2,1)S(1)}, bf16[64,1024]{1,0:T(8,128)(2,1)S(1)}, u32[]{:S(2)}, u32[]{:S(2)}) collective-permute-start(bf16[64,1024]{1,0:T(8,128)(2,1)S(1)} %get-tuple-element.63), channel_id=1, source_target_pairs={{0,1},{1,2},{2,3},{3,0},{4,5},{5,6},{6,7},{7,4},{8,9},{9,10},{10,1... | collective-permute-start | bytes 393224 | tf_op jit(solution)/shard_map/ppermute | solution.py:33
  37.4 6.4 %collective-permute-start.3 = (bf16[64,1024]{1,0:T(8,128)(2,1)S(1)}, bf16[64,1024]{1,0:T(8,128)(2,1)S(1)}, u32[]{:S(2)}, u32[]{:S(2)}) collective-permute-start(bf16[64,1024]{1,0:T(8,128)(2,1)S(1)} %get-tuple-element.64), channel_id=1, source_target_pairs={{0,2},{1,3},{2,0},{3,1},{4,6},{5,7},{6,4},{7,5},{8,10},{9,11},{10,... | collective-permute-start | bytes 393224 | tf_op jit(solution)/shard_map/ppermute | solution.py:33
  38.9 6.0 %collective-permute-start.4 = (bf16[64,1024]{1,0:T(8,128)(2,1)S(1)}, bf16[64,1024]{1,0:T(8,128)(2,1)S(1)}, u32[]{:S(2)}, u32[]{:S(2)}) collective-permute-start(bf16[64,1024]{1,0:T(8,128)(2,1)S(1)} %get-tuple-element.65), channel_id=1, source_target_pairs={{0,3},{1,0},{2,1},{3,2},{4,7},{5,4},{6,5},{7,6},{8,11},{9,8},{10,9... | collective-permute-start | bytes 393224 | tf_op jit(solution)/shard_map/ppermute | solution.py:33
  46.2 9.1 %collective-permute-start.5 = (bf16[64,2048]{1,0:T(8,128)(2,1)S(1)}, bf16[64,2048]{1,0:T(8,128)(2,1)S(1)}, u32[]{:S(2)}, u32[]{:S(2)}) collective-permute-start(bf16[64,2048]{1,0:T(8,128)(2,1)S(1)} %activation.4.refs_0_), channel_id=1, source_target_pairs={{0,2},{1,3},{2,0},{3,1},{4,6},{5,7},{6,4},{7,5},{8,10},{9,11},{10,... | collective-permute-start | bytes 786440 | tf_op jit(solution)/shard_map/ppermute | solution.py:33
  47.9 7.9 %collective-permute-start.6 = (bf16[64,2048]{1,0:T(8,128)(2,1)S(1)}, bf16[64,2048]{1,0:T(8,128)(2,1)S(1)}, u32[]{:S(2)}, u32[]{:S(2)}) collective-permute-start(bf16[64,2048]{1,0:T(8,128)(2,1)S(1)} %activation.4.refs_0_), channel_id=1, source_target_pairs={{0,1},{1,0},{2,3},{3,2},{4,5},{5,4},{6,7},{7,6},{8,9},{9,8},{10,11... | collective-permute-start | bytes 786440 | tf_op jit(solution)/shard_map/ppermute | solution.py:38
  55.3 1.7 %collective-permute-start.7 = (bf16[64,2048]{1,0:T(8,128)(2,1)S(1)}, bf16[64,2048]{1,0:T(8,128)(2,1)S(1)}, u32[]{:S(2)}, u32[]{:S(2)}) collective-permute-start(bf16[64,2048]{1,0:T(8,128)(2,1)S(1)} %collective-permute-done.5.refs_2_), channel_id=1, source_target_pairs={{0,1},{1,0},{2,3},{3,2},{4,5},{5,4},{6,7},{7,6},{8,9},{9,8},{10,11... | collective-permute-start | bytes 786440 | tf_op jit(solution)/shard_map/ppermute | solution.py:38
  55.5 34.8 %collective-permute-start.15 = (bf16[4,64,1792]{2,1,0:T(8,128)(2,1)S(1)}, bf16[4,64,1792]{2,1,0:T(8,128)(2,1)S(1)}, u32[]{:S(2)}, u32[]{:S(2)}) collective-permute-start(bf16[4,64,1792]{2,1,0:T(8,128)(2,1)S(1)} %copy-done.3), channel_id=1, source_target_pairs={{0,28},{4,0},{8,4},{12,8},{16,12},{20,16},{24,20},{28,24},{1,29},{... | collective-permute-start | bytes 2752520 | tf_op jit(solution)/shard_map/ppermute | solution.py:28
  55.5 12.0 %collective-permute-start.9 = (bf16[64,1024]{1,0:T(8,128)(2,1)S(1)}, bf16[64,1024]{1,0:T(8,128)(2,1)S(1)}, u32[]{:S(2)}, u32[]{:S(2)}) collective-permute-start(bf16[64,1024]{1,0:T(8,128)(2,1)S(1)} %get-tuple-element.74), channel_id=1, source_target_pairs={{0,1},{1,2},{2,3},{3,0},{4,5},{5,6},{6,7},{7,4},{8,9},{9,10},{10,1... | collective-permute-start | bytes 393224 | tf_op jit(solution)/shard_map/ppermute | solution.py:33
  55.8 11.7 %collective-permute-start.10 = (bf16[64,1024]{1,0:T(8,128)(2,1)S(1)}, bf16[64,1024]{1,0:T(8,128)(2,1)S(1)}, u32[]{:S(2)}, u32[]{:S(2)}) collective-permute-start(bf16[64,1024]{1,0:T(8,128)(2,1)S(1)} %get-tuple-element.75), channel_id=1, source_target_pairs={{0,2},{1,3},{2,0},{3,1},{4,6},{5,7},{6,4},{7,5},{8,10},{9,11},{10,... | collective-permute-start | bytes 393224 | tf_op jit(solution)/shard_map/ppermute | solution.py:33
  57.0 10.6 %collective-permute-start.11 = (bf16[64,1024]{1,0:T(8,128)(2,1)S(1)}, bf16[64,1024]{1,0:T(8,128)(2,1)S(1)}, u32[]{:S(2)}, u32[]{:S(2)}) collective-permute-start(bf16[64,1024]{1,0:T(8,128)(2,1)S(1)} %get-tuple-element.76), channel_id=1, source_target_pairs={{0,3},{1,0},{2,1},{3,2},{4,7},{5,4},{6,5},{7,6},{8,11},{9,8},{10,9... | collective-permute-start | bytes 393224 | tf_op jit(solution)/shard_map/ppermute | solution.py:33
  68.7 6.4 %collective-permute-start.12 = (bf16[64,2048]{1,0:T(8,128)(2,1)S(1)}, bf16[64,2048]{1,0:T(8,128)(2,1)S(1)}, u32[]{:S(2)}, u32[]{:S(2)}) collective-permute-start(bf16[64,2048]{1,0:T(8,128)(2,1)S(1)} %activation.5.refs_0_), channel_id=1, source_target_pairs={{0,2},{1,3},{2,0},{3,1},{4,6},{5,7},{6,4},{7,5},{8,10},{9,11},{10,... | collective-permute-start | bytes 786440 | tf_op jit(solution)/shard_map/ppermute | solution.py:33
  70.3 10.2 %collective-permute-start.13 = (bf16[64,2048]{1,0:T(8,128)(2,1)S(1)}, bf16[64,2048]{1,0:T(8,128)(2,1)S(1)}, u32[]{:S(2)}, u32[]{:S(2)}) collective-permute-start(bf16[64,2048]{1,0:T(8,128)(2,1)S(1)} %activation.5.refs_0_), channel_id=1, source_target_pairs={{0,1},{1,0},{2,3},{3,2},{4,5},{5,4},{6,7},{7,6},{8,9},{9,8},{10,11... | collective-permute-start | bytes 786440 | tf_op jit(solution)/shard_map/ppermute | solution.py:38
  75.2 6.9 %collective-permute-start.14 = (bf16[64,2048]{1,0:T(8,128)(2,1)S(1)}, bf16[64,2048]{1,0:T(8,128)(2,1)S(1)}, u32[]{:S(2)}, u32[]{:S(2)}) collective-permute-start(bf16[64,2048]{1,0:T(8,128)(2,1)S(1)} %collective-permute-done.12.refs_2_), channel_id=1, source_target_pairs={{0,1},{1,0},{2,3},{3,2},{4,5},{5,4},{6,7},{7,6},{8,9},{9,8},{10,11... | collective-permute-start | bytes 786440 | tf_op jit(solution)/shard_map/ppermute | solution.py:38
  75.2 34.8 %collective-permute-start.22 = (bf16[4,64,1792]{2,1,0:T(8,128)(2,1)S(1)}, bf16[4,64,1792]{2,1,0:T(8,128)(2,1)S(1)}, u32[]{:S(2)}, u32[]{:S(2)}) collective-permute-start(bf16[4,64,1792]{2,1,0:T(8,128)(2,1)S(1)} %second_product.4), channel_id=1, source_target_pairs={{0,28},{4,0},{8,4},{12,8},{16,12},{20,16},{24,20},{28,24},{1,29},{... | collective-permute-start | bytes 2752520 | tf_op jit(solution)/shard_map/ppermute | solution.py:28
  80.2 10.1 %collective-permute-start.16 = (bf16[64,1024]{1,0:T(8,128)(2,1)S(1)}, bf16[64,1024]{1,0:T(8,128)(2,1)S(1)}, u32[]{:S(2)}, u32[]{:S(2)}) collective-permute-start(bf16[64,1024]{1,0:T(8,128)(2,1)S(1)} %get-tuple-element.85), channel_id=1, source_target_pairs={{0,1},{1,2},{2,3},{3,0},{4,5},{5,6},{6,7},{7,4},{8,9},{9,10},{10,1... | collective-permute-start | bytes 393224 | tf_op jit(solution)/shard_map/ppermute | solution.py:33
  80.5 9.9 %collective-permute-start.17 = (bf16[64,1024]{1,0:T(8,128)(2,1)S(1)}, bf16[64,1024]{1,0:T(8,128)(2,1)S(1)}, u32[]{:S(2)}, u32[]{:S(2)}) collective-permute-start(bf16[64,1024]{1,0:T(8,128)(2,1)S(1)} %get-tuple-element.86), channel_id=1, source_target_pairs={{0,2},{1,3},{2,0},{3,1},{4,6},{5,7},{6,4},{7,5},{8,10},{9,11},{10,... | collective-permute-start | bytes 393224 | tf_op jit(solution)/shard_map/ppermute | solution.py:33
  82.0 8.3 %collective-permute-start.18 = (bf16[64,1024]{1,0:T(8,128)(2,1)S(1)}, bf16[64,1024]{1,0:T(8,128)(2,1)S(1)}, u32[]{:S(2)}, u32[]{:S(2)}) collective-permute-start(bf16[64,1024]{1,0:T(8,128)(2,1)S(1)} %get-tuple-element.87), channel_id=1, source_target_pairs={{0,3},{1,0},{2,1},{3,2},{4,7},{5,4},{6,5},{7,6},{8,11},{9,8},{10,9... | collective-permute-start | bytes 393224 | tf_op jit(solution)/shard_map/ppermute | solution.py:33
  91.5 7.6 %collective-permute-start.19 = (bf16[64,2048]{1,0:T(8,128)(2,1)S(1)}, bf16[64,2048]{1,0:T(8,128)(2,1)S(1)}, u32[]{:S(2)}, u32[]{:S(2)}) collective-permute-start(bf16[64,2048]{1,0:T(8,128)(2,1)S(1)} %activation.6.refs_0_), channel_id=1, source_target_pairs={{0,2},{1,3},{2,0},{3,1},{4,6},{5,7},{6,4},{7,5},{8,10},{9,11},{10,... | collective-permute-start | bytes 786440 | tf_op jit(solution)/shard_map/ppermute | solution.py:33
  92.1 8.0 %collective-permute-start.20 = (bf16[64,2048]{1,0:T(8,128)(2,1)S(1)}, bf16[64,2048]{1,0:T(8,128)(2,1)S(1)}, u32[]{:S(2)}, u32[]{:S(2)}) collective-permute-start(bf16[64,2048]{1,0:T(8,128)(2,1)S(1)} %activation.6.refs_0_), channel_id=1, source_target_pairs={{0,1},{1,0},{2,3},{3,2},{4,5},{5,4},{6,7},{7,6},{8,9},{9,8},{10,11... | collective-permute-start | bytes 786440 | tf_op jit(solution)/shard_map/ppermute | solution.py:38
  99.1 2.6 %collective-permute-start.21 = (bf16[64,2048]{1,0:T(8,128)(2,1)S(1)}, bf16[64,2048]{1,0:T(8,128)(2,1)S(1)}, u32[]{:S(2)}, u32[]{:S(2)}) collective-permute-start(bf16[64,2048]{1,0:T(8,128)(2,1)S(1)} %collective-permute-done.19.refs_2_), channel_id=1, source_target_pairs={{0,1},{1,0},{2,3},{3,2},{4,5},{5,4},{6,7},{7,6},{8,9},{9,8},{10,11... | collective-permute-start | bytes 786440 | tf_op jit(solution)/shard_map/ppermute | solution.py:38
  99.1 27.3 %collective-permute-start.29 = (bf16[4,64,1792]{2,1,0:T(8,128)(2,1)S(1)}, bf16[4,64,1792]{2,1,0:T(8,128)(2,1)S(1)}, u32[]{:S(2)}, u32[]{:S(2)}) collective-permute-start(bf16[4,64,1792]{2,1,0:T(8,128)(2,1)S(1)} %second_product.5), channel_id=1, source_target_pairs={{0,28},{4,0},{8,4},{12,8},{16,12},{20,16},{24,20},{28,24},{1,29},{... | collective-permute-start | bytes 2752520 | tf_op jit(solution)/shard_map/ppermute | solution.py:28
  99.9 10.1 %collective-permute-start.23 = (bf16[64,1024]{1,0:T(8,128)(2,1)S(1)}, bf16[64,1024]{1,0:T(8,128)(2,1)S(1)}, u32[]{:S(2)}, u32[]{:S(2)}) collective-permute-start(bf16[64,1024]{1,0:T(8,128)(2,1)S(1)} %get-tuple-element.95), channel_id=1, source_target_pairs={{0,1},{1,2},{2,3},{3,0},{4,5},{5,6},{6,7},{7,4},{8,9},{9,10},{10,1... | collective-permute-start | bytes 393224 | tf_op jit(solution)/shard_map/ppermute | solution.py:33
  100.1 9.9 %collective-permute-start.24 = (bf16[64,1024]{1,0:T(8,128)(2,1)S(1)}, bf16[64,1024]{1,0:T(8,128)(2,1)S(1)}, u32[]{:S(2)}, u32[]{:S(2)}) collective-permute-start(bf16[64,1024]{1,0:T(8,128)(2,1)S(1)} %get-tuple-element.96), channel_id=1, source_target_pairs={{0,2},{1,3},{2,0},{3,1},{4,6},{5,7},{6,4},{7,5},{8,10},{9,11},{10,... | collective-permute-start | bytes 393224 | tf_op jit(solution)/shard_map/ppermute | solution.py:33
  101.7 8.3 %collective-permute-start.25 = (bf16[64,1024]{1,0:T(8,128)(2,1)S(1)}, bf16[64,1024]{1,0:T(8,128)(2,1)S(1)}, u32[]{:S(2)}, u32[]{:S(2)}) collective-permute-start(bf16[64,1024]{1,0:T(8,128)(2,1)S(1)} %get-tuple-element.97), channel_id=1, source_target_pairs={{0,3},{1,0},{2,1},{3,2},{4,7},{5,4},{6,5},{7,6},{8,11},{9,8},{10,9... | collective-permute-start | bytes 393224 | tf_op jit(solution)/shard_map/ppermute | solution.py:33
  111.2 7.6 %collective-permute-start.27 = (bf16[64,2048]{1,0:T(8,128)(2,1)S(1)}, bf16[64,2048]{1,0:T(8,128)(2,1)S(1)}, u32[]{:S(2)}, u32[]{:S(2)}) collective-permute-start(bf16[64,2048]{1,0:T(8,128)(2,1)S(1)} %activation.7.refs_0_), channel_id=1, source_target_pairs={{0,2},{1,3},{2,0},{3,1},{4,6},{5,7},{6,4},{7,5},{8,10},{9,11},{10,... | collective-permute-start | bytes 786440 | tf_op jit(solution)/shard_map/ppermute | solution.py:33
  118.8 7.6 %collective-permute-start.28 = (bf16[64,2048]{1,0:T(8,128)(2,1)S(1)}, bf16[64,2048]{1,0:T(8,128)(2,1)S(1)}, u32[]{:S(2)}, u32[]{:S(2)}) collective-permute-start(bf16[64,2048]{1,0:T(8,128)(2,1)S(1)} %collective-permute-done.27.refs_2_), channel_id=1, source_target_pairs={{0,1},{1,0},{2,3},{3,2},{4,5},{5,4},{6,7},{7,6},{8,9},{9,8},{10,11... | collective-permute-start | bytes 786440 | tf_op jit(solution)/shard_map/ppermute | solution.py:38
  118.8 7.6 %collective-permute-start.26 = (bf16[64,2048]{1,0:T(8,128)(2,1)S(1)}, bf16[64,2048]{1,0:T(8,128)(2,1)S(1)}, u32[]{:S(2)}, u32[]{:S(2)}) collective-permute-start(bf16[64,2048]{1,0:T(8,128)(2,1)S(1)} %activation.7.refs_0_), channel_id=1, source_target_pairs={{0,1},{1,0},{2,3},{3,2},{4,5},{5,4},{6,7},{7,6},{8,9},{9,8},{10,11... | collective-permute-start | bytes 786440 | tf_op jit(solution)/shard_map/ppermute | solution.py:38
  119.3 26.8 %collective-permute-start.31 = (bf16[4,64,1792]{2,1,0:T(8,128)(2,1)S(1)}, bf16[4,64,1792]{2,1,0:T(8,128)(2,1)S(1)}, u32[]{:S(2)}, u32[]{:S(2)}) collective-permute-start(bf16[4,64,1792]{2,1,0:T(8,128)(2,1)S(1)} %second_product.6), channel_id=1, source_target_pairs={{0,28},{4,0},{8,4},{12,8},{16,12},{20,16},{24,20},{28,24},{1,29},{... | collective-permute-start | bytes 2752520 | tf_op jit(solution)/shard_map/ppermute | solution.py:28
  133.5 31.1 %collective-permute-start.30 = (bf16[4,64,1792]{2,1,0:T(8,128)(2,1)S(1)}, bf16[4,64,1792]{2,1,0:T(8,128)(2,1)S(1)}, u32[]{:S(2)}, u32[]{:S(2)}) collective-permute-start(bf16[4,64,1792]{2,1,0:T(8,128)(2,1)S(1)} %second_product.7), channel_id=1, source_target_pairs={{0,28},{4,0},{8,4},{12,8},{16,12},{20,16},{24,20},{28,24},{1,29},{... | collective-permute-start | bytes 2752520 | tf_op jit(solution)/shard_map/ppermute | solution.py:28
  (4 other events, 75.8 us)

commit v5 on v4

--- a/solution.py
+++ b/solution.py
@@ -8,6 +8,7 @@
 from jax.sharding import PartitionSpec as P
 
 CHUNKS = 4
+LAST = 16
 IN_FLIGHT = 2
 NEED = {("act", 1): (2,), ("act", 2): (3,)}
 WAIT = {("act", 3): (0,), ("mm2", 3): (1,), ("out", 2): (0,), ("out", 3): (1,)}
@@ -52,68 +53,41 @@
     )
 
 
-def take_kernel(c, pieces, source, target, sems):
-    n, part, _ = target.shape
-    step = part // pieces
-    copies = []
-    for i in range(n):
-        for k in range(pieces):
-            copy = pltpu.make_async_copy(
-                source.at[i, pl.ds(c * part + k * step, step)],
-                target.at[i, pl.ds(k * step, step)],
-                sems.at[i, k],
-            )
-            copy.start()
-            copies.append(copy)
-    for copy in copies:
-        copy.wait()
-
-
-def put_kernel(c, pieces, source, old, target, sems):
+def take_kernel(start, source, target, sem):
+    here = pl.ds(start, target.shape[1])
+    copy = pltpu.make_async_copy(source.at[:, here], target, sem)
+    copy.start()
+    copy.wait()
+
+
+def put_kernel(start, source, old, target, sem):
     del old
-    n, part, _ = source.shape
-    step = part // pieces
-    copies = []
-    for i in range(n):
-        for k in range(pieces):
-            copy = pltpu.make_async_copy(
-                source.at[i, pl.ds(k * step, step)],
-                target.at[i, pl.ds(c * part + k * step, step)],
-                sems.at[i, k],
-            )
-            copy.start()
-            copies.append(copy)
-    for copy in copies:
-        copy.wait()
-
-
-def pieces_of(part):
-    return 2 if part % 32 == 0 else 1
-
-
-def take_rows(array, c, part):
+    here = pl.ds(start, source.shape[1])
+    copy = pltpu.make_async_copy(source, target.at[:, here], sem)
+    copy.start()
+    copy.wait()
+
+
+def take_rows(array, start, size):
     n, _, width = array.shape
-    pieces = pieces_of(part)
-    return pl.pallas_call(
-        functools.partial(take_kernel, c, pieces),
-        out_shape=pltpu.VMEM((n, part, width), array.dtype),
+    return pl.pallas_call(
+        functools.partial(take_kernel, start),
+        out_shape=pltpu.VMEM((n, size, width), array.dtype),
         in_specs=[pl.BlockSpec(memory_space=pltpu.HBM)],
         out_specs=pl.BlockSpec(memory_space=pltpu.VMEM),
-        scratch_shapes=[pltpu.SemaphoreType.DMA((n, pieces))],
+        scratch_shapes=[pltpu.SemaphoreType.DMA],
         cost_estimate=FREE,
         name="take_rows",
     )(in_hbm(array))
 
 
-def put_rows(out, piece, c):
-    n, part, _ = piece.shape
-    pieces = pieces_of(part)
-    return pl.pallas_call(
-        functools.partial(put_kernel, c, pieces),
+def put_rows(out, piece, start):
+    return pl.pallas_call(
+        functools.partial(put_kernel, start),
         out_shape=jax.ShapeDtypeStruct(out.shape, out.dtype),
         in_specs=[pl.BlockSpec(memory_space=pltpu.VMEM), pl.BlockSpec(memory_space=pltpu.HBM)],
         out_specs=pl.BlockSpec(memory_space=pltpu.HBM),
-        scratch_shapes=[pltpu.SemaphoreType.DMA((n, pieces))],
+        scratch_shapes=[pltpu.SemaphoreType.DMA],
         input_output_aliases={1: 0},
         cost_estimate=FREE,
         name="put_rows",
@@ -210,7 +184,7 @@
 
 
 def second_kernel(n, me_ref, dense_ref, gate_ref, up_ref, router_ref, *refs):
-    *block_refs, out_ref, held = refs
+    block_refs, out_refs, held = refs[:n], refs[n:-1], refs[-1]
     chips = n // 2
     hidden = gate_ref.shape[1]
 
@@ -228,10 +202,15 @@
     result = result + contract_last(both[:, hidden:], up_ref[...])
     dense = dense_ref[...].reshape(both.shape[0], -1)
     result = result + contract_last(dense, router_ref[...])
-    out_ref[...] = result.astype(out_ref.dtype).reshape(out_ref.shape)
-
-
-def second_product(me, blocks, c, dense, w_gate, w_up, w_router):
+    result = result.astype(jnp.bfloat16).reshape(n, held.shape[1], -1)
+    first = 0
+    for out_ref in out_refs:
+        size = out_ref.shape[1]
+        out_ref[...] = result[:, first : first + size]
+        first += size
+
+
+def second_product(me, blocks, c, dense, w_gate, w_up, w_router, sizes):
     n = len(blocks)
     part, both = blocks[0].shape
     width, hidden = w_gate.shape
@@ -239,7 +218,7 @@
     block = block_of(width, 256)
     return pl.pallas_call(
         functools.partial(second_kernel, n),
-        out_shape=jax.ShapeDtypeStruct((n, part, width), jnp.bfloat16),
+        out_shape=[jax.ShapeDtypeStruct((n, size, width), jnp.bfloat16) for size in sizes],
         grid_spec=pltpu.PrefetchScalarGridSpec(
             num_scalar_prefetch=1,
             grid=(width // block,),
@@ -250,7 +229,7 @@
                 pl.BlockSpec((block, n_experts), lambda i, me: (i, 0)),
             ]
             + [pl.BlockSpec((part, both), lambda i, me: (0, 0))] * n,
-            out_specs=pl.BlockSpec((n, part, block), lambda i, me: (0, 0, i)),
+            out_specs=[pl.BlockSpec((n, size, block), lambda i, me: (0, 0, i)) for size in sizes],
             scratch_shapes=[pltpu.VMEM((n, part, both), jnp.bfloat16)],
         ),
         compiler_params=params(),
@@ -283,7 +262,7 @@
     dense = routed_grad(gate_grad[0], gate_scores[0], expert_ids[0], router_weight.shape[2])
     for c in range(chunks):
         if c == 0:
-            piece = take_rows(grads, c, part)
+            piece = take_rows(grads, 0, part)
             grads, dense = in_order(grads, dense)
         else:
             piece = grads[:, c * part : (c + 1) * part]
@@ -318,8 +297,11 @@
         far += [to_other_core(x) for x in near[1:]]
         far[-1] = at("mm2", c, far[-1])
         blocks = [x for pair in zip(near, far) for x in pair]
-        result = second_product(
-            me, blocks, c, dense, shared_gate[0], shared_up[0], router_weight[0]
+        sizes = [part]
+        if c + 1 == chunks and part > LAST:
+            sizes = [part - LAST, LAST]
+        result, *last = second_product(
+            me, blocks, c, dense, shared_gate[0], shared_up[0], router_weight[0], sizes
         )
         if c + 1 < chunks:
             partials[0], result = in_order(partials[0], result)
@@ -330,7 +312,9 @@
     out = jnp.zeros((n, rows, width), jnp.bfloat16)
     for c in range(chunks - 1):
         out = lax.dynamic_update_slice(out, sent[c], (0, c * part, 0))
-    out = put_rows(out, sent[-1], chunks - 1)
+    out = put_rows(out, sent[-1], (chunks - 1) * part)
+    for piece in last:
+        out = put_rows(out, back_one(piece), rows - LAST)
     return out.reshape(1, tokens, width)
 
 

time: 167 us -> 166 us (level)
  waiting for transfers between devices: 67.9 us -> 64.8 us
  starting transfers between devices: 40.2 us -> 42.4 us
    ppermute x16, waiting for transfers between devices: 24.7 us -> 21.7 us  [to_expert(): return lax.ppermute(x, 'expert', [(i, (i + by) % n) for i in range(n)])]
    ppermute x8 -> x9, starting transfers between devices: 23.6 us -> 25.8 us  [back_one(): lax.ppermute(x, 'pipe', [(i, (i - 1) % length) for i in range(length)])]
    pallas_call x6 -> x7, Pallas kernels: 30.6 us -> 31 us  [the longest x4 28.3 us: second_product(): pl.pallas_call(functools.partial(second_kernel, n), out_shape=[jax.ShapeD...]
    ppermute x8 -> x9, waiting for transfers between devices: 43.2 us -> 43 us  [back_one(): lax.ppermute(x, 'pipe', [(i, (i - 1) % length) for i in range(length)])]
  transfers between devices with their start and end apart: 32 -> 33, of which waited for: 13 -> 14; matrix products, arithmetic and copies ran while one was open for 4% -> 4% of each run, Pallas kernels for 29% -> 29%
where the time goes in v5:
time: 166 us; the launch traced here: 165 us
  waiting for transfers between devices  64.8 us (39%)
  Pallas kernels  50.3 us (30%)
  starting transfers between devices  42.4 us (26%)
  local copies, waits for them, and re-layouts  7.4 us (4%)
    ppermute x9, waiting for transfers between devices, back_one(): lax.ppermute(x, 'pipe', [(i, (i - 1) % length) for i in range(length)])  43 us
    pallas_call x4, Pallas kernels, second_product(): pl.pallas_call(functools.partial(second_kernel, n), out_shape=[jax.ShapeD...  28.3 us
    ppermute x9, starting transfers between devices, back_one(): lax.ppermute(x, 'pipe', [(i, (i - 1) % length) for i in range(length)])  25.8 us
    ppermute x16, waiting for transfers between devices, to_expert(): return lax.ppermute(x, 'expert', [(i, (i + by) % n) for i in range(n)])  21.7 us
    ppermute x16, starting transfers between devices, to_expert(): return lax.ppermute(x, 'expert', [(i, (i + by) % n) for i in range(n)])  15.2 us
    pallas_call x4, Pallas kernels, first_product(): pl.pallas_call(functools.partial(first_kernel, n), out_shape=[jax.ShapeDt...  9.55 us
    pallas_call x1, Pallas kernels, routed_grad(): pl.pallas_call(routed_kernel, out_shape=jax.ShapeDtypeStruct((tokens, n_e...  5.07 us
    pallas_call x4, Pallas kernels, activation(): pl.pallas_call(activation_kernel, out_shape=jax.ShapeDtypeStruct((part, 2...  4.69 us
  transfers between devices with their start and end apart: 33, of which 14 were waited for; matrix products, arithmetic and copies ran while one was open for 4% of the time, Pallas kernels for 29%

profile of v5, /device:TPU:0, one launch (start us, length us, event | category | flops | bytes accessed | tf_op | source)
XLA Modules:
  0.0 165.2 jit_solution(1547247087952656162)
XLA Ops:
  1.2 6.0 %collective-permute-start = (bf16[4,64,1792]{2,1,0:T(8,128)(2,1)S(1)}, bf16[4,64,1792]{2,1,0:T(8,128)(2,1)S(1)}, u32[]{:S(2)}, u32[]{:S(2)}) collective-permute-start(bf16[4,64,1792]{2,1,0:T(8,128)(2,1)S(1)} %take_rows.1), channel_id=1, source_target_pairs={{0,28},{4,0},{8,4},{12,8},{16,12},{20,16},{24,20},{28,24},{1,29},{... | collective-permute-start | bytes 2752520 | tf_op jit(solution)/shard_map/ppermute | solution.py:29
  7.2 5.1 %routed_grad.1 = bf16[1024,256]{1,0:T(8,128)(2,1)} custom-call(f32[8,1024]{1,0:T(8,128)} %bitcast.49, f32[8,1024]{1,0:T(8,128)} %bitcast.50, s32[8,1024]{1,0:T(8,128)} %bitcast.51), custom_call_target="tpu_custom_call" | custom-call | tf_op jit(solution)/shard_map/routed_grad/pallas_call | solution.py:114
  12.3 3.3 %fusion = (bf16[4,64,1792]{2,1,0:T(8,128)(2,1)}, bf16[4,64,1792]{2,1,0:T(8,128)(2,1)}, bf16[4,64,1792]{2,1,0:T(8,128)(2,1)}) fusion(bf16[4,256,1792]{2,1,0:T(8,128)(2,1)} %bitcast.40), kind=kLoop, calls=%fused_computation.2 | loop fusion | bytes 5505024 | tf_op jit(solution)/shard_map/slice | solution.py:268
  16.2 11.8 %collective-permute-done.rows_ref = bf16[4,64,1792]{2,1,0:T(8,128)(2,1)S(1)} collective-permute-done((bf16[4,64,1792]{2,1,0:T(8,128)(2,1)S(1)}, bf16[4,64,1792]{2,1,0:T(8,128)(2,1)S(1)}, u32[]{:S(2)}, u32[]{:S(2)}) %collective-permute-start) | collective-permute-done | bytes 917536 | tf_op jit(solution)/shard_map/ppermute | solution.py:29
  28.0 5.2 %collective-permute-start.8 = (bf16[4,64,1792]{2,1,0:T(8,128)(2,1)}, bf16[4,64,1792]{2,1,0:T(8,128)(2,1)S(1)}, u32[]{:S(2)}, u32[]{:S(2)}) collective-permute-start(bf16[4,64,1792]{2,1,0:T(8,128)(2,1)} %get-tuple-element.73), channel_id=1, source_target_pairs={{0,28},{4,0},{8,4},{12,8},{16,12},{20,16},{24,20},{28,24},{1,29},{... | collective-permute-start | bytes 2752520 | tf_op jit(solution)/shard_map/ppermute | solution.py:29
  33.2 4.0 %first_product.4 = (bf16[64,1024]{1,0:T(8,128)(2,1)S(1)}, bf16[64,1024]{1,0:T(8,128)(2,1)S(1)}, bf16[64,1024]{1,0:T(8,128)(2,1)S(1)}, bf16[64,1024]{1,0:T(8,128)(2,1)S(1)}) custom-call(s32[1]{0:T(128)} %bitcast.me_ref, bf16[4,64,1792]{2,1,0:T(8,128)(2,1)S(1)} %collective-permute-done.rows_ref, bf16[1024,1792]{1,0:T(8,128)(2,1)} %bitcast.19), custom_call_target="tpu_custom_call" | custom-call | tf_op jit(solution)/shard_map/first_product/pallas_call | solution.py:138
  37.2 1.6 collective-permute-start.3
  40.2 2.2 %collective-permute-done.2.refs_1_ = bf16[64,1024]{1,0:T(8,128)(2,1)S(1)} collective-permute-done((bf16[64,1024]{1,0:T(8,128)(2,1)S(1)}, bf16[64,1024]{1,0:T(8,128)(2,1)S(1)}, u32[]{:S(2)}, u32[]{:S(2)}) %collective-permute-start.2) | collective-permute-done | bytes 131104 | tf_op jit(solution)/shard_map/ppermute | solution.py:34
  48.4 1.9 %first_product.5 = (bf16[64,1024]{1,0:T(8,128)(2,1)S(1)}, bf16[64,1024]{1,0:T(8,128)(2,1)S(1)}, bf16[64,1024]{1,0:T(8,128)(2,1)S(1)}, bf16[64,1024]{1,0:T(8,128)(2,1)S(1)}) custom-call(s32[1]{0:T(128)} %bitcast.me_ref, bf16[4,64,1792]{2,1,0:T(8,128)(2,1)S(1)} %collective-permute-done.1.rows_ref, bf16[1024,1792]{1,0:T(8,128)(2,1)S(1)} %bitcast.20), custom_call_target="tpu_custom_call" | custom-call | tf_op jit(solution)/shard_map/first_product/pallas_call | solution.py:138
  50.3 4.9 %collective-permute-done.5.refs_2_ = bf16[64,2048]{1,0:T(8,128)(2,1)S(1)} collective-permute-done((bf16[64,2048]{1,0:T(8,128)(2,1)S(1)}, bf16[64,2048]{1,0:T(8,128)(2,1)S(1)}, u32[]{:S(2)}, u32[]{:S(2)}) %collective-permute-start.5) | collective-permute-done | bytes 262176 | tf_op jit(solution)/shard_map/ppermute | solution.py:34
  56.8 1.4 collective-permute-start.11
  58.3 7.1 %second_product.4 = bf16[4,64,1792]{2,1,0:T(8,128)(2,1)S(1)} custom-call(s32[1]{0:T(128)} %bitcast.me_ref, bf16[4,256,256]{2,1,0:T(8,128)(2,1)S(1)} %bitcast.27, bf16[1792,1024]{1,0:T(8,128)(2,1)} %bitcast.31, bf16[1792,1024]{1,0:T(8,128)(2,1)} %bitcast.35, bf16[1792,256]{1,0:T(8,128)(2,1)S(1)} %bitcast.23, bf16[64,2048]{1,0:T(8,128)(2,1)S(1)} %activation.4.refs_0_, ...), custom_call_target="tpu_custom_call" | custom-call | tf_op jit(solution)/shard_map/second_product/pallas_call | solution.py:219
  65.4 2.0 %collective-permute-done.8.rows_ref = bf16[4,64,1792]{2,1,0:T(8,128)(2,1)S(1)} collective-permute-done((bf16[4,64,1792]{2,1,0:T(8,128)(2,1)}, bf16[4,64,1792]{2,1,0:T(8,128)(2,1)S(1)}, u32[]{:S(2)}, u32[]{:S(2)}) %collective-permute-start.8) | collective-permute-done | bytes 917536 | tf_op jit(solution)/shard_map/ppermute | solution.py:29
  68.6 1.6 collective-permute-start.12
  70.2 1.9 %first_product.6 = (bf16[64,1024]{1,0:T(8,128)(2,1)S(1)}, bf16[64,1024]{1,0:T(8,128)(2,1)S(1)}, bf16[64,1024]{1,0:T(8,128)(2,1)S(1)}, bf16[64,1024]{1,0:T(8,128)(2,1)S(1)}) custom-call(s32[1]{0:T(128)} %bitcast.me_ref, bf16[4,64,1792]{2,1,0:T(8,128)(2,1)S(1)} %collective-permute-done.8.rows_ref, bf16[1024,1792]{1,0:T(8,128)(2,1)S(1)} %bitcast.21), custom_call_target="tpu_custom_call" | custom-call | tf_op jit(solution)/shard_map/first_product/pallas_call | solution.py:138
  72.1 3.0 %collective-permute-done.12.refs_2_ = bf16[64,2048]{1,0:T(8,128)(2,1)S(1)} collective-permute-done((bf16[64,2048]{1,0:T(8,128)(2,1)S(1)}, bf16[64,2048]{1,0:T(8,128)(2,1)S(1)}, u32[]{:S(2)}, u32[]{:S(2)}) %collective-permute-start.12) | collective-permute-done | bytes 262176 | tf_op jit(solution)/shard_map/ppermute | solution.py:34
  75.0 5.1 %collective-permute-start.22 = (bf16[4,64,1792]{2,1,0:T(8,128)(2,1)S(1)}, bf16[4,64,1792]{2,1,0:T(8,128)(2,1)S(1)}, u32[]{:S(2)}, u32[]{:S(2)}) collective-permute-start(bf16[4,64,1792]{2,1,0:T(8,128)(2,1)S(1)} %second_product.4), channel_id=1, source_target_pairs={{0,28},{4,0},{8,4},{12,8},{16,12},{20,16},{24,20},{28,24},{1,29},{... | collective-permute-start | bytes 2752520 | tf_op jit(solution)/shard_map/ppermute | solution.py:29
  80.3 1.6 collective-permute-start.17
  83.1 7.1 %second_product.5 = bf16[4,64,1792]{2,1,0:T(8,128)(2,1)S(1)} custom-call(s32[1]{0:T(128)} %bitcast.me_ref, bf16[4,256,256]{2,1,0:T(8,128)(2,1)S(1)} %bitcast.28, bf16[1792,1024]{1,0:T(8,128)(2,1)} %bitcast.32, bf16[1792,1024]{1,0:T(8,128)(2,1)} %bitcast.36, bf16[1792,256]{1,0:T(8,128)(2,1)S(1)} %bitcast.24, bf16[64,2048]{1,0:T(8,128)(2,1)S(1)} %activation.5.refs_0_, ...), custom_call_target="tpu_custom_call" | custom-call | tf_op jit(solution)/shard_map/second_product/pallas_call | solution.py:219
  92.0 1.8 %first_product.7 = (bf16[64,1024]{1,0:T(8,128)(2,1)S(1)}, bf16[64,1024]{1,0:T(8,128)(2,1)S(1)}, bf16[64,1024]{1,0:T(8,128)(2,1)S(1)}, bf16[64,1024]{1,0:T(8,128)(2,1)S(1)}) custom-call(s32[1]{0:T(128)} %bitcast.me_ref, bf16[4,64,1792]{2,1,0:T(8,128)(2,1)S(1)} %collective-permute-done.15.rows_ref, bf16[1024,1792]{1,0:T(8,128)(2,1)S(1)} %bitcast.22), custom_call_target="tpu_custom_call" | custom-call | tf_op jit(solution)/shard_map/first_product/pallas_call | solution.py:138
  93.8 5.2 %collective-permute-done.19.refs_2_ = bf16[64,2048]{1,0:T(8,128)(2,1)S(1)} collective-permute-done((bf16[64,2048]{1,0:T(8,128)(2,1)S(1)}, bf16[64,2048]{1,0:T(8,128)(2,1)S(1)}, u32[]{:S(2)}, u32[]{:S(2)}) %collective-permute-start.19) | collective-permute-done | bytes 262176 | tf_op jit(solution)/shard_map/ppermute | solution.py:34
  100.0 1.6 collective-permute-start.24
  102.8 7.1 %second_product.6 = bf16[4,64,1792]{2,1,0:T(8,128)(2,1)S(1)} custom-call(s32[1]{0:T(128)} %bitcast.me_ref, bf16[4,256,256]{2,1,0:T(8,128)(2,1)S(1)} %bitcast.29, bf16[1792,1024]{1,0:T(8,128)(2,1)} %bitcast.33, bf16[1792,1024]{1,0:T(8,128)(2,1)} %bitcast.37, bf16[1792,256]{1,0:T(8,128)(2,1)S(1)} %bitcast.25, bf16[64,2048]{1,0:T(8,128)(2,1)S(1)} %activation.6.refs_0_, ...), custom_call_target="tpu_custom_call" | custom-call | tf_op jit(solution)/shard_map/second_product/pallas_call | solution.py:219
  111.6 2.9 %collective-permute-start.32 = (bf16[4,64,1792]{2,1,0:T(8,128)(2,1)S(1)}, bf16[4,64,1792]{2,1,0:T(8,128)(2,1)S(1)}, u32[]{:S(2)}, u32[]{:S(2)}) collective-permute-start(bf16[4,64,1792]{2,1,0:T(8,128)(2,1)S(1)} %second_product.6), channel_id=1, source_target_pairs={{0,28},{4,0},{8,4},{12,8},{16,12},{20,16},{24,20},{28,24},{1,29},{... | collective-permute-start | bytes 2752520 | tf_op jit(solution)/shard_map/ppermute | solution.py:29
  114.6 4.1 %collective-permute-done.27.refs_2_ = bf16[64,2048]{1,0:T(8,128)(2,1)S(1)} collective-permute-done((bf16[64,2048]{1,0:T(8,128)(2,1)S(1)}, bf16[64,2048]{1,0:T(8,128)(2,1)S(1)}, u32[]{:S(2)}, u32[]{:S(2)}) %collective-permute-start.27) | collective-permute-done | bytes 262176 | tf_op jit(solution)/shard_map/ppermute | solution.py:34
  119.2 7.1 %collective-permute-done.29 = bf16[4,64,1792]{2,1,0:T(8,128)(2,1)S(1)} collective-permute-done((bf16[4,64,1792]{2,1,0:T(8,128)(2,1)S(1)}, bf16[4,64,1792]{2,1,0:T(8,128)(2,1)S(1)}, u32[]{:S(2)}, u32[]{:S(2)}) %collective-permute-start.29) | collective-permute-done | bytes 917536 | tf_op jit(solution)/shard_map/ppermute | solution.py:29
  126.3 7.1 %second_product.7 = (bf16[4,48,1792]{2,1,0:T(8,128)(2,1)S(1)}, bf16[4,16,1792]{2,1,0:T(8,128)(2,1)S(1)}) custom-call(s32[1]{0:T(128)} %bitcast.me_ref, bf16[4,256,256]{2,1,0:T(8,128)(2,1)S(1)} %bitcast.30, bf16[1792,1024]{1,0:T(8,128)(2,1)} %bitcast.34, bf16[1792,1024]{1,0:T(8,128)(2,1)} %bitcast.38, bf16[1792,256]{1,0:T(8,128)(2,1)S(1)} %bitcast.26, ...), custom_call_target="tpu_custom_call" | custom-call | tf_op jit(solution)/shard_map/second_product/pallas_call | solution.py:219
  133.4 5.2 %collective-permute-start.31 = (bf16[4,48,1792]{2,1,0:T(8,128)(2,1)S(1)}, bf16[4,48,1792]{2,1,0:T(8,128)(2,1)S(1)}, u32[]{:S(2)}, u32[]{:S(2)}) collective-permute-start(bf16[4,48,1792]{2,1,0:T(8,128)(2,1)S(1)} %get-tuple-element.105), channel_id=1, source_target_pairs={{0,28},{4,0},{8,4},{12,8},{16,12},{20,16},{24,20},{28,24},{1,29},{... | collective-permute-start | bytes 2064392 | tf_op jit(solution)/shard_map/ppermute | solution.py:29
  138.6 2.1 %dynamic_update_slice.9 = bf16[4,256,1792]{2,1,0:T(8,128)(2,1)} pad(bf16[4,64,1792]{2,1,0:T(8,128)(2,1)S(1)} %collective-permute-done.22, bf16[]{:T(256)} %constant.1.clone.1), padding=0_0x0_192x0_0 | pad | bytes 4587522 | tf_op jit(solution)/shard_map/dynamic_update_slice | solution.py:314
  141.7 4.2 %collective-permute-done.32 = bf16[4,64,1792]{2,1,0:T(8,128)(2,1)S(1)} collective-permute-done((bf16[4,64,1792]{2,1,0:T(8,128)(2,1)S(1)}, bf16[4,64,1792]{2,1,0:T(8,128)(2,1)S(1)}, u32[]{:S(2)}, u32[]{:S(2)}) %collective-permute-start.32) | collective-permute-done | bytes 917536 | tf_op jit(solution)/shard_map/ppermute | solution.py:29
  146.9 13.8 %collective-permute-done.31.source = bf16[4,48,1792]{2,1,0:T(8,128)(2,1)S(1)} collective-permute-done((bf16[4,48,1792]{2,1,0:T(8,128)(2,1)S(1)}, bf16[4,48,1792]{2,1,0:T(8,128)(2,1)S(1)}, u32[]{:S(2)}, u32[]{:S(2)}) %collective-permute-start.31) | collective-permute-done | bytes 688160 | tf_op jit(solution)/shard_map/ppermute | solution.py:29
  161.6 2.9 %collective-permute-done.30.source = bf16[4,16,1792]{2,1,0:T(8,128)(2,1)S(1)} collective-permute-done((bf16[4,16,1792]{2,1,0:T(8,128)(2,1)S(1)}, bf16[4,16,1792]{2,1,0:T(8,128)(2,1)S(1)}, u32[]{:S(2)}, u32[]{:S(2)}) %collective-permute-start.30) | collective-permute-done | bytes 229408 | tf_op jit(solution)/shard_map/ppermute | solution.py:29
  (62 shorter events, 23.3 us)
Async XLA Ops:
  1.2 26.8 %collective-permute-start = (bf16[4,64,1792]{2,1,0:T(8,128)(2,1)S(1)}, bf16[4,64,1792]{2,1,0:T(8,128)(2,1)S(1)}, u32[]{:S(2)}, u32[]{:S(2)}) collective-permute-start(bf16[4,64,1792]{2,1,0:T(8,128)(2,1)S(1)} %take_rows.1), channel_id=1, source_target_pairs={{0,28},{4,0},{8,4},{12,8},{16,12},{20,16},{24,20},{28,24},{1,29},{... | collective-permute-start | bytes 2752520 | tf_op jit(solution)/shard_map/ppermute | solution.py:29
  15.6 32.1 %collective-permute-start.1 = (bf16[4,64,1792]{2,1,0:T(8,128)(2,1)}, bf16[4,64,1792]{2,1,0:T(8,128)(2,1)S(1)}, u32[]{:S(2)}, u32[]{:S(2)}) collective-permute-start(bf16[4,64,1792]{2,1,0:T(8,128)(2,1)} %get-tuple-element.111), channel_id=1, source_target_pairs={{0,28},{4,0},{8,4},{12,8},{16,12},{20,16},{24,20},{28,24},{1,29},{... | collective-permute-start | bytes 2752520 | tf_op jit(solution)/shard_map/ppermute | solution.py:29
  28.0 39.4 %collective-permute-start.8 = (bf16[4,64,1792]{2,1,0:T(8,128)(2,1)}, bf16[4,64,1792]{2,1,0:T(8,128)(2,1)S(1)}, u32[]{:S(2)}, u32[]{:S(2)}) collective-permute-start(bf16[4,64,1792]{2,1,0:T(8,128)(2,1)} %get-tuple-element.73), channel_id=1, source_target_pairs={{0,28},{4,0},{8,4},{12,8},{16,12},{20,16},{24,20},{28,24},{1,29},{... | collective-permute-start | bytes 2752520 | tf_op jit(solution)/shard_map/ppermute | solution.py:29
  37.2 5.2 %collective-permute-start.2 = (bf16[64,1024]{1,0:T(8,128)(2,1)S(1)}, bf16[64,1024]{1,0:T(8,128)(2,1)S(1)}, u32[]{:S(2)}, u32[]{:S(2)}) collective-permute-start(bf16[64,1024]{1,0:T(8,128)(2,1)S(1)} %get-tuple-element.65), channel_id=1, source_target_pairs={{0,1},{1,2},{2,3},{3,0},{4,5},{5,6},{6,7},{7,4},{8,9},{9,10},{10,1... | collective-permute-start | bytes 393224 | tf_op jit(solution)/shard_map/ppermute | solution.py:34
  37.2 6.4 %collective-permute-start.3 = (bf16[64,1024]{1,0:T(8,128)(2,1)S(1)}, bf16[64,1024]{1,0:T(8,128)(2,1)S(1)}, u32[]{:S(2)}, u32[]{:S(2)}) collective-permute-start(bf16[64,1024]{1,0:T(8,128)(2,1)S(1)} %get-tuple-element.66), channel_id=1, source_target_pairs={{0,2},{1,3},{2,0},{3,1},{4,6},{5,7},{6,4},{7,5},{8,10},{9,11},{10,... | collective-permute-start | bytes 393224 | tf_op jit(solution)/shard_map/ppermute | solution.py:34
  38.8 6.0 %collective-permute-start.4 = (bf16[64,1024]{1,0:T(8,128)(2,1)S(1)}, bf16[64,1024]{1,0:T(8,128)(2,1)S(1)}, u32[]{:S(2)}, u32[]{:S(2)}) collective-permute-start(bf16[64,1024]{1,0:T(8,128)(2,1)S(1)} %get-tuple-element.67), channel_id=1, source_target_pairs={{0,3},{1,0},{2,1},{3,2},{4,7},{5,4},{6,5},{7,6},{8,11},{9,8},{10,9... | collective-permute-start | bytes 393224 | tf_op jit(solution)/shard_map/ppermute | solution.py:34
  46.0 9.1 %collective-permute-start.5 = (bf16[64,2048]{1,0:T(8,128)(2,1)S(1)}, bf16[64,2048]{1,0:T(8,128)(2,1)S(1)}, u32[]{:S(2)}, u32[]{:S(2)}) collective-permute-start(bf16[64,2048]{1,0:T(8,128)(2,1)S(1)} %activation.4.refs_0_), channel_id=1, source_target_pairs={{0,2},{1,3},{2,0},{3,1},{4,6},{5,7},{6,4},{7,5},{8,10},{9,11},{10,... | collective-permute-start | bytes 786440 | tf_op jit(solution)/shard_map/ppermute | solution.py:34
  47.7 7.9 %collective-permute-start.6 = (bf16[64,2048]{1,0:T(8,128)(2,1)S(1)}, bf16[64,2048]{1,0:T(8,128)(2,1)S(1)}, u32[]{:S(2)}, u32[]{:S(2)}) collective-permute-start(bf16[64,2048]{1,0:T(8,128)(2,1)S(1)} %activation.4.refs_0_), channel_id=1, source_target_pairs={{0,1},{1,0},{2,3},{3,2},{4,5},{5,4},{6,7},{7,6},{8,9},{9,8},{10,11... | collective-permute-start | bytes 786440 | tf_op jit(solution)/shard_map/ppermute | solution.py:39
  55.4 34.8 %collective-permute-start.15 = (bf16[4,64,1792]{2,1,0:T(8,128)(2,1)S(1)}, bf16[4,64,1792]{2,1,0:T(8,128)(2,1)S(1)}, u32[]{:S(2)}, u32[]{:S(2)}) collective-permute-start(bf16[4,64,1792]{2,1,0:T(8,128)(2,1)S(1)} %copy-done.3), channel_id=1, source_target_pairs={{0,28},{4,0},{8,4},{12,8},{16,12},{20,16},{24,20},{28,24},{1,29},{... | collective-permute-start | bytes 2752520 | tf_op jit(solution)/shard_map/ppermute | solution.py:29
  55.4 12.0 %collective-permute-start.9 = (bf16[64,1024]{1,0:T(8,128)(2,1)S(1)}, bf16[64,1024]{1,0:T(8,128)(2,1)S(1)}, u32[]{:S(2)}, u32[]{:S(2)}) collective-permute-start(bf16[64,1024]{1,0:T(8,128)(2,1)S(1)} %get-tuple-element.76), channel_id=1, source_target_pairs={{0,1},{1,2},{2,3},{3,0},{4,5},{5,6},{6,7},{7,4},{8,9},{9,10},{10,1... | collective-permute-start | bytes 393224 | tf_op jit(solution)/shard_map/ppermute | solution.py:34
  55.7 11.7 %collective-permute-start.10 = (bf16[64,1024]{1,0:T(8,128)(2,1)S(1)}, bf16[64,1024]{1,0:T(8,128)(2,1)S(1)}, u32[]{:S(2)}, u32[]{:S(2)}) collective-permute-start(bf16[64,1024]{1,0:T(8,128)(2,1)S(1)} %get-tuple-element.77), channel_id=1, source_target_pairs={{0,2},{1,3},{2,0},{3,1},{4,6},{5,7},{6,4},{7,5},{8,10},{9,11},{10,... | collective-permute-start | bytes 393224 | tf_op jit(solution)/shard_map/ppermute | solution.py:34
  56.8 10.6 %collective-permute-start.11 = (bf16[64,1024]{1,0:T(8,128)(2,1)S(1)}, bf16[64,1024]{1,0:T(8,128)(2,1)S(1)}, u32[]{:S(2)}, u32[]{:S(2)}) collective-permute-start(bf16[64,1024]{1,0:T(8,128)(2,1)S(1)} %get-tuple-element.78), channel_id=1, source_target_pairs={{0,3},{1,0},{2,1},{3,2},{4,7},{5,4},{6,5},{7,6},{8,11},{9,8},{10,9... | collective-permute-start | bytes 393224 | tf_op jit(solution)/shard_map/ppermute | solution.py:34
  68.6 6.4 %collective-permute-start.12 = (bf16[64,2048]{1,0:T(8,128)(2,1)S(1)}, bf16[64,2048]{1,0:T(8,128)(2,1)S(1)}, u32[]{:S(2)}, u32[]{:S(2)}) collective-permute-start(bf16[64,2048]{1,0:T(8,128)(2,1)S(1)} %activation.5.refs_0_), channel_id=1, source_target_pairs={{0,2},{1,3},{2,0},{3,1},{4,6},{5,7},{6,4},{7,5},{8,10},{9,11},{10,... | collective-permute-start | bytes 786440 | tf_op jit(solution)/shard_map/ppermute | solution.py:34
  70.2 10.2 %collective-permute-start.13 = (bf16[64,2048]{1,0:T(8,128)(2,1)S(1)}, bf16[64,2048]{1,0:T(8,128)(2,1)S(1)}, u32[]{:S(2)}, u32[]{:S(2)}) collective-permute-start(bf16[64,2048]{1,0:T(8,128)(2,1)S(1)} %activation.5.refs_0_), channel_id=1, source_target_pairs={{0,1},{1,0},{2,3},{3,2},{4,5},{5,4},{6,7},{7,6},{8,9},{9,8},{10,11... | collective-permute-start | bytes 786440 | tf_op jit(solution)/shard_map/ppermute | solution.py:39
  75.0 6.9 %collective-permute-start.14 = (bf16[64,2048]{1,0:T(8,128)(2,1)S(1)}, bf16[64,2048]{1,0:T(8,128)(2,1)S(1)}, u32[]{:S(2)}, u32[]{:S(2)}) collective-permute-start(bf16[64,2048]{1,0:T(8,128)(2,1)S(1)} %collective-permute-done.12.refs_2_), channel_id=1, source_target_pairs={{0,1},{1,0},{2,3},{3,2},{4,5},{5,4},{6,7},{7,6},{8,9},{9,8},{10,11... | collective-permute-start | bytes 786440 | tf_op jit(solution)/shard_map/ppermute | solution.py:39
  75.0 34.8 %collective-permute-start.22 = (bf16[4,64,1792]{2,1,0:T(8,128)(2,1)S(1)}, bf16[4,64,1792]{2,1,0:T(8,128)(2,1)S(1)}, u32[]{:S(2)}, u32[]{:S(2)}) collective-permute-start(bf16[4,64,1792]{2,1,0:T(8,128)(2,1)S(1)} %second_product.4), channel_id=1, source_target_pairs={{0,28},{4,0},{8,4},{12,8},{16,12},{20,16},{24,20},{28,24},{1,29},{... | collective-permute-start | bytes 2752520 | tf_op jit(solution)/shard_map/ppermute | solution.py:29
  80.1 10.1 %collective-permute-start.16 = (bf16[64,1024]{1,0:T(8,128)(2,1)S(1)}, bf16[64,1024]{1,0:T(8,128)(2,1)S(1)}, u32[]{:S(2)}, u32[]{:S(2)}) collective-permute-start(bf16[64,1024]{1,0:T(8,128)(2,1)S(1)} %get-tuple-element.87), channel_id=1, source_target_pairs={{0,1},{1,2},{2,3},{3,0},{4,5},{5,6},{6,7},{7,4},{8,9},{9,10},{10,1... | collective-permute-start | bytes 393224 | tf_op jit(solution)/shard_map/ppermute | solution.py:34
  80.3 9.9 %collective-permute-start.17 = (bf16[64,1024]{1,0:T(8,128)(2,1)S(1)}, bf16[64,1024]{1,0:T(8,128)(2,1)S(1)}, u32[]{:S(2)}, u32[]{:S(2)}) collective-permute-start(bf16[64,1024]{1,0:T(8,128)(2,1)S(1)} %get-tuple-element.88), channel_id=1, source_target_pairs={{0,2},{1,3},{2,0},{3,1},{4,6},{5,7},{6,4},{7,5},{8,10},{9,11},{10,... | collective-permute-start | bytes 393224 | tf_op jit(solution)/shard_map/ppermute | solution.py:34
  81.9 8.3 %collective-permute-start.18 = (bf16[64,1024]{1,0:T(8,128)(2,1)S(1)}, bf16[64,1024]{1,0:T(8,128)(2,1)S(1)}, u32[]{:S(2)}, u32[]{:S(2)}) collective-permute-start(bf16[64,1024]{1,0:T(8,128)(2,1)S(1)} %get-tuple-element.89), channel_id=1, source_target_pairs={{0,3},{1,0},{2,1},{3,2},{4,7},{5,4},{6,5},{7,6},{8,11},{9,8},{10,9... | collective-permute-start | bytes 393224 | tf_op jit(solution)/shard_map/ppermute | solution.py:34
  91.4 7.6 %collective-permute-start.19 = (bf16[64,2048]{1,0:T(8,128)(2,1)S(1)}, bf16[64,2048]{1,0:T(8,128)(2,1)S(1)}, u32[]{:S(2)}, u32[]{:S(2)}) collective-permute-start(bf16[64,2048]{1,0:T(8,128)(2,1)S(1)} %activation.6.refs_0_), channel_id=1, source_target_pairs={{0,2},{1,3},{2,0},{3,1},{4,6},{5,7},{6,4},{7,5},{8,10},{9,11},{10,... | collective-permute-start | bytes 786440 | tf_op jit(solution)/shard_map/ppermute | solution.py:34
  92.0 8.0 %collective-permute-start.20 = (bf16[64,2048]{1,0:T(8,128)(2,1)S(1)}, bf16[64,2048]{1,0:T(8,128)(2,1)S(1)}, u32[]{:S(2)}, u32[]{:S(2)}) collective-permute-start(bf16[64,2048]{1,0:T(8,128)(2,1)S(1)} %activation.6.refs_0_), channel_id=1, source_target_pairs={{0,1},{1,0},{2,3},{3,2},{4,5},{5,4},{6,7},{7,6},{8,9},{9,8},{10,11... | collective-permute-start | bytes 786440 | tf_op jit(solution)/shard_map/ppermute | solution.py:39
  99.0 2.6 %collective-permute-start.21 = (bf16[64,2048]{1,0:T(8,128)(2,1)S(1)}, bf16[64,2048]{1,0:T(8,128)(2,1)S(1)}, u32[]{:S(2)}, u32[]{:S(2)}) collective-permute-start(bf16[64,2048]{1,0:T(8,128)(2,1)S(1)} %collective-permute-done.19.refs_2_), channel_id=1, source_target_pairs={{0,1},{1,0},{2,3},{3,2},{4,5},{5,4},{6,7},{7,6},{8,9},{9,8},{10,11... | collective-permute-start | bytes 786440 | tf_op jit(solution)/shard_map/ppermute | solution.py:39
  99.0 27.3 %collective-permute-start.29 = (bf16[4,64,1792]{2,1,0:T(8,128)(2,1)S(1)}, bf16[4,64,1792]{2,1,0:T(8,128)(2,1)S(1)}, u32[]{:S(2)}, u32[]{:S(2)}) collective-permute-start(bf16[4,64,1792]{2,1,0:T(8,128)(2,1)S(1)} %second_product.5), channel_id=1, source_target_pairs={{0,28},{4,0},{8,4},{12,8},{16,12},{20,16},{24,20},{28,24},{1,29},{... | collective-permute-start | bytes 2752520 | tf_op jit(solution)/shard_map/ppermute | solution.py:29
  99.8 10.1 %collective-permute-start.23 = (bf16[64,1024]{1,0:T(8,128)(2,1)S(1)}, bf16[64,1024]{1,0:T(8,128)(2,1)S(1)}, u32[]{:S(2)}, u32[]{:S(2)}) collective-permute-start(bf16[64,1024]{1,0:T(8,128)(2,1)S(1)} %get-tuple-element.97), channel_id=1, source_target_pairs={{0,1},{1,2},{2,3},{3,0},{4,5},{5,6},{6,7},{7,4},{8,9},{9,10},{10,1... | collective-permute-start | bytes 393224 | tf_op jit(solution)/shard_map/ppermute | solution.py:34
  100.0 9.9 %collective-permute-start.24 = (bf16[64,1024]{1,0:T(8,128)(2,1)S(1)}, bf16[64,1024]{1,0:T(8,128)(2,1)S(1)}, u32[]{:S(2)}, u32[]{:S(2)}) collective-permute-start(bf16[64,1024]{1,0:T(8,128)(2,1)S(1)} %get-tuple-element.98), channel_id=1, source_target_pairs={{0,2},{1,3},{2,0},{3,1},{4,6},{5,7},{6,4},{7,5},{8,10},{9,11},{10,... | collective-permute-start | bytes 393224 | tf_op jit(solution)/shard_map/ppermute | solution.py:34
  101.6 8.3 %collective-permute-start.25 = (bf16[64,1024]{1,0:T(8,128)(2,1)S(1)}, bf16[64,1024]{1,0:T(8,128)(2,1)S(1)}, u32[]{:S(2)}, u32[]{:S(2)}) collective-permute-start(bf16[64,1024]{1,0:T(8,128)(2,1)S(1)} %get-tuple-element.99), channel_id=1, source_target_pairs={{0,3},{1,0},{2,1},{3,2},{4,7},{5,4},{6,5},{7,6},{8,11},{9,8},{10,9... | collective-permute-start | bytes 393224 | tf_op jit(solution)/shard_map/ppermute | solution.py:34
  111.1 7.6 %collective-permute-start.27 = (bf16[64,2048]{1,0:T(8,128)(2,1)S(1)}, bf16[64,2048]{1,0:T(8,128)(2,1)S(1)}, u32[]{:S(2)}, u32[]{:S(2)}) collective-permute-start(bf16[64,2048]{1,0:T(8,128)(2,1)S(1)} %activation.7.refs_0_), channel_id=1, source_target_pairs={{0,2},{1,3},{2,0},{3,1},{4,6},{5,7},{6,4},{7,5},{8,10},{9,11},{10,... | collective-permute-start | bytes 786440 | tf_op jit(solution)/shard_map/ppermute | solution.py:34
  111.6 34.3 %collective-permute-start.32 = (bf16[4,64,1792]{2,1,0:T(8,128)(2,1)S(1)}, bf16[4,64,1792]{2,1,0:T(8,128)(2,1)S(1)}, u32[]{:S(2)}, u32[]{:S(2)}) collective-permute-start(bf16[4,64,1792]{2,1,0:T(8,128)(2,1)S(1)} %second_product.6), channel_id=1, source_target_pairs={{0,28},{4,0},{8,4},{12,8},{16,12},{20,16},{24,20},{28,24},{1,29},{... | collective-permute-start | bytes 2752520 | tf_op jit(solution)/shard_map/ppermute | solution.py:29
  118.6 7.6 %collective-permute-start.28 = (bf16[64,2048]{1,0:T(8,128)(2,1)S(1)}, bf16[64,2048]{1,0:T(8,128)(2,1)S(1)}, u32[]{:S(2)}, u32[]{:S(2)}) collective-permute-start(bf16[64,2048]{1,0:T(8,128)(2,1)S(1)} %collective-permute-done.27.refs_2_), channel_id=1, source_target_pairs={{0,1},{1,0},{2,3},{3,2},{4,5},{5,4},{6,7},{7,6},{8,9},{9,8},{10,11... | collective-permute-start | bytes 786440 | tf_op jit(solution)/shard_map/ppermute | solution.py:39
  118.6 7.6 %collective-permute-start.26 = (bf16[64,2048]{1,0:T(8,128)(2,1)S(1)}, bf16[64,2048]{1,0:T(8,128)(2,1)S(1)}, u32[]{:S(2)}, u32[]{:S(2)}) collective-permute-start(bf16[64,2048]{1,0:T(8,128)(2,1)S(1)} %activation.7.refs_0_), channel_id=1, source_target_pairs={{0,1},{1,0},{2,3},{3,2},{4,5},{5,4},{6,7},{7,6},{8,9},{9,8},{10,11... | collective-permute-start | bytes 786440 | tf_op jit(solution)/shard_map/ppermute | solution.py:39
  133.4 27.3 %collective-permute-start.31 = (bf16[4,48,1792]{2,1,0:T(8,128)(2,1)S(1)}, bf16[4,48,1792]{2,1,0:T(8,128)(2,1)S(1)}, u32[]{:S(2)}, u32[]{:S(2)}) collective-permute-start(bf16[4,48,1792]{2,1,0:T(8,128)(2,1)S(1)} %get-tuple-element.105), channel_id=1, source_target_pairs={{0,28},{4,0},{8,4},{12,8},{16,12},{20,16},{24,20},{28,24},{1,29},{... | collective-permute-start | bytes 2064392 | tf_op jit(solution)/shard_map/ppermute | solution.py:29
  140.7 23.8 %collective-permute-start.30 = (bf16[4,16,1792]{2,1,0:T(8,128)(2,1)S(1)}, bf16[4,16,1792]{2,1,0:T(8,128)(2,1)S(1)}, u32[]{:S(2)}, u32[]{:S(2)}) collective-permute-start(bf16[4,16,1792]{2,1,0:T(8,128)(2,1)S(1)} %get-tuple-element.102), channel_id=1, source_target_pairs={{0,28},{4,0},{8,4},{12,8},{16,12},{20,16},{24,20},{28,24},{1,29},{... | collective-permute-start | bytes 688136 | tf_op jit(solution)/shard_map/ppermute | solution.py:29
  (5 other events, 77.5 us)

commit v6 on v5

--- a/solution.py
+++ b/solution.py
@@ -7,7 +7,7 @@
 from jax.experimental.pallas import tpu as pltpu
 from jax.sharding import PartitionSpec as P
 
-CHUNKS = 4
+PARTS = (3, 5, 4, 4)
 LAST = 16
 IN_FLIGHT = 2
 NEED = {("act", 1): (2,), ("act", 2): (3,)}
@@ -17,6 +17,12 @@
 
 def params(**kwargs):
     return pltpu.CompilerParams(vmem_limit_bytes=48 * 1024 * 1024, **kwargs)
+
+
+def cut(rows):
+    if rows % 256 == 0:
+        return [rows // 16 * share for share in PARTS]
+    return [rows // 4] * 4 if rows % 64 == 0 else [rows]
 
 
 def block_of(size, most):
@@ -153,14 +159,15 @@
     )(me, rows, weight if late else in_hbm(weight))
 
 
-def activation_kernel(gate_ref, up_ref, *refs):
+def activation_kernel(start, gate_ref, up_ref, *refs):
     *part_refs, out_ref = refs
-    hidden = gate_ref.shape[1]
+    part, hidden = part_refs[0].shape
+    here = slice(start, start + part)
     hidden_grad = part_refs[0][...].astype(jnp.float32)
     for ref in part_refs[1:]:
         hidden_grad = hidden_grad + ref[...].astype(jnp.float32)
-    act_a = gate_ref[...].astype(jnp.float32)
-    act_b = up_ref[...].astype(jnp.float32)
+    act_a = gate_ref[here].astype(jnp.float32)
+    act_b = up_ref[here].astype(jnp.float32)
     sigma = 1.0 / (1.0 + jnp.exp(-act_a))
     gate_part = hidden_grad * act_b * sigma * (1.0 + act_a * (1.0 - sigma))
     up_part = hidden_grad * act_a * sigma
@@ -168,11 +175,11 @@
     out_ref[:, hidden:] = up_part.astype(out_ref.dtype)
 
 
-def activation(gate_pre, up_pre, c, partials):
+def activation(gate_pre, up_pre, start, partials):
     part, hidden = partials[0].shape
-    saved = pl.BlockSpec((part, hidden), lambda i: (c, 0))
-    return pl.pallas_call(
-        activation_kernel,
+    saved = pl.BlockSpec(gate_pre.shape, lambda i: (0, 0))
+    return pl.pallas_call(
+        functools.partial(activation_kernel, start),
         out_shape=jax.ShapeDtypeStruct((part, 2 * hidden), jnp.bfloat16),
         grid=(1,),
         in_specs=[saved, saved] + [pl.BlockSpec((part, hidden), lambda i: (0, 0))] * len(partials),
@@ -183,7 +190,7 @@
     )(in_hbm(gate_pre), in_hbm(up_pre), *partials)
 
 
-def second_kernel(n, me_ref, dense_ref, gate_ref, up_ref, router_ref, *refs):
+def second_kernel(n, start, me_ref, dense_ref, gate_ref, up_ref, router_ref, *refs):
     block_refs, out_refs, held = refs[:n], refs[n:-1], refs[-1]
     chips = n // 2
     hidden = gate_ref.shape[1]
@@ -200,7 +207,7 @@
     both = held[...].reshape(-1, 2 * hidden)
     result = contract_last(both[:, :hidden], gate_ref[...])
     result = result + contract_last(both[:, hidden:], up_ref[...])
-    dense = dense_ref[...].reshape(both.shape[0], -1)
+    dense = dense_ref[:, start : start + held.shape[1]].reshape(both.shape[0], -1)
     result = result + contract_last(dense, router_ref[...])
     result = result.astype(jnp.bfloat16).reshape(n, held.shape[1], -1)
     first = 0
@@ -210,20 +217,20 @@
         first += size
 
 
-def second_product(me, blocks, c, dense, w_gate, w_up, w_router, sizes):
+def second_product(me, blocks, start, dense, w_gate, w_up, w_router, sizes):
     n = len(blocks)
     part, both = blocks[0].shape
     width, hidden = w_gate.shape
     n_experts = w_router.shape[1]
     block = block_of(width, 256)
     return pl.pallas_call(
-        functools.partial(second_kernel, n),
+        functools.partial(second_kernel, n, start),
         out_shape=[jax.ShapeDtypeStruct((n, size, width), jnp.bfloat16) for size in sizes],
         grid_spec=pltpu.PrefetchScalarGridSpec(
             num_scalar_prefetch=1,
             grid=(width // block,),
             in_specs=[
-                pl.BlockSpec((n, part, n_experts), lambda i, me: (0, c, 0)),
+                pl.BlockSpec(dense.shape, lambda i, me: (0, 0, 0)),
                 pl.BlockSpec((block, hidden), lambda i, me: (i, 0)),
                 pl.BlockSpec((block, hidden), lambda i, me: (i, 0)),
                 pl.BlockSpec((block, n_experts), lambda i, me: (i, 0)),
@@ -255,17 +262,18 @@
     me = lax.axis_index("expert").astype(jnp.int32).reshape(1)
     tokens, width = upstream.shape[1:]
     rows = tokens // n
-    chunks = min(CHUNKS, rows // 16)
-    part = rows // chunks
+    sizes = cut(rows)
+    starts = [sum(sizes[:c]) for c in range(len(sizes))]
+    chunks = len(sizes)
     grads = upstream.reshape(n, rows, width)
     arrived, sent = [], []
     dense = routed_grad(gate_grad[0], gate_scores[0], expert_ids[0], router_weight.shape[2])
     for c in range(chunks):
         if c == 0:
-            piece = take_rows(grads, 0, part)
+            piece = take_rows(grads, 0, sizes[0])
             grads, dense = in_order(grads, dense)
         else:
-            piece = grads[:, c * part : (c + 1) * part]
+            piece = grads[:, starts[c] : starts[c] + sizes[c]]
         if c >= IN_FLIGHT:
             piece, arrived[c - IN_FLIGHT] = in_order(piece, arrived[c - IN_FLIGHT])
         arrived.append(back_one(piece))
@@ -284,7 +292,7 @@
         return [own] + [to_expert(x, j + 1) for j, x in enumerate(others)]
 
     arrived[0], dense = in_order(arrived[0], dense)
-    own = activation(gate_pre[0], up_pre[0], 0, partial_sums(0))
+    own = activation(gate_pre[0], up_pre[0], starts[0], partial_sums(0))
     for c in range(chunks):
         own = at("agy", c, own)
         near = [own] + [to_expert(own, 2 * step) for step in range(1, chips)]
@@ -297,22 +305,22 @@
         far += [to_other_core(x) for x in near[1:]]
         far[-1] = at("mm2", c, far[-1])
         blocks = [x for pair in zip(near, far) for x in pair]
-        sizes = [part]
-        if c + 1 == chunks and part > LAST:
-            sizes = [part - LAST, LAST]
+        pieces = [sizes[c]]
+        if c + 1 == chunks and sizes[c] > LAST:
+            pieces = [sizes[c] - LAST, LAST]
         result, *last = second_product(
-            me, blocks, c, dense, shared_gate[0], shared_up[0], router_weight[0], sizes
+            me, blocks, starts[c], dense, shared_gate[0], shared_up[0], router_weight[0], pieces
         )
         if c + 1 < chunks:
             partials[0], result = in_order(partials[0], result)
             partials[0] = at("act", c + 1, partials[0])
-            own = activation(gate_pre[0], up_pre[0], c + 1, partials)
+            own = activation(gate_pre[0], up_pre[0], starts[c + 1], partials)
         result = at("out", c, result)
         sent.append(back_one(result))
     out = jnp.zeros((n, rows, width), jnp.bfloat16)
     for c in range(chunks - 1):
-        out = lax.dynamic_update_slice(out, sent[c], (0, c * part, 0))
-    out = put_rows(out, sent[-1], (chunks - 1) * part)
+        out = lax.dynamic_update_slice(out, sent[c], (0, starts[c], 0))
+    out = put_rows(out, sent[-1], starts[-1])
     for piece in last:
         out = put_rows(out, back_one(piece), rows - LAST)
     return out.reshape(1, tokens, width)

time: 166 us -> 166 us (level)
  waiting for transfers between devices: 64.8 us -> 57.3 us
  starting transfers between devices: 42.4 us -> 46.4 us
  local copies, waits for them, and re-layouts: 7.4 us -> 9.32 us
    ppermute x9, waiting for transfers between devices: 43 us -> 38.5 us  [back_one(): lax.ppermute(x, 'pipe', [(i, (i - 1) % length) for i in range(length)])]
    ppermute x16, waiting for transfers between devices: 21.7 us -> 17.6 us  [to_expert(): return lax.ppermute(x, 'expert', [(i, (i + by) % n) for i in range(n)])]
    ppermute x9, starting transfers between devices: 25.8 us -> 28.8 us  [back_one(): lax.ppermute(x, 'pipe', [(i, (i - 1) % length) for i in range(length)])]
    slice x1 -> x2, local copies, waits for them, and re-layouts: 3.34 us -> 5.17 us  [shards(): piece = grads[:, starts[c]:starts[c] + sizes[c]]]
  transfers between devices with their start and end apart: 33 -> 33, of which waited for: 14 -> 15; matrix products, arithmetic and copies ran while one was open for 4% -> 6% of each run, Pallas kernels for 29% -> 30%
where the time goes in v6:
time: 166 us; the launch traced here: 165 us
  waiting for transfers between devices  57.3 us (35%)
  Pallas kernels  51.9 us (31%)
  starting transfers between devices  46.4 us (28%)
  local copies, waits for them, and re-layouts  9.32 us (6%)
    ppermute x9, waiting for transfers between devices, back_one(): lax.ppermute(x, 'pipe', [(i, (i - 1) % length) for i in range(length)])  38.5 us
    ppermute x9, starting transfers between devices, back_one(): lax.ppermute(x, 'pipe', [(i, (i - 1) % length) for i in range(length)])  28.8 us
    pallas_call x4, Pallas kernels, second_product(): pl.pallas_call(functools.partial(second_kernel, n, start), out_shape=[jax...  28.7 us
    ppermute x16, waiting for transfers between devices, to_expert(): return lax.ppermute(x, 'expert', [(i, (i + by) % n) for i in range(n)])  17.6 us
    ppermute x16, starting transfers between devices, to_expert(): return lax.ppermute(x, 'expert', [(i, (i + by) % n) for i in range(n)])  15.7 us
    pallas_call x4, Pallas kernels, first_product(): pl.pallas_call(functools.partial(first_kernel, n), out_shape=[jax.ShapeDt...  9.85 us
    pallas_call x4, Pallas kernels, activation(): pl.pallas_call(functools.partial(activation_kernel, start), out_shape=jax...  5.61 us
    slice x2, local copies, waits for them, and re-layouts, shards(): piece = grads[:, starts[c]:starts[c] + sizes[c]]  5.17 us
  transfers between devices with their start and end apart: 33, of which 15 were waited for; matrix products, arithmetic and copies ran while one was open for 6% of the time, Pallas kernels for 30%

profile of v6, /device:TPU:0, one launch (start us, length us, event | category | flops | bytes accessed | tf_op | source)
XLA Modules:
  0.0 165.1 jit_solution(16065628042254367506)
XLA Ops:
  1.1 6.0 %collective-permute-start = (bf16[4,48,1792]{2,1,0:T(8,128)(2,1)S(1)}, bf16[4,48,1792]{2,1,0:T(8,128)(2,1)S(1)}, u32[]{:S(2)}, u32[]{:S(2)}) collective-permute-start(bf16[4,48,1792]{2,1,0:T(8,128)(2,1)S(1)} %take_rows.1), channel_id=1, source_target_pairs={{0,28},{4,0},{8,4},{12,8},{16,12},{20,16},{24,20},{28,24},{1,29},{... | collective-permute-start | bytes 2064392 | tf_op jit(solution)/shard_map/ppermute | solution.py:35
  7.1 5.1 %routed_grad.1 = bf16[1024,256]{1,0:T(8,128)(2,1)} custom-call(f32[8,1024]{1,0:T(8,128)} %bitcast.50, f32[8,1024]{1,0:T(8,128)} %bitcast.51, s32[8,1024]{1,0:T(8,128)} %bitcast.52), custom_call_target="tpu_custom_call" | custom-call | tf_op jit(solution)/shard_map/routed_grad/pallas_call | solution.py:120
  12.2 2.3 %slice.11 = bf16[4,80,1792]{2,1,0:T(8,128)(2,1)} slice(bf16[4,256,1792]{2,1,0:T(8,128)(2,1)} %bitcast.40), slice={[0:4], [48:128], [0:1792]} | slice | bytes 2293760 | tf_op jit(solution)/shard_map/slice | solution.py:276
  15.1 2.8 %fusion = (bf16[4,64,1792]{2,1,0:T(8,128)(2,1)}, bf16[4,64,1792]{2,1,0:T(8,128)(2,1)}) fusion(bf16[4,256,1792]{2,1,0:T(8,128)(2,1)} %bitcast.41), kind=kLoop, calls=%fused_computation.2 | loop fusion | bytes 3670016 | tf_op jit(solution)/shard_map/slice | solution.py:276
  17.9 5.1 %collective-permute-done.rows_ref = bf16[4,48,1792]{2,1,0:T(8,128)(2,1)S(1)} collective-permute-done((bf16[4,48,1792]{2,1,0:T(8,128)(2,1)S(1)}, bf16[4,48,1792]{2,1,0:T(8,128)(2,1)S(1)}, u32[]{:S(2)}, u32[]{:S(2)}) %collective-permute-start) | collective-permute-done | bytes 688160 | tf_op jit(solution)/shard_map/ppermute | solution.py:35
  23.0 5.2 %collective-permute-start.8 = (bf16[4,64,1792]{2,1,0:T(8,128)(2,1)}, bf16[4,64,1792]{2,1,0:T(8,128)(2,1)S(1)}, u32[]{:S(2)}, u32[]{:S(2)}) collective-permute-start(bf16[4,64,1792]{2,1,0:T(8,128)(2,1)} %get-tuple-element.73), channel_id=1, source_target_pairs={{0,28},{4,0},{8,4},{12,8},{16,12},{20,16},{24,20},{28,24},{1,29},{... | collective-permute-start | bytes 2752520 | tf_op jit(solution)/shard_map/ppermute | solution.py:35
  28.2 4.1 %first_product.4 = (bf16[48,1024]{1,0:T(8,128)(2,1)S(1)}, bf16[48,1024]{1,0:T(8,128)(2,1)S(1)}, bf16[48,1024]{1,0:T(8,128)(2,1)S(1)}, bf16[48,1024]{1,0:T(8,128)(2,1)S(1)}) custom-call(s32[1]{0:T(128)} %bitcast.me_ref, bf16[4,48,1792]{2,1,0:T(8,128)(2,1)S(1)} %collective-permute-done.rows_ref, bf16[1024,1792]{1,0:T(8,128)(2,1)} %bitcast.19), custom_call_target="tpu_custom_call" | custom-call | tf_op jit(solution)/shard_map/first_product/pallas_call | solution.py:144
  32.3 1.6 collective-permute-start.3
  35.3 1.5 collective-permute-done.2.refs_1_
  42.3 5.4 %collective-permute-done.1.rows_ref = bf16[4,80,1792]{2,1,0:T(8,128)(2,1)S(1)} collective-permute-done((bf16[4,80,1792]{2,1,0:T(8,128)(2,1)}, bf16[4,80,1792]{2,1,0:T(8,128)(2,1)S(1)}, u32[]{:S(2)}, u32[]{:S(2)}) %collective-permute-start.1) | collective-permute-done | bytes 1146912 | tf_op jit(solution)/shard_map/ppermute | solution.py:35
  47.7 2.1 %first_product.5 = (bf16[80,1024]{1,0:T(8,128)(2,1)S(1)}, bf16[80,1024]{1,0:T(8,128)(2,1)S(1)}, bf16[80,1024]{1,0:T(8,128)(2,1)S(1)}, bf16[80,1024]{1,0:T(8,128)(2,1)S(1)}) custom-call(s32[1]{0:T(128)} %bitcast.me_ref, bf16[4,80,1792]{2,1,0:T(8,128)(2,1)S(1)} %collective-permute-done.1.rows_ref, bf16[1024,1792]{1,0:T(8,128)(2,1)S(1)} %bitcast.20), custom_call_target="tpu_custom_call" | custom-call | tf_op jit(solution)/shard_map/first_product/pallas_call | solution.py:144
  49.9 5.1 %collective-permute-start.15 = (bf16[4,64,1792]{2,1,0:T(8,128)(2,1)S(1)}, bf16[4,64,1792]{2,1,0:T(8,128)(2,1)S(1)}, u32[]{:S(2)}, u32[]{:S(2)}) collective-permute-start(bf16[4,64,1792]{2,1,0:T(8,128)(2,1)S(1)} %copy-done.3), channel_id=1, source_target_pairs={{0,28},{4,0},{8,4},{12,8},{16,12},{20,16},{24,20},{28,24},{1,29},{... | collective-permute-start | bytes 2752520 | tf_op jit(solution)/shard_map/ppermute | solution.py:35
  55.2 1.5 collective-permute-start.10
  58.0 7.2 %second_product.4 = bf16[4,48,1792]{2,1,0:T(8,128)(2,1)S(1)} custom-call(s32[1]{0:T(128)} %bitcast.me_ref, bf16[4,256,256]{2,1,0:T(8,128)(2,1)S(1)} %bitcast.27, bf16[1792,1024]{1,0:T(8,128)(2,1)} %bitcast.31, bf16[1792,1024]{1,0:T(8,128)(2,1)} %bitcast.35, bf16[1792,256]{1,0:T(8,128)(2,1)S(1)} %bitcast.23, bf16[48,2048]{1,0:T(8,128)(2,1)S(1)} %activation.4.refs_0_, ...), custom_call_target="tpu_custom_call" | custom-call | tf_op jit(solution)/shard_map/second_product/pallas_call | solution.py:226
  65.2 2.1 %collective-permute-done.8.rows_ref = bf16[4,64,1792]{2,1,0:T(8,128)(2,1)S(1)} collective-permute-done((bf16[4,64,1792]{2,1,0:T(8,128)(2,1)}, bf16[4,64,1792]{2,1,0:T(8,128)(2,1)S(1)}, u32[]{:S(2)}, u32[]{:S(2)}) %collective-permute-start.8) | collective-permute-done | bytes 917536 | tf_op jit(solution)/shard_map/ppermute | solution.py:35
  68.8 1.6 collective-permute-start.12
  70.4 1.9 %first_product.6 = (bf16[64,1024]{1,0:T(8,128)(2,1)S(1)}, bf16[64,1024]{1,0:T(8,128)(2,1)S(1)}, bf16[64,1024]{1,0:T(8,128)(2,1)S(1)}, bf16[64,1024]{1,0:T(8,128)(2,1)S(1)}) custom-call(s32[1]{0:T(128)} %bitcast.me_ref, bf16[4,64,1792]{2,1,0:T(8,128)(2,1)S(1)} %collective-permute-done.8.rows_ref, bf16[1024,1792]{1,0:T(8,128)(2,1)S(1)} %bitcast.21), custom_call_target="tpu_custom_call" | custom-call | tf_op jit(solution)/shard_map/first_product/pallas_call | solution.py:144
  72.3 4.0 %collective-permute-done.12.refs_2_ = bf16[80,2048]{1,0:T(8,128)(2,1)S(1)} collective-permute-done((bf16[80,2048]{1,0:T(8,128)(2,1)S(1)}, bf16[80,2048]{1,0:T(8,128)(2,1)S(1)}, u32[]{:S(2)}, u32[]{:S(2)}) %collective-permute-start.12) | collective-permute-done | bytes 327712 | tf_op jit(solution)/shard_map/ppermute | solution.py:40
  76.8 1.5 collective-permute-start.17
  79.3 5.1 %collective-permute-start.22 = (bf16[4,48,1792]{2,1,0:T(8,128)(2,1)S(1)}, bf16[4,48,1792]{2,1,0:T(8,128)(2,1)S(1)}, u32[]{:S(2)}, u32[]{:S(2)}) collective-permute-start(bf16[4,48,1792]{2,1,0:T(8,128)(2,1)S(1)} %second_product.4), channel_id=1, source_target_pairs={{0,28},{4,0},{8,4},{12,8},{16,12},{20,16},{24,20},{28,24},{1,29},{... | collective-permute-start | bytes 2064392 | tf_op jit(solution)/shard_map/ppermute | solution.py:35
  84.4 7.4 %second_product.5 = bf16[4,80,1792]{2,1,0:T(8,128)(2,1)S(1)} custom-call(s32[1]{0:T(128)} %bitcast.me_ref, bf16[4,256,256]{2,1,0:T(8,128)(2,1)S(1)} %bitcast.28, bf16[1792,1024]{1,0:T(8,128)(2,1)} %bitcast.32, bf16[1792,1024]{1,0:T(8,128)(2,1)} %bitcast.36, bf16[1792,256]{1,0:T(8,128)(2,1)S(1)} %bitcast.24, bf16[80,2048]{1,0:T(8,128)(2,1)S(1)} %activation.5.refs_0_, ...), custom_call_target="tpu_custom_call" | custom-call | tf_op jit(solution)/shard_map/second_product/pallas_call | solution.py:226
  95.1 1.8 %first_product.7 = (bf16[64,1024]{1,0:T(8,128)(2,1)S(1)}, bf16[64,1024]{1,0:T(8,128)(2,1)S(1)}, bf16[64,1024]{1,0:T(8,128)(2,1)S(1)}, bf16[64,1024]{1,0:T(8,128)(2,1)S(1)}) custom-call(s32[1]{0:T(128)} %bitcast.me_ref, bf16[4,64,1792]{2,1,0:T(8,128)(2,1)S(1)} %collective-permute-done.15.rows_ref, bf16[1024,1792]{1,0:T(8,128)(2,1)S(1)} %bitcast.22), custom_call_target="tpu_custom_call" | custom-call | tf_op jit(solution)/shard_map/first_product/pallas_call | solution.py:144
  96.9 3.8 %collective-permute-done.19.refs_2_ = bf16[64,2048]{1,0:T(8,128)(2,1)S(1)} collective-permute-done((bf16[64,2048]{1,0:T(8,128)(2,1)S(1)}, bf16[64,2048]{1,0:T(8,128)(2,1)S(1)}, u32[]{:S(2)}, u32[]{:S(2)}) %collective-permute-start.19) | collective-permute-done | bytes 262176 | tf_op jit(solution)/shard_map/ppermute | solution.py:40
  103.1 7.0 %second_product.6 = bf16[4,64,1792]{2,1,0:T(8,128)(2,1)S(1)} custom-call(s32[1]{0:T(128)} %bitcast.me_ref, bf16[4,256,256]{2,1,0:T(8,128)(2,1)S(1)} %bitcast.29, bf16[1792,1024]{1,0:T(8,128)(2,1)} %bitcast.33, bf16[1792,1024]{1,0:T(8,128)(2,1)} %bitcast.37, bf16[1792,256]{1,0:T(8,128)(2,1)S(1)} %bitcast.25, bf16[64,2048]{1,0:T(8,128)(2,1)S(1)} %activation.6.refs_0_, ...), custom_call_target="tpu_custom_call" | custom-call | tf_op jit(solution)/shard_map/second_product/pallas_call | solution.py:226
  113.1 6.5 %collective-permute-done.27.refs_2_ = bf16[64,2048]{1,0:T(8,128)(2,1)S(1)} collective-permute-done((bf16[64,2048]{1,0:T(8,128)(2,1)S(1)}, bf16[64,2048]{1,0:T(8,128)(2,1)S(1)}, u32[]{:S(2)}, u32[]{:S(2)}) %collective-permute-start.27) | collective-permute-done | bytes 262176 | tf_op jit(solution)/shard_map/ppermute | solution.py:40
  121.1 5.1 %collective-permute-done.29 = bf16[4,80,1792]{2,1,0:T(8,128)(2,1)S(1)} collective-permute-done((bf16[4,80,1792]{2,1,0:T(8,128)(2,1)S(1)}, bf16[4,80,1792]{2,1,0:T(8,128)(2,1)S(1)}, u32[]{:S(2)}, u32[]{:S(2)}) %collective-permute-start.29) | collective-permute-done | bytes 1146912 | tf_op jit(solution)/shard_map/ppermute | solution.py:35
  126.2 7.1 %second_product.7 = (bf16[4,48,1792]{2,1,0:T(8,128)(2,1)S(1)}, bf16[4,16,1792]{2,1,0:T(8,128)(2,1)S(1)}) custom-call(s32[1]{0:T(128)} %bitcast.me_ref, bf16[4,256,256]{2,1,0:T(8,128)(2,1)S(1)} %bitcast.30, bf16[1792,1024]{1,0:T(8,128)(2,1)} %bitcast.34, bf16[1792,1024]{1,0:T(8,128)(2,1)} %bitcast.38, bf16[1792,256]{1,0:T(8,128)(2,1)S(1)} %bitcast.26, ...), custom_call_target="tpu_custom_call" | custom-call | tf_op jit(solution)/shard_map/second_product/pallas_call | solution.py:226
  133.3 5.2 %collective-permute-start.31 = (bf16[4,48,1792]{2,1,0:T(8,128)(2,1)S(1)}, bf16[4,48,1792]{2,1,0:T(8,128)(2,1)S(1)}, u32[]{:S(2)}, u32[]{:S(2)}) collective-permute-start(bf16[4,48,1792]{2,1,0:T(8,128)(2,1)S(1)} %get-tuple-element.105), channel_id=1, source_target_pairs={{0,28},{4,0},{8,4},{12,8},{16,12},{20,16},{24,20},{28,24},{1,29},{... | collective-permute-start | bytes 2064392 | tf_op jit(solution)/shard_map/ppermute | solution.py:35
  138.5 2.1 %dynamic_update_slice.9 = bf16[4,256,1792]{2,1,0:T(8,128)(2,1)} pad(bf16[4,48,1792]{2,1,0:T(8,128)(2,1)S(1)} %collective-permute-done.22, bf16[]{:T(256)} %constant.1.clone.1), padding=0_0x0_208x0_0 | pad | bytes 4358146 | tf_op jit(solution)/shard_map/dynamic_update_slice | solution.py:322
  141.7 4.2 %collective-permute-done.32 = bf16[4,64,1792]{2,1,0:T(8,128)(2,1)S(1)} collective-permute-done((bf16[4,64,1792]{2,1,0:T(8,128)(2,1)S(1)}, bf16[4,64,1792]{2,1,0:T(8,128)(2,1)S(1)}, u32[]{:S(2)}, u32[]{:S(2)}) %collective-permute-start.32) | collective-permute-done | bytes 917536 | tf_op jit(solution)/shard_map/ppermute | solution.py:35
  146.9 13.8 %collective-permute-done.31.source = bf16[4,48,1792]{2,1,0:T(8,128)(2,1)S(1)} collective-permute-done((bf16[4,48,1792]{2,1,0:T(8,128)(2,1)S(1)}, bf16[4,48,1792]{2,1,0:T(8,128)(2,1)S(1)}, u32[]{:S(2)}, u32[]{:S(2)}) %collective-permute-start.31) | collective-permute-done | bytes 688160 | tf_op jit(solution)/shard_map/ppermute | solution.py:35
  161.5 2.9 %collective-permute-done.30.source = bf16[4,16,1792]{2,1,0:T(8,128)(2,1)S(1)} collective-permute-done((bf16[4,16,1792]{2,1,0:T(8,128)(2,1)S(1)}, bf16[4,16,1792]{2,1,0:T(8,128)(2,1)S(1)}, u32[]{:S(2)}, u32[]{:S(2)}) %collective-permute-start.30) | collective-permute-done | bytes 229408 | tf_op jit(solution)/shard_map/ppermute | solution.py:35
  (63 shorter events, 26.8 us)
Async XLA Ops:
  1.1 21.9 %collective-permute-start = (bf16[4,48,1792]{2,1,0:T(8,128)(2,1)S(1)}, bf16[4,48,1792]{2,1,0:T(8,128)(2,1)S(1)}, u32[]{:S(2)}, u32[]{:S(2)}) collective-permute-start(bf16[4,48,1792]{2,1,0:T(8,128)(2,1)S(1)} %take_rows.1), channel_id=1, source_target_pairs={{0,28},{4,0},{8,4},{12,8},{16,12},{20,16},{24,20},{28,24},{1,29},{... | collective-permute-start | bytes 2064392 | tf_op jit(solution)/shard_map/ppermute | solution.py:35
  14.5 33.1 %collective-permute-start.1 = (bf16[4,80,1792]{2,1,0:T(8,128)(2,1)}, bf16[4,80,1792]{2,1,0:T(8,128)(2,1)S(1)}, u32[]{:S(2)}, u32[]{:S(2)}) collective-permute-start(bf16[4,80,1792]{2,1,0:T(8,128)(2,1)} %slice.11), channel_id=1, source_target_pairs={{0,28},{4,0},{8,4},{12,8},{16,12},{20,16},{24,20},{28,24},{1,29},{... | collective-permute-start | bytes 3440648 | tf_op jit(solution)/shard_map/ppermute | solution.py:35
  23.0 44.3 %collective-permute-start.8 = (bf16[4,64,1792]{2,1,0:T(8,128)(2,1)}, bf16[4,64,1792]{2,1,0:T(8,128)(2,1)S(1)}, u32[]{:S(2)}, u32[]{:S(2)}) collective-permute-start(bf16[4,64,1792]{2,1,0:T(8,128)(2,1)} %get-tuple-element.73), channel_id=1, source_target_pairs={{0,28},{4,0},{8,4},{12,8},{16,12},{20,16},{24,20},{28,24},{1,29},{... | collective-permute-start | bytes 2752520 | tf_op jit(solution)/shard_map/ppermute | solution.py:35
  32.3 4.5 %collective-permute-start.2 = (bf16[48,1024]{1,0:T(8,128)(2,1)S(1)}, bf16[48,1024]{1,0:T(8,128)(2,1)S(1)}, u32[]{:S(2)}, u32[]{:S(2)}) collective-permute-start(bf16[48,1024]{1,0:T(8,128)(2,1)S(1)} %get-tuple-element.65), channel_id=1, source_target_pairs={{0,1},{1,2},{2,3},{3,0},{4,5},{5,6},{6,7},{7,4},{8,9},{9,10},{10,1... | collective-permute-start | bytes 294920 | tf_op jit(solution)/shard_map/ppermute | solution.py:40
  32.3 5.7 %collective-permute-start.3 = (bf16[48,1024]{1,0:T(8,128)(2,1)S(1)}, bf16[48,1024]{1,0:T(8,128)(2,1)S(1)}, u32[]{:S(2)}, u32[]{:S(2)}) collective-permute-start(bf16[48,1024]{1,0:T(8,128)(2,1)S(1)} %get-tuple-element.66), channel_id=1, source_target_pairs={{0,2},{1,3},{2,0},{3,1},{4,6},{5,7},{6,4},{7,5},{8,10},{9,11},{10,... | collective-permute-start | bytes 294920 | tf_op jit(solution)/shard_map/ppermute | solution.py:40
  33.9 4.6 %collective-permute-start.4 = (bf16[48,1024]{1,0:T(8,128)(2,1)S(1)}, bf16[48,1024]{1,0:T(8,128)(2,1)S(1)}, u32[]{:S(2)}, u32[]{:S(2)}) collective-permute-start(bf16[48,1024]{1,0:T(8,128)(2,1)S(1)} %get-tuple-element.67), channel_id=1, source_target_pairs={{0,3},{1,0},{2,1},{3,2},{4,7},{5,4},{6,5},{7,6},{8,11},{9,8},{10,9... | collective-permute-start | bytes 294920 | tf_op jit(solution)/shard_map/ppermute | solution.py:40
  39.9 9.9 %collective-permute-start.5 = (bf16[48,2048]{1,0:T(8,128)(2,1)S(1)}, bf16[48,2048]{1,0:T(8,128)(2,1)S(1)}, u32[]{:S(2)}, u32[]{:S(2)}) collective-permute-start(bf16[48,2048]{1,0:T(8,128)(2,1)S(1)} %activation.4.refs_0_), channel_id=1, source_target_pairs={{0,2},{1,3},{2,0},{3,1},{4,6},{5,7},{6,4},{7,5},{8,10},{9,11},{10,... | collective-permute-start | bytes 589832 | tf_op jit(solution)/shard_map/ppermute | solution.py:40
  41.0 14.2 %collective-permute-start.6 = (bf16[48,2048]{1,0:T(8,128)(2,1)S(1)}, bf16[48,2048]{1,0:T(8,128)(2,1)S(1)}, u32[]{:S(2)}, u32[]{:S(2)}) collective-permute-start(bf16[48,2048]{1,0:T(8,128)(2,1)S(1)} %activation.4.refs_0_), channel_id=1, source_target_pairs={{0,1},{1,0},{2,3},{3,2},{4,5},{5,4},{6,7},{7,6},{8,9},{9,8},{10,11... | collective-permute-start | bytes 589832 | tf_op jit(solution)/shard_map/ppermute | solution.py:45
  49.8 6.9 %collective-permute-start.7 = (bf16[48,2048]{1,0:T(8,128)(2,1)S(1)}, bf16[48,2048]{1,0:T(8,128)(2,1)S(1)}, u32[]{:S(2)}, u32[]{:S(2)}) collective-permute-start(bf16[48,2048]{1,0:T(8,128)(2,1)S(1)} %collective-permute-done.5.refs_2_), channel_id=1, source_target_pairs={{0,1},{1,0},{2,3},{3,2},{4,5},{5,4},{6,7},{7,6},{8,9},{9,8},{10,11... | collective-permute-start | bytes 589832 | tf_op jit(solution)/shard_map/ppermute | solution.py:45
  49.9 41.9 %collective-permute-start.15 = (bf16[4,64,1792]{2,1,0:T(8,128)(2,1)S(1)}, bf16[4,64,1792]{2,1,0:T(8,128)(2,1)S(1)}, u32[]{:S(2)}, u32[]{:S(2)}) collective-permute-start(bf16[4,64,1792]{2,1,0:T(8,128)(2,1)S(1)} %copy-done.3), channel_id=1, source_target_pairs={{0,28},{4,0},{8,4},{12,8},{16,12},{20,16},{24,20},{28,24},{1,29},{... | collective-permute-start | bytes 2752520 | tf_op jit(solution)/shard_map/ppermute | solution.py:35
  55.0 12.3 %collective-permute-start.9 = (bf16[80,1024]{1,0:T(8,128)(2,1)S(1)}, bf16[80,1024]{1,0:T(8,128)(2,1)S(1)}, u32[]{:S(2)}, u32[]{:S(2)}) collective-permute-start(bf16[80,1024]{1,0:T(8,128)(2,1)S(1)} %get-tuple-element.76), channel_id=1, source_target_pairs={{0,1},{1,2},{2,3},{3,0},{4,5},{5,6},{6,7},{7,4},{8,9},{9,10},{10,1... | collective-permute-start | bytes 491528 | tf_op jit(solution)/shard_map/ppermute | solution.py:40
  55.2 12.2 %collective-permute-start.10 = (bf16[80,1024]{1,0:T(8,128)(2,1)S(1)}, bf16[80,1024]{1,0:T(8,128)(2,1)S(1)}, u32[]{:S(2)}, u32[]{:S(2)}) collective-permute-start(bf16[80,1024]{1,0:T(8,128)(2,1)S(1)} %get-tuple-element.77), channel_id=1, source_target_pairs={{0,2},{1,3},{2,0},{3,1},{4,6},{5,7},{6,4},{7,5},{8,10},{9,11},{10,... | collective-permute-start | bytes 491528 | tf_op jit(solution)/shard_map/ppermute | solution.py:40
  56.7 10.7 %collective-permute-start.11 = (bf16[80,1024]{1,0:T(8,128)(2,1)S(1)}, bf16[80,1024]{1,0:T(8,128)(2,1)S(1)}, u32[]{:S(2)}, u32[]{:S(2)}) collective-permute-start(bf16[80,1024]{1,0:T(8,128)(2,1)S(1)} %get-tuple-element.78), channel_id=1, source_target_pairs={{0,3},{1,0},{2,1},{3,2},{4,7},{5,4},{6,5},{7,6},{8,11},{9,8},{10,9... | collective-permute-start | bytes 491528 | tf_op jit(solution)/shard_map/ppermute | solution.py:40
  68.8 7.5 %collective-permute-start.12 = (bf16[80,2048]{1,0:T(8,128)(2,1)S(1)}, bf16[80,2048]{1,0:T(8,128)(2,1)S(1)}, u32[]{:S(2)}, u32[]{:S(2)}) collective-permute-start(bf16[80,2048]{1,0:T(8,128)(2,1)S(1)} %activation.5.refs_0_), channel_id=1, source_target_pairs={{0,2},{1,3},{2,0},{3,1},{4,6},{5,7},{6,4},{7,5},{8,10},{9,11},{10,... | collective-permute-start | bytes 983048 | tf_op jit(solution)/shard_map/ppermute | solution.py:40
  70.4 7.9 %collective-permute-start.13 = (bf16[80,2048]{1,0:T(8,128)(2,1)S(1)}, bf16[80,2048]{1,0:T(8,128)(2,1)S(1)}, u32[]{:S(2)}, u32[]{:S(2)}) collective-permute-start(bf16[80,2048]{1,0:T(8,128)(2,1)S(1)} %activation.5.refs_0_), channel_id=1, source_target_pairs={{0,1},{1,0},{2,3},{3,2},{4,5},{5,4},{6,7},{7,6},{8,9},{9,8},{10,11... | collective-permute-start | bytes 983048 | tf_op jit(solution)/shard_map/ppermute | solution.py:45
  76.3 3.0 %collective-permute-start.14 = (bf16[80,2048]{1,0:T(8,128)(2,1)S(1)}, bf16[80,2048]{1,0:T(8,128)(2,1)S(1)}, u32[]{:S(2)}, u32[]{:S(2)}) collective-permute-start(bf16[80,2048]{1,0:T(8,128)(2,1)S(1)} %collective-permute-done.12.refs_2_), channel_id=1, source_target_pairs={{0,1},{1,0},{2,3},{3,2},{4,5},{5,4},{6,7},{7,6},{8,9},{9,8},{10,11... | collective-permute-start | bytes 983048 | tf_op jit(solution)/shard_map/ppermute | solution.py:45
  76.3 15.5 %collective-permute-start.16 = (bf16[64,1024]{1,0:T(8,128)(2,1)S(1)}, bf16[64,1024]{1,0:T(8,128)(2,1)S(1)}, u32[]{:S(2)}, u32[]{:S(2)}) collective-permute-start(bf16[64,1024]{1,0:T(8,128)(2,1)S(1)} %get-tuple-element.87), channel_id=1, source_target_pairs={{0,1},{1,2},{2,3},{3,0},{4,5},{5,6},{6,7},{7,4},{8,9},{9,10},{10,1... | collective-permute-start | bytes 393224 | tf_op jit(solution)/shard_map/ppermute | solution.py:40
  76.8 15.0 %collective-permute-start.17 = (bf16[64,1024]{1,0:T(8,128)(2,1)S(1)}, bf16[64,1024]{1,0:T(8,128)(2,1)S(1)}, u32[]{:S(2)}, u32[]{:S(2)}) collective-permute-start(bf16[64,1024]{1,0:T(8,128)(2,1)S(1)} %get-tuple-element.88), channel_id=1, source_target_pairs={{0,2},{1,3},{2,0},{3,1},{4,6},{5,7},{6,4},{7,5},{8,10},{9,11},{10,... | collective-permute-start | bytes 393224 | tf_op jit(solution)/shard_map/ppermute | solution.py:40
  78.3 13.5 %collective-permute-start.18 = (bf16[64,1024]{1,0:T(8,128)(2,1)S(1)}, bf16[64,1024]{1,0:T(8,128)(2,1)S(1)}, u32[]{:S(2)}, u32[]{:S(2)}) collective-permute-start(bf16[64,1024]{1,0:T(8,128)(2,1)S(1)} %get-tuple-element.89), channel_id=1, source_target_pairs={{0,3},{1,0},{2,1},{3,2},{4,7},{5,4},{6,5},{7,6},{8,11},{9,8},{10,9... | collective-permute-start | bytes 393224 | tf_op jit(solution)/shard_map/ppermute | solution.py:40
  79.3 30.9 %collective-permute-start.22 = (bf16[4,48,1792]{2,1,0:T(8,128)(2,1)S(1)}, bf16[4,48,1792]{2,1,0:T(8,128)(2,1)S(1)}, u32[]{:S(2)}, u32[]{:S(2)}) collective-permute-start(bf16[4,48,1792]{2,1,0:T(8,128)(2,1)S(1)} %second_product.4), channel_id=1, source_target_pairs={{0,28},{4,0},{8,4},{12,8},{16,12},{20,16},{24,20},{28,24},{1,29},{... | collective-permute-start | bytes 2064392 | tf_op jit(solution)/shard_map/ppermute | solution.py:35
  93.2 7.5 %collective-permute-start.19 = (bf16[64,2048]{1,0:T(8,128)(2,1)S(1)}, bf16[64,2048]{1,0:T(8,128)(2,1)S(1)}, u32[]{:S(2)}, u32[]{:S(2)}) collective-permute-start(bf16[64,2048]{1,0:T(8,128)(2,1)S(1)} %activation.6.refs_0_), channel_id=1, source_target_pairs={{0,2},{1,3},{2,0},{3,1},{4,6},{5,7},{6,4},{7,5},{8,10},{9,11},{10,... | collective-permute-start | bytes 786440 | tf_op jit(solution)/shard_map/ppermute | solution.py:40
  93.8 32.4 %collective-permute-start.29 = (bf16[4,80,1792]{2,1,0:T(8,128)(2,1)S(1)}, bf16[4,80,1792]{2,1,0:T(8,128)(2,1)S(1)}, u32[]{:S(2)}, u32[]{:S(2)}) collective-permute-start(bf16[4,80,1792]{2,1,0:T(8,128)(2,1)S(1)} %second_product.5), channel_id=1, source_target_pairs={{0,28},{4,0},{8,4},{12,8},{16,12},{20,16},{24,20},{28,24},{1,29},{... | collective-permute-start | bytes 3440648 | tf_op jit(solution)/shard_map/ppermute | solution.py:35
  95.1 6.2 %collective-permute-start.20 = (bf16[64,2048]{1,0:T(8,128)(2,1)S(1)}, bf16[64,2048]{1,0:T(8,128)(2,1)S(1)}, u32[]{:S(2)}, u32[]{:S(2)}) collective-permute-start(bf16[64,2048]{1,0:T(8,128)(2,1)S(1)} %activation.6.refs_0_), channel_id=1, source_target_pairs={{0,1},{1,0},{2,3},{3,2},{4,5},{5,4},{6,7},{7,6},{8,9},{9,8},{10,11... | collective-permute-start | bytes 786440 | tf_op jit(solution)/shard_map/ppermute | solution.py:45
  100.7 1.5 collective-permute-start.21
  100.8 9.4 %collective-permute-start.23 = (bf16[64,1024]{1,0:T(8,128)(2,1)S(1)}, bf16[64,1024]{1,0:T(8,128)(2,1)S(1)}, u32[]{:S(2)}, u32[]{:S(2)}) collective-permute-start(bf16[64,1024]{1,0:T(8,128)(2,1)S(1)} %get-tuple-element.97), channel_id=1, source_target_pairs={{0,1},{1,2},{2,3},{3,0},{4,5},{5,6},{6,7},{7,4},{8,9},{9,10},{10,1... | collective-permute-start | bytes 393224 | tf_op jit(solution)/shard_map/ppermute | solution.py:40
  101.3 8.9 %collective-permute-start.24 = (bf16[64,1024]{1,0:T(8,128)(2,1)S(1)}, bf16[64,1024]{1,0:T(8,128)(2,1)S(1)}, u32[]{:S(2)}, u32[]{:S(2)}) collective-permute-start(bf16[64,1024]{1,0:T(8,128)(2,1)S(1)} %get-tuple-element.98), channel_id=1, source_target_pairs={{0,2},{1,3},{2,0},{3,1},{4,6},{5,7},{6,4},{7,5},{8,10},{9,11},{10,... | collective-permute-start | bytes 393224 | tf_op jit(solution)/shard_map/ppermute | solution.py:40
  102.3 7.9 %collective-permute-start.25 = (bf16[64,1024]{1,0:T(8,128)(2,1)S(1)}, bf16[64,1024]{1,0:T(8,128)(2,1)S(1)}, u32[]{:S(2)}, u32[]{:S(2)}) collective-permute-start(bf16[64,1024]{1,0:T(8,128)(2,1)S(1)} %get-tuple-element.99), channel_id=1, source_target_pairs={{0,3},{1,0},{2,1},{3,2},{4,7},{5,4},{6,5},{7,6},{8,11},{9,8},{10,9... | collective-permute-start | bytes 393224 | tf_op jit(solution)/shard_map/ppermute | solution.py:40
  111.6 7.9 %collective-permute-start.27 = (bf16[64,2048]{1,0:T(8,128)(2,1)S(1)}, bf16[64,2048]{1,0:T(8,128)(2,1)S(1)}, u32[]{:S(2)}, u32[]{:S(2)}) collective-permute-start(bf16[64,2048]{1,0:T(8,128)(2,1)S(1)} %activation.7.refs_0_), channel_id=1, source_target_pairs={{0,2},{1,3},{2,0},{3,1},{4,6},{5,7},{6,4},{7,5},{8,10},{9,11},{10,... | collective-permute-start | bytes 786440 | tf_op jit(solution)/shard_map/ppermute | solution.py:40
  112.8 33.1 %collective-permute-start.32 = (bf16[4,64,1792]{2,1,0:T(8,128)(2,1)S(1)}, bf16[4,64,1792]{2,1,0:T(8,128)(2,1)S(1)}, u32[]{:S(2)}, u32[]{:S(2)}) collective-permute-start(bf16[4,64,1792]{2,1,0:T(8,128)(2,1)S(1)} %second_product.6), channel_id=1, source_target_pairs={{0,28},{4,0},{8,4},{12,8},{16,12},{20,16},{24,20},{28,24},{1,29},{... | collective-permute-start | bytes 2752520 | tf_op jit(solution)/shard_map/ppermute | solution.py:35
  119.6 6.6 %collective-permute-start.26 = (bf16[64,2048]{1,0:T(8,128)(2,1)S(1)}, bf16[64,2048]{1,0:T(8,128)(2,1)S(1)}, u32[]{:S(2)}, u32[]{:S(2)}) collective-permute-start(bf16[64,2048]{1,0:T(8,128)(2,1)S(1)} %activation.7.refs_0_), channel_id=1, source_target_pairs={{0,1},{1,0},{2,3},{3,2},{4,5},{5,4},{6,7},{7,6},{8,9},{9,8},{10,11... | collective-permute-start | bytes 786440 | tf_op jit(solution)/shard_map/ppermute | solution.py:45
  133.3 27.3 %collective-permute-start.31 = (bf16[4,48,1792]{2,1,0:T(8,128)(2,1)S(1)}, bf16[4,48,1792]{2,1,0:T(8,128)(2,1)S(1)}, u32[]{:S(2)}, u32[]{:S(2)}) collective-permute-start(bf16[4,48,1792]{2,1,0:T(8,128)(2,1)S(1)} %get-tuple-element.105), channel_id=1, source_target_pairs={{0,28},{4,0},{8,4},{12,8},{16,12},{20,16},{24,20},{28,24},{1,29},{... | collective-permute-start | bytes 2064392 | tf_op jit(solution)/shard_map/ppermute | solution.py:35
  140.6 23.8 %collective-permute-start.30 = (bf16[4,16,1792]{2,1,0:T(8,128)(2,1)S(1)}, bf16[4,16,1792]{2,1,0:T(8,128)(2,1)S(1)}, u32[]{:S(2)}, u32[]{:S(2)}) collective-permute-start(bf16[4,16,1792]{2,1,0:T(8,128)(2,1)S(1)} %get-tuple-element.102), channel_id=1, source_target_pairs={{0,28},{4,0},{8,4},{12,8},{16,12},{20,16},{24,20},{28,24},{1,29},{... | collective-permute-start | bytes 688136 | tf_op jit(solution)/shard_map/ppermute | solution.py:35
  (5 other events, 90.2 us)

commit v7 on v5

--- a/solution.py
+++ b/solution.py
@@ -60,12 +60,20 @@
     copy.wait()
 
 
-def put_kernel(start, source, old, target, sem):
+def put_kernel(start, on, source, old, target, sem):
     del old
-    here = pl.ds(start, source.shape[1])
-    copy = pltpu.make_async_copy(source, target.at[:, here], sem)
-    copy.start()
-    copy.wait()
+
+    def put():
+        here = pl.ds(start, source.shape[1])
+        copy = pltpu.make_async_copy(source, target.at[:, here], sem)
+        copy.start()
+        copy.wait()
+
+    is_last = lax.axis_index("pipe") == lax.axis_size("pipe") - 1
+    if on == "all":
+        put()
+    else:
+        pl.when(is_last if on == "last" else jnp.logical_not(is_last))(put)
 
 
 def take_rows(array, start, size):
@@ -81,9 +89,9 @@
     )(in_hbm(array))
 
 
-def put_rows(out, piece, start):
-    return pl.pallas_call(
-        functools.partial(put_kernel, start),
+def put_rows(out, piece, start, on="all"):
+    return pl.pallas_call(
+        functools.partial(put_kernel, start, on),
         out_shape=jax.ShapeDtypeStruct(out.shape, out.dtype),
         in_specs=[pl.BlockSpec(memory_space=pltpu.VMEM), pl.BlockSpec(memory_space=pltpu.HBM)],
         out_specs=pl.BlockSpec(memory_space=pltpu.HBM),
@@ -313,8 +321,12 @@
     for c in range(chunks - 1):
         out = lax.dynamic_update_slice(out, sent[c], (0, c * part, 0))
     out = put_rows(out, sent[-1], (chunks - 1) * part)
+    length = lax.axis_size("pipe")
     for piece in last:
-        out = put_rows(out, back_one(piece), rows - LAST)
+        near = lax.ppermute(piece, "pipe", [(i, i - 1) for i in range(1, length)])
+        far = lax.ppermute(piece, "pipe", [(0, length - 1)])
+        out = put_rows(out, near, rows - LAST, "others")
+        out = put_rows(out, far, rows - LAST, "last")
     return out.reshape(1, tokens, width)
 
 

time: 166 us -> 165 us (level)
  waiting for transfers between devices: 64.8 us -> 61.2 us
  starting transfers between devices: 42.4 us -> 45.3 us
    ppermute x9 -> x8, waiting for transfers between devices: 43 us -> 37.2 us  [back_one(): lax.ppermute(x, 'pipe', [(i, (i - 1) % length) for i in range(length)])]
    ppermute x0 -> x2, starting transfers between devices: none -> 3.93 us  [the longest x1 2.65 us: shards(): far = lax.ppermute(piece, 'pipe', [(0, length - 1)])]
    ppermute x0 -> x2, waiting for transfers between devices: none -> 2.2 us  [the longest x1 1.59 us: shards(): far = lax.ppermute(piece, 'pipe', [(0, length - 1)])]
    ppermute x9 -> x8, starting transfers between devices: 25.8 us -> 25.8 us  [back_one(): lax.ppermute(x, 'pipe', [(i, (i - 1) % length) for i in range(length)])]
  transfers between devices with their start and end apart: 33 -> 34, of which waited for: 14 -> 15; matrix products, arithmetic and copies ran while one was open for 4% -> 4% of each run, Pallas kernels for 29% -> 30%
where the time goes in v7:
time: 165 us; the launch traced here: 164 us
  waiting for transfers between devices  61.2 us (37%)
  Pallas kernels  50.3 us (30%)
  starting transfers between devices  45.3 us (27%)
  local copies, waits for them, and re-layouts  7.4 us (4%)
    ppermute x8, waiting for transfers between devices, back_one(): lax.ppermute(x, 'pipe', [(i, (i - 1) % length) for i in range(length)])  37.2 us
    pallas_call x4, Pallas kernels, second_product(): pl.pallas_call(functools.partial(second_kernel, n), out_shape=[jax.ShapeD...  28.3 us
    ppermute x8, starting transfers between devices, back_one(): lax.ppermute(x, 'pipe', [(i, (i - 1) % length) for i in range(length)])  25.8 us
    ppermute x16, waiting for transfers between devices, to_expert(): return lax.ppermute(x, 'expert', [(i, (i + by) % n) for i in range(n)])  21.8 us
    ppermute x16, starting transfers between devices, to_expert(): return lax.ppermute(x, 'expert', [(i, (i + by) % n) for i in range(n)])  14.2 us
    pallas_call x4, Pallas kernels, first_product(): pl.pallas_call(functools.partial(first_kernel, n), out_shape=[jax.ShapeDt...  9.48 us
    pallas_call x1, Pallas kernels, routed_grad(): pl.pallas_call(routed_kernel, out_shape=jax.ShapeDtypeStruct((tokens, n_e...  5.05 us
    pallas_call x4, Pallas kernels, activation(): pl.pallas_call(activation_kernel, out_shape=jax.ShapeDtypeStruct((part, 2...  4.69 us
  transfers between devices with their start and end apart: 34, of which 15 were waited for; matrix products, arithmetic and copies ran while one was open for 4% of the time, Pallas kernels for 30%

profile of v7, /device:TPU:0, one launch (start us, length us, event | category | flops | bytes accessed | tf_op | source)
XLA Modules:
  0.0 164.5 jit_solution(8182607316500352260)
XLA Ops:
  1.2 6.0 %collective-permute-start = (bf16[4,64,1792]{2,1,0:T(8,128)(2,1)S(1)}, bf16[4,64,1792]{2,1,0:T(8,128)(2,1)S(1)}, u32[]{:S(2)}, u32[]{:S(2)}) collective-permute-start(bf16[4,64,1792]{2,1,0:T(8,128)(2,1)S(1)} %take_rows.1), channel_id=1, source_target_pairs={{0,28},{4,0},{8,4},{12,8},{16,12},{20,16},{24,20},{28,24},{1,29},{... | collective-permute-start | bytes 2752520 | tf_op jit(solution)/shard_map/ppermute | solution.py:29
  7.2 5.0 %routed_grad.1 = bf16[1024,256]{1,0:T(8,128)(2,1)} custom-call(f32[8,1024]{1,0:T(8,128)} %bitcast.49, f32[8,1024]{1,0:T(8,128)} %bitcast.50, s32[8,1024]{1,0:T(8,128)} %bitcast.51), custom_call_target="tpu_custom_call" | custom-call | tf_op jit(solution)/shard_map/routed_grad/pallas_call | solution.py:122
  12.3 3.3 %fusion = (bf16[4,64,1792]{2,1,0:T(8,128)(2,1)}, bf16[4,64,1792]{2,1,0:T(8,128)(2,1)}, bf16[4,64,1792]{2,1,0:T(8,128)(2,1)}) fusion(bf16[4,256,1792]{2,1,0:T(8,128)(2,1)} %bitcast.40), kind=kLoop, calls=%fused_computation.2 | loop fusion | bytes 5505024 | tf_op jit(solution)/shard_map/slice | solution.py:276
  16.1 11.8 %collective-permute-done.rows_ref = bf16[4,64,1792]{2,1,0:T(8,128)(2,1)S(1)} collective-permute-done((bf16[4,64,1792]{2,1,0:T(8,128)(2,1)S(1)}, bf16[4,64,1792]{2,1,0:T(8,128)(2,1)S(1)}, u32[]{:S(2)}, u32[]{:S(2)}) %collective-permute-start) | collective-permute-done | bytes 917536 | tf_op jit(solution)/shard_map/ppermute | solution.py:29
  28.0 5.2 %collective-permute-start.8 = (bf16[4,64,1792]{2,1,0:T(8,128)(2,1)}, bf16[4,64,1792]{2,1,0:T(8,128)(2,1)S(1)}, u32[]{:S(2)}, u32[]{:S(2)}) collective-permute-start(bf16[4,64,1792]{2,1,0:T(8,128)(2,1)} %get-tuple-element.73), channel_id=1, source_target_pairs={{0,28},{4,0},{8,4},{12,8},{16,12},{20,16},{24,20},{28,24},{1,29},{... | collective-permute-start | bytes 2752520 | tf_op jit(solution)/shard_map/ppermute | solution.py:29
  33.2 4.0 %first_product.4 = (bf16[64,1024]{1,0:T(8,128)(2,1)S(1)}, bf16[64,1024]{1,0:T(8,128)(2,1)S(1)}, bf16[64,1024]{1,0:T(8,128)(2,1)S(1)}, bf16[64,1024]{1,0:T(8,128)(2,1)S(1)}) custom-call(s32[1]{0:T(128)} %bitcast.me_ref, bf16[4,64,1792]{2,1,0:T(8,128)(2,1)S(1)} %collective-permute-done.rows_ref, bf16[1024,1792]{1,0:T(8,128)(2,1)} %bitcast.19), custom_call_target="tpu_custom_call" | custom-call | tf_op jit(solution)/shard_map/first_product/pallas_call | solution.py:146
  37.2 1.6 collective-permute-start.3
  38.8 1.4 collective-permute-start.4
  40.2 2.2 %collective-permute-done.2.refs_1_ = bf16[64,1024]{1,0:T(8,128)(2,1)S(1)} collective-permute-done((bf16[64,1024]{1,0:T(8,128)(2,1)S(1)}, bf16[64,1024]{1,0:T(8,128)(2,1)S(1)}, u32[]{:S(2)}, u32[]{:S(2)}) %collective-permute-start.2) | collective-permute-done | bytes 131104 | tf_op jit(solution)/shard_map/ppermute | solution.py:34
  48.4 1.8 %first_product.5 = (bf16[64,1024]{1,0:T(8,128)(2,1)S(1)}, bf16[64,1024]{1,0:T(8,128)(2,1)S(1)}, bf16[64,1024]{1,0:T(8,128)(2,1)S(1)}, bf16[64,1024]{1,0:T(8,128)(2,1)S(1)}) custom-call(s32[1]{0:T(128)} %bitcast.me_ref, bf16[4,64,1792]{2,1,0:T(8,128)(2,1)S(1)} %collective-permute-done.1.rows_ref, bf16[1024,1792]{1,0:T(8,128)(2,1)S(1)} %bitcast.20), custom_call_target="tpu_custom_call" | custom-call | tf_op jit(solution)/shard_map/first_product/pallas_call | solution.py:146
  50.3 4.9 %collective-permute-done.5.refs_2_ = bf16[64,2048]{1,0:T(8,128)(2,1)S(1)} collective-permute-done((bf16[64,2048]{1,0:T(8,128)(2,1)S(1)}, bf16[64,2048]{1,0:T(8,128)(2,1)S(1)}, u32[]{:S(2)}, u32[]{:S(2)}) %collective-permute-start.5) | collective-permute-done | bytes 262176 | tf_op jit(solution)/shard_map/ppermute | solution.py:34
  57.3 7.1 %second_product.4 = bf16[4,64,1792]{2,1,0:T(8,128)(2,1)S(1)} custom-call(s32[1]{0:T(128)} %bitcast.me_ref, bf16[4,256,256]{2,1,0:T(8,128)(2,1)S(1)} %bitcast.27, bf16[1792,1024]{1,0:T(8,128)(2,1)} %bitcast.31, bf16[1792,1024]{1,0:T(8,128)(2,1)} %bitcast.35, bf16[1792,256]{1,0:T(8,128)(2,1)S(1)} %bitcast.23, bf16[64,2048]{1,0:T(8,128)(2,1)S(1)} %activation.4.refs_0_, ...), custom_call_target="tpu_custom_call" | custom-call | tf_op jit(solution)/shard_map/second_product/pallas_call | solution.py:227
  64.4 3.0 %collective-permute-done.8.rows_ref = bf16[4,64,1792]{2,1,0:T(8,128)(2,1)S(1)} collective-permute-done((bf16[4,64,1792]{2,1,0:T(8,128)(2,1)}, bf16[4,64,1792]{2,1,0:T(8,128)(2,1)S(1)}, u32[]{:S(2)}, u32[]{:S(2)}) %collective-permute-start.8) | collective-permute-done | bytes 917536 | tf_op jit(solution)/shard_map/ppermute | solution.py:29
  68.6 1.6 collective-permute-start.12
  70.2 1.8 %first_product.6 = (bf16[64,1024]{1,0:T(8,128)(2,1)S(1)}, bf16[64,1024]{1,0:T(8,128)(2,1)S(1)}, bf16[64,1024]{1,0:T(8,128)(2,1)S(1)}, bf16[64,1024]{1,0:T(8,128)(2,1)S(1)}) custom-call(s32[1]{0:T(128)} %bitcast.me_ref, bf16[4,64,1792]{2,1,0:T(8,128)(2,1)S(1)} %collective-permute-done.8.rows_ref, bf16[1024,1792]{1,0:T(8,128)(2,1)S(1)} %bitcast.21), custom_call_target="tpu_custom_call" | custom-call | tf_op jit(solution)/shard_map/first_product/pallas_call | solution.py:146
  72.0 3.0 %collective-permute-done.12.refs_2_ = bf16[64,2048]{1,0:T(8,128)(2,1)S(1)} collective-permute-done((bf16[64,2048]{1,0:T(8,128)(2,1)S(1)}, bf16[64,2048]{1,0:T(8,128)(2,1)S(1)}, u32[]{:S(2)}, u32[]{:S(2)}) %collective-permute-start.12) | collective-permute-done | bytes 262176 | tf_op jit(solution)/shard_map/ppermute | solution.py:34
  75.0 5.1 %collective-permute-start.22 = (bf16[4,64,1792]{2,1,0:T(8,128)(2,1)S(1)}, bf16[4,64,1792]{2,1,0:T(8,128)(2,1)S(1)}, u32[]{:S(2)}, u32[]{:S(2)}) collective-permute-start(bf16[4,64,1792]{2,1,0:T(8,128)(2,1)S(1)} %second_product.4), channel_id=1, source_target_pairs={{0,28},{4,0},{8,4},{12,8},{16,12},{20,16},{24,20},{28,24},{1,29},{... | collective-permute-start | bytes 2752520 | tf_op jit(solution)/shard_map/ppermute | solution.py:29
  80.3 1.6 collective-permute-start.17
  83.1 7.1 %second_product.5 = bf16[4,64,1792]{2,1,0:T(8,128)(2,1)S(1)} custom-call(s32[1]{0:T(128)} %bitcast.me_ref, bf16[4,256,256]{2,1,0:T(8,128)(2,1)S(1)} %bitcast.28, bf16[1792,1024]{1,0:T(8,128)(2,1)} %bitcast.32, bf16[1792,1024]{1,0:T(8,128)(2,1)} %bitcast.36, bf16[1792,256]{1,0:T(8,128)(2,1)S(1)} %bitcast.24, bf16[64,2048]{1,0:T(8,128)(2,1)S(1)} %activation.5.refs_0_, ...), custom_call_target="tpu_custom_call" | custom-call | tf_op jit(solution)/shard_map/second_product/pallas_call | solution.py:227
  92.0 1.8 %first_product.7 = (bf16[64,1024]{1,0:T(8,128)(2,1)S(1)}, bf16[64,1024]{1,0:T(8,128)(2,1)S(1)}, bf16[64,1024]{1,0:T(8,128)(2,1)S(1)}, bf16[64,1024]{1,0:T(8,128)(2,1)S(1)}) custom-call(s32[1]{0:T(128)} %bitcast.me_ref, bf16[4,64,1792]{2,1,0:T(8,128)(2,1)S(1)} %collective-permute-done.15.rows_ref, bf16[1024,1792]{1,0:T(8,128)(2,1)S(1)} %bitcast.22), custom_call_target="tpu_custom_call" | custom-call | tf_op jit(solution)/shard_map/first_product/pallas_call | solution.py:146
  93.8 5.2 %collective-permute-done.19.refs_2_ = bf16[64,2048]{1,0:T(8,128)(2,1)S(1)} collective-permute-done((bf16[64,2048]{1,0:T(8,128)(2,1)S(1)}, bf16[64,2048]{1,0:T(8,128)(2,1)S(1)}, u32[]{:S(2)}, u32[]{:S(2)}) %collective-permute-start.19) | collective-permute-done | bytes 262176 | tf_op jit(solution)/shard_map/ppermute | solution.py:34
  100.0 1.6 collective-permute-start.24
  102.8 7.1 %second_product.6 = bf16[4,64,1792]{2,1,0:T(8,128)(2,1)S(1)} custom-call(s32[1]{0:T(128)} %bitcast.me_ref, bf16[4,256,256]{2,1,0:T(8,128)(2,1)S(1)} %bitcast.29, bf16[1792,1024]{1,0:T(8,128)(2,1)} %bitcast.33, bf16[1792,1024]{1,0:T(8,128)(2,1)} %bitcast.37, bf16[1792,256]{1,0:T(8,128)(2,1)S(1)} %bitcast.25, bf16[64,2048]{1,0:T(8,128)(2,1)S(1)} %activation.6.refs_0_, ...), custom_call_target="tpu_custom_call" | custom-call | tf_op jit(solution)/shard_map/second_product/pallas_call | solution.py:227
  111.6 2.9 %collective-permute-start.33 = (bf16[4,64,1792]{2,1,0:T(8,128)(2,1)S(1)}, bf16[4,64,1792]{2,1,0:T(8,128)(2,1)S(1)}, u32[]{:S(2)}, u32[]{:S(2)}) collective-permute-start(bf16[4,64,1792]{2,1,0:T(8,128)(2,1)S(1)} %second_product.6), channel_id=1, source_target_pairs={{0,28},{4,0},{8,4},{12,8},{16,12},{20,16},{24,20},{28,24},{1,29},{... | collective-permute-start | bytes 2752520 | tf_op jit(solution)/shard_map/ppermute | solution.py:29
  114.6 4.1 %collective-permute-done.27.refs_2_ = bf16[64,2048]{1,0:T(8,128)(2,1)S(1)} collective-permute-done((bf16[64,2048]{1,0:T(8,128)(2,1)S(1)}, bf16[64,2048]{1,0:T(8,128)(2,1)S(1)}, u32[]{:S(2)}, u32[]{:S(2)}) %collective-permute-start.27) | collective-permute-done | bytes 262176 | tf_op jit(solution)/shard_map/ppermute | solution.py:34
  119.2 7.1 %collective-permute-done.29 = bf16[4,64,1792]{2,1,0:T(8,128)(2,1)S(1)} collective-permute-done((bf16[4,64,1792]{2,1,0:T(8,128)(2,1)S(1)}, bf16[4,64,1792]{2,1,0:T(8,128)(2,1)S(1)}, u32[]{:S(2)}, u32[]{:S(2)}) %collective-permute-start.29) | collective-permute-done | bytes 917536 | tf_op jit(solution)/shard_map/ppermute | solution.py:29
  126.3 7.1 %second_product.7 = (bf16[4,48,1792]{2,1,0:T(8,128)(2,1)S(1)}, bf16[4,16,1792]{2,1,0:T(8,128)(2,1)S(1)}) custom-call(s32[1]{0:T(128)} %bitcast.me_ref, bf16[4,256,256]{2,1,0:T(8,128)(2,1)S(1)} %bitcast.30, bf16[1792,1024]{1,0:T(8,128)(2,1)} %bitcast.34, bf16[1792,1024]{1,0:T(8,128)(2,1)} %bitcast.38, bf16[1792,256]{1,0:T(8,128)(2,1)S(1)} %bitcast.26, ...), custom_call_target="tpu_custom_call" | custom-call | tf_op jit(solution)/shard_map/second_product/pallas_call | solution.py:227
  133.4 5.2 %collective-permute-start.32 = (bf16[4,48,1792]{2,1,0:T(8,128)(2,1)S(1)}, bf16[4,48,1792]{2,1,0:T(8,128)(2,1)S(1)}, u32[]{:S(2)}, u32[]{:S(2)}) collective-permute-start(bf16[4,48,1792]{2,1,0:T(8,128)(2,1)S(1)} %get-tuple-element.105), channel_id=1, source_target_pairs={{0,28},{4,0},{8,4},{12,8},{16,12},{20,16},{24,20},{28,24},{1,29},{... | collective-permute-start | bytes 2064392 | tf_op jit(solution)/shard_map/ppermute | solution.py:29
  138.6 2.1 %dynamic_update_slice.9 = bf16[4,256,1792]{2,1,0:T(8,128)(2,1)} pad(bf16[4,64,1792]{2,1,0:T(8,128)(2,1)S(1)} %collective-permute-done.22, bf16[]{:T(256)} %constant.1.clone.1), padding=0_0x0_192x0_0 | pad | bytes 4587522 | tf_op jit(solution)/shard_map/dynamic_update_slice | solution.py:322
  142.0 2.7 %collective-permute-start.30 = (bf16[4,16,1792]{2,1,0:T(8,128)(2,1)S(1)}, bf16[4,16,1792]{2,1,0:T(8,128)(2,1)S(1)}, u32[]{:S(2)}, u32[]{:S(2)}) collective-permute-start(bf16[4,16,1792]{2,1,0:T(8,128)(2,1)S(1)} %get-tuple-element.102), channel_id=1, source_target_pairs={{0,28},{1,29},{2,30},{3,31}} | collective-permute-start | bytes 688136 | tf_op jit(solution)/shard_map/ppermute | solution.py:327
  146.9 13.8 %collective-permute-done.32.source = bf16[4,48,1792]{2,1,0:T(8,128)(2,1)S(1)} collective-permute-done((bf16[4,48,1792]{2,1,0:T(8,128)(2,1)S(1)}, bf16[4,48,1792]{2,1,0:T(8,128)(2,1)S(1)}, u32[]{:S(2)}, u32[]{:S(2)}) %collective-permute-start.32) | collective-permute-done | bytes 688160 | tf_op jit(solution)/shard_map/ppermute | solution.py:29
  162.9 1.6 collective-permute-done.30.source
  (65 shorter events, 24.5 us)
Async XLA Ops:
  1.2 26.8 %collective-permute-start = (bf16[4,64,1792]{2,1,0:T(8,128)(2,1)S(1)}, bf16[4,64,1792]{2,1,0:T(8,128)(2,1)S(1)}, u32[]{:S(2)}, u32[]{:S(2)}) collective-permute-start(bf16[4,64,1792]{2,1,0:T(8,128)(2,1)S(1)} %take_rows.1), channel_id=1, source_target_pairs={{0,28},{4,0},{8,4},{12,8},{16,12},{20,16},{24,20},{28,24},{1,29},{... | collective-permute-start | bytes 2752520 | tf_op jit(solution)/shard_map/ppermute | solution.py:29
  15.6 32.1 %collective-permute-start.1 = (bf16[4,64,1792]{2,1,0:T(8,128)(2,1)}, bf16[4,64,1792]{2,1,0:T(8,128)(2,1)S(1)}, u32[]{:S(2)}, u32[]{:S(2)}) collective-permute-start(bf16[4,64,1792]{2,1,0:T(8,128)(2,1)} %get-tuple-element.111), channel_id=1, source_target_pairs={{0,28},{4,0},{8,4},{12,8},{16,12},{20,16},{24,20},{28,24},{1,29},{... | collective-permute-start | bytes 2752520 | tf_op jit(solution)/shard_map/ppermute | solution.py:29
  28.0 39.4 %collective-permute-start.8 = (bf16[4,64,1792]{2,1,0:T(8,128)(2,1)}, bf16[4,64,1792]{2,1,0:T(8,128)(2,1)S(1)}, u32[]{:S(2)}, u32[]{:S(2)}) collective-permute-start(bf16[4,64,1792]{2,1,0:T(8,128)(2,1)} %get-tuple-element.73), channel_id=1, source_target_pairs={{0,28},{4,0},{8,4},{12,8},{16,12},{20,16},{24,20},{28,24},{1,29},{... | collective-permute-start | bytes 2752520 | tf_op jit(solution)/shard_map/ppermute | solution.py:29
  37.2 5.2 %collective-permute-start.2 = (bf16[64,1024]{1,0:T(8,128)(2,1)S(1)}, bf16[64,1024]{1,0:T(8,128)(2,1)S(1)}, u32[]{:S(2)}, u32[]{:S(2)}) collective-permute-start(bf16[64,1024]{1,0:T(8,128)(2,1)S(1)} %get-tuple-element.65), channel_id=1, source_target_pairs={{0,1},{1,2},{2,3},{3,0},{4,5},{5,6},{6,7},{7,4},{8,9},{9,10},{10,1... | collective-permute-start | bytes 393224 | tf_op jit(solution)/shard_map/ppermute | solution.py:34
  37.2 6.4 %collective-permute-start.3 = (bf16[64,1024]{1,0:T(8,128)(2,1)S(1)}, bf16[64,1024]{1,0:T(8,128)(2,1)S(1)}, u32[]{:S(2)}, u32[]{:S(2)}) collective-permute-start(bf16[64,1024]{1,0:T(8,128)(2,1)S(1)} %get-tuple-element.66), channel_id=1, source_target_pairs={{0,2},{1,3},{2,0},{3,1},{4,6},{5,7},{6,4},{7,5},{8,10},{9,11},{10,... | collective-permute-start | bytes 393224 | tf_op jit(solution)/shard_map/ppermute | solution.py:34
  38.8 6.0 %collective-permute-start.4 = (bf16[64,1024]{1,0:T(8,128)(2,1)S(1)}, bf16[64,1024]{1,0:T(8,128)(2,1)S(1)}, u32[]{:S(2)}, u32[]{:S(2)}) collective-permute-start(bf16[64,1024]{1,0:T(8,128)(2,1)S(1)} %get-tuple-element.67), channel_id=1, source_target_pairs={{0,3},{1,0},{2,1},{3,2},{4,7},{5,4},{6,5},{7,6},{8,11},{9,8},{10,9... | collective-permute-start | bytes 393224 | tf_op jit(solution)/shard_map/ppermute | solution.py:34
  46.0 9.1 %collective-permute-start.5 = (bf16[64,2048]{1,0:T(8,128)(2,1)S(1)}, bf16[64,2048]{1,0:T(8,128)(2,1)S(1)}, u32[]{:S(2)}, u32[]{:S(2)}) collective-permute-start(bf16[64,2048]{1,0:T(8,128)(2,1)S(1)} %activation.4.refs_0_), channel_id=1, source_target_pairs={{0,2},{1,3},{2,0},{3,1},{4,6},{5,7},{6,4},{7,5},{8,10},{9,11},{10,... | collective-permute-start | bytes 786440 | tf_op jit(solution)/shard_map/ppermute | solution.py:34
  47.7 9.0 %collective-permute-start.6 = (bf16[64,2048]{1,0:T(8,128)(2,1)S(1)}, bf16[64,2048]{1,0:T(8,128)(2,1)S(1)}, u32[]{:S(2)}, u32[]{:S(2)}) collective-permute-start(bf16[64,2048]{1,0:T(8,128)(2,1)S(1)} %activation.4.refs_0_), channel_id=1, source_target_pairs={{0,1},{1,0},{2,3},{3,2},{4,5},{5,4},{6,7},{7,6},{8,9},{9,8},{10,11... | collective-permute-start | bytes 786440 | tf_op jit(solution)/shard_map/ppermute | solution.py:39
  55.4 34.8 %collective-permute-start.15 = (bf16[4,64,1792]{2,1,0:T(8,128)(2,1)S(1)}, bf16[4,64,1792]{2,1,0:T(8,128)(2,1)S(1)}, u32[]{:S(2)}, u32[]{:S(2)}) collective-permute-start(bf16[4,64,1792]{2,1,0:T(8,128)(2,1)S(1)} %copy-done.3), channel_id=1, source_target_pairs={{0,28},{4,0},{8,4},{12,8},{16,12},{20,16},{24,20},{28,24},{1,29},{... | collective-permute-start | bytes 2752520 | tf_op jit(solution)/shard_map/ppermute | solution.py:29
  55.4 12.0 %collective-permute-start.10 = (bf16[64,1024]{1,0:T(8,128)(2,1)S(1)}, bf16[64,1024]{1,0:T(8,128)(2,1)S(1)}, u32[]{:S(2)}, u32[]{:S(2)}) collective-permute-start(bf16[64,1024]{1,0:T(8,128)(2,1)S(1)} %get-tuple-element.77), channel_id=1, source_target_pairs={{0,2},{1,3},{2,0},{3,1},{4,6},{5,7},{6,4},{7,5},{8,10},{9,11},{10,... | collective-permute-start | bytes 393224 | tf_op jit(solution)/shard_map/ppermute | solution.py:34
  56.8 10.6 %collective-permute-start.11 = (bf16[64,1024]{1,0:T(8,128)(2,1)S(1)}, bf16[64,1024]{1,0:T(8,128)(2,1)S(1)}, u32[]{:S(2)}, u32[]{:S(2)}) collective-permute-start(bf16[64,1024]{1,0:T(8,128)(2,1)S(1)} %get-tuple-element.78), channel_id=1, source_target_pairs={{0,3},{1,0},{2,1},{3,2},{4,7},{5,4},{6,5},{7,6},{8,11},{9,8},{10,9... | collective-permute-start | bytes 393224 | tf_op jit(solution)/shard_map/ppermute | solution.py:34
  57.0 10.4 %collective-permute-start.9 = (bf16[64,1024]{1,0:T(8,128)(2,1)S(1)}, bf16[64,1024]{1,0:T(8,128)(2,1)S(1)}, u32[]{:S(2)}, u32[]{:S(2)}) collective-permute-start(bf16[64,1024]{1,0:T(8,128)(2,1)S(1)} %get-tuple-element.76), channel_id=1, source_target_pairs={{0,1},{1,2},{2,3},{3,0},{4,5},{5,6},{6,7},{7,4},{8,9},{9,10},{10,1... | collective-permute-start | bytes 393224 | tf_op jit(solution)/shard_map/ppermute | solution.py:34
  68.6 6.4 %collective-permute-start.12 = (bf16[64,2048]{1,0:T(8,128)(2,1)S(1)}, bf16[64,2048]{1,0:T(8,128)(2,1)S(1)}, u32[]{:S(2)}, u32[]{:S(2)}) collective-permute-start(bf16[64,2048]{1,0:T(8,128)(2,1)S(1)} %activation.5.refs_0_), channel_id=1, source_target_pairs={{0,2},{1,3},{2,0},{3,1},{4,6},{5,7},{6,4},{7,5},{8,10},{9,11},{10,... | collective-permute-start | bytes 786440 | tf_op jit(solution)/shard_map/ppermute | solution.py:34
  70.2 10.2 %collective-permute-start.13 = (bf16[64,2048]{1,0:T(8,128)(2,1)S(1)}, bf16[64,2048]{1,0:T(8,128)(2,1)S(1)}, u32[]{:S(2)}, u32[]{:S(2)}) collective-permute-start(bf16[64,2048]{1,0:T(8,128)(2,1)S(1)} %activation.5.refs_0_), channel_id=1, source_target_pairs={{0,1},{1,0},{2,3},{3,2},{4,5},{5,4},{6,7},{7,6},{8,9},{9,8},{10,11... | collective-permute-start | bytes 786440 | tf_op jit(solution)/shard_map/ppermute | solution.py:39
  75.0 6.9 %collective-permute-start.14 = (bf16[64,2048]{1,0:T(8,128)(2,1)S(1)}, bf16[64,2048]{1,0:T(8,128)(2,1)S(1)}, u32[]{:S(2)}, u32[]{:S(2)}) collective-permute-start(bf16[64,2048]{1,0:T(8,128)(2,1)S(1)} %collective-permute-done.12.refs_2_), channel_id=1, source_target_pairs={{0,1},{1,0},{2,3},{3,2},{4,5},{5,4},{6,7},{7,6},{8,9},{9,8},{10,11... | collective-permute-start | bytes 786440 | tf_op jit(solution)/shard_map/ppermute | solution.py:39
  75.0 34.8 %collective-permute-start.22 = (bf16[4,64,1792]{2,1,0:T(8,128)(2,1)S(1)}, bf16[4,64,1792]{2,1,0:T(8,128)(2,1)S(1)}, u32[]{:S(2)}, u32[]{:S(2)}) collective-permute-start(bf16[4,64,1792]{2,1,0:T(8,128)(2,1)S(1)} %second_product.4), channel_id=1, source_target_pairs={{0,28},{4,0},{8,4},{12,8},{16,12},{20,16},{24,20},{28,24},{1,29},{... | collective-permute-start | bytes 2752520 | tf_op jit(solution)/shard_map/ppermute | solution.py:29
  80.1 10.1 %collective-permute-start.16 = (bf16[64,1024]{1,0:T(8,128)(2,1)S(1)}, bf16[64,1024]{1,0:T(8,128)(2,1)S(1)}, u32[]{:S(2)}, u32[]{:S(2)}) collective-permute-start(bf16[64,1024]{1,0:T(8,128)(2,1)S(1)} %get-tuple-element.87), channel_id=1, source_target_pairs={{0,1},{1,2},{2,3},{3,0},{4,5},{5,6},{6,7},{7,4},{8,9},{9,10},{10,1... | collective-permute-start | bytes 393224 | tf_op jit(solution)/shard_map/ppermute | solution.py:34
  80.3 9.9 %collective-permute-start.17 = (bf16[64,1024]{1,0:T(8,128)(2,1)S(1)}, bf16[64,1024]{1,0:T(8,128)(2,1)S(1)}, u32[]{:S(2)}, u32[]{:S(2)}) collective-permute-start(bf16[64,1024]{1,0:T(8,128)(2,1)S(1)} %get-tuple-element.88), channel_id=1, source_target_pairs={{0,2},{1,3},{2,0},{3,1},{4,6},{5,7},{6,4},{7,5},{8,10},{9,11},{10,... | collective-permute-start | bytes 393224 | tf_op jit(solution)/shard_map/ppermute | solution.py:34
  81.9 8.3 %collective-permute-start.18 = (bf16[64,1024]{1,0:T(8,128)(2,1)S(1)}, bf16[64,1024]{1,0:T(8,128)(2,1)S(1)}, u32[]{:S(2)}, u32[]{:S(2)}) collective-permute-start(bf16[64,1024]{1,0:T(8,128)(2,1)S(1)} %get-tuple-element.89), channel_id=1, source_target_pairs={{0,3},{1,0},{2,1},{3,2},{4,7},{5,4},{6,5},{7,6},{8,11},{9,8},{10,9... | collective-permute-start | bytes 393224 | tf_op jit(solution)/shard_map/ppermute | solution.py:34
  91.4 7.6 %collective-permute-start.19 = (bf16[64,2048]{1,0:T(8,128)(2,1)S(1)}, bf16[64,2048]{1,0:T(8,128)(2,1)S(1)}, u32[]{:S(2)}, u32[]{:S(2)}) collective-permute-start(bf16[64,2048]{1,0:T(8,128)(2,1)S(1)} %activation.6.refs_0_), channel_id=1, source_target_pairs={{0,2},{1,3},{2,0},{3,1},{4,6},{5,7},{6,4},{7,5},{8,10},{9,11},{10,... | collective-permute-start | bytes 786440 | tf_op jit(solution)/shard_map/ppermute | solution.py:34
  92.0 8.0 %collective-permute-start.20 = (bf16[64,2048]{1,0:T(8,128)(2,1)S(1)}, bf16[64,2048]{1,0:T(8,128)(2,1)S(1)}, u32[]{:S(2)}, u32[]{:S(2)}) collective-permute-start(bf16[64,2048]{1,0:T(8,128)(2,1)S(1)} %activation.6.refs_0_), channel_id=1, source_target_pairs={{0,1},{1,0},{2,3},{3,2},{4,5},{5,4},{6,7},{7,6},{8,9},{9,8},{10,11... | collective-permute-start | bytes 786440 | tf_op jit(solution)/shard_map/ppermute | solution.py:39
  99.0 27.3 %collective-permute-start.29 = (bf16[4,64,1792]{2,1,0:T(8,128)(2,1)S(1)}, bf16[4,64,1792]{2,1,0:T(8,128)(2,1)S(1)}, u32[]{:S(2)}, u32[]{:S(2)}) collective-permute-start(bf16[4,64,1792]{2,1,0:T(8,128)(2,1)S(1)} %second_product.5), channel_id=1, source_target_pairs={{0,28},{4,0},{8,4},{12,8},{16,12},{20,16},{24,20},{28,24},{1,29},{... | collective-permute-start | bytes 2752520 | tf_op jit(solution)/shard_map/ppermute | solution.py:29
  99.8 10.1 %collective-permute-start.23 = (bf16[64,1024]{1,0:T(8,128)(2,1)S(1)}, bf16[64,1024]{1,0:T(8,128)(2,1)S(1)}, u32[]{:S(2)}, u32[]{:S(2)}) collective-permute-start(bf16[64,1024]{1,0:T(8,128)(2,1)S(1)} %get-tuple-element.97), channel_id=1, source_target_pairs={{0,1},{1,2},{2,3},{3,0},{4,5},{5,6},{6,7},{7,4},{8,9},{9,10},{10,1... | collective-permute-start | bytes 393224 | tf_op jit(solution)/shard_map/ppermute | solution.py:34
  100.0 9.9 %collective-permute-start.24 = (bf16[64,1024]{1,0:T(8,128)(2,1)S(1)}, bf16[64,1024]{1,0:T(8,128)(2,1)S(1)}, u32[]{:S(2)}, u32[]{:S(2)}) collective-permute-start(bf16[64,1024]{1,0:T(8,128)(2,1)S(1)} %get-tuple-element.98), channel_id=1, source_target_pairs={{0,2},{1,3},{2,0},{3,1},{4,6},{5,7},{6,4},{7,5},{8,10},{9,11},{10,... | collective-permute-start | bytes 393224 | tf_op jit(solution)/shard_map/ppermute | solution.py:34
  101.6 8.3 %collective-permute-start.25 = (bf16[64,1024]{1,0:T(8,128)(2,1)S(1)}, bf16[64,1024]{1,0:T(8,128)(2,1)S(1)}, u32[]{:S(2)}, u32[]{:S(2)}) collective-permute-start(bf16[64,1024]{1,0:T(8,128)(2,1)S(1)} %get-tuple-element.99), channel_id=1, source_target_pairs={{0,3},{1,0},{2,1},{3,2},{4,7},{5,4},{6,5},{7,6},{8,11},{9,8},{10,9... | collective-permute-start | bytes 393224 | tf_op jit(solution)/shard_map/ppermute | solution.py:34
  111.1 7.6 %collective-permute-start.27 = (bf16[64,2048]{1,0:T(8,128)(2,1)S(1)}, bf16[64,2048]{1,0:T(8,128)(2,1)S(1)}, u32[]{:S(2)}, u32[]{:S(2)}) collective-permute-start(bf16[64,2048]{1,0:T(8,128)(2,1)S(1)} %activation.7.refs_0_), channel_id=1, source_target_pairs={{0,2},{1,3},{2,0},{3,1},{4,6},{5,7},{6,4},{7,5},{8,10},{9,11},{10,... | collective-permute-start | bytes 786440 | tf_op jit(solution)/shard_map/ppermute | solution.py:34
  111.6 34.3 %collective-permute-start.33 = (bf16[4,64,1792]{2,1,0:T(8,128)(2,1)S(1)}, bf16[4,64,1792]{2,1,0:T(8,128)(2,1)S(1)}, u32[]{:S(2)}, u32[]{:S(2)}) collective-permute-start(bf16[4,64,1792]{2,1,0:T(8,128)(2,1)S(1)} %second_product.6), channel_id=1, source_target_pairs={{0,28},{4,0},{8,4},{12,8},{16,12},{20,16},{24,20},{28,24},{1,29},{... | collective-permute-start | bytes 2752520 | tf_op jit(solution)/shard_map/ppermute | solution.py:29
  118.6 7.6 %collective-permute-start.28 = (bf16[64,2048]{1,0:T(8,128)(2,1)S(1)}, bf16[64,2048]{1,0:T(8,128)(2,1)S(1)}, u32[]{:S(2)}, u32[]{:S(2)}) collective-permute-start(bf16[64,2048]{1,0:T(8,128)(2,1)S(1)} %collective-permute-done.27.refs_2_), channel_id=1, source_target_pairs={{0,1},{1,0},{2,3},{3,2},{4,5},{5,4},{6,7},{7,6},{8,9},{9,8},{10,11... | collective-permute-start | bytes 786440 | tf_op jit(solution)/shard_map/ppermute | solution.py:39
  118.6 7.6 %collective-permute-start.26 = (bf16[64,2048]{1,0:T(8,128)(2,1)S(1)}, bf16[64,2048]{1,0:T(8,128)(2,1)S(1)}, u32[]{:S(2)}, u32[]{:S(2)}) collective-permute-start(bf16[64,2048]{1,0:T(8,128)(2,1)S(1)} %activation.7.refs_0_), channel_id=1, source_target_pairs={{0,1},{1,0},{2,3},{3,2},{4,5},{5,4},{6,7},{7,6},{8,9},{9,8},{10,11... | collective-permute-start | bytes 786440 | tf_op jit(solution)/shard_map/ppermute | solution.py:39
  133.4 27.3 %collective-permute-start.32 = (bf16[4,48,1792]{2,1,0:T(8,128)(2,1)S(1)}, bf16[4,48,1792]{2,1,0:T(8,128)(2,1)S(1)}, u32[]{:S(2)}, u32[]{:S(2)}) collective-permute-start(bf16[4,48,1792]{2,1,0:T(8,128)(2,1)S(1)} %get-tuple-element.105), channel_id=1, source_target_pairs={{0,28},{4,0},{8,4},{12,8},{16,12},{20,16},{24,20},{28,24},{1,29},{... | collective-permute-start | bytes 2064392 | tf_op jit(solution)/shard_map/ppermute | solution.py:29
  140.7 21.5 %collective-permute-start.31 = (bf16[4,16,1792]{2,1,0:T(8,128)(2,1)S(1)}, bf16[4,16,1792]{2,1,0:T(8,128)(2,1)S(1)}, u32[]{:S(2)}, u32[]{:S(2)}) collective-permute-start(bf16[4,16,1792]{2,1,0:T(8,128)(2,1)S(1)} %get-tuple-element.102), channel_id=1, source_target_pairs={{4,0},{8,4},{12,8},{16,12},{20,16},{24,20},{28,24},{5,1},{9,5},{13... | collective-permute-start | bytes 688136 | tf_op jit(solution)/shard_map/ppermute | solution.py:326
  142.0 22.5 %collective-permute-start.30 = (bf16[4,16,1792]{2,1,0:T(8,128)(2,1)S(1)}, bf16[4,16,1792]{2,1,0:T(8,128)(2,1)S(1)}, u32[]{:S(2)}, u32[]{:S(2)}) collective-permute-start(bf16[4,16,1792]{2,1,0:T(8,128)(2,1)S(1)} %get-tuple-element.102), channel_id=1, source_target_pairs={{0,28},{1,29},{2,30},{3,31}} | collective-permute-start | bytes 688136 | tf_op jit(solution)/shard_map/ppermute | solution.py:327
  (6 other events, 78.3 us)

commit v8 on v6

--- a/solution.py
+++ b/solution.py
@@ -66,12 +66,20 @@
     copy.wait()
 
 
-def put_kernel(start, source, old, target, sem):
+def put_kernel(start, on, source, old, target, sem):
     del old
-    here = pl.ds(start, source.shape[1])
-    copy = pltpu.make_async_copy(source, target.at[:, here], sem)
-    copy.start()
-    copy.wait()
+
+    def put():
+        here = pl.ds(start, source.shape[1])
+        copy = pltpu.make_async_copy(source, target.at[:, here], sem)
+        copy.start()
+        copy.wait()
+
+    is_last = lax.axis_index("pipe") == lax.axis_size("pipe") - 1
+    if on == "all":
+        put()
+    else:
+        pl.when(is_last if on == "last" else jnp.logical_not(is_last))(put)
 
 
 def take_rows(array, start, size):
@@ -87,9 +95,9 @@
     )(in_hbm(array))
 
 
-def put_rows(out, piece, start):
-    return pl.pallas_call(
-        functools.partial(put_kernel, start),
+def put_rows(out, piece, start, on="all"):
+    return pl.pallas_call(
+        functools.partial(put_kernel, start, on),
         out_shape=jax.ShapeDtypeStruct(out.shape, out.dtype),
         in_specs=[pl.BlockSpec(memory_space=pltpu.VMEM), pl.BlockSpec(memory_space=pltpu.HBM)],
         out_specs=pl.BlockSpec(memory_space=pltpu.HBM),
@@ -321,8 +329,12 @@
     for c in range(chunks - 1):
         out = lax.dynamic_update_slice(out, sent[c], (0, starts[c], 0))
     out = put_rows(out, sent[-1], starts[-1])
+    length = lax.axis_size("pipe")
     for piece in last:
-        out = put_rows(out, back_one(piece), rows - LAST)
+        near = lax.ppermute(piece, "pipe", [(i, i - 1) for i in range(1, length)])
+        far = lax.ppermute(piece, "pipe", [(0, length - 1)])
+        out = put_rows(out, near, rows - LAST, "others")
+        out = put_rows(out, far, rows - LAST, "last")
     return out.reshape(1, tokens, width)
 
 

time: 166 us -> 165 us (level)
  waiting for transfers between devices: 57.3 us -> 53.9 us
  starting transfers between devices: 46.4 us -> 49.1 us
    ppermute x9 -> x8, waiting for transfers between devices: 38.5 us -> 32.6 us  [back_one(): lax.ppermute(x, 'pipe', [(i, (i - 1) % length) for i in range(length)])]
    ppermute x0 -> x2, starting transfers between devices: none -> 3.93 us  [the longest x1 2.65 us: shards(): far = lax.ppermute(piece, 'pipe', [(0, length - 1)])]
    ppermute x0 -> x2, waiting for transfers between devices: none -> 2.2 us  [the longest x1 1.59 us: shards(): far = lax.ppermute(piece, 'pipe', [(0, length - 1)])]
    ppermute x9 -> x8, starting transfers between devices: 28.8 us -> 28.8 us  [back_one(): lax.ppermute(x, 'pipe', [(i, (i - 1) % length) for i in range(length)])]
  transfers between devices with their start and end apart: 33 -> 34, of which waited for: 15 -> 16; matrix products, arithmetic and copies ran while one was open for 6% -> 6% of each run, Pallas kernels for 30% -> 31%
where the time goes in v8:
time: 165 us; the launch traced here: 164 us
  waiting for transfers between devices  53.9 us (33%)
  Pallas kernels  51.9 us (31%)
  starting transfers between devices  49.1 us (30%)
  local copies, waits for them, and re-layouts  9.31 us (6%)
    ppermute x8, waiting for transfers between devices, back_one(): lax.ppermute(x, 'pipe', [(i, (i - 1) % length) for i in range(length)])  32.6 us
    ppermute x8, starting transfers between devices, back_one(): lax.ppermute(x, 'pipe', [(i, (i - 1) % length) for i in range(length)])  28.8 us
    pallas_call x4, Pallas kernels, second_product(): pl.pallas_call(functools.partial(second_kernel, n, start), out_shape=[jax...  28.7 us
    ppermute x16, waiting for transfers between devices, to_expert(): return lax.ppermute(x, 'expert', [(i, (i + by) % n) for i in range(n)])  17.9 us
    ppermute x16, starting transfers between devices, to_expert(): return lax.ppermute(x, 'expert', [(i, (i + by) % n) for i in range(n)])  14.5 us
    pallas_call x4, Pallas kernels, first_product(): pl.pallas_call(functools.partial(first_kernel, n), out_shape=[jax.ShapeDt...  9.85 us
    pallas_call x4, Pallas kernels, activation(): pl.pallas_call(functools.partial(activation_kernel, start), out_shape=jax...  5.61 us
    slice x2, local copies, waits for them, and re-layouts, shards(): piece = grads[:, starts[c]:starts[c] + sizes[c]]  5.15 us
  transfers between devices with their start and end apart: 34, of which 16 were waited for; matrix products, arithmetic and copies ran while one was open for 6% of the time, Pallas kernels for 31%

profile of v8, /device:TPU:0, one launch (start us, length us, event | category | flops | bytes accessed | tf_op | source)
XLA Modules:
  0.0 164.4 jit_solution(14212504106478616231)
XLA Ops:
  1.1 6.0 %collective-permute-start = (bf16[4,48,1792]{2,1,0:T(8,128)(2,1)S(1)}, bf16[4,48,1792]{2,1,0:T(8,128)(2,1)S(1)}, u32[]{:S(2)}, u32[]{:S(2)}) collective-permute-start(bf16[4,48,1792]{2,1,0:T(8,128)(2,1)S(1)} %take_rows.1), channel_id=1, source_target_pairs={{0,28},{4,0},{8,4},{12,8},{16,12},{20,16},{24,20},{28,24},{1,29},{... | collective-permute-start | bytes 2064392 | tf_op jit(solution)/shard_map/ppermute | solution.py:35
  7.1 5.0 %routed_grad.1 = bf16[1024,256]{1,0:T(8,128)(2,1)} custom-call(f32[8,1024]{1,0:T(8,128)} %bitcast.50, f32[8,1024]{1,0:T(8,128)} %bitcast.51, s32[8,1024]{1,0:T(8,128)} %bitcast.52), custom_call_target="tpu_custom_call" | custom-call | tf_op jit(solution)/shard_map/routed_grad/pallas_call | solution.py:128
  12.2 2.3 %slice.11 = bf16[4,80,1792]{2,1,0:T(8,128)(2,1)} slice(bf16[4,256,1792]{2,1,0:T(8,128)(2,1)} %bitcast.40), slice={[0:4], [48:128], [0:1792]} | slice | bytes 2293760 | tf_op jit(solution)/shard_map/slice | solution.py:284
  15.1 2.8 %fusion = (bf16[4,64,1792]{2,1,0:T(8,128)(2,1)}, bf16[4,64,1792]{2,1,0:T(8,128)(2,1)}) fusion(bf16[4,256,1792]{2,1,0:T(8,128)(2,1)} %bitcast.41), kind=kLoop, calls=%fused_computation.2 | loop fusion | bytes 3670016 | tf_op jit(solution)/shard_map/slice | solution.py:284
  17.9 5.1 %collective-permute-done.rows_ref = bf16[4,48,1792]{2,1,0:T(8,128)(2,1)S(1)} collective-permute-done((bf16[4,48,1792]{2,1,0:T(8,128)(2,1)S(1)}, bf16[4,48,1792]{2,1,0:T(8,128)(2,1)S(1)}, u32[]{:S(2)}, u32[]{:S(2)}) %collective-permute-start) | collective-permute-done | bytes 688160 | tf_op jit(solution)/shard_map/ppermute | solution.py:35
  23.0 5.2 %collective-permute-start.8 = (bf16[4,64,1792]{2,1,0:T(8,128)(2,1)}, bf16[4,64,1792]{2,1,0:T(8,128)(2,1)S(1)}, u32[]{:S(2)}, u32[]{:S(2)}) collective-permute-start(bf16[4,64,1792]{2,1,0:T(8,128)(2,1)} %get-tuple-element.73), channel_id=1, source_target_pairs={{0,28},{4,0},{8,4},{12,8},{16,12},{20,16},{24,20},{28,24},{1,29},{... | collective-permute-start | bytes 2752520 | tf_op jit(solution)/shard_map/ppermute | solution.py:35
  28.2 4.1 %first_product.4 = (bf16[48,1024]{1,0:T(8,128)(2,1)S(1)}, bf16[48,1024]{1,0:T(8,128)(2,1)S(1)}, bf16[48,1024]{1,0:T(8,128)(2,1)S(1)}, bf16[48,1024]{1,0:T(8,128)(2,1)S(1)}) custom-call(s32[1]{0:T(128)} %bitcast.me_ref, bf16[4,48,1792]{2,1,0:T(8,128)(2,1)S(1)} %collective-permute-done.rows_ref, bf16[1024,1792]{1,0:T(8,128)(2,1)} %bitcast.19), custom_call_target="tpu_custom_call" | custom-call | tf_op jit(solution)/shard_map/first_product/pallas_call | solution.py:152
  32.3 1.6 collective-permute-start.3
  35.3 1.5 collective-permute-done.2.refs_1_
  42.3 5.4 %collective-permute-done.1.rows_ref = bf16[4,80,1792]{2,1,0:T(8,128)(2,1)S(1)} collective-permute-done((bf16[4,80,1792]{2,1,0:T(8,128)(2,1)}, bf16[4,80,1792]{2,1,0:T(8,128)(2,1)S(1)}, u32[]{:S(2)}, u32[]{:S(2)}) %collective-permute-start.1) | collective-permute-done | bytes 1146912 | tf_op jit(solution)/shard_map/ppermute | solution.py:35
  47.7 2.1 %first_product.5 = (bf16[80,1024]{1,0:T(8,128)(2,1)S(1)}, bf16[80,1024]{1,0:T(8,128)(2,1)S(1)}, bf16[80,1024]{1,0:T(8,128)(2,1)S(1)}, bf16[80,1024]{1,0:T(8,128)(2,1)S(1)}) custom-call(s32[1]{0:T(128)} %bitcast.me_ref, bf16[4,80,1792]{2,1,0:T(8,128)(2,1)S(1)} %collective-permute-done.1.rows_ref, bf16[1024,1792]{1,0:T(8,128)(2,1)S(1)} %bitcast.20), custom_call_target="tpu_custom_call" | custom-call | tf_op jit(solution)/shard_map/first_product/pallas_call | solution.py:152
  49.9 5.1 %collective-permute-start.15 = (bf16[4,64,1792]{2,1,0:T(8,128)(2,1)S(1)}, bf16[4,64,1792]{2,1,0:T(8,128)(2,1)S(1)}, u32[]{:S(2)}, u32[]{:S(2)}) collective-permute-start(bf16[4,64,1792]{2,1,0:T(8,128)(2,1)S(1)} %copy-done.3), channel_id=1, source_target_pairs={{0,28},{4,0},{8,4},{12,8},{16,12},{20,16},{24,20},{28,24},{1,29},{... | collective-permute-start | bytes 2752520 | tf_op jit(solution)/shard_map/ppermute | solution.py:35
  55.0 1.5 collective-permute-start.10
  57.1 7.2 %second_product.4 = bf16[4,48,1792]{2,1,0:T(8,128)(2,1)S(1)} custom-call(s32[1]{0:T(128)} %bitcast.me_ref, bf16[4,256,256]{2,1,0:T(8,128)(2,1)S(1)} %bitcast.27, bf16[1792,1024]{1,0:T(8,128)(2,1)} %bitcast.31, bf16[1792,1024]{1,0:T(8,128)(2,1)} %bitcast.35, bf16[1792,256]{1,0:T(8,128)(2,1)S(1)} %bitcast.23, bf16[48,2048]{1,0:T(8,128)(2,1)S(1)} %activation.4.refs_0_, ...), custom_call_target="tpu_custom_call" | custom-call | tf_op jit(solution)/shard_map/second_product/pallas_call | solution.py:234
  64.3 3.0 %collective-permute-done.8.rows_ref = bf16[4,64,1792]{2,1,0:T(8,128)(2,1)S(1)} collective-permute-done((bf16[4,64,1792]{2,1,0:T(8,128)(2,1)}, bf16[4,64,1792]{2,1,0:T(8,128)(2,1)S(1)}, u32[]{:S(2)}, u32[]{:S(2)}) %collective-permute-start.8) | collective-permute-done | bytes 917536 | tf_op jit(solution)/shard_map/ppermute | solution.py:35
  67.3 1.5 activation.5.refs_0_
  68.8 1.6 collective-permute-start.12
  70.4 1.9 %first_product.6 = (bf16[64,1024]{1,0:T(8,128)(2,1)S(1)}, bf16[64,1024]{1,0:T(8,128)(2,1)S(1)}, bf16[64,1024]{1,0:T(8,128)(2,1)S(1)}, bf16[64,1024]{1,0:T(8,128)(2,1)S(1)}) custom-call(s32[1]{0:T(128)} %bitcast.me_ref, bf16[4,64,1792]{2,1,0:T(8,128)(2,1)S(1)} %collective-permute-done.8.rows_ref, bf16[1024,1792]{1,0:T(8,128)(2,1)S(1)} %bitcast.21), custom_call_target="tpu_custom_call" | custom-call | tf_op jit(solution)/shard_map/first_product/pallas_call | solution.py:152
  72.3 4.3 %collective-permute-done.12.refs_2_ = bf16[80,2048]{1,0:T(8,128)(2,1)S(1)} collective-permute-done((bf16[80,2048]{1,0:T(8,128)(2,1)S(1)}, bf16[80,2048]{1,0:T(8,128)(2,1)S(1)}, u32[]{:S(2)}, u32[]{:S(2)}) %collective-permute-start.12) | collective-permute-done | bytes 327712 | tf_op jit(solution)/shard_map/ppermute | solution.py:40
  79.3 5.1 %collective-permute-start.22 = (bf16[4,48,1792]{2,1,0:T(8,128)(2,1)S(1)}, bf16[4,48,1792]{2,1,0:T(8,128)(2,1)S(1)}, u32[]{:S(2)}, u32[]{:S(2)}) collective-permute-start(bf16[4,48,1792]{2,1,0:T(8,128)(2,1)S(1)} %second_product.4), channel_id=1, source_target_pairs={{0,28},{4,0},{8,4},{12,8},{16,12},{20,16},{24,20},{28,24},{1,29},{... | collective-permute-start | bytes 2064392 | tf_op jit(solution)/shard_map/ppermute | solution.py:35
  84.4 7.4 %second_product.5 = bf16[4,80,1792]{2,1,0:T(8,128)(2,1)S(1)} custom-call(s32[1]{0:T(128)} %bitcast.me_ref, bf16[4,256,256]{2,1,0:T(8,128)(2,1)S(1)} %bitcast.28, bf16[1792,1024]{1,0:T(8,128)(2,1)} %bitcast.32, bf16[1792,1024]{1,0:T(8,128)(2,1)} %bitcast.36, bf16[1792,256]{1,0:T(8,128)(2,1)S(1)} %bitcast.24, bf16[80,2048]{1,0:T(8,128)(2,1)S(1)} %activation.5.refs_0_, ...), custom_call_target="tpu_custom_call" | custom-call | tf_op jit(solution)/shard_map/second_product/pallas_call | solution.py:234
  95.1 1.8 %first_product.7 = (bf16[64,1024]{1,0:T(8,128)(2,1)S(1)}, bf16[64,1024]{1,0:T(8,128)(2,1)S(1)}, bf16[64,1024]{1,0:T(8,128)(2,1)S(1)}, bf16[64,1024]{1,0:T(8,128)(2,1)S(1)}) custom-call(s32[1]{0:T(128)} %bitcast.me_ref, bf16[4,64,1792]{2,1,0:T(8,128)(2,1)S(1)} %collective-permute-done.15.rows_ref, bf16[1024,1792]{1,0:T(8,128)(2,1)S(1)} %bitcast.22), custom_call_target="tpu_custom_call" | custom-call | tf_op jit(solution)/shard_map/first_product/pallas_call | solution.py:152
  96.9 3.8 %collective-permute-done.19.refs_2_ = bf16[64,2048]{1,0:T(8,128)(2,1)S(1)} collective-permute-done((bf16[64,2048]{1,0:T(8,128)(2,1)S(1)}, bf16[64,2048]{1,0:T(8,128)(2,1)S(1)}, u32[]{:S(2)}, u32[]{:S(2)}) %collective-permute-start.19) | collective-permute-done | bytes 262176 | tf_op jit(solution)/shard_map/ppermute | solution.py:40
  103.1 7.0 %second_product.6 = bf16[4,64,1792]{2,1,0:T(8,128)(2,1)S(1)} custom-call(s32[1]{0:T(128)} %bitcast.me_ref, bf16[4,256,256]{2,1,0:T(8,128)(2,1)S(1)} %bitcast.29, bf16[1792,1024]{1,0:T(8,128)(2,1)} %bitcast.33, bf16[1792,1024]{1,0:T(8,128)(2,1)} %bitcast.37, bf16[1792,256]{1,0:T(8,128)(2,1)S(1)} %bitcast.25, bf16[64,2048]{1,0:T(8,128)(2,1)S(1)} %activation.6.refs_0_, ...), custom_call_target="tpu_custom_call" | custom-call | tf_op jit(solution)/shard_map/second_product/pallas_call | solution.py:234
  113.1 6.5 %collective-permute-done.27.refs_2_ = bf16[64,2048]{1,0:T(8,128)(2,1)S(1)} collective-permute-done((bf16[64,2048]{1,0:T(8,128)(2,1)S(1)}, bf16[64,2048]{1,0:T(8,128)(2,1)S(1)}, u32[]{:S(2)}, u32[]{:S(2)}) %collective-permute-start.27) | collective-permute-done | bytes 262176 | tf_op jit(solution)/shard_map/ppermute | solution.py:40
  121.1 5.1 %collective-permute-done.29 = bf16[4,80,1792]{2,1,0:T(8,128)(2,1)S(1)} collective-permute-done((bf16[4,80,1792]{2,1,0:T(8,128)(2,1)S(1)}, bf16[4,80,1792]{2,1,0:T(8,128)(2,1)S(1)}, u32[]{:S(2)}, u32[]{:S(2)}) %collective-permute-start.29) | collective-permute-done | bytes 1146912 | tf_op jit(solution)/shard_map/ppermute | solution.py:35
  126.2 7.1 %second_product.7 = (bf16[4,48,1792]{2,1,0:T(8,128)(2,1)S(1)}, bf16[4,16,1792]{2,1,0:T(8,128)(2,1)S(1)}) custom-call(s32[1]{0:T(128)} %bitcast.me_ref, bf16[4,256,256]{2,1,0:T(8,128)(2,1)S(1)} %bitcast.30, bf16[1792,1024]{1,0:T(8,128)(2,1)} %bitcast.34, bf16[1792,1024]{1,0:T(8,128)(2,1)} %bitcast.38, bf16[1792,256]{1,0:T(8,128)(2,1)S(1)} %bitcast.26, ...), custom_call_target="tpu_custom_call" | custom-call | tf_op jit(solution)/shard_map/second_product/pallas_call | solution.py:234
  133.3 5.2 %collective-permute-start.32 = (bf16[4,48,1792]{2,1,0:T(8,128)(2,1)S(1)}, bf16[4,48,1792]{2,1,0:T(8,128)(2,1)S(1)}, u32[]{:S(2)}, u32[]{:S(2)}) collective-permute-start(bf16[4,48,1792]{2,1,0:T(8,128)(2,1)S(1)} %get-tuple-element.105), channel_id=1, source_target_pairs={{0,28},{4,0},{8,4},{12,8},{16,12},{20,16},{24,20},{28,24},{1,29},{... | collective-permute-start | bytes 2064392 | tf_op jit(solution)/shard_map/ppermute | solution.py:35
  138.5 2.1 %dynamic_update_slice.9 = bf16[4,256,1792]{2,1,0:T(8,128)(2,1)} pad(bf16[4,48,1792]{2,1,0:T(8,128)(2,1)S(1)} %collective-permute-done.22, bf16[]{:T(256)} %constant.1.clone.1), padding=0_0x0_208x0_0 | pad | bytes 4358146 | tf_op jit(solution)/shard_map/dynamic_update_slice | solution.py:330
  141.9 2.7 %collective-permute-start.30 = (bf16[4,16,1792]{2,1,0:T(8,128)(2,1)S(1)}, bf16[4,16,1792]{2,1,0:T(8,128)(2,1)S(1)}, u32[]{:S(2)}, u32[]{:S(2)}) collective-permute-start(bf16[4,16,1792]{2,1,0:T(8,128)(2,1)S(1)} %get-tuple-element.102), channel_id=1, source_target_pairs={{0,28},{1,29},{2,30},{3,31}} | collective-permute-start | bytes 688136 | tf_op jit(solution)/shard_map/ppermute | solution.py:335
  146.9 13.8 %collective-permute-done.32.source = bf16[4,48,1792]{2,1,0:T(8,128)(2,1)S(1)} collective-permute-done((bf16[4,48,1792]{2,1,0:T(8,128)(2,1)S(1)}, bf16[4,48,1792]{2,1,0:T(8,128)(2,1)S(1)}, u32[]{:S(2)}, u32[]{:S(2)}) %collective-permute-start.32) | collective-permute-done | bytes 688160 | tf_op jit(solution)/shard_map/ppermute | solution.py:35
  162.8 1.6 collective-permute-done.30.source
  (66 shorter events, 27.8 us)
Async XLA Ops:
  1.1 21.9 %collective-permute-start = (bf16[4,48,1792]{2,1,0:T(8,128)(2,1)S(1)}, bf16[4,48,1792]{2,1,0:T(8,128)(2,1)S(1)}, u32[]{:S(2)}, u32[]{:S(2)}) collective-permute-start(bf16[4,48,1792]{2,1,0:T(8,128)(2,1)S(1)} %take_rows.1), channel_id=1, source_target_pairs={{0,28},{4,0},{8,4},{12,8},{16,12},{20,16},{24,20},{28,24},{1,29},{... | collective-permute-start | bytes 2064392 | tf_op jit(solution)/shard_map/ppermute | solution.py:35
  14.5 33.1 %collective-permute-start.1 = (bf16[4,80,1792]{2,1,0:T(8,128)(2,1)}, bf16[4,80,1792]{2,1,0:T(8,128)(2,1)S(1)}, u32[]{:S(2)}, u32[]{:S(2)}) collective-permute-start(bf16[4,80,1792]{2,1,0:T(8,128)(2,1)} %slice.11), channel_id=1, source_target_pairs={{0,28},{4,0},{8,4},{12,8},{16,12},{20,16},{24,20},{28,24},{1,29},{... | collective-permute-start | bytes 3440648 | tf_op jit(solution)/shard_map/ppermute | solution.py:35
  23.0 44.3 %collective-permute-start.8 = (bf16[4,64,1792]{2,1,0:T(8,128)(2,1)}, bf16[4,64,1792]{2,1,0:T(8,128)(2,1)S(1)}, u32[]{:S(2)}, u32[]{:S(2)}) collective-permute-start(bf16[4,64,1792]{2,1,0:T(8,128)(2,1)} %get-tuple-element.73), channel_id=1, source_target_pairs={{0,28},{4,0},{8,4},{12,8},{16,12},{20,16},{24,20},{28,24},{1,29},{... | collective-permute-start | bytes 2752520 | tf_op jit(solution)/shard_map/ppermute | solution.py:35
  32.3 4.5 %collective-permute-start.2 = (bf16[48,1024]{1,0:T(8,128)(2,1)S(1)}, bf16[48,1024]{1,0:T(8,128)(2,1)S(1)}, u32[]{:S(2)}, u32[]{:S(2)}) collective-permute-start(bf16[48,1024]{1,0:T(8,128)(2,1)S(1)} %get-tuple-element.65), channel_id=1, source_target_pairs={{0,1},{1,2},{2,3},{3,0},{4,5},{5,6},{6,7},{7,4},{8,9},{9,10},{10,1... | collective-permute-start | bytes 294920 | tf_op jit(solution)/shard_map/ppermute | solution.py:40
  32.3 5.7 %collective-permute-start.3 = (bf16[48,1024]{1,0:T(8,128)(2,1)S(1)}, bf16[48,1024]{1,0:T(8,128)(2,1)S(1)}, u32[]{:S(2)}, u32[]{:S(2)}) collective-permute-start(bf16[48,1024]{1,0:T(8,128)(2,1)S(1)} %get-tuple-element.66), channel_id=1, source_target_pairs={{0,2},{1,3},{2,0},{3,1},{4,6},{5,7},{6,4},{7,5},{8,10},{9,11},{10,... | collective-permute-start | bytes 294920 | tf_op jit(solution)/shard_map/ppermute | solution.py:40
  33.9 4.6 %collective-permute-start.4 = (bf16[48,1024]{1,0:T(8,128)(2,1)S(1)}, bf16[48,1024]{1,0:T(8,128)(2,1)S(1)}, u32[]{:S(2)}, u32[]{:S(2)}) collective-permute-start(bf16[48,1024]{1,0:T(8,128)(2,1)S(1)} %get-tuple-element.67), channel_id=1, source_target_pairs={{0,3},{1,0},{2,1},{3,2},{4,7},{5,4},{6,5},{7,6},{8,11},{9,8},{10,9... | collective-permute-start | bytes 294920 | tf_op jit(solution)/shard_map/ppermute | solution.py:40
  39.9 9.9 %collective-permute-start.5 = (bf16[48,2048]{1,0:T(8,128)(2,1)S(1)}, bf16[48,2048]{1,0:T(8,128)(2,1)S(1)}, u32[]{:S(2)}, u32[]{:S(2)}) collective-permute-start(bf16[48,2048]{1,0:T(8,128)(2,1)S(1)} %activation.4.refs_0_), channel_id=1, source_target_pairs={{0,2},{1,3},{2,0},{3,1},{4,6},{5,7},{6,4},{7,5},{8,10},{9,11},{10,... | collective-permute-start | bytes 589832 | tf_op jit(solution)/shard_map/ppermute | solution.py:40
  41.0 15.6 %collective-permute-start.6 = (bf16[48,2048]{1,0:T(8,128)(2,1)S(1)}, bf16[48,2048]{1,0:T(8,128)(2,1)S(1)}, u32[]{:S(2)}, u32[]{:S(2)}) collective-permute-start(bf16[48,2048]{1,0:T(8,128)(2,1)S(1)} %activation.4.refs_0_), channel_id=1, source_target_pairs={{0,1},{1,0},{2,3},{3,2},{4,5},{5,4},{6,7},{7,6},{8,9},{9,8},{10,11... | collective-permute-start | bytes 589832 | tf_op jit(solution)/shard_map/ppermute | solution.py:45
  49.8 6.8 %collective-permute-start.7 = (bf16[48,2048]{1,0:T(8,128)(2,1)S(1)}, bf16[48,2048]{1,0:T(8,128)(2,1)S(1)}, u32[]{:S(2)}, u32[]{:S(2)}) collective-permute-start(bf16[48,2048]{1,0:T(8,128)(2,1)S(1)} %collective-permute-done.5.refs_2_), channel_id=1, source_target_pairs={{0,1},{1,0},{2,3},{3,2},{4,5},{5,4},{6,7},{7,6},{8,9},{9,8},{10,11... | collective-permute-start | bytes 589832 | tf_op jit(solution)/shard_map/ppermute | solution.py:45
  49.9 41.9 %collective-permute-start.15 = (bf16[4,64,1792]{2,1,0:T(8,128)(2,1)S(1)}, bf16[4,64,1792]{2,1,0:T(8,128)(2,1)S(1)}, u32[]{:S(2)}, u32[]{:S(2)}) collective-permute-start(bf16[4,64,1792]{2,1,0:T(8,128)(2,1)S(1)} %copy-done.3), channel_id=1, source_target_pairs={{0,28},{4,0},{8,4},{12,8},{16,12},{20,16},{24,20},{28,24},{1,29},{... | collective-permute-start | bytes 2752520 | tf_op jit(solution)/shard_map/ppermute | solution.py:35
  55.0 12.3 %collective-permute-start.10 = (bf16[80,1024]{1,0:T(8,128)(2,1)S(1)}, bf16[80,1024]{1,0:T(8,128)(2,1)S(1)}, u32[]{:S(2)}, u32[]{:S(2)}) collective-permute-start(bf16[80,1024]{1,0:T(8,128)(2,1)S(1)} %get-tuple-element.77), channel_id=1, source_target_pairs={{0,2},{1,3},{2,0},{3,1},{4,6},{5,7},{6,4},{7,5},{8,10},{9,11},{10,... | collective-permute-start | bytes 491528 | tf_op jit(solution)/shard_map/ppermute | solution.py:40
  56.5 10.8 %collective-permute-start.11 = (bf16[80,1024]{1,0:T(8,128)(2,1)S(1)}, bf16[80,1024]{1,0:T(8,128)(2,1)S(1)}, u32[]{:S(2)}, u32[]{:S(2)}) collective-permute-start(bf16[80,1024]{1,0:T(8,128)(2,1)S(1)} %get-tuple-element.78), channel_id=1, source_target_pairs={{0,3},{1,0},{2,1},{3,2},{4,7},{5,4},{6,5},{7,6},{8,11},{9,8},{10,9... | collective-permute-start | bytes 491528 | tf_op jit(solution)/shard_map/ppermute | solution.py:40
  56.6 10.8 %collective-permute-start.9 = (bf16[80,1024]{1,0:T(8,128)(2,1)S(1)}, bf16[80,1024]{1,0:T(8,128)(2,1)S(1)}, u32[]{:S(2)}, u32[]{:S(2)}) collective-permute-start(bf16[80,1024]{1,0:T(8,128)(2,1)S(1)} %get-tuple-element.76), channel_id=1, source_target_pairs={{0,1},{1,2},{2,3},{3,0},{4,5},{5,6},{6,7},{7,4},{8,9},{9,10},{10,1... | collective-permute-start | bytes 491528 | tf_op jit(solution)/shard_map/ppermute | solution.py:40
  68.8 7.8 %collective-permute-start.12 = (bf16[80,2048]{1,0:T(8,128)(2,1)S(1)}, bf16[80,2048]{1,0:T(8,128)(2,1)S(1)}, u32[]{:S(2)}, u32[]{:S(2)}) collective-permute-start(bf16[80,2048]{1,0:T(8,128)(2,1)S(1)} %activation.5.refs_0_), channel_id=1, source_target_pairs={{0,2},{1,3},{2,0},{3,1},{4,6},{5,7},{6,4},{7,5},{8,10},{9,11},{10,... | collective-permute-start | bytes 983048 | tf_op jit(solution)/shard_map/ppermute | solution.py:40
  70.4 8.0 %collective-permute-start.13 = (bf16[80,2048]{1,0:T(8,128)(2,1)S(1)}, bf16[80,2048]{1,0:T(8,128)(2,1)S(1)}, u32[]{:S(2)}, u32[]{:S(2)}) collective-permute-start(bf16[80,2048]{1,0:T(8,128)(2,1)S(1)} %activation.5.refs_0_), channel_id=1, source_target_pairs={{0,1},{1,0},{2,3},{3,2},{4,5},{5,4},{6,7},{7,6},{8,9},{9,8},{10,11... | collective-permute-start | bytes 983048 | tf_op jit(solution)/shard_map/ppermute | solution.py:45
  76.6 2.7 %collective-permute-start.14 = (bf16[80,2048]{1,0:T(8,128)(2,1)S(1)}, bf16[80,2048]{1,0:T(8,128)(2,1)S(1)}, u32[]{:S(2)}, u32[]{:S(2)}) collective-permute-start(bf16[80,2048]{1,0:T(8,128)(2,1)S(1)} %collective-permute-done.12.refs_2_), channel_id=1, source_target_pairs={{0,1},{1,0},{2,3},{3,2},{4,5},{5,4},{6,7},{7,6},{8,9},{9,8},{10,11... | collective-permute-start | bytes 983048 | tf_op jit(solution)/shard_map/ppermute | solution.py:45
  76.6 15.2 %collective-permute-start.16 = (bf16[64,1024]{1,0:T(8,128)(2,1)S(1)}, bf16[64,1024]{1,0:T(8,128)(2,1)S(1)}, u32[]{:S(2)}, u32[]{:S(2)}) collective-permute-start(bf16[64,1024]{1,0:T(8,128)(2,1)S(1)} %get-tuple-element.87), channel_id=1, source_target_pairs={{0,1},{1,2},{2,3},{3,0},{4,5},{5,6},{6,7},{7,4},{8,9},{9,10},{10,1... | collective-permute-start | bytes 393224 | tf_op jit(solution)/shard_map/ppermute | solution.py:40
  77.1 14.7 %collective-permute-start.17 = (bf16[64,1024]{1,0:T(8,128)(2,1)S(1)}, bf16[64,1024]{1,0:T(8,128)(2,1)S(1)}, u32[]{:S(2)}, u32[]{:S(2)}) collective-permute-start(bf16[64,1024]{1,0:T(8,128)(2,1)S(1)} %get-tuple-element.88), channel_id=1, source_target_pairs={{0,2},{1,3},{2,0},{3,1},{4,6},{5,7},{6,4},{7,5},{8,10},{9,11},{10,... | collective-permute-start | bytes 393224 | tf_op jit(solution)/shard_map/ppermute | solution.py:40
  78.4 13.4 %collective-permute-start.18 = (bf16[64,1024]{1,0:T(8,128)(2,1)S(1)}, bf16[64,1024]{1,0:T(8,128)(2,1)S(1)}, u32[]{:S(2)}, u32[]{:S(2)}) collective-permute-start(bf16[64,1024]{1,0:T(8,128)(2,1)S(1)} %get-tuple-element.89), channel_id=1, source_target_pairs={{0,3},{1,0},{2,1},{3,2},{4,7},{5,4},{6,5},{7,6},{8,11},{9,8},{10,9... | collective-permute-start | bytes 393224 | tf_op jit(solution)/shard_map/ppermute | solution.py:40
  79.3 30.9 %collective-permute-start.22 = (bf16[4,48,1792]{2,1,0:T(8,128)(2,1)S(1)}, bf16[4,48,1792]{2,1,0:T(8,128)(2,1)S(1)}, u32[]{:S(2)}, u32[]{:S(2)}) collective-permute-start(bf16[4,48,1792]{2,1,0:T(8,128)(2,1)S(1)} %second_product.4), channel_id=1, source_target_pairs={{0,28},{4,0},{8,4},{12,8},{16,12},{20,16},{24,20},{28,24},{1,29},{... | collective-permute-start | bytes 2064392 | tf_op jit(solution)/shard_map/ppermute | solution.py:35
  93.2 7.5 %collective-permute-start.19 = (bf16[64,2048]{1,0:T(8,128)(2,1)S(1)}, bf16[64,2048]{1,0:T(8,128)(2,1)S(1)}, u32[]{:S(2)}, u32[]{:S(2)}) collective-permute-start(bf16[64,2048]{1,0:T(8,128)(2,1)S(1)} %activation.6.refs_0_), channel_id=1, source_target_pairs={{0,2},{1,3},{2,0},{3,1},{4,6},{5,7},{6,4},{7,5},{8,10},{9,11},{10,... | collective-permute-start | bytes 786440 | tf_op jit(solution)/shard_map/ppermute | solution.py:40
  93.8 32.4 %collective-permute-start.29 = (bf16[4,80,1792]{2,1,0:T(8,128)(2,1)S(1)}, bf16[4,80,1792]{2,1,0:T(8,128)(2,1)S(1)}, u32[]{:S(2)}, u32[]{:S(2)}) collective-permute-start(bf16[4,80,1792]{2,1,0:T(8,128)(2,1)S(1)} %second_product.5), channel_id=1, source_target_pairs={{0,28},{4,0},{8,4},{12,8},{16,12},{20,16},{24,20},{28,24},{1,29},{... | collective-permute-start | bytes 3440648 | tf_op jit(solution)/shard_map/ppermute | solution.py:35
  95.1 6.2 %collective-permute-start.20 = (bf16[64,2048]{1,0:T(8,128)(2,1)S(1)}, bf16[64,2048]{1,0:T(8,128)(2,1)S(1)}, u32[]{:S(2)}, u32[]{:S(2)}) collective-permute-start(bf16[64,2048]{1,0:T(8,128)(2,1)S(1)} %activation.6.refs_0_), channel_id=1, source_target_pairs={{0,1},{1,0},{2,3},{3,2},{4,5},{5,4},{6,7},{7,6},{8,9},{9,8},{10,11... | collective-permute-start | bytes 786440 | tf_op jit(solution)/shard_map/ppermute | solution.py:45
  100.8 9.4 %collective-permute-start.23 = (bf16[64,1024]{1,0:T(8,128)(2,1)S(1)}, bf16[64,1024]{1,0:T(8,128)(2,1)S(1)}, u32[]{:S(2)}, u32[]{:S(2)}) collective-permute-start(bf16[64,1024]{1,0:T(8,128)(2,1)S(1)} %get-tuple-element.97), channel_id=1, source_target_pairs={{0,1},{1,2},{2,3},{3,0},{4,5},{5,6},{6,7},{7,4},{8,9},{9,10},{10,1... | collective-permute-start | bytes 393224 | tf_op jit(solution)/shard_map/ppermute | solution.py:40
  101.3 8.9 %collective-permute-start.24 = (bf16[64,1024]{1,0:T(8,128)(2,1)S(1)}, bf16[64,1024]{1,0:T(8,128)(2,1)S(1)}, u32[]{:S(2)}, u32[]{:S(2)}) collective-permute-start(bf16[64,1024]{1,0:T(8,128)(2,1)S(1)} %get-tuple-element.98), channel_id=1, source_target_pairs={{0,2},{1,3},{2,0},{3,1},{4,6},{5,7},{6,4},{7,5},{8,10},{9,11},{10,... | collective-permute-start | bytes 393224 | tf_op jit(solution)/shard_map/ppermute | solution.py:40
  102.3 7.9 %collective-permute-start.25 = (bf16[64,1024]{1,0:T(8,128)(2,1)S(1)}, bf16[64,1024]{1,0:T(8,128)(2,1)S(1)}, u32[]{:S(2)}, u32[]{:S(2)}) collective-permute-start(bf16[64,1024]{1,0:T(8,128)(2,1)S(1)} %get-tuple-element.99), channel_id=1, source_target_pairs={{0,3},{1,0},{2,1},{3,2},{4,7},{5,4},{6,5},{7,6},{8,11},{9,8},{10,9... | collective-permute-start | bytes 393224 | tf_op jit(solution)/shard_map/ppermute | solution.py:40
  111.6 7.9 %collective-permute-start.27 = (bf16[64,2048]{1,0:T(8,128)(2,1)S(1)}, bf16[64,2048]{1,0:T(8,128)(2,1)S(1)}, u32[]{:S(2)}, u32[]{:S(2)}) collective-permute-start(bf16[64,2048]{1,0:T(8,128)(2,1)S(1)} %activation.7.refs_0_), channel_id=1, source_target_pairs={{0,2},{1,3},{2,0},{3,1},{4,6},{5,7},{6,4},{7,5},{8,10},{9,11},{10,... | collective-permute-start | bytes 786440 | tf_op jit(solution)/shard_map/ppermute | solution.py:40
  112.8 33.1 %collective-permute-start.33 = (bf16[4,64,1792]{2,1,0:T(8,128)(2,1)S(1)}, bf16[4,64,1792]{2,1,0:T(8,128)(2,1)S(1)}, u32[]{:S(2)}, u32[]{:S(2)}) collective-permute-start(bf16[4,64,1792]{2,1,0:T(8,128)(2,1)S(1)} %second_product.6), channel_id=1, source_target_pairs={{0,28},{4,0},{8,4},{12,8},{16,12},{20,16},{24,20},{28,24},{1,29},{... | collective-permute-start | bytes 2752520 | tf_op jit(solution)/shard_map/ppermute | solution.py:35
  119.6 6.6 %collective-permute-start.26 = (bf16[64,2048]{1,0:T(8,128)(2,1)S(1)}, bf16[64,2048]{1,0:T(8,128)(2,1)S(1)}, u32[]{:S(2)}, u32[]{:S(2)}) collective-permute-start(bf16[64,2048]{1,0:T(8,128)(2,1)S(1)} %activation.7.refs_0_), channel_id=1, source_target_pairs={{0,1},{1,0},{2,3},{3,2},{4,5},{5,4},{6,7},{7,6},{8,9},{9,8},{10,11... | collective-permute-start | bytes 786440 | tf_op jit(solution)/shard_map/ppermute | solution.py:45
  133.3 27.3 %collective-permute-start.32 = (bf16[4,48,1792]{2,1,0:T(8,128)(2,1)S(1)}, bf16[4,48,1792]{2,1,0:T(8,128)(2,1)S(1)}, u32[]{:S(2)}, u32[]{:S(2)}) collective-permute-start(bf16[4,48,1792]{2,1,0:T(8,128)(2,1)S(1)} %get-tuple-element.105), channel_id=1, source_target_pairs={{0,28},{4,0},{8,4},{12,8},{16,12},{20,16},{24,20},{28,24},{1,29},{... | collective-permute-start | bytes 2064392 | tf_op jit(solution)/shard_map/ppermute | solution.py:35
  140.6 21.5 %collective-permute-start.31 = (bf16[4,16,1792]{2,1,0:T(8,128)(2,1)S(1)}, bf16[4,16,1792]{2,1,0:T(8,128)(2,1)S(1)}, u32[]{:S(2)}, u32[]{:S(2)}) collective-permute-start(bf16[4,16,1792]{2,1,0:T(8,128)(2,1)S(1)} %get-tuple-element.102), channel_id=1, source_target_pairs={{4,0},{8,4},{12,8},{16,12},{20,16},{24,20},{28,24},{5,1},{9,5},{13... | collective-permute-start | bytes 688136 | tf_op jit(solution)/shard_map/ppermute | solution.py:334
  141.9 22.5 %collective-permute-start.30 = (bf16[4,16,1792]{2,1,0:T(8,128)(2,1)S(1)}, bf16[4,16,1792]{2,1,0:T(8,128)(2,1)S(1)}, u32[]{:S(2)}, u32[]{:S(2)}) collective-permute-start(bf16[4,16,1792]{2,1,0:T(8,128)(2,1)S(1)} %get-tuple-element.102), channel_id=1, source_target_pairs={{0,28},{1,29},{2,30},{3,31}} | collective-permute-start | bytes 688136 | tf_op jit(solution)/shard_map/ppermute | solution.py:335
  (6 other events, 89.9 us)

commit v9 on v8

--- a/solution.py
+++ b/solution.py
@@ -59,11 +59,19 @@
     )
 
 
-def take_kernel(start, source, target, sem):
+def take_kernel(start, source, target, sems):
     here = pl.ds(start, target.shape[1])
-    copy = pltpu.make_async_copy(source.at[:, here], target, sem)
-    copy.start()
-    copy.wait()
+    half = target.shape[0] // 2
+    copies = [
+        pltpu.make_async_copy(
+            source.at[pl.ds(i * half, half), here], target.at[pl.ds(i * half, half)], sems.at[i]
+        )
+        for i in range(2)
+    ]
+    for copy in copies:
+        copy.start()
+    for copy in copies:
+        copy.wait()
 
 
 def put_kernel(start, on, source, old, target, sem):
@@ -89,7 +97,7 @@
         out_shape=pltpu.VMEM((n, size, width), array.dtype),
         in_specs=[pl.BlockSpec(memory_space=pltpu.HBM)],
         out_specs=pl.BlockSpec(memory_space=pltpu.VMEM),
-        scratch_shapes=[pltpu.SemaphoreType.DMA],
+        scratch_shapes=[pltpu.SemaphoreType.DMA((2,))],
         cost_estimate=FREE,
         name="take_rows",
     )(in_hbm(array))

time: 165 us -> 165 us (level)
  no operation moved by 1% of the time
where the time goes in v9:
time: 165 us; the launch traced here: 164 us
  waiting for transfers between devices  53.9 us (33%)
  Pallas kernels  51.9 us (31%)
  starting transfers between devices  49.1 us (30%)
  local copies, waits for them, and re-layouts  9.31 us (6%)
    ppermute x8, waiting for transfers between devices, back_one(): lax.ppermute(x, 'pipe', [(i, (i - 1) % length) for i in range(length)])  32.6 us
    ppermute x8, starting transfers between devices, back_one(): lax.ppermute(x, 'pipe', [(i, (i - 1) % length) for i in range(length)])  28.8 us
    pallas_call x4, Pallas kernels, second_product(): pl.pallas_call(functools.partial(second_kernel, n, start), out_shape=[jax...  28.7 us
    ppermute x16, waiting for transfers between devices, to_expert(): return lax.ppermute(x, 'expert', [(i, (i + by) % n) for i in range(n)])  17.9 us
    ppermute x16, starting transfers between devices, to_expert(): return lax.ppermute(x, 'expert', [(i, (i + by) % n) for i in range(n)])  14.5 us
    pallas_call x4, Pallas kernels, first_product(): pl.pallas_call(functools.partial(first_kernel, n), out_shape=[jax.ShapeDt...  9.85 us
    pallas_call x4, Pallas kernels, activation(): pl.pallas_call(functools.partial(activation_kernel, start), out_shape=jax...  5.61 us
    slice x2, local copies, waits for them, and re-layouts, shards(): piece = grads[:, starts[c]:starts[c] + sizes[c]]  5.15 us
  transfers between devices with their start and end apart: 34, of which 16 were waited for; matrix products, arithmetic and copies ran while one was open for 6% of the time, Pallas kernels for 31%

profile of v9, /device:TPU:0, one launch (start us, length us, event | category | flops | bytes accessed | tf_op | source)
XLA Modules:
  0.0 164.4 jit_solution(16523361458241589716)
XLA Ops:
  1.1 6.0 %collective-permute-start = (bf16[4,48,1792]{2,1,0:T(8,128)(2,1)S(1)}, bf16[4,48,1792]{2,1,0:T(8,128)(2,1)S(1)}, u32[]{:S(2)}, u32[]{:S(2)}) collective-permute-start(bf16[4,48,1792]{2,1,0:T(8,128)(2,1)S(1)} %take_rows.1), channel_id=1, source_target_pairs={{0,28},{4,0},{8,4},{12,8},{16,12},{20,16},{24,20},{28,24},{1,29},{... | collective-permute-start | bytes 2064392 | tf_op jit(solution)/shard_map/ppermute | solution.py:35
  7.1 5.0 %routed_grad.1 = bf16[1024,256]{1,0:T(8,128)(2,1)} custom-call(f32[8,1024]{1,0:T(8,128)} %bitcast.50, f32[8,1024]{1,0:T(8,128)} %bitcast.51, s32[8,1024]{1,0:T(8,128)} %bitcast.52), custom_call_target="tpu_custom_call" | custom-call | tf_op jit(solution)/shard_map/routed_grad/pallas_call | solution.py:136
  12.2 2.3 %slice.11 = bf16[4,80,1792]{2,1,0:T(8,128)(2,1)} slice(bf16[4,256,1792]{2,1,0:T(8,128)(2,1)} %bitcast.40), slice={[0:4], [48:128], [0:1792]} | slice | bytes 2293760 | tf_op jit(solution)/shard_map/slice | solution.py:292
  15.1 2.8 %fusion = (bf16[4,64,1792]{2,1,0:T(8,128)(2,1)}, bf16[4,64,1792]{2,1,0:T(8,128)(2,1)}) fusion(bf16[4,256,1792]{2,1,0:T(8,128)(2,1)} %bitcast.41), kind=kLoop, calls=%fused_computation.2 | loop fusion | bytes 3670016 | tf_op jit(solution)/shard_map/slice | solution.py:292
  17.9 5.1 %collective-permute-done.rows_ref = bf16[4,48,1792]{2,1,0:T(8,128)(2,1)S(1)} collective-permute-done((bf16[4,48,1792]{2,1,0:T(8,128)(2,1)S(1)}, bf16[4,48,1792]{2,1,0:T(8,128)(2,1)S(1)}, u32[]{:S(2)}, u32[]{:S(2)}) %collective-permute-start) | collective-permute-done | bytes 688160 | tf_op jit(solution)/shard_map/ppermute | solution.py:35
  23.0 5.2 %collective-permute-start.8 = (bf16[4,64,1792]{2,1,0:T(8,128)(2,1)}, bf16[4,64,1792]{2,1,0:T(8,128)(2,1)S(1)}, u32[]{:S(2)}, u32[]{:S(2)}) collective-permute-start(bf16[4,64,1792]{2,1,0:T(8,128)(2,1)} %get-tuple-element.73), channel_id=1, source_target_pairs={{0,28},{4,0},{8,4},{12,8},{16,12},{20,16},{24,20},{28,24},{1,29},{... | collective-permute-start | bytes 2752520 | tf_op jit(solution)/shard_map/ppermute | solution.py:35
  28.2 4.1 %first_product.4 = (bf16[48,1024]{1,0:T(8,128)(2,1)S(1)}, bf16[48,1024]{1,0:T(8,128)(2,1)S(1)}, bf16[48,1024]{1,0:T(8,128)(2,1)S(1)}, bf16[48,1024]{1,0:T(8,128)(2,1)S(1)}) custom-call(s32[1]{0:T(128)} %bitcast.me_ref, bf16[4,48,1792]{2,1,0:T(8,128)(2,1)S(1)} %collective-permute-done.rows_ref, bf16[1024,1792]{1,0:T(8,128)(2,1)} %bitcast.19), custom_call_target="tpu_custom_call" | custom-call | tf_op jit(solution)/shard_map/first_product/pallas_call | solution.py:160
  32.3 1.6 collective-permute-start.3
  35.3 1.5 collective-permute-done.2.refs_1_
  42.3 5.4 %collective-permute-done.1.rows_ref = bf16[4,80,1792]{2,1,0:T(8,128)(2,1)S(1)} collective-permute-done((bf16[4,80,1792]{2,1,0:T(8,128)(2,1)}, bf16[4,80,1792]{2,1,0:T(8,128)(2,1)S(1)}, u32[]{:S(2)}, u32[]{:S(2)}) %collective-permute-start.1) | collective-permute-done | bytes 1146912 | tf_op jit(solution)/shard_map/ppermute | solution.py:35
  47.7 2.1 %first_product.5 = (bf16[80,1024]{1,0:T(8,128)(2,1)S(1)}, bf16[80,1024]{1,0:T(8,128)(2,1)S(1)}, bf16[80,1024]{1,0:T(8,128)(2,1)S(1)}, bf16[80,1024]{1,0:T(8,128)(2,1)S(1)}) custom-call(s32[1]{0:T(128)} %bitcast.me_ref, bf16[4,80,1792]{2,1,0:T(8,128)(2,1)S(1)} %collective-permute-done.1.rows_ref, bf16[1024,1792]{1,0:T(8,128)(2,1)S(1)} %bitcast.20), custom_call_target="tpu_custom_call" | custom-call | tf_op jit(solution)/shard_map/first_product/pallas_call | solution.py:160
  49.9 5.1 %collective-permute-start.15 = (bf16[4,64,1792]{2,1,0:T(8,128)(2,1)S(1)}, bf16[4,64,1792]{2,1,0:T(8,128)(2,1)S(1)}, u32[]{:S(2)}, u32[]{:S(2)}) collective-permute-start(bf16[4,64,1792]{2,1,0:T(8,128)(2,1)S(1)} %copy-done.3), channel_id=1, source_target_pairs={{0,28},{4,0},{8,4},{12,8},{16,12},{20,16},{24,20},{28,24},{1,29},{... | collective-permute-start | bytes 2752520 | tf_op jit(solution)/shard_map/ppermute | solution.py:35
  55.0 1.5 collective-permute-start.10
  57.1 7.2 %second_product.4 = bf16[4,48,1792]{2,1,0:T(8,128)(2,1)S(1)} custom-call(s32[1]{0:T(128)} %bitcast.me_ref, bf16[4,256,256]{2,1,0:T(8,128)(2,1)S(1)} %bitcast.27, bf16[1792,1024]{1,0:T(8,128)(2,1)} %bitcast.31, bf16[1792,1024]{1,0:T(8,128)(2,1)} %bitcast.35, bf16[1792,256]{1,0:T(8,128)(2,1)S(1)} %bitcast.23, bf16[48,2048]{1,0:T(8,128)(2,1)S(1)} %activation.4.refs_0_, ...), custom_call_target="tpu_custom_call" | custom-call | tf_op jit(solution)/shard_map/second_product/pallas_call | solution.py:242
  64.3 3.0 %collective-permute-done.8.rows_ref = bf16[4,64,1792]{2,1,0:T(8,128)(2,1)S(1)} collective-permute-done((bf16[4,64,1792]{2,1,0:T(8,128)(2,1)}, bf16[4,64,1792]{2,1,0:T(8,128)(2,1)S(1)}, u32[]{:S(2)}, u32[]{:S(2)}) %collective-permute-start.8) | collective-permute-done | bytes 917536 | tf_op jit(solution)/shard_map/ppermute | solution.py:35
  67.3 1.5 activation.5.refs_0_
  68.8 1.6 collective-permute-start.12
  70.4 1.9 %first_product.6 = (bf16[64,1024]{1,0:T(8,128)(2,1)S(1)}, bf16[64,1024]{1,0:T(8,128)(2,1)S(1)}, bf16[64,1024]{1,0:T(8,128)(2,1)S(1)}, bf16[64,1024]{1,0:T(8,128)(2,1)S(1)}) custom-call(s32[1]{0:T(128)} %bitcast.me_ref, bf16[4,64,1792]{2,1,0:T(8,128)(2,1)S(1)} %collective-permute-done.8.rows_ref, bf16[1024,1792]{1,0:T(8,128)(2,1)S(1)} %bitcast.21), custom_call_target="tpu_custom_call" | custom-call | tf_op jit(solution)/shard_map/first_product/pallas_call | solution.py:160
  72.3 4.3 %collective-permute-done.12.refs_2_ = bf16[80,2048]{1,0:T(8,128)(2,1)S(1)} collective-permute-done((bf16[80,2048]{1,0:T(8,128)(2,1)S(1)}, bf16[80,2048]{1,0:T(8,128)(2,1)S(1)}, u32[]{:S(2)}, u32[]{:S(2)}) %collective-permute-start.12) | collective-permute-done | bytes 327712 | tf_op jit(solution)/shard_map/ppermute | solution.py:40
  79.3 5.1 %collective-permute-start.22 = (bf16[4,48,1792]{2,1,0:T(8,128)(2,1)S(1)}, bf16[4,48,1792]{2,1,0:T(8,128)(2,1)S(1)}, u32[]{:S(2)}, u32[]{:S(2)}) collective-permute-start(bf16[4,48,1792]{2,1,0:T(8,128)(2,1)S(1)} %second_product.4), channel_id=1, source_target_pairs={{0,28},{4,0},{8,4},{12,8},{16,12},{20,16},{24,20},{28,24},{1,29},{... | collective-permute-start | bytes 2064392 | tf_op jit(solution)/shard_map/ppermute | solution.py:35
  84.4 7.4 %second_product.5 = bf16[4,80,1792]{2,1,0:T(8,128)(2,1)S(1)} custom-call(s32[1]{0:T(128)} %bitcast.me_ref, bf16[4,256,256]{2,1,0:T(8,128)(2,1)S(1)} %bitcast.28, bf16[1792,1024]{1,0:T(8,128)(2,1)} %bitcast.32, bf16[1792,1024]{1,0:T(8,128)(2,1)} %bitcast.36, bf16[1792,256]{1,0:T(8,128)(2,1)S(1)} %bitcast.24, bf16[80,2048]{1,0:T(8,128)(2,1)S(1)} %activation.5.refs_0_, ...), custom_call_target="tpu_custom_call" | custom-call | tf_op jit(solution)/shard_map/second_product/pallas_call | solution.py:242
  95.1 1.8 %first_product.7 = (bf16[64,1024]{1,0:T(8,128)(2,1)S(1)}, bf16[64,1024]{1,0:T(8,128)(2,1)S(1)}, bf16[64,1024]{1,0:T(8,128)(2,1)S(1)}, bf16[64,1024]{1,0:T(8,128)(2,1)S(1)}) custom-call(s32[1]{0:T(128)} %bitcast.me_ref, bf16[4,64,1792]{2,1,0:T(8,128)(2,1)S(1)} %collective-permute-done.15.rows_ref, bf16[1024,1792]{1,0:T(8,128)(2,1)S(1)} %bitcast.22), custom_call_target="tpu_custom_call" | custom-call | tf_op jit(solution)/shard_map/first_product/pallas_call | solution.py:160
  96.9 3.8 %collective-permute-done.19.refs_2_ = bf16[64,2048]{1,0:T(8,128)(2,1)S(1)} collective-permute-done((bf16[64,2048]{1,0:T(8,128)(2,1)S(1)}, bf16[64,2048]{1,0:T(8,128)(2,1)S(1)}, u32[]{:S(2)}, u32[]{:S(2)}) %collective-permute-start.19) | collective-permute-done | bytes 262176 | tf_op jit(solution)/shard_map/ppermute | solution.py:40
  103.1 7.0 %second_product.6 = bf16[4,64,1792]{2,1,0:T(8,128)(2,1)S(1)} custom-call(s32[1]{0:T(128)} %bitcast.me_ref, bf16[4,256,256]{2,1,0:T(8,128)(2,1)S(1)} %bitcast.29, bf16[1792,1024]{1,0:T(8,128)(2,1)} %bitcast.33, bf16[1792,1024]{1,0:T(8,128)(2,1)} %bitcast.37, bf16[1792,256]{1,0:T(8,128)(2,1)S(1)} %bitcast.25, bf16[64,2048]{1,0:T(8,128)(2,1)S(1)} %activation.6.refs_0_, ...), custom_call_target="tpu_custom_call" | custom-call | tf_op jit(solution)/shard_map/second_product/pallas_call | solution.py:242
  113.1 6.5 %collective-permute-done.27.refs_2_ = bf16[64,2048]{1,0:T(8,128)(2,1)S(1)} collective-permute-done((bf16[64,2048]{1,0:T(8,128)(2,1)S(1)}, bf16[64,2048]{1,0:T(8,128)(2,1)S(1)}, u32[]{:S(2)}, u32[]{:S(2)}) %collective-permute-start.27) | collective-permute-done | bytes 262176 | tf_op jit(solution)/shard_map/ppermute | solution.py:40
  121.1 5.1 %collective-permute-done.29 = bf16[4,80,1792]{2,1,0:T(8,128)(2,1)S(1)} collective-permute-done((bf16[4,80,1792]{2,1,0:T(8,128)(2,1)S(1)}, bf16[4,80,1792]{2,1,0:T(8,128)(2,1)S(1)}, u32[]{:S(2)}, u32[]{:S(2)}) %collective-permute-start.29) | collective-permute-done | bytes 1146912 | tf_op jit(solution)/shard_map/ppermute | solution.py:35
  126.2 7.1 %second_product.7 = (bf16[4,48,1792]{2,1,0:T(8,128)(2,1)S(1)}, bf16[4,16,1792]{2,1,0:T(8,128)(2,1)S(1)}) custom-call(s32[1]{0:T(128)} %bitcast.me_ref, bf16[4,256,256]{2,1,0:T(8,128)(2,1)S(1)} %bitcast.30, bf16[1792,1024]{1,0:T(8,128)(2,1)} %bitcast.34, bf16[1792,1024]{1,0:T(8,128)(2,1)} %bitcast.38, bf16[1792,256]{1,0:T(8,128)(2,1)S(1)} %bitcast.26, ...), custom_call_target="tpu_custom_call" | custom-call | tf_op jit(solution)/shard_map/second_product/pallas_call | solution.py:242
  133.3 5.2 %collective-permute-start.32 = (bf16[4,48,1792]{2,1,0:T(8,128)(2,1)S(1)}, bf16[4,48,1792]{2,1,0:T(8,128)(2,1)S(1)}, u32[]{:S(2)}, u32[]{:S(2)}) collective-permute-start(bf16[4,48,1792]{2,1,0:T(8,128)(2,1)S(1)} %get-tuple-element.105), channel_id=1, source_target_pairs={{0,28},{4,0},{8,4},{12,8},{16,12},{20,16},{24,20},{28,24},{1,29},{... | collective-permute-start | bytes 2064392 | tf_op jit(solution)/shard_map/ppermute | solution.py:35
  138.5 2.1 %dynamic_update_slice.9 = bf16[4,256,1792]{2,1,0:T(8,128)(2,1)} pad(bf16[4,48,1792]{2,1,0:T(8,128)(2,1)S(1)} %collective-permute-done.22, bf16[]{:T(256)} %constant.1.clone.1), padding=0_0x0_208x0_0 | pad | bytes 4358146 | tf_op jit(solution)/shard_map/dynamic_update_slice | solution.py:338
  141.9 2.7 %collective-permute-start.30 = (bf16[4,16,1792]{2,1,0:T(8,128)(2,1)S(1)}, bf16[4,16,1792]{2,1,0:T(8,128)(2,1)S(1)}, u32[]{:S(2)}, u32[]{:S(2)}) collective-permute-start(bf16[4,16,1792]{2,1,0:T(8,128)(2,1)S(1)} %get-tuple-element.102), channel_id=1, source_target_pairs={{0,28},{1,29},{2,30},{3,31}} | collective-permute-start | bytes 688136 | tf_op jit(solution)/shard_map/ppermute | solution.py:343
  146.8 13.8 %collective-permute-done.32.source = bf16[4,48,1792]{2,1,0:T(8,128)(2,1)S(1)} collective-permute-done((bf16[4,48,1792]{2,1,0:T(8,128)(2,1)S(1)}, bf16[4,48,1792]{2,1,0:T(8,128)(2,1)S(1)}, u32[]{:S(2)}, u32[]{:S(2)}) %collective-permute-start.32) | collective-permute-done | bytes 688160 | tf_op jit(solution)/shard_map/ppermute | solution.py:35
  162.8 1.6 collective-permute-done.30.source
  (66 shorter events, 27.8 us)
Async XLA Ops:
  1.1 21.9 %collective-permute-start = (bf16[4,48,1792]{2,1,0:T(8,128)(2,1)S(1)}, bf16[4,48,1792]{2,1,0:T(8,128)(2,1)S(1)}, u32[]{:S(2)}, u32[]{:S(2)}) collective-permute-start(bf16[4,48,1792]{2,1,0:T(8,128)(2,1)S(1)} %take_rows.1), channel_id=1, source_target_pairs={{0,28},{4,0},{8,4},{12,8},{16,12},{20,16},{24,20},{28,24},{1,29},{... | collective-permute-start | bytes 2064392 | tf_op jit(solution)/shard_map/ppermute | solution.py:35
  14.5 33.1 %collective-permute-start.1 = (bf16[4,80,1792]{2,1,0:T(8,128)(2,1)}, bf16[4,80,1792]{2,1,0:T(8,128)(2,1)S(1)}, u32[]{:S(2)}, u32[]{:S(2)}) collective-permute-start(bf16[4,80,1792]{2,1,0:T(8,128)(2,1)} %slice.11), channel_id=1, source_target_pairs={{0,28},{4,0},{8,4},{12,8},{16,12},{20,16},{24,20},{28,24},{1,29},{... | collective-permute-start | bytes 3440648 | tf_op jit(solution)/shard_map/ppermute | solution.py:35
  23.0 44.3 %collective-permute-start.8 = (bf16[4,64,1792]{2,1,0:T(8,128)(2,1)}, bf16[4,64,1792]{2,1,0:T(8,128)(2,1)S(1)}, u32[]{:S(2)}, u32[]{:S(2)}) collective-permute-start(bf16[4,64,1792]{2,1,0:T(8,128)(2,1)} %get-tuple-element.73), channel_id=1, source_target_pairs={{0,28},{4,0},{8,4},{12,8},{16,12},{20,16},{24,20},{28,24},{1,29},{... | collective-permute-start | bytes 2752520 | tf_op jit(solution)/shard_map/ppermute | solution.py:35
  32.3 4.5 %collective-permute-start.2 = (bf16[48,1024]{1,0:T(8,128)(2,1)S(1)}, bf16[48,1024]{1,0:T(8,128)(2,1)S(1)}, u32[]{:S(2)}, u32[]{:S(2)}) collective-permute-start(bf16[48,1024]{1,0:T(8,128)(2,1)S(1)} %get-tuple-element.65), channel_id=1, source_target_pairs={{0,1},{1,2},{2,3},{3,0},{4,5},{5,6},{6,7},{7,4},{8,9},{9,10},{10,1... | collective-permute-start | bytes 294920 | tf_op jit(solution)/shard_map/ppermute | solution.py:40
  32.3 5.7 %collective-permute-start.3 = (bf16[48,1024]{1,0:T(8,128)(2,1)S(1)}, bf16[48,1024]{1,0:T(8,128)(2,1)S(1)}, u32[]{:S(2)}, u32[]{:S(2)}) collective-permute-start(bf16[48,1024]{1,0:T(8,128)(2,1)S(1)} %get-tuple-element.66), channel_id=1, source_target_pairs={{0,2},{1,3},{2,0},{3,1},{4,6},{5,7},{6,4},{7,5},{8,10},{9,11},{10,... | collective-permute-start | bytes 294920 | tf_op jit(solution)/shard_map/ppermute | solution.py:40
  33.9 4.6 %collective-permute-start.4 = (bf16[48,1024]{1,0:T(8,128)(2,1)S(1)}, bf16[48,1024]{1,0:T(8,128)(2,1)S(1)}, u32[]{:S(2)}, u32[]{:S(2)}) collective-permute-start(bf16[48,1024]{1,0:T(8,128)(2,1)S(1)} %get-tuple-element.67), channel_id=1, source_target_pairs={{0,3},{1,0},{2,1},{3,2},{4,7},{5,4},{6,5},{7,6},{8,11},{9,8},{10,9... | collective-permute-start | bytes 294920 | tf_op jit(solution)/shard_map/ppermute | solution.py:40
  39.9 9.9 %collective-permute-start.5 = (bf16[48,2048]{1,0:T(8,128)(2,1)S(1)}, bf16[48,2048]{1,0:T(8,128)(2,1)S(1)}, u32[]{:S(2)}, u32[]{:S(2)}) collective-permute-start(bf16[48,2048]{1,0:T(8,128)(2,1)S(1)} %activation.4.refs_0_), channel_id=1, source_target_pairs={{0,2},{1,3},{2,0},{3,1},{4,6},{5,7},{6,4},{7,5},{8,10},{9,11},{10,... | collective-permute-start | bytes 589832 | tf_op jit(solution)/shard_map/ppermute | solution.py:40
  41.0 15.6 %collective-permute-start.6 = (bf16[48,2048]{1,0:T(8,128)(2,1)S(1)}, bf16[48,2048]{1,0:T(8,128)(2,1)S(1)}, u32[]{:S(2)}, u32[]{:S(2)}) collective-permute-start(bf16[48,2048]{1,0:T(8,128)(2,1)S(1)} %activation.4.refs_0_), channel_id=1, source_target_pairs={{0,1},{1,0},{2,3},{3,2},{4,5},{5,4},{6,7},{7,6},{8,9},{9,8},{10,11... | collective-permute-start | bytes 589832 | tf_op jit(solution)/shard_map/ppermute | solution.py:45
  49.8 6.8 %collective-permute-start.7 = (bf16[48,2048]{1,0:T(8,128)(2,1)S(1)}, bf16[48,2048]{1,0:T(8,128)(2,1)S(1)}, u32[]{:S(2)}, u32[]{:S(2)}) collective-permute-start(bf16[48,2048]{1,0:T(8,128)(2,1)S(1)} %collective-permute-done.5.refs_2_), channel_id=1, source_target_pairs={{0,1},{1,0},{2,3},{3,2},{4,5},{5,4},{6,7},{7,6},{8,9},{9,8},{10,11... | collective-permute-start | bytes 589832 | tf_op jit(solution)/shard_map/ppermute | solution.py:45
  49.9 41.9 %collective-permute-start.15 = (bf16[4,64,1792]{2,1,0:T(8,128)(2,1)S(1)}, bf16[4,64,1792]{2,1,0:T(8,128)(2,1)S(1)}, u32[]{:S(2)}, u32[]{:S(2)}) collective-permute-start(bf16[4,64,1792]{2,1,0:T(8,128)(2,1)S(1)} %copy-done.3), channel_id=1, source_target_pairs={{0,28},{4,0},{8,4},{12,8},{16,12},{20,16},{24,20},{28,24},{1,29},{... | collective-permute-start | bytes 2752520 | tf_op jit(solution)/shard_map/ppermute | solution.py:35
  55.0 12.3 %collective-permute-start.10 = (bf16[80,1024]{1,0:T(8,128)(2,1)S(1)}, bf16[80,1024]{1,0:T(8,128)(2,1)S(1)}, u32[]{:S(2)}, u32[]{:S(2)}) collective-permute-start(bf16[80,1024]{1,0:T(8,128)(2,1)S(1)} %get-tuple-element.77), channel_id=1, source_target_pairs={{0,2},{1,3},{2,0},{3,1},{4,6},{5,7},{6,4},{7,5},{8,10},{9,11},{10,... | collective-permute-start | bytes 491528 | tf_op jit(solution)/shard_map/ppermute | solution.py:40
  56.5 10.8 %collective-permute-start.11 = (bf16[80,1024]{1,0:T(8,128)(2,1)S(1)}, bf16[80,1024]{1,0:T(8,128)(2,1)S(1)}, u32[]{:S(2)}, u32[]{:S(2)}) collective-permute-start(bf16[80,1024]{1,0:T(8,128)(2,1)S(1)} %get-tuple-element.78), channel_id=1, source_target_pairs={{0,3},{1,0},{2,1},{3,2},{4,7},{5,4},{6,5},{7,6},{8,11},{9,8},{10,9... | collective-permute-start | bytes 491528 | tf_op jit(solution)/shard_map/ppermute | solution.py:40
  56.5 10.8 %collective-permute-start.9 = (bf16[80,1024]{1,0:T(8,128)(2,1)S(1)}, bf16[80,1024]{1,0:T(8,128)(2,1)S(1)}, u32[]{:S(2)}, u32[]{:S(2)}) collective-permute-start(bf16[80,1024]{1,0:T(8,128)(2,1)S(1)} %get-tuple-element.76), channel_id=1, source_target_pairs={{0,1},{1,2},{2,3},{3,0},{4,5},{5,6},{6,7},{7,4},{8,9},{9,10},{10,1... | collective-permute-start | bytes 491528 | tf_op jit(solution)/shard_map/ppermute | solution.py:40
  68.8 7.8 %collective-permute-start.12 = (bf16[80,2048]{1,0:T(8,128)(2,1)S(1)}, bf16[80,2048]{1,0:T(8,128)(2,1)S(1)}, u32[]{:S(2)}, u32[]{:S(2)}) collective-permute-start(bf16[80,2048]{1,0:T(8,128)(2,1)S(1)} %activation.5.refs_0_), channel_id=1, source_target_pairs={{0,2},{1,3},{2,0},{3,1},{4,6},{5,7},{6,4},{7,5},{8,10},{9,11},{10,... | collective-permute-start | bytes 983048 | tf_op jit(solution)/shard_map/ppermute | solution.py:40
  70.4 8.0 %collective-permute-start.13 = (bf16[80,2048]{1,0:T(8,128)(2,1)S(1)}, bf16[80,2048]{1,0:T(8,128)(2,1)S(1)}, u32[]{:S(2)}, u32[]{:S(2)}) collective-permute-start(bf16[80,2048]{1,0:T(8,128)(2,1)S(1)} %activation.5.refs_0_), channel_id=1, source_target_pairs={{0,1},{1,0},{2,3},{3,2},{4,5},{5,4},{6,7},{7,6},{8,9},{9,8},{10,11... | collective-permute-start | bytes 983048 | tf_op jit(solution)/shard_map/ppermute | solution.py:45
  76.6 2.7 %collective-permute-start.14 = (bf16[80,2048]{1,0:T(8,128)(2,1)S(1)}, bf16[80,2048]{1,0:T(8,128)(2,1)S(1)}, u32[]{:S(2)}, u32[]{:S(2)}) collective-permute-start(bf16[80,2048]{1,0:T(8,128)(2,1)S(1)} %collective-permute-done.12.refs_2_), channel_id=1, source_target_pairs={{0,1},{1,0},{2,3},{3,2},{4,5},{5,4},{6,7},{7,6},{8,9},{9,8},{10,11... | collective-permute-start | bytes 983048 | tf_op jit(solution)/shard_map/ppermute | solution.py:45
  76.6 15.2 %collective-permute-start.16 = (bf16[64,1024]{1,0:T(8,128)(2,1)S(1)}, bf16[64,1024]{1,0:T(8,128)(2,1)S(1)}, u32[]{:S(2)}, u32[]{:S(2)}) collective-permute-start(bf16[64,1024]{1,0:T(8,128)(2,1)S(1)} %get-tuple-element.87), channel_id=1, source_target_pairs={{0,1},{1,2},{2,3},{3,0},{4,5},{5,6},{6,7},{7,4},{8,9},{9,10},{10,1... | collective-permute-start | bytes 393224 | tf_op jit(solution)/shard_map/ppermute | solution.py:40
  77.1 14.7 %collective-permute-start.17 = (bf16[64,1024]{1,0:T(8,128)(2,1)S(1)}, bf16[64,1024]{1,0:T(8,128)(2,1)S(1)}, u32[]{:S(2)}, u32[]{:S(2)}) collective-permute-start(bf16[64,1024]{1,0:T(8,128)(2,1)S(1)} %get-tuple-element.88), channel_id=1, source_target_pairs={{0,2},{1,3},{2,0},{3,1},{4,6},{5,7},{6,4},{7,5},{8,10},{9,11},{10,... | collective-permute-start | bytes 393224 | tf_op jit(solution)/shard_map/ppermute | solution.py:40
  78.3 13.4 %collective-permute-start.18 = (bf16[64,1024]{1,0:T(8,128)(2,1)S(1)}, bf16[64,1024]{1,0:T(8,128)(2,1)S(1)}, u32[]{:S(2)}, u32[]{:S(2)}) collective-permute-start(bf16[64,1024]{1,0:T(8,128)(2,1)S(1)} %get-tuple-element.89), channel_id=1, source_target_pairs={{0,3},{1,0},{2,1},{3,2},{4,7},{5,4},{6,5},{7,6},{8,11},{9,8},{10,9... | collective-permute-start | bytes 393224 | tf_op jit(solution)/shard_map/ppermute | solution.py:40
  79.3 30.9 %collective-permute-start.22 = (bf16[4,48,1792]{2,1,0:T(8,128)(2,1)S(1)}, bf16[4,48,1792]{2,1,0:T(8,128)(2,1)S(1)}, u32[]{:S(2)}, u32[]{:S(2)}) collective-permute-start(bf16[4,48,1792]{2,1,0:T(8,128)(2,1)S(1)} %second_product.4), channel_id=1, source_target_pairs={{0,28},{4,0},{8,4},{12,8},{16,12},{20,16},{24,20},{28,24},{1,29},{... | collective-permute-start | bytes 2064392 | tf_op jit(solution)/shard_map/ppermute | solution.py:35
  93.2 7.5 %collective-permute-start.19 = (bf16[64,2048]{1,0:T(8,128)(2,1)S(1)}, bf16[64,2048]{1,0:T(8,128)(2,1)S(1)}, u32[]{:S(2)}, u32[]{:S(2)}) collective-permute-start(bf16[64,2048]{1,0:T(8,128)(2,1)S(1)} %activation.6.refs_0_), channel_id=1, source_target_pairs={{0,2},{1,3},{2,0},{3,1},{4,6},{5,7},{6,4},{7,5},{8,10},{9,11},{10,... | collective-permute-start | bytes 786440 | tf_op jit(solution)/shard_map/ppermute | solution.py:40
  93.8 32.4 %collective-permute-start.29 = (bf16[4,80,1792]{2,1,0:T(8,128)(2,1)S(1)}, bf16[4,80,1792]{2,1,0:T(8,128)(2,1)S(1)}, u32[]{:S(2)}, u32[]{:S(2)}) collective-permute-start(bf16[4,80,1792]{2,1,0:T(8,128)(2,1)S(1)} %second_product.5), channel_id=1, source_target_pairs={{0,28},{4,0},{8,4},{12,8},{16,12},{20,16},{24,20},{28,24},{1,29},{... | collective-permute-start | bytes 3440648 | tf_op jit(solution)/shard_map/ppermute | solution.py:35
  95.1 6.2 %collective-permute-start.20 = (bf16[64,2048]{1,0:T(8,128)(2,1)S(1)}, bf16[64,2048]{1,0:T(8,128)(2,1)S(1)}, u32[]{:S(2)}, u32[]{:S(2)}) collective-permute-start(bf16[64,2048]{1,0:T(8,128)(2,1)S(1)} %activation.6.refs_0_), channel_id=1, source_target_pairs={{0,1},{1,0},{2,3},{3,2},{4,5},{5,4},{6,7},{7,6},{8,9},{9,8},{10,11... | collective-permute-start | bytes 786440 | tf_op jit(solution)/shard_map/ppermute | solution.py:45
  100.7 9.4 %collective-permute-start.23 = (bf16[64,1024]{1,0:T(8,128)(2,1)S(1)}, bf16[64,1024]{1,0:T(8,128)(2,1)S(1)}, u32[]{:S(2)}, u32[]{:S(2)}) collective-permute-start(bf16[64,1024]{1,0:T(8,128)(2,1)S(1)} %get-tuple-element.97), channel_id=1, source_target_pairs={{0,1},{1,2},{2,3},{3,0},{4,5},{5,6},{6,7},{7,4},{8,9},{9,10},{10,1... | collective-permute-start | bytes 393224 | tf_op jit(solution)/shard_map/ppermute | solution.py:40
  101.3 8.9 %collective-permute-start.24 = (bf16[64,1024]{1,0:T(8,128)(2,1)S(1)}, bf16[64,1024]{1,0:T(8,128)(2,1)S(1)}, u32[]{:S(2)}, u32[]{:S(2)}) collective-permute-start(bf16[64,1024]{1,0:T(8,128)(2,1)S(1)} %get-tuple-element.98), channel_id=1, source_target_pairs={{0,2},{1,3},{2,0},{3,1},{4,6},{5,7},{6,4},{7,5},{8,10},{9,11},{10,... | collective-permute-start | bytes 393224 | tf_op jit(solution)/shard_map/ppermute | solution.py:40
  102.3 7.9 %collective-permute-start.25 = (bf16[64,1024]{1,0:T(8,128)(2,1)S(1)}, bf16[64,1024]{1,0:T(8,128)(2,1)S(1)}, u32[]{:S(2)}, u32[]{:S(2)}) collective-permute-start(bf16[64,1024]{1,0:T(8,128)(2,1)S(1)} %get-tuple-element.99), channel_id=1, source_target_pairs={{0,3},{1,0},{2,1},{3,2},{4,7},{5,4},{6,5},{7,6},{8,11},{9,8},{10,9... | collective-permute-start | bytes 393224 | tf_op jit(solution)/shard_map/ppermute | solution.py:40
  111.6 7.9 %collective-permute-start.27 = (bf16[64,2048]{1,0:T(8,128)(2,1)S(1)}, bf16[64,2048]{1,0:T(8,128)(2,1)S(1)}, u32[]{:S(2)}, u32[]{:S(2)}) collective-permute-start(bf16[64,2048]{1,0:T(8,128)(2,1)S(1)} %activation.7.refs_0_), channel_id=1, source_target_pairs={{0,2},{1,3},{2,0},{3,1},{4,6},{5,7},{6,4},{7,5},{8,10},{9,11},{10,... | collective-permute-start | bytes 786440 | tf_op jit(solution)/shard_map/ppermute | solution.py:40
  112.8 33.1 %collective-permute-start.33 = (bf16[4,64,1792]{2,1,0:T(8,128)(2,1)S(1)}, bf16[4,64,1792]{2,1,0:T(8,128)(2,1)S(1)}, u32[]{:S(2)}, u32[]{:S(2)}) collective-permute-start(bf16[4,64,1792]{2,1,0:T(8,128)(2,1)S(1)} %second_product.6), channel_id=1, source_target_pairs={{0,28},{4,0},{8,4},{12,8},{16,12},{20,16},{24,20},{28,24},{1,29},{... | collective-permute-start | bytes 2752520 | tf_op jit(solution)/shard_map/ppermute | solution.py:35
  119.6 6.6 %collective-permute-start.26 = (bf16[64,2048]{1,0:T(8,128)(2,1)S(1)}, bf16[64,2048]{1,0:T(8,128)(2,1)S(1)}, u32[]{:S(2)}, u32[]{:S(2)}) collective-permute-start(bf16[64,2048]{1,0:T(8,128)(2,1)S(1)} %activation.7.refs_0_), channel_id=1, source_target_pairs={{0,1},{1,0},{2,3},{3,2},{4,5},{5,4},{6,7},{7,6},{8,9},{9,8},{10,11... | collective-permute-start | bytes 786440 | tf_op jit(solution)/shard_map/ppermute | solution.py:45
  133.3 27.3 %collective-permute-start.32 = (bf16[4,48,1792]{2,1,0:T(8,128)(2,1)S(1)}, bf16[4,48,1792]{2,1,0:T(8,128)(2,1)S(1)}, u32[]{:S(2)}, u32[]{:S(2)}) collective-permute-start(bf16[4,48,1792]{2,1,0:T(8,128)(2,1)S(1)} %get-tuple-element.105), channel_id=1, source_target_pairs={{0,28},{4,0},{8,4},{12,8},{16,12},{20,16},{24,20},{28,24},{1,29},{... | collective-permute-start | bytes 2064392 | tf_op jit(solution)/shard_map/ppermute | solution.py:35
  140.6 21.5 %collective-permute-start.31 = (bf16[4,16,1792]{2,1,0:T(8,128)(2,1)S(1)}, bf16[4,16,1792]{2,1,0:T(8,128)(2,1)S(1)}, u32[]{:S(2)}, u32[]{:S(2)}) collective-permute-start(bf16[4,16,1792]{2,1,0:T(8,128)(2,1)S(1)} %get-tuple-element.102), channel_id=1, source_target_pairs={{4,0},{8,4},{12,8},{16,12},{20,16},{24,20},{28,24},{5,1},{9,5},{13... | collective-permute-start | bytes 688136 | tf_op jit(solution)/shard_map/ppermute | solution.py:342
  141.9 22.5 %collective-permute-start.30 = (bf16[4,16,1792]{2,1,0:T(8,128)(2,1)S(1)}, bf16[4,16,1792]{2,1,0:T(8,128)(2,1)S(1)}, u32[]{:S(2)}, u32[]{:S(2)}) collective-permute-start(bf16[4,16,1792]{2,1,0:T(8,128)(2,1)S(1)} %get-tuple-element.102), channel_id=1, source_target_pairs={{0,28},{1,29},{2,30},{3,31}} | collective-permute-start | bytes 688136 | tf_op jit(solution)/shard_map/ppermute | solution.py:343
  (6 other events, 89.9 us)

commit v10 on v9

--- a/solution.py
+++ b/solution.py
@@ -131,7 +131,7 @@
 
 def routed_grad(grad, scores, chosen, n_experts):
     tokens, top = grad.shape
-    block = block_of(tokens, 128)
+    block = block_of(tokens, 512)
     spec = pl.BlockSpec((top, block), lambda i: (0, i))
     return pl.pallas_call(
         routed_kernel,

time: 165 us -> 165 us (level)
  Pallas kernels: 51.9 us -> 49.5 us
  waiting for transfers between devices: 53.9 us -> 56.2 us
    pallas_call x1, Pallas kernels: 5.05 us -> 2.67 us  [routed_grad(): pl.pallas_call(routed_kernel, out_shape=jax.ShapeDtypeStruct((tokens, n_e...]
    ppermute x8, waiting for transfers between devices: 32.6 us -> 35 us  [back_one(): lax.ppermute(x, 'pipe', [(i, (i - 1) % length) for i in range(length)])]
  transfers between devices with their start and end apart: 34 -> 34, of which waited for: 16 -> 16; matrix products, arithmetic and copies ran while one was open for 6% -> 6% of each run, Pallas kernels for 31% -> 29%
where the time goes in v10:
time: 165 us; the launch traced here: 164 us
  waiting for transfers between devices  56.2 us (34%)
  Pallas kernels  49.5 us (30%)
  starting transfers between devices  49.1 us (30%)
  local copies, waits for them, and re-layouts  9.31 us (6%)
    ppermute x8, waiting for transfers between devices, back_one(): lax.ppermute(x, 'pipe', [(i, (i - 1) % length) for i in range(length)])  35 us
    ppermute x8, starting transfers between devices, back_one(): lax.ppermute(x, 'pipe', [(i, (i - 1) % length) for i in range(length)])  28.8 us
    pallas_call x4, Pallas kernels, second_product(): pl.pallas_call(functools.partial(second_kernel, n, start), out_shape=[jax...  28.7 us
    ppermute x16, waiting for transfers between devices, to_expert(): return lax.ppermute(x, 'expert', [(i, (i + by) % n) for i in range(n)])  17.9 us
    ppermute x16, starting transfers between devices, to_expert(): return lax.ppermute(x, 'expert', [(i, (i + by) % n) for i in range(n)])  14.5 us
    pallas_call x4, Pallas kernels, first_product(): pl.pallas_call(functools.partial(first_kernel, n), out_shape=[jax.ShapeDt...  9.85 us
    pallas_call x4, Pallas kernels, activation(): pl.pallas_call(functools.partial(activation_kernel, start), out_shape=jax...  5.61 us
    slice x2, local copies, waits for them, and re-layouts, shards(): piece = grads[:, starts[c]:starts[c] + sizes[c]]  5.15 us
  transfers between devices with their start and end apart: 34, of which 16 were waited for; matrix products, arithmetic and copies ran while one was open for 6% of the time, Pallas kernels for 29%

profile of v10, /device:TPU:0, one launch (start us, length us, event | category | flops | bytes accessed | tf_op | source)
XLA Modules:
  0.0 164.4 jit_solution(5688420731205965552)
XLA Ops:
  1.1 6.0 %collective-permute-start = (bf16[4,48,1792]{2,1,0:T(8,128)(2,1)S(1)}, bf16[4,48,1792]{2,1,0:T(8,128)(2,1)S(1)}, u32[]{:S(2)}, u32[]{:S(2)}) collective-permute-start(bf16[4,48,1792]{2,1,0:T(8,128)(2,1)S(1)} %take_rows.1), channel_id=1, source_target_pairs={{0,28},{4,0},{8,4},{12,8},{16,12},{20,16},{24,20},{28,24},{1,29},{... | collective-permute-start | bytes 2064392 | tf_op jit(solution)/shard_map/ppermute | solution.py:35
  7.1 2.7 %routed_grad.1 = bf16[1024,256]{1,0:T(8,128)(2,1)} custom-call(f32[8,1024]{1,0:T(8,128)} %bitcast.50, f32[8,1024]{1,0:T(8,128)} %bitcast.51, s32[8,1024]{1,0:T(8,128)} %bitcast.52), custom_call_target="tpu_custom_call" | custom-call | tf_op jit(solution)/shard_map/routed_grad/pallas_call | solution.py:136
  9.8 2.3 %slice.11 = bf16[4,80,1792]{2,1,0:T(8,128)(2,1)} slice(bf16[4,256,1792]{2,1,0:T(8,128)(2,1)} %bitcast.40), slice={[0:4], [48:128], [0:1792]} | slice | bytes 2293760 | tf_op jit(solution)/shard_map/slice | solution.py:292
  12.7 2.8 %fusion = (bf16[4,64,1792]{2,1,0:T(8,128)(2,1)}, bf16[4,64,1792]{2,1,0:T(8,128)(2,1)}) fusion(bf16[4,256,1792]{2,1,0:T(8,128)(2,1)} %bitcast.41), kind=kLoop, calls=%fused_computation.2 | loop fusion | bytes 3670016 | tf_op jit(solution)/shard_map/slice | solution.py:292
  15.5 7.5 %collective-permute-done.rows_ref = bf16[4,48,1792]{2,1,0:T(8,128)(2,1)S(1)} collective-permute-done((bf16[4,48,1792]{2,1,0:T(8,128)(2,1)S(1)}, bf16[4,48,1792]{2,1,0:T(8,128)(2,1)S(1)}, u32[]{:S(2)}, u32[]{:S(2)}) %collective-permute-start) | collective-permute-done | bytes 688160 | tf_op jit(solution)/shard_map/ppermute | solution.py:35
  23.0 5.2 %collective-permute-start.8 = (bf16[4,64,1792]{2,1,0:T(8,128)(2,1)}, bf16[4,64,1792]{2,1,0:T(8,128)(2,1)S(1)}, u32[]{:S(2)}, u32[]{:S(2)}) collective-permute-start(bf16[4,64,1792]{2,1,0:T(8,128)(2,1)} %get-tuple-element.73), channel_id=1, source_target_pairs={{0,28},{4,0},{8,4},{12,8},{16,12},{20,16},{24,20},{28,24},{1,29},{... | collective-permute-start | bytes 2752520 | tf_op jit(solution)/shard_map/ppermute | solution.py:35
  28.2 4.1 %first_product.4 = (bf16[48,1024]{1,0:T(8,128)(2,1)S(1)}, bf16[48,1024]{1,0:T(8,128)(2,1)S(1)}, bf16[48,1024]{1,0:T(8,128)(2,1)S(1)}, bf16[48,1024]{1,0:T(8,128)(2,1)S(1)}) custom-call(s32[1]{0:T(128)} %bitcast.me_ref, bf16[4,48,1792]{2,1,0:T(8,128)(2,1)S(1)} %collective-permute-done.rows_ref, bf16[1024,1792]{1,0:T(8,128)(2,1)} %bitcast.19), custom_call_target="tpu_custom_call" | custom-call | tf_op jit(solution)/shard_map/first_product/pallas_call | solution.py:160
  32.3 1.6 collective-permute-start.3
  35.3 1.5 collective-permute-done.2.refs_1_
  42.3 5.4 %collective-permute-done.1.rows_ref = bf16[4,80,1792]{2,1,0:T(8,128)(2,1)S(1)} collective-permute-done((bf16[4,80,1792]{2,1,0:T(8,128)(2,1)}, bf16[4,80,1792]{2,1,0:T(8,128)(2,1)S(1)}, u32[]{:S(2)}, u32[]{:S(2)}) %collective-permute-start.1) | collective-permute-done | bytes 1146912 | tf_op jit(solution)/shard_map/ppermute | solution.py:35
  47.7 2.1 %first_product.5 = (bf16[80,1024]{1,0:T(8,128)(2,1)S(1)}, bf16[80,1024]{1,0:T(8,128)(2,1)S(1)}, bf16[80,1024]{1,0:T(8,128)(2,1)S(1)}, bf16[80,1024]{1,0:T(8,128)(2,1)S(1)}) custom-call(s32[1]{0:T(128)} %bitcast.me_ref, bf16[4,80,1792]{2,1,0:T(8,128)(2,1)S(1)} %collective-permute-done.1.rows_ref, bf16[1024,1792]{1,0:T(8,128)(2,1)S(1)} %bitcast.20), custom_call_target="tpu_custom_call" | custom-call | tf_op jit(solution)/shard_map/first_product/pallas_call | solution.py:160
  49.9 5.1 %collective-permute-start.15 = (bf16[4,64,1792]{2,1,0:T(8,128)(2,1)S(1)}, bf16[4,64,1792]{2,1,0:T(8,128)(2,1)S(1)}, u32[]{:S(2)}, u32[]{:S(2)}) collective-permute-start(bf16[4,64,1792]{2,1,0:T(8,128)(2,1)S(1)} %copy-done.3), channel_id=1, source_target_pairs={{0,28},{4,0},{8,4},{12,8},{16,12},{20,16},{24,20},{28,24},{1,29},{... | collective-permute-start | bytes 2752520 | tf_op jit(solution)/shard_map/ppermute | solution.py:35
  55.0 1.5 collective-permute-start.10
  57.1 7.2 %second_product.4 = bf16[4,48,1792]{2,1,0:T(8,128)(2,1)S(1)} custom-call(s32[1]{0:T(128)} %bitcast.me_ref, bf16[4,256,256]{2,1,0:T(8,128)(2,1)S(1)} %bitcast.27, bf16[1792,1024]{1,0:T(8,128)(2,1)} %bitcast.31, bf16[1792,1024]{1,0:T(8,128)(2,1)} %bitcast.35, bf16[1792,256]{1,0:T(8,128)(2,1)S(1)} %bitcast.23, bf16[48,2048]{1,0:T(8,128)(2,1)S(1)} %activation.4.refs_0_, ...), custom_call_target="tpu_custom_call" | custom-call | tf_op jit(solution)/shard_map/second_product/pallas_call | solution.py:242
  64.3 3.0 %collective-permute-done.8.rows_ref = bf16[4,64,1792]{2,1,0:T(8,128)(2,1)S(1)} collective-permute-done((bf16[4,64,1792]{2,1,0:T(8,128)(2,1)}, bf16[4,64,1792]{2,1,0:T(8,128)(2,1)S(1)}, u32[]{:S(2)}, u32[]{:S(2)}) %collective-permute-start.8) | collective-permute-done | bytes 917536 | tf_op jit(solution)/shard_map/ppermute | solution.py:35
  67.3 1.5 activation.5.refs_0_
  68.8 1.6 collective-permute-start.12
  70.4 1.9 %first_product.6 = (bf16[64,1024]{1,0:T(8,128)(2,1)S(1)}, bf16[64,1024]{1,0:T(8,128)(2,1)S(1)}, bf16[64,1024]{1,0:T(8,128)(2,1)S(1)}, bf16[64,1024]{1,0:T(8,128)(2,1)S(1)}) custom-call(s32[1]{0:T(128)} %bitcast.me_ref, bf16[4,64,1792]{2,1,0:T(8,128)(2,1)S(1)} %collective-permute-done.8.rows_ref, bf16[1024,1792]{1,0:T(8,128)(2,1)S(1)} %bitcast.21), custom_call_target="tpu_custom_call" | custom-call | tf_op jit(solution)/shard_map/first_product/pallas_call | solution.py:160
  72.3 4.3 %collective-permute-done.12.refs_2_ = bf16[80,2048]{1,0:T(8,128)(2,1)S(1)} collective-permute-done((bf16[80,2048]{1,0:T(8,128)(2,1)S(1)}, bf16[80,2048]{1,0:T(8,128)(2,1)S(1)}, u32[]{:S(2)}, u32[]{:S(2)}) %collective-permute-start.12) | collective-permute-done | bytes 327712 | tf_op jit(solution)/shard_map/ppermute | solution.py:40
  79.3 5.1 %collective-permute-start.22 = (bf16[4,48,1792]{2,1,0:T(8,128)(2,1)S(1)}, bf16[4,48,1792]{2,1,0:T(8,128)(2,1)S(1)}, u32[]{:S(2)}, u32[]{:S(2)}) collective-permute-start(bf16[4,48,1792]{2,1,0:T(8,128)(2,1)S(1)} %second_product.4), channel_id=1, source_target_pairs={{0,28},{4,0},{8,4},{12,8},{16,12},{20,16},{24,20},{28,24},{1,29},{... | collective-permute-start | bytes 2064392 | tf_op jit(solution)/shard_map/ppermute | solution.py:35
  84.4 7.4 %second_product.5 = bf16[4,80,1792]{2,1,0:T(8,128)(2,1)S(1)} custom-call(s32[1]{0:T(128)} %bitcast.me_ref, bf16[4,256,256]{2,1,0:T(8,128)(2,1)S(1)} %bitcast.28, bf16[1792,1024]{1,0:T(8,128)(2,1)} %bitcast.32, bf16[1792,1024]{1,0:T(8,128)(2,1)} %bitcast.36, bf16[1792,256]{1,0:T(8,128)(2,1)S(1)} %bitcast.24, bf16[80,2048]{1,0:T(8,128)(2,1)S(1)} %activation.5.refs_0_, ...), custom_call_target="tpu_custom_call" | custom-call | tf_op jit(solution)/shard_map/second_product/pallas_call | solution.py:242
  95.1 1.8 %first_product.7 = (bf16[64,1024]{1,0:T(8,128)(2,1)S(1)}, bf16[64,1024]{1,0:T(8,128)(2,1)S(1)}, bf16[64,1024]{1,0:T(8,128)(2,1)S(1)}, bf16[64,1024]{1,0:T(8,128)(2,1)S(1)}) custom-call(s32[1]{0:T(128)} %bitcast.me_ref, bf16[4,64,1792]{2,1,0:T(8,128)(2,1)S(1)} %collective-permute-done.15.rows_ref, bf16[1024,1792]{1,0:T(8,128)(2,1)S(1)} %bitcast.22), custom_call_target="tpu_custom_call" | custom-call | tf_op jit(solution)/shard_map/first_product/pallas_call | solution.py:160
  96.9 3.8 %collective-permute-done.19.refs_2_ = bf16[64,2048]{1,0:T(8,128)(2,1)S(1)} collective-permute-done((bf16[64,2048]{1,0:T(8,128)(2,1)S(1)}, bf16[64,2048]{1,0:T(8,128)(2,1)S(1)}, u32[]{:S(2)}, u32[]{:S(2)}) %collective-permute-start.19) | collective-permute-done | bytes 262176 | tf_op jit(solution)/shard_map/ppermute | solution.py:40
  103.1 7.0 %second_product.6 = bf16[4,64,1792]{2,1,0:T(8,128)(2,1)S(1)} custom-call(s32[1]{0:T(128)} %bitcast.me_ref, bf16[4,256,256]{2,1,0:T(8,128)(2,1)S(1)} %bitcast.29, bf16[1792,1024]{1,0:T(8,128)(2,1)} %bitcast.33, bf16[1792,1024]{1,0:T(8,128)(2,1)} %bitcast.37, bf16[1792,256]{1,0:T(8,128)(2,1)S(1)} %bitcast.25, bf16[64,2048]{1,0:T(8,128)(2,1)S(1)} %activation.6.refs_0_, ...), custom_call_target="tpu_custom_call" | custom-call | tf_op jit(solution)/shard_map/second_product/pallas_call | solution.py:242
  113.1 6.5 %collective-permute-done.27.refs_2_ = bf16[64,2048]{1,0:T(8,128)(2,1)S(1)} collective-permute-done((bf16[64,2048]{1,0:T(8,128)(2,1)S(1)}, bf16[64,2048]{1,0:T(8,128)(2,1)S(1)}, u32[]{:S(2)}, u32[]{:S(2)}) %collective-permute-start.27) | collective-permute-done | bytes 262176 | tf_op jit(solution)/shard_map/ppermute | solution.py:40
  121.1 5.1 %collective-permute-done.29 = bf16[4,80,1792]{2,1,0:T(8,128)(2,1)S(1)} collective-permute-done((bf16[4,80,1792]{2,1,0:T(8,128)(2,1)S(1)}, bf16[4,80,1792]{2,1,0:T(8,128)(2,1)S(1)}, u32[]{:S(2)}, u32[]{:S(2)}) %collective-permute-start.29) | collective-permute-done | bytes 1146912 | tf_op jit(solution)/shard_map/ppermute | solution.py:35
  126.2 7.1 %second_product.7 = (bf16[4,48,1792]{2,1,0:T(8,128)(2,1)S(1)}, bf16[4,16,1792]{2,1,0:T(8,128)(2,1)S(1)}) custom-call(s32[1]{0:T(128)} %bitcast.me_ref, bf16[4,256,256]{2,1,0:T(8,128)(2,1)S(1)} %bitcast.30, bf16[1792,1024]{1,0:T(8,128)(2,1)} %bitcast.34, bf16[1792,1024]{1,0:T(8,128)(2,1)} %bitcast.38, bf16[1792,256]{1,0:T(8,128)(2,1)S(1)} %bitcast.26, ...), custom_call_target="tpu_custom_call" | custom-call | tf_op jit(solution)/shard_map/second_product/pallas_call | solution.py:242
  133.3 5.2 %collective-permute-start.32 = (bf16[4,48,1792]{2,1,0:T(8,128)(2,1)S(1)}, bf16[4,48,1792]{2,1,0:T(8,128)(2,1)S(1)}, u32[]{:S(2)}, u32[]{:S(2)}) collective-permute-start(bf16[4,48,1792]{2,1,0:T(8,128)(2,1)S(1)} %get-tuple-element.105), channel_id=1, source_target_pairs={{0,28},{4,0},{8,4},{12,8},{16,12},{20,16},{24,20},{28,24},{1,29},{... | collective-permute-start | bytes 2064392 | tf_op jit(solution)/shard_map/ppermute | solution.py:35
  138.5 2.1 %dynamic_update_slice.9 = bf16[4,256,1792]{2,1,0:T(8,128)(2,1)} pad(bf16[4,48,1792]{2,1,0:T(8,128)(2,1)S(1)} %collective-permute-done.22, bf16[]{:T(256)} %constant.1.clone.1), padding=0_0x0_208x0_0 | pad | bytes 4358146 | tf_op jit(solution)/shard_map/dynamic_update_slice | solution.py:338
  141.9 2.7 %collective-permute-start.30 = (bf16[4,16,1792]{2,1,0:T(8,128)(2,1)S(1)}, bf16[4,16,1792]{2,1,0:T(8,128)(2,1)S(1)}, u32[]{:S(2)}, u32[]{:S(2)}) collective-permute-start(bf16[4,16,1792]{2,1,0:T(8,128)(2,1)S(1)} %get-tuple-element.102), channel_id=1, source_target_pairs={{0,28},{1,29},{2,30},{3,31}} | collective-permute-start | bytes 688136 | tf_op jit(solution)/shard_map/ppermute | solution.py:343
  146.8 13.8 %collective-permute-done.32.source = bf16[4,48,1792]{2,1,0:T(8,128)(2,1)S(1)} collective-permute-done((bf16[4,48,1792]{2,1,0:T(8,128)(2,1)S(1)}, bf16[4,48,1792]{2,1,0:T(8,128)(2,1)S(1)}, u32[]{:S(2)}, u32[]{:S(2)}) %collective-permute-start.32) | collective-permute-done | bytes 688160 | tf_op jit(solution)/shard_map/ppermute | solution.py:35
  162.8 1.6 collective-permute-done.30.source
  (66 shorter events, 27.8 us)
Async XLA Ops:
  1.1 21.9 %collective-permute-start = (bf16[4,48,1792]{2,1,0:T(8,128)(2,1)S(1)}, bf16[4,48,1792]{2,1,0:T(8,128)(2,1)S(1)}, u32[]{:S(2)}, u32[]{:S(2)}) collective-permute-start(bf16[4,48,1792]{2,1,0:T(8,128)(2,1)S(1)} %take_rows.1), channel_id=1, source_target_pairs={{0,28},{4,0},{8,4},{12,8},{16,12},{20,16},{24,20},{28,24},{1,29},{... | collective-permute-start | bytes 2064392 | tf_op jit(solution)/shard_map/ppermute | solution.py:35
  12.1 35.5 %collective-permute-start.1 = (bf16[4,80,1792]{2,1,0:T(8,128)(2,1)}, bf16[4,80,1792]{2,1,0:T(8,128)(2,1)S(1)}, u32[]{:S(2)}, u32[]{:S(2)}) collective-permute-start(bf16[4,80,1792]{2,1,0:T(8,128)(2,1)} %slice.11), channel_id=1, source_target_pairs={{0,28},{4,0},{8,4},{12,8},{16,12},{20,16},{24,20},{28,24},{1,29},{... | collective-permute-start | bytes 3440648 | tf_op jit(solution)/shard_map/ppermute | solution.py:35
  23.0 44.3 %collective-permute-start.8 = (bf16[4,64,1792]{2,1,0:T(8,128)(2,1)}, bf16[4,64,1792]{2,1,0:T(8,128)(2,1)S(1)}, u32[]{:S(2)}, u32[]{:S(2)}) collective-permute-start(bf16[4,64,1792]{2,1,0:T(8,128)(2,1)} %get-tuple-element.73), channel_id=1, source_target_pairs={{0,28},{4,0},{8,4},{12,8},{16,12},{20,16},{24,20},{28,24},{1,29},{... | collective-permute-start | bytes 2752520 | tf_op jit(solution)/shard_map/ppermute | solution.py:35
  32.3 4.5 %collective-permute-start.2 = (bf16[48,1024]{1,0:T(8,128)(2,1)S(1)}, bf16[48,1024]{1,0:T(8,128)(2,1)S(1)}, u32[]{:S(2)}, u32[]{:S(2)}) collective-permute-start(bf16[48,1024]{1,0:T(8,128)(2,1)S(1)} %get-tuple-element.65), channel_id=1, source_target_pairs={{0,1},{1,2},{2,3},{3,0},{4,5},{5,6},{6,7},{7,4},{8,9},{9,10},{10,1... | collective-permute-start | bytes 294920 | tf_op jit(solution)/shard_map/ppermute | solution.py:40
  32.3 5.7 %collective-permute-start.3 = (bf16[48,1024]{1,0:T(8,128)(2,1)S(1)}, bf16[48,1024]{1,0:T(8,128)(2,1)S(1)}, u32[]{:S(2)}, u32[]{:S(2)}) collective-permute-start(bf16[48,1024]{1,0:T(8,128)(2,1)S(1)} %get-tuple-element.66), channel_id=1, source_target_pairs={{0,2},{1,3},{2,0},{3,1},{4,6},{5,7},{6,4},{7,5},{8,10},{9,11},{10,... | collective-permute-start | bytes 294920 | tf_op jit(solution)/shard_map/ppermute | solution.py:40
  33.9 4.6 %collective-permute-start.4 = (bf16[48,1024]{1,0:T(8,128)(2,1)S(1)}, bf16[48,1024]{1,0:T(8,128)(2,1)S(1)}, u32[]{:S(2)}, u32[]{:S(2)}) collective-permute-start(bf16[48,1024]{1,0:T(8,128)(2,1)S(1)} %get-tuple-element.67), channel_id=1, source_target_pairs={{0,3},{1,0},{2,1},{3,2},{4,7},{5,4},{6,5},{7,6},{8,11},{9,8},{10,9... | collective-permute-start | bytes 294920 | tf_op jit(solution)/shard_map/ppermute | solution.py:40
  39.9 9.9 %collective-permute-start.5 = (bf16[48,2048]{1,0:T(8,128)(2,1)S(1)}, bf16[48,2048]{1,0:T(8,128)(2,1)S(1)}, u32[]{:S(2)}, u32[]{:S(2)}) collective-permute-start(bf16[48,2048]{1,0:T(8,128)(2,1)S(1)} %activation.4.refs_0_), channel_id=1, source_target_pairs={{0,2},{1,3},{2,0},{3,1},{4,6},{5,7},{6,4},{7,5},{8,10},{9,11},{10,... | collective-permute-start | bytes 589832 | tf_op jit(solution)/shard_map/ppermute | solution.py:40
  41.0 15.6 %collective-permute-start.6 = (bf16[48,2048]{1,0:T(8,128)(2,1)S(1)}, bf16[48,2048]{1,0:T(8,128)(2,1)S(1)}, u32[]{:S(2)}, u32[]{:S(2)}) collective-permute-start(bf16[48,2048]{1,0:T(8,128)(2,1)S(1)} %activation.4.refs_0_), channel_id=1, source_target_pairs={{0,1},{1,0},{2,3},{3,2},{4,5},{5,4},{6,7},{7,6},{8,9},{9,8},{10,11... | collective-permute-start | bytes 589832 | tf_op jit(solution)/shard_map/ppermute | solution.py:45
  49.8 6.8 %collective-permute-start.7 = (bf16[48,2048]{1,0:T(8,128)(2,1)S(1)}, bf16[48,2048]{1,0:T(8,128)(2,1)S(1)}, u32[]{:S(2)}, u32[]{:S(2)}) collective-permute-start(bf16[48,2048]{1,0:T(8,128)(2,1)S(1)} %collective-permute-done.5.refs_2_), channel_id=1, source_target_pairs={{0,1},{1,0},{2,3},{3,2},{4,5},{5,4},{6,7},{7,6},{8,9},{9,8},{10,11... | collective-permute-start | bytes 589832 | tf_op jit(solution)/shard_map/ppermute | solution.py:45
  49.9 41.9 %collective-permute-start.15 = (bf16[4,64,1792]{2,1,0:T(8,128)(2,1)S(1)}, bf16[4,64,1792]{2,1,0:T(8,128)(2,1)S(1)}, u32[]{:S(2)}, u32[]{:S(2)}) collective-permute-start(bf16[4,64,1792]{2,1,0:T(8,128)(2,1)S(1)} %copy-done.3), channel_id=1, source_target_pairs={{0,28},{4,0},{8,4},{12,8},{16,12},{20,16},{24,20},{28,24},{1,29},{... | collective-permute-start | bytes 2752520 | tf_op jit(solution)/shard_map/ppermute | solution.py:35
  55.0 12.3 %collective-permute-start.10 = (bf16[80,1024]{1,0:T(8,128)(2,1)S(1)}, bf16[80,1024]{1,0:T(8,128)(2,1)S(1)}, u32[]{:S(2)}, u32[]{:S(2)}) collective-permute-start(bf16[80,1024]{1,0:T(8,128)(2,1)S(1)} %get-tuple-element.77), channel_id=1, source_target_pairs={{0,2},{1,3},{2,0},{3,1},{4,6},{5,7},{6,4},{7,5},{8,10},{9,11},{10,... | collective-permute-start | bytes 491528 | tf_op jit(solution)/shard_map/ppermute | solution.py:40
  56.5 10.8 %collective-permute-start.11 = (bf16[80,1024]{1,0:T(8,128)(2,1)S(1)}, bf16[80,1024]{1,0:T(8,128)(2,1)S(1)}, u32[]{:S(2)}, u32[]{:S(2)}) collective-permute-start(bf16[80,1024]{1,0:T(8,128)(2,1)S(1)} %get-tuple-element.78), channel_id=1, source_target_pairs={{0,3},{1,0},{2,1},{3,2},{4,7},{5,4},{6,5},{7,6},{8,11},{9,8},{10,9... | collective-permute-start | bytes 491528 | tf_op jit(solution)/shard_map/ppermute | solution.py:40
  56.5 10.8 %collective-permute-start.9 = (bf16[80,1024]{1,0:T(8,128)(2,1)S(1)}, bf16[80,1024]{1,0:T(8,128)(2,1)S(1)}, u32[]{:S(2)}, u32[]{:S(2)}) collective-permute-start(bf16[80,1024]{1,0:T(8,128)(2,1)S(1)} %get-tuple-element.76), channel_id=1, source_target_pairs={{0,1},{1,2},{2,3},{3,0},{4,5},{5,6},{6,7},{7,4},{8,9},{9,10},{10,1... | collective-permute-start | bytes 491528 | tf_op jit(solution)/shard_map/ppermute | solution.py:40
  68.8 7.8 %collective-permute-start.12 = (bf16[80,2048]{1,0:T(8,128)(2,1)S(1)}, bf16[80,2048]{1,0:T(8,128)(2,1)S(1)}, u32[]{:S(2)}, u32[]{:S(2)}) collective-permute-start(bf16[80,2048]{1,0:T(8,128)(2,1)S(1)} %activation.5.refs_0_), channel_id=1, source_target_pairs={{0,2},{1,3},{2,0},{3,1},{4,6},{5,7},{6,4},{7,5},{8,10},{9,11},{10,... | collective-permute-start | bytes 983048 | tf_op jit(solution)/shard_map/ppermute | solution.py:40
  70.4 8.0 %collective-permute-start.13 = (bf16[80,2048]{1,0:T(8,128)(2,1)S(1)}, bf16[80,2048]{1,0:T(8,128)(2,1)S(1)}, u32[]{:S(2)}, u32[]{:S(2)}) collective-permute-start(bf16[80,2048]{1,0:T(8,128)(2,1)S(1)} %activation.5.refs_0_), channel_id=1, source_target_pairs={{0,1},{1,0},{2,3},{3,2},{4,5},{5,4},{6,7},{7,6},{8,9},{9,8},{10,11... | collective-permute-start | bytes 983048 | tf_op jit(solution)/shard_map/ppermute | solution.py:45
  76.6 2.7 %collective-permute-start.14 = (bf16[80,2048]{1,0:T(8,128)(2,1)S(1)}, bf16[80,2048]{1,0:T(8,128)(2,1)S(1)}, u32[]{:S(2)}, u32[]{:S(2)}) collective-permute-start(bf16[80,2048]{1,0:T(8,128)(2,1)S(1)} %collective-permute-done.12.refs_2_), channel_id=1, source_target_pairs={{0,1},{1,0},{2,3},{3,2},{4,5},{5,4},{6,7},{7,6},{8,9},{9,8},{10,11... | collective-permute-start | bytes 983048 | tf_op jit(solution)/shard_map/ppermute | solution.py:45
  76.6 15.2 %collective-permute-start.16 = (bf16[64,1024]{1,0:T(8,128)(2,1)S(1)}, bf16[64,1024]{1,0:T(8,128)(2,1)S(1)}, u32[]{:S(2)}, u32[]{:S(2)}) collective-permute-start(bf16[64,1024]{1,0:T(8,128)(2,1)S(1)} %get-tuple-element.87), channel_id=1, source_target_pairs={{0,1},{1,2},{2,3},{3,0},{4,5},{5,6},{6,7},{7,4},{8,9},{9,10},{10,1... | collective-permute-start | bytes 393224 | tf_op jit(solution)/shard_map/ppermute | solution.py:40
  77.1 14.7 %collective-permute-start.17 = (bf16[64,1024]{1,0:T(8,128)(2,1)S(1)}, bf16[64,1024]{1,0:T(8,128)(2,1)S(1)}, u32[]{:S(2)}, u32[]{:S(2)}) collective-permute-start(bf16[64,1024]{1,0:T(8,128)(2,1)S(1)} %get-tuple-element.88), channel_id=1, source_target_pairs={{0,2},{1,3},{2,0},{3,1},{4,6},{5,7},{6,4},{7,5},{8,10},{9,11},{10,... | collective-permute-start | bytes 393224 | tf_op jit(solution)/shard_map/ppermute | solution.py:40
  78.3 13.4 %collective-permute-start.18 = (bf16[64,1024]{1,0:T(8,128)(2,1)S(1)}, bf16[64,1024]{1,0:T(8,128)(2,1)S(1)}, u32[]{:S(2)}, u32[]{:S(2)}) collective-permute-start(bf16[64,1024]{1,0:T(8,128)(2,1)S(1)} %get-tuple-element.89), channel_id=1, source_target_pairs={{0,3},{1,0},{2,1},{3,2},{4,7},{5,4},{6,5},{7,6},{8,11},{9,8},{10,9... | collective-permute-start | bytes 393224 | tf_op jit(solution)/shard_map/ppermute | solution.py:40
  79.3 30.9 %collective-permute-start.22 = (bf16[4,48,1792]{2,1,0:T(8,128)(2,1)S(1)}, bf16[4,48,1792]{2,1,0:T(8,128)(2,1)S(1)}, u32[]{:S(2)}, u32[]{:S(2)}) collective-permute-start(bf16[4,48,1792]{2,1,0:T(8,128)(2,1)S(1)} %second_product.4), channel_id=1, source_target_pairs={{0,28},{4,0},{8,4},{12,8},{16,12},{20,16},{24,20},{28,24},{1,29},{... | collective-permute-start | bytes 2064392 | tf_op jit(solution)/shard_map/ppermute | solution.py:35
  93.2 7.5 %collective-permute-start.19 = (bf16[64,2048]{1,0:T(8,128)(2,1)S(1)}, bf16[64,2048]{1,0:T(8,128)(2,1)S(1)}, u32[]{:S(2)}, u32[]{:S(2)}) collective-permute-start(bf16[64,2048]{1,0:T(8,128)(2,1)S(1)} %activation.6.refs_0_), channel_id=1, source_target_pairs={{0,2},{1,3},{2,0},{3,1},{4,6},{5,7},{6,4},{7,5},{8,10},{9,11},{10,... | collective-permute-start | bytes 786440 | tf_op jit(solution)/shard_map/ppermute | solution.py:40
  93.8 32.4 %collective-permute-start.29 = (bf16[4,80,1792]{2,1,0:T(8,128)(2,1)S(1)}, bf16[4,80,1792]{2,1,0:T(8,128)(2,1)S(1)}, u32[]{:S(2)}, u32[]{:S(2)}) collective-permute-start(bf16[4,80,1792]{2,1,0:T(8,128)(2,1)S(1)} %second_product.5), channel_id=1, source_target_pairs={{0,28},{4,0},{8,4},{12,8},{16,12},{20,16},{24,20},{28,24},{1,29},{... | collective-permute-start | bytes 3440648 | tf_op jit(solution)/shard_map/ppermute | solution.py:35
  95.1 6.2 %collective-permute-start.20 = (bf16[64,2048]{1,0:T(8,128)(2,1)S(1)}, bf16[64,2048]{1,0:T(8,128)(2,1)S(1)}, u32[]{:S(2)}, u32[]{:S(2)}) collective-permute-start(bf16[64,2048]{1,0:T(8,128)(2,1)S(1)} %activation.6.refs_0_), channel_id=1, source_target_pairs={{0,1},{1,0},{2,3},{3,2},{4,5},{5,4},{6,7},{7,6},{8,9},{9,8},{10,11... | collective-permute-start | bytes 786440 | tf_op jit(solution)/shard_map/ppermute | solution.py:45
  100.7 9.4 %collective-permute-start.23 = (bf16[64,1024]{1,0:T(8,128)(2,1)S(1)}, bf16[64,1024]{1,0:T(8,128)(2,1)S(1)}, u32[]{:S(2)}, u32[]{:S(2)}) collective-permute-start(bf16[64,1024]{1,0:T(8,128)(2,1)S(1)} %get-tuple-element.97), channel_id=1, source_target_pairs={{0,1},{1,2},{2,3},{3,0},{4,5},{5,6},{6,7},{7,4},{8,9},{9,10},{10,1... | collective-permute-start | bytes 393224 | tf_op jit(solution)/shard_map/ppermute | solution.py:40
  101.3 8.9 %collective-permute-start.24 = (bf16[64,1024]{1,0:T(8,128)(2,1)S(1)}, bf16[64,1024]{1,0:T(8,128)(2,1)S(1)}, u32[]{:S(2)}, u32[]{:S(2)}) collective-permute-start(bf16[64,1024]{1,0:T(8,128)(2,1)S(1)} %get-tuple-element.98), channel_id=1, source_target_pairs={{0,2},{1,3},{2,0},{3,1},{4,6},{5,7},{6,4},{7,5},{8,10},{9,11},{10,... | collective-permute-start | bytes 393224 | tf_op jit(solution)/shard_map/ppermute | solution.py:40
  102.3 7.9 %collective-permute-start.25 = (bf16[64,1024]{1,0:T(8,128)(2,1)S(1)}, bf16[64,1024]{1,0:T(8,128)(2,1)S(1)}, u32[]{:S(2)}, u32[]{:S(2)}) collective-permute-start(bf16[64,1024]{1,0:T(8,128)(2,1)S(1)} %get-tuple-element.99), channel_id=1, source_target_pairs={{0,3},{1,0},{2,1},{3,2},{4,7},{5,4},{6,5},{7,6},{8,11},{9,8},{10,9... | collective-permute-start | bytes 393224 | tf_op jit(solution)/shard_map/ppermute | solution.py:40
  111.6 7.9 %collective-permute-start.27 = (bf16[64,2048]{1,0:T(8,128)(2,1)S(1)}, bf16[64,2048]{1,0:T(8,128)(2,1)S(1)}, u32[]{:S(2)}, u32[]{:S(2)}) collective-permute-start(bf16[64,2048]{1,0:T(8,128)(2,1)S(1)} %activation.7.refs_0_), channel_id=1, source_target_pairs={{0,2},{1,3},{2,0},{3,1},{4,6},{5,7},{6,4},{7,5},{8,10},{9,11},{10,... | collective-permute-start | bytes 786440 | tf_op jit(solution)/shard_map/ppermute | solution.py:40
  112.8 33.1 %collective-permute-start.33 = (bf16[4,64,1792]{2,1,0:T(8,128)(2,1)S(1)}, bf16[4,64,1792]{2,1,0:T(8,128)(2,1)S(1)}, u32[]{:S(2)}, u32[]{:S(2)}) collective-permute-start(bf16[4,64,1792]{2,1,0:T(8,128)(2,1)S(1)} %second_product.6), channel_id=1, source_target_pairs={{0,28},{4,0},{8,4},{12,8},{16,12},{20,16},{24,20},{28,24},{1,29},{... | collective-permute-start | bytes 2752520 | tf_op jit(solution)/shard_map/ppermute | solution.py:35
  119.6 6.6 %collective-permute-start.26 = (bf16[64,2048]{1,0:T(8,128)(2,1)S(1)}, bf16[64,2048]{1,0:T(8,128)(2,1)S(1)}, u32[]{:S(2)}, u32[]{:S(2)}) collective-permute-start(bf16[64,2048]{1,0:T(8,128)(2,1)S(1)} %activation.7.refs_0_), channel_id=1, source_target_pairs={{0,1},{1,0},{2,3},{3,2},{4,5},{5,4},{6,7},{7,6},{8,9},{9,8},{10,11... | collective-permute-start | bytes 786440 | tf_op jit(solution)/shard_map/ppermute | solution.py:45
  133.3 27.3 %collective-permute-start.32 = (bf16[4,48,1792]{2,1,0:T(8,128)(2,1)S(1)}, bf16[4,48,1792]{2,1,0:T(8,128)(2,1)S(1)}, u32[]{:S(2)}, u32[]{:S(2)}) collective-permute-start(bf16[4,48,1792]{2,1,0:T(8,128)(2,1)S(1)} %get-tuple-element.105), channel_id=1, source_target_pairs={{0,28},{4,0},{8,4},{12,8},{16,12},{20,16},{24,20},{28,24},{1,29},{... | collective-permute-start | bytes 2064392 | tf_op jit(solution)/shard_map/ppermute | solution.py:35
  140.6 21.5 %collective-permute-start.31 = (bf16[4,16,1792]{2,1,0:T(8,128)(2,1)S(1)}, bf16[4,16,1792]{2,1,0:T(8,128)(2,1)S(1)}, u32[]{:S(2)}, u32[]{:S(2)}) collective-permute-start(bf16[4,16,1792]{2,1,0:T(8,128)(2,1)S(1)} %get-tuple-element.102), channel_id=1, source_target_pairs={{4,0},{8,4},{12,8},{16,12},{20,16},{24,20},{28,24},{5,1},{9,5},{13... | collective-permute-start | bytes 688136 | tf_op jit(solution)/shard_map/ppermute | solution.py:342
  141.9 22.5 %collective-permute-start.30 = (bf16[4,16,1792]{2,1,0:T(8,128)(2,1)S(1)}, bf16[4,16,1792]{2,1,0:T(8,128)(2,1)S(1)}, u32[]{:S(2)}, u32[]{:S(2)}) collective-permute-start(bf16[4,16,1792]{2,1,0:T(8,128)(2,1)S(1)} %get-tuple-element.102), channel_id=1, source_target_pairs={{0,28},{1,29},{2,30},{3,31}} | collective-permute-start | bytes 688136 | tf_op jit(solution)/shard_map/ppermute | solution.py:343
  (6 other events, 89.9 us)

commit v11 on v10

--- a/solution.py
+++ b/solution.py
@@ -131,7 +131,7 @@
 
 def routed_grad(grad, scores, chosen, n_experts):
     tokens, top = grad.shape
-    block = block_of(tokens, 512)
+    block = block_of(tokens, 1024)
     spec = pl.BlockSpec((top, block), lambda i: (0, i))
     return pl.pallas_call(
         routed_kernel,

time: 165 us -> 165 us (level)
  no operation moved by 1% of the time
where the time goes in v11:
time: 165 us; the launch traced here: 164 us
  waiting for transfers between devices  56.2 us (34%)
  Pallas kernels  49.5 us (30%)
  starting transfers between devices  49.1 us (30%)
  local copies, waits for them, and re-layouts  9.31 us (6%)
    ppermute x8, waiting for transfers between devices, back_one(): lax.ppermute(x, 'pipe', [(i, (i - 1) % length) for i in range(length)])  35 us
    ppermute x8, starting transfers between devices, back_one(): lax.ppermute(x, 'pipe', [(i, (i - 1) % length) for i in range(length)])  28.8 us
    pallas_call x4, Pallas kernels, second_product(): pl.pallas_call(functools.partial(second_kernel, n, start), out_shape=[jax...  28.7 us
    ppermute x16, waiting for transfers between devices, to_expert(): return lax.ppermute(x, 'expert', [(i, (i + by) % n) for i in range(n)])  17.9 us
    ppermute x16, starting transfers between devices, to_expert(): return lax.ppermute(x, 'expert', [(i, (i + by) % n) for i in range(n)])  14.5 us
    pallas_call x4, Pallas kernels, first_product(): pl.pallas_call(functools.partial(first_kernel, n), out_shape=[jax.ShapeDt...  9.85 us
    pallas_call x4, Pallas kernels, activation(): pl.pallas_call(functools.partial(activation_kernel, start), out_shape=jax...  5.61 us
    slice x2, local copies, waits for them, and re-layouts, shards(): piece = grads[:, starts[c]:starts[c] + sizes[c]]  5.15 us
  transfers between devices with their start and end apart: 34, of which 16 were waited for; matrix products, arithmetic and copies ran while one was open for 6% of the time, Pallas kernels for 29%

profile of v11, /device:TPU:0, one launch (start us, length us, event | category | flops | bytes accessed | tf_op | source)
XLA Modules:
  0.0 164.4 jit_solution(9106269853533722930)
XLA Ops:
  1.1 6.0 %collective-permute-start = (bf16[4,48,1792]{2,1,0:T(8,128)(2,1)S(1)}, bf16[4,48,1792]{2,1,0:T(8,128)(2,1)S(1)}, u32[]{:S(2)}, u32[]{:S(2)}) collective-permute-start(bf16[4,48,1792]{2,1,0:T(8,128)(2,1)S(1)} %take_rows.1), channel_id=1, source_target_pairs={{0,28},{4,0},{8,4},{12,8},{16,12},{20,16},{24,20},{28,24},{1,29},{... | collective-permute-start | bytes 2064392 | tf_op jit(solution)/shard_map/ppermute | solution.py:35
  7.1 2.7 %routed_grad.1 = bf16[1024,256]{1,0:T(8,128)(2,1)} custom-call(f32[8,1024]{1,0:T(8,128)} %bitcast.50, f32[8,1024]{1,0:T(8,128)} %bitcast.51, s32[8,1024]{1,0:T(8,128)} %bitcast.52), custom_call_target="tpu_custom_call" | custom-call | tf_op jit(solution)/shard_map/routed_grad/pallas_call | solution.py:136
  9.8 2.3 %slice.11 = bf16[4,80,1792]{2,1,0:T(8,128)(2,1)} slice(bf16[4,256,1792]{2,1,0:T(8,128)(2,1)} %bitcast.40), slice={[0:4], [48:128], [0:1792]} | slice | bytes 2293760 | tf_op jit(solution)/shard_map/slice | solution.py:292
  12.7 2.8 %fusion = (bf16[4,64,1792]{2,1,0:T(8,128)(2,1)}, bf16[4,64,1792]{2,1,0:T(8,128)(2,1)}) fusion(bf16[4,256,1792]{2,1,0:T(8,128)(2,1)} %bitcast.41), kind=kLoop, calls=%fused_computation.2 | loop fusion | bytes 3670016 | tf_op jit(solution)/shard_map/slice | solution.py:292
  15.5 7.4 %collective-permute-done.rows_ref = bf16[4,48,1792]{2,1,0:T(8,128)(2,1)S(1)} collective-permute-done((bf16[4,48,1792]{2,1,0:T(8,128)(2,1)S(1)}, bf16[4,48,1792]{2,1,0:T(8,128)(2,1)S(1)}, u32[]{:S(2)}, u32[]{:S(2)}) %collective-permute-start) | collective-permute-done | bytes 688160 | tf_op jit(solution)/shard_map/ppermute | solution.py:35
  23.0 5.2 %collective-permute-start.8 = (bf16[4,64,1792]{2,1,0:T(8,128)(2,1)}, bf16[4,64,1792]{2,1,0:T(8,128)(2,1)S(1)}, u32[]{:S(2)}, u32[]{:S(2)}) collective-permute-start(bf16[4,64,1792]{2,1,0:T(8,128)(2,1)} %get-tuple-element.73), channel_id=1, source_target_pairs={{0,28},{4,0},{8,4},{12,8},{16,12},{20,16},{24,20},{28,24},{1,29},{... | collective-permute-start | bytes 2752520 | tf_op jit(solution)/shard_map/ppermute | solution.py:35
  28.2 4.1 %first_product.4 = (bf16[48,1024]{1,0:T(8,128)(2,1)S(1)}, bf16[48,1024]{1,0:T(8,128)(2,1)S(1)}, bf16[48,1024]{1,0:T(8,128)(2,1)S(1)}, bf16[48,1024]{1,0:T(8,128)(2,1)S(1)}) custom-call(s32[1]{0:T(128)} %bitcast.me_ref, bf16[4,48,1792]{2,1,0:T(8,128)(2,1)S(1)} %collective-permute-done.rows_ref, bf16[1024,1792]{1,0:T(8,128)(2,1)} %bitcast.19), custom_call_target="tpu_custom_call" | custom-call | tf_op jit(solution)/shard_map/first_product/pallas_call | solution.py:160
  32.3 1.6 collective-permute-start.3
  35.3 1.5 collective-permute-done.2.refs_1_
  42.3 5.4 %collective-permute-done.1.rows_ref = bf16[4,80,1792]{2,1,0:T(8,128)(2,1)S(1)} collective-permute-done((bf16[4,80,1792]{2,1,0:T(8,128)(2,1)}, bf16[4,80,1792]{2,1,0:T(8,128)(2,1)S(1)}, u32[]{:S(2)}, u32[]{:S(2)}) %collective-permute-start.1) | collective-permute-done | bytes 1146912 | tf_op jit(solution)/shard_map/ppermute | solution.py:35
  47.7 2.1 %first_product.5 = (bf16[80,1024]{1,0:T(8,128)(2,1)S(1)}, bf16[80,1024]{1,0:T(8,128)(2,1)S(1)}, bf16[80,1024]{1,0:T(8,128)(2,1)S(1)}, bf16[80,1024]{1,0:T(8,128)(2,1)S(1)}) custom-call(s32[1]{0:T(128)} %bitcast.me_ref, bf16[4,80,1792]{2,1,0:T(8,128)(2,1)S(1)} %collective-permute-done.1.rows_ref, bf16[1024,1792]{1,0:T(8,128)(2,1)S(1)} %bitcast.20), custom_call_target="tpu_custom_call" | custom-call | tf_op jit(solution)/shard_map/first_product/pallas_call | solution.py:160
  49.9 5.1 %collective-permute-start.15 = (bf16[4,64,1792]{2,1,0:T(8,128)(2,1)S(1)}, bf16[4,64,1792]{2,1,0:T(8,128)(2,1)S(1)}, u32[]{:S(2)}, u32[]{:S(2)}) collective-permute-start(bf16[4,64,1792]{2,1,0:T(8,128)(2,1)S(1)} %copy-done.3), channel_id=1, source_target_pairs={{0,28},{4,0},{8,4},{12,8},{16,12},{20,16},{24,20},{28,24},{1,29},{... | collective-permute-start | bytes 2752520 | tf_op jit(solution)/shard_map/ppermute | solution.py:35
  55.0 1.5 collective-permute-start.10
  57.1 7.2 %second_product.4 = bf16[4,48,1792]{2,1,0:T(8,128)(2,1)S(1)} custom-call(s32[1]{0:T(128)} %bitcast.me_ref, bf16[4,256,256]{2,1,0:T(8,128)(2,1)S(1)} %bitcast.27, bf16[1792,1024]{1,0:T(8,128)(2,1)} %bitcast.31, bf16[1792,1024]{1,0:T(8,128)(2,1)} %bitcast.35, bf16[1792,256]{1,0:T(8,128)(2,1)S(1)} %bitcast.23, bf16[48,2048]{1,0:T(8,128)(2,1)S(1)} %activation.4.refs_0_, ...), custom_call_target="tpu_custom_call" | custom-call | tf_op jit(solution)/shard_map/second_product/pallas_call | solution.py:242
  64.3 3.0 %collective-permute-done.8.rows_ref = bf16[4,64,1792]{2,1,0:T(8,128)(2,1)S(1)} collective-permute-done((bf16[4,64,1792]{2,1,0:T(8,128)(2,1)}, bf16[4,64,1792]{2,1,0:T(8,128)(2,1)S(1)}, u32[]{:S(2)}, u32[]{:S(2)}) %collective-permute-start.8) | collective-permute-done | bytes 917536 | tf_op jit(solution)/shard_map/ppermute | solution.py:35
  67.3 1.5 activation.5.refs_0_
  68.8 1.6 collective-permute-start.12
  70.4 1.9 %first_product.6 = (bf16[64,1024]{1,0:T(8,128)(2,1)S(1)}, bf16[64,1024]{1,0:T(8,128)(2,1)S(1)}, bf16[64,1024]{1,0:T(8,128)(2,1)S(1)}, bf16[64,1024]{1,0:T(8,128)(2,1)S(1)}) custom-call(s32[1]{0:T(128)} %bitcast.me_ref, bf16[4,64,1792]{2,1,0:T(8,128)(2,1)S(1)} %collective-permute-done.8.rows_ref, bf16[1024,1792]{1,0:T(8,128)(2,1)S(1)} %bitcast.21), custom_call_target="tpu_custom_call" | custom-call | tf_op jit(solution)/shard_map/first_product/pallas_call | solution.py:160
  72.3 4.3 %collective-permute-done.12.refs_2_ = bf16[80,2048]{1,0:T(8,128)(2,1)S(1)} collective-permute-done((bf16[80,2048]{1,0:T(8,128)(2,1)S(1)}, bf16[80,2048]{1,0:T(8,128)(2,1)S(1)}, u32[]{:S(2)}, u32[]{:S(2)}) %collective-permute-start.12) | collective-permute-done | bytes 327712 | tf_op jit(solution)/shard_map/ppermute | solution.py:40
  79.3 5.1 %collective-permute-start.22 = (bf16[4,48,1792]{2,1,0:T(8,128)(2,1)S(1)}, bf16[4,48,1792]{2,1,0:T(8,128)(2,1)S(1)}, u32[]{:S(2)}, u32[]{:S(2)}) collective-permute-start(bf16[4,48,1792]{2,1,0:T(8,128)(2,1)S(1)} %second_product.4), channel_id=1, source_target_pairs={{0,28},{4,0},{8,4},{12,8},{16,12},{20,16},{24,20},{28,24},{1,29},{... | collective-permute-start | bytes 2064392 | tf_op jit(solution)/shard_map/ppermute | solution.py:35
  84.4 7.4 %second_product.5 = bf16[4,80,1792]{2,1,0:T(8,128)(2,1)S(1)} custom-call(s32[1]{0:T(128)} %bitcast.me_ref, bf16[4,256,256]{2,1,0:T(8,128)(2,1)S(1)} %bitcast.28, bf16[1792,1024]{1,0:T(8,128)(2,1)} %bitcast.32, bf16[1792,1024]{1,0:T(8,128)(2,1)} %bitcast.36, bf16[1792,256]{1,0:T(8,128)(2,1)S(1)} %bitcast.24, bf16[80,2048]{1,0:T(8,128)(2,1)S(1)} %activation.5.refs_0_, ...), custom_call_target="tpu_custom_call" | custom-call | tf_op jit(solution)/shard_map/second_product/pallas_call | solution.py:242
  95.1 1.8 %first_product.7 = (bf16[64,1024]{1,0:T(8,128)(2,1)S(1)}, bf16[64,1024]{1,0:T(8,128)(2,1)S(1)}, bf16[64,1024]{1,0:T(8,128)(2,1)S(1)}, bf16[64,1024]{1,0:T(8,128)(2,1)S(1)}) custom-call(s32[1]{0:T(128)} %bitcast.me_ref, bf16[4,64,1792]{2,1,0:T(8,128)(2,1)S(1)} %collective-permute-done.15.rows_ref, bf16[1024,1792]{1,0:T(8,128)(2,1)S(1)} %bitcast.22), custom_call_target="tpu_custom_call" | custom-call | tf_op jit(solution)/shard_map/first_product/pallas_call | solution.py:160
  96.9 3.8 %collective-permute-done.19.refs_2_ = bf16[64,2048]{1,0:T(8,128)(2,1)S(1)} collective-permute-done((bf16[64,2048]{1,0:T(8,128)(2,1)S(1)}, bf16[64,2048]{1,0:T(8,128)(2,1)S(1)}, u32[]{:S(2)}, u32[]{:S(2)}) %collective-permute-start.19) | collective-permute-done | bytes 262176 | tf_op jit(solution)/shard_map/ppermute | solution.py:40
  103.1 7.0 %second_product.6 = bf16[4,64,1792]{2,1,0:T(8,128)(2,1)S(1)} custom-call(s32[1]{0:T(128)} %bitcast.me_ref, bf16[4,256,256]{2,1,0:T(8,128)(2,1)S(1)} %bitcast.29, bf16[1792,1024]{1,0:T(8,128)(2,1)} %bitcast.33, bf16[1792,1024]{1,0:T(8,128)(2,1)} %bitcast.37, bf16[1792,256]{1,0:T(8,128)(2,1)S(1)} %bitcast.25, bf16[64,2048]{1,0:T(8,128)(2,1)S(1)} %activation.6.refs_0_, ...), custom_call_target="tpu_custom_call" | custom-call | tf_op jit(solution)/shard_map/second_product/pallas_call | solution.py:242
  113.1 6.5 %collective-permute-done.27.refs_2_ = bf16[64,2048]{1,0:T(8,128)(2,1)S(1)} collective-permute-done((bf16[64,2048]{1,0:T(8,128)(2,1)S(1)}, bf16[64,2048]{1,0:T(8,128)(2,1)S(1)}, u32[]{:S(2)}, u32[]{:S(2)}) %collective-permute-start.27) | collective-permute-done | bytes 262176 | tf_op jit(solution)/shard_map/ppermute | solution.py:40
  121.1 5.1 %collective-permute-done.29 = bf16[4,80,1792]{2,1,0:T(8,128)(2,1)S(1)} collective-permute-done((bf16[4,80,1792]{2,1,0:T(8,128)(2,1)S(1)}, bf16[4,80,1792]{2,1,0:T(8,128)(2,1)S(1)}, u32[]{:S(2)}, u32[]{:S(2)}) %collective-permute-start.29) | collective-permute-done | bytes 1146912 | tf_op jit(solution)/shard_map/ppermute | solution.py:35
  126.2 7.1 %second_product.7 = (bf16[4,48,1792]{2,1,0:T(8,128)(2,1)S(1)}, bf16[4,16,1792]{2,1,0:T(8,128)(2,1)S(1)}) custom-call(s32[1]{0:T(128)} %bitcast.me_ref, bf16[4,256,256]{2,1,0:T(8,128)(2,1)S(1)} %bitcast.30, bf16[1792,1024]{1,0:T(8,128)(2,1)} %bitcast.34, bf16[1792,1024]{1,0:T(8,128)(2,1)} %bitcast.38, bf16[1792,256]{1,0:T(8,128)(2,1)S(1)} %bitcast.26, ...), custom_call_target="tpu_custom_call" | custom-call | tf_op jit(solution)/shard_map/second_product/pallas_call | solution.py:242
  133.3 5.2 %collective-permute-start.32 = (bf16[4,48,1792]{2,1,0:T(8,128)(2,1)S(1)}, bf16[4,48,1792]{2,1,0:T(8,128)(2,1)S(1)}, u32[]{:S(2)}, u32[]{:S(2)}) collective-permute-start(bf16[4,48,1792]{2,1,0:T(8,128)(2,1)S(1)} %get-tuple-element.105), channel_id=1, source_target_pairs={{0,28},{4,0},{8,4},{12,8},{16,12},{20,16},{24,20},{28,24},{1,29},{... | collective-permute-start | bytes 2064392 | tf_op jit(solution)/shard_map/ppermute | solution.py:35
  138.5 2.1 %dynamic_update_slice.9 = bf16[4,256,1792]{2,1,0:T(8,128)(2,1)} pad(bf16[4,48,1792]{2,1,0:T(8,128)(2,1)S(1)} %collective-permute-done.22, bf16[]{:T(256)} %constant.1.clone.1), padding=0_0x0_208x0_0 | pad | bytes 4358146 | tf_op jit(solution)/shard_map/dynamic_update_slice | solution.py:338
  141.9 2.7 %collective-permute-start.30 = (bf16[4,16,1792]{2,1,0:T(8,128)(2,1)S(1)}, bf16[4,16,1792]{2,1,0:T(8,128)(2,1)S(1)}, u32[]{:S(2)}, u32[]{:S(2)}) collective-permute-start(bf16[4,16,1792]{2,1,0:T(8,128)(2,1)S(1)} %get-tuple-element.102), channel_id=1, source_target_pairs={{0,28},{1,29},{2,30},{3,31}} | collective-permute-start | bytes 688136 | tf_op jit(solution)/shard_map/ppermute | solution.py:343
  146.8 13.8 %collective-permute-done.32.source = bf16[4,48,1792]{2,1,0:T(8,128)(2,1)S(1)} collective-permute-done((bf16[4,48,1792]{2,1,0:T(8,128)(2,1)S(1)}, bf16[4,48,1792]{2,1,0:T(8,128)(2,1)S(1)}, u32[]{:S(2)}, u32[]{:S(2)}) %collective-permute-start.32) | collective-permute-done | bytes 688160 | tf_op jit(solution)/shard_map/ppermute | solution.py:35
  162.8 1.6 collective-permute-done.30.source
  (66 shorter events, 27.8 us)
Async XLA Ops:
  1.1 21.9 %collective-permute-start = (bf16[4,48,1792]{2,1,0:T(8,128)(2,1)S(1)}, bf16[4,48,1792]{2,1,0:T(8,128)(2,1)S(1)}, u32[]{:S(2)}, u32[]{:S(2)}) collective-permute-start(bf16[4,48,1792]{2,1,0:T(8,128)(2,1)S(1)} %take_rows.1), channel_id=1, source_target_pairs={{0,28},{4,0},{8,4},{12,8},{16,12},{20,16},{24,20},{28,24},{1,29},{... | collective-permute-start | bytes 2064392 | tf_op jit(solution)/shard_map/ppermute | solution.py:35
  12.2 35.5 %collective-permute-start.1 = (bf16[4,80,1792]{2,1,0:T(8,128)(2,1)}, bf16[4,80,1792]{2,1,0:T(8,128)(2,1)S(1)}, u32[]{:S(2)}, u32[]{:S(2)}) collective-permute-start(bf16[4,80,1792]{2,1,0:T(8,128)(2,1)} %slice.11), channel_id=1, source_target_pairs={{0,28},{4,0},{8,4},{12,8},{16,12},{20,16},{24,20},{28,24},{1,29},{... | collective-permute-start | bytes 3440648 | tf_op jit(solution)/shard_map/ppermute | solution.py:35
  23.0 44.3 %collective-permute-start.8 = (bf16[4,64,1792]{2,1,0:T(8,128)(2,1)}, bf16[4,64,1792]{2,1,0:T(8,128)(2,1)S(1)}, u32[]{:S(2)}, u32[]{:S(2)}) collective-permute-start(bf16[4,64,1792]{2,1,0:T(8,128)(2,1)} %get-tuple-element.73), channel_id=1, source_target_pairs={{0,28},{4,0},{8,4},{12,8},{16,12},{20,16},{24,20},{28,24},{1,29},{... | collective-permute-start | bytes 2752520 | tf_op jit(solution)/shard_map/ppermute | solution.py:35
  32.3 4.5 %collective-permute-start.2 = (bf16[48,1024]{1,0:T(8,128)(2,1)S(1)}, bf16[48,1024]{1,0:T(8,128)(2,1)S(1)}, u32[]{:S(2)}, u32[]{:S(2)}) collective-permute-start(bf16[48,1024]{1,0:T(8,128)(2,1)S(1)} %get-tuple-element.65), channel_id=1, source_target_pairs={{0,1},{1,2},{2,3},{3,0},{4,5},{5,6},{6,7},{7,4},{8,9},{9,10},{10,1... | collective-permute-start | bytes 294920 | tf_op jit(solution)/shard_map/ppermute | solution.py:40
  32.3 5.7 %collective-permute-start.3 = (bf16[48,1024]{1,0:T(8,128)(2,1)S(1)}, bf16[48,1024]{1,0:T(8,128)(2,1)S(1)}, u32[]{:S(2)}, u32[]{:S(2)}) collective-permute-start(bf16[48,1024]{1,0:T(8,128)(2,1)S(1)} %get-tuple-element.66), channel_id=1, source_target_pairs={{0,2},{1,3},{2,0},{3,1},{4,6},{5,7},{6,4},{7,5},{8,10},{9,11},{10,... | collective-permute-start | bytes 294920 | tf_op jit(solution)/shard_map/ppermute | solution.py:40
  33.9 4.6 %collective-permute-start.4 = (bf16[48,1024]{1,0:T(8,128)(2,1)S(1)}, bf16[48,1024]{1,0:T(8,128)(2,1)S(1)}, u32[]{:S(2)}, u32[]{:S(2)}) collective-permute-start(bf16[48,1024]{1,0:T(8,128)(2,1)S(1)} %get-tuple-element.67), channel_id=1, source_target_pairs={{0,3},{1,0},{2,1},{3,2},{4,7},{5,4},{6,5},{7,6},{8,11},{9,8},{10,9... | collective-permute-start | bytes 294920 | tf_op jit(solution)/shard_map/ppermute | solution.py:40
  39.9 9.9 %collective-permute-start.5 = (bf16[48,2048]{1,0:T(8,128)(2,1)S(1)}, bf16[48,2048]{1,0:T(8,128)(2,1)S(1)}, u32[]{:S(2)}, u32[]{:S(2)}) collective-permute-start(bf16[48,2048]{1,0:T(8,128)(2,1)S(1)} %activation.4.refs_0_), channel_id=1, source_target_pairs={{0,2},{1,3},{2,0},{3,1},{4,6},{5,7},{6,4},{7,5},{8,10},{9,11},{10,... | collective-permute-start | bytes 589832 | tf_op jit(solution)/shard_map/ppermute | solution.py:40
  41.0 15.6 %collective-permute-start.6 = (bf16[48,2048]{1,0:T(8,128)(2,1)S(1)}, bf16[48,2048]{1,0:T(8,128)(2,1)S(1)}, u32[]{:S(2)}, u32[]{:S(2)}) collective-permute-start(bf16[48,2048]{1,0:T(8,128)(2,1)S(1)} %activation.4.refs_0_), channel_id=1, source_target_pairs={{0,1},{1,0},{2,3},{3,2},{4,5},{5,4},{6,7},{7,6},{8,9},{9,8},{10,11... | collective-permute-start | bytes 589832 | tf_op jit(solution)/shard_map/ppermute | solution.py:45
  49.8 6.8 %collective-permute-start.7 = (bf16[48,2048]{1,0:T(8,128)(2,1)S(1)}, bf16[48,2048]{1,0:T(8,128)(2,1)S(1)}, u32[]{:S(2)}, u32[]{:S(2)}) collective-permute-start(bf16[48,2048]{1,0:T(8,128)(2,1)S(1)} %collective-permute-done.5.refs_2_), channel_id=1, source_target_pairs={{0,1},{1,0},{2,3},{3,2},{4,5},{5,4},{6,7},{7,6},{8,9},{9,8},{10,11... | collective-permute-start | bytes 589832 | tf_op jit(solution)/shard_map/ppermute | solution.py:45
  49.9 41.9 %collective-permute-start.15 = (bf16[4,64,1792]{2,1,0:T(8,128)(2,1)S(1)}, bf16[4,64,1792]{2,1,0:T(8,128)(2,1)S(1)}, u32[]{:S(2)}, u32[]{:S(2)}) collective-permute-start(bf16[4,64,1792]{2,1,0:T(8,128)(2,1)S(1)} %copy-done.3), channel_id=1, source_target_pairs={{0,28},{4,0},{8,4},{12,8},{16,12},{20,16},{24,20},{28,24},{1,29},{... | collective-permute-start | bytes 2752520 | tf_op jit(solution)/shard_map/ppermute | solution.py:35
  55.0 12.3 %collective-permute-start.10 = (bf16[80,1024]{1,0:T(8,128)(2,1)S(1)}, bf16[80,1024]{1,0:T(8,128)(2,1)S(1)}, u32[]{:S(2)}, u32[]{:S(2)}) collective-permute-start(bf16[80,1024]{1,0:T(8,128)(2,1)S(1)} %get-tuple-element.77), channel_id=1, source_target_pairs={{0,2},{1,3},{2,0},{3,1},{4,6},{5,7},{6,4},{7,5},{8,10},{9,11},{10,... | collective-permute-start | bytes 491528 | tf_op jit(solution)/shard_map/ppermute | solution.py:40
  56.5 10.8 %collective-permute-start.11 = (bf16[80,1024]{1,0:T(8,128)(2,1)S(1)}, bf16[80,1024]{1,0:T(8,128)(2,1)S(1)}, u32[]{:S(2)}, u32[]{:S(2)}) collective-permute-start(bf16[80,1024]{1,0:T(8,128)(2,1)S(1)} %get-tuple-element.78), channel_id=1, source_target_pairs={{0,3},{1,0},{2,1},{3,2},{4,7},{5,4},{6,5},{7,6},{8,11},{9,8},{10,9... | collective-permute-start | bytes 491528 | tf_op jit(solution)/shard_map/ppermute | solution.py:40
  56.5 10.8 %collective-permute-start.9 = (bf16[80,1024]{1,0:T(8,128)(2,1)S(1)}, bf16[80,1024]{1,0:T(8,128)(2,1)S(1)}, u32[]{:S(2)}, u32[]{:S(2)}) collective-permute-start(bf16[80,1024]{1,0:T(8,128)(2,1)S(1)} %get-tuple-element.76), channel_id=1, source_target_pairs={{0,1},{1,2},{2,3},{3,0},{4,5},{5,6},{6,7},{7,4},{8,9},{9,10},{10,1... | collective-permute-start | bytes 491528 | tf_op jit(solution)/shard_map/ppermute | solution.py:40
  68.8 7.8 %collective-permute-start.12 = (bf16[80,2048]{1,0:T(8,128)(2,1)S(1)}, bf16[80,2048]{1,0:T(8,128)(2,1)S(1)}, u32[]{:S(2)}, u32[]{:S(2)}) collective-permute-start(bf16[80,2048]{1,0:T(8,128)(2,1)S(1)} %activation.5.refs_0_), channel_id=1, source_target_pairs={{0,2},{1,3},{2,0},{3,1},{4,6},{5,7},{6,4},{7,5},{8,10},{9,11},{10,... | collective-permute-start | bytes 983048 | tf_op jit(solution)/shard_map/ppermute | solution.py:40
  70.4 8.0 %collective-permute-start.13 = (bf16[80,2048]{1,0:T(8,128)(2,1)S(1)}, bf16[80,2048]{1,0:T(8,128)(2,1)S(1)}, u32[]{:S(2)}, u32[]{:S(2)}) collective-permute-start(bf16[80,2048]{1,0:T(8,128)(2,1)S(1)} %activation.5.refs_0_), channel_id=1, source_target_pairs={{0,1},{1,0},{2,3},{3,2},{4,5},{5,4},{6,7},{7,6},{8,9},{9,8},{10,11... | collective-permute-start | bytes 983048 | tf_op jit(solution)/shard_map/ppermute | solution.py:45
  76.6 2.7 %collective-permute-start.14 = (bf16[80,2048]{1,0:T(8,128)(2,1)S(1)}, bf16[80,2048]{1,0:T(8,128)(2,1)S(1)}, u32[]{:S(2)}, u32[]{:S(2)}) collective-permute-start(bf16[80,2048]{1,0:T(8,128)(2,1)S(1)} %collective-permute-done.12.refs_2_), channel_id=1, source_target_pairs={{0,1},{1,0},{2,3},{3,2},{4,5},{5,4},{6,7},{7,6},{8,9},{9,8},{10,11... | collective-permute-start | bytes 983048 | tf_op jit(solution)/shard_map/ppermute | solution.py:45
  76.6 15.2 %collective-permute-start.16 = (bf16[64,1024]{1,0:T(8,128)(2,1)S(1)}, bf16[64,1024]{1,0:T(8,128)(2,1)S(1)}, u32[]{:S(2)}, u32[]{:S(2)}) collective-permute-start(bf16[64,1024]{1,0:T(8,128)(2,1)S(1)} %get-tuple-element.87), channel_id=1, source_target_pairs={{0,1},{1,2},{2,3},{3,0},{4,5},{5,6},{6,7},{7,4},{8,9},{9,10},{10,1... | collective-permute-start | bytes 393224 | tf_op jit(solution)/shard_map/ppermute | solution.py:40
  77.1 14.7 %collective-permute-start.17 = (bf16[64,1024]{1,0:T(8,128)(2,1)S(1)}, bf16[64,1024]{1,0:T(8,128)(2,1)S(1)}, u32[]{:S(2)}, u32[]{:S(2)}) collective-permute-start(bf16[64,1024]{1,0:T(8,128)(2,1)S(1)} %get-tuple-element.88), channel_id=1, source_target_pairs={{0,2},{1,3},{2,0},{3,1},{4,6},{5,7},{6,4},{7,5},{8,10},{9,11},{10,... | collective-permute-start | bytes 393224 | tf_op jit(solution)/shard_map/ppermute | solution.py:40
  78.3 13.4 %collective-permute-start.18 = (bf16[64,1024]{1,0:T(8,128)(2,1)S(1)}, bf16[64,1024]{1,0:T(8,128)(2,1)S(1)}, u32[]{:S(2)}, u32[]{:S(2)}) collective-permute-start(bf16[64,1024]{1,0:T(8,128)(2,1)S(1)} %get-tuple-element.89), channel_id=1, source_target_pairs={{0,3},{1,0},{2,1},{3,2},{4,7},{5,4},{6,5},{7,6},{8,11},{9,8},{10,9... | collective-permute-start | bytes 393224 | tf_op jit(solution)/shard_map/ppermute | solution.py:40
  79.3 30.9 %collective-permute-start.22 = (bf16[4,48,1792]{2,1,0:T(8,128)(2,1)S(1)}, bf16[4,48,1792]{2,1,0:T(8,128)(2,1)S(1)}, u32[]{:S(2)}, u32[]{:S(2)}) collective-permute-start(bf16[4,48,1792]{2,1,0:T(8,128)(2,1)S(1)} %second_product.4), channel_id=1, source_target_pairs={{0,28},{4,0},{8,4},{12,8},{16,12},{20,16},{24,20},{28,24},{1,29},{... | collective-permute-start | bytes 2064392 | tf_op jit(solution)/shard_map/ppermute | solution.py:35
  93.2 7.5 %collective-permute-start.19 = (bf16[64,2048]{1,0:T(8,128)(2,1)S(1)}, bf16[64,2048]{1,0:T(8,128)(2,1)S(1)}, u32[]{:S(2)}, u32[]{:S(2)}) collective-permute-start(bf16[64,2048]{1,0:T(8,128)(2,1)S(1)} %activation.6.refs_0_), channel_id=1, source_target_pairs={{0,2},{1,3},{2,0},{3,1},{4,6},{5,7},{6,4},{7,5},{8,10},{9,11},{10,... | collective-permute-start | bytes 786440 | tf_op jit(solution)/shard_map/ppermute | solution.py:40
  93.8 32.4 %collective-permute-start.29 = (bf16[4,80,1792]{2,1,0:T(8,128)(2,1)S(1)}, bf16[4,80,1792]{2,1,0:T(8,128)(2,1)S(1)}, u32[]{:S(2)}, u32[]{:S(2)}) collective-permute-start(bf16[4,80,1792]{2,1,0:T(8,128)(2,1)S(1)} %second_product.5), channel_id=1, source_target_pairs={{0,28},{4,0},{8,4},{12,8},{16,12},{20,16},{24,20},{28,24},{1,29},{... | collective-permute-start | bytes 3440648 | tf_op jit(solution)/shard_map/ppermute | solution.py:35
  95.1 6.2 %collective-permute-start.20 = (bf16[64,2048]{1,0:T(8,128)(2,1)S(1)}, bf16[64,2048]{1,0:T(8,128)(2,1)S(1)}, u32[]{:S(2)}, u32[]{:S(2)}) collective-permute-start(bf16[64,2048]{1,0:T(8,128)(2,1)S(1)} %activation.6.refs_0_), channel_id=1, source_target_pairs={{0,1},{1,0},{2,3},{3,2},{4,5},{5,4},{6,7},{7,6},{8,9},{9,8},{10,11... | collective-permute-start | bytes 786440 | tf_op jit(solution)/shard_map/ppermute | solution.py:45
  100.7 9.4 %collective-permute-start.23 = (bf16[64,1024]{1,0:T(8,128)(2,1)S(1)}, bf16[64,1024]{1,0:T(8,128)(2,1)S(1)}, u32[]{:S(2)}, u32[]{:S(2)}) collective-permute-start(bf16[64,1024]{1,0:T(8,128)(2,1)S(1)} %get-tuple-element.97), channel_id=1, source_target_pairs={{0,1},{1,2},{2,3},{3,0},{4,5},{5,6},{6,7},{7,4},{8,9},{9,10},{10,1... | collective-permute-start | bytes 393224 | tf_op jit(solution)/shard_map/ppermute | solution.py:40
  101.3 8.9 %collective-permute-start.24 = (bf16[64,1024]{1,0:T(8,128)(2,1)S(1)}, bf16[64,1024]{1,0:T(8,128)(2,1)S(1)}, u32[]{:S(2)}, u32[]{:S(2)}) collective-permute-start(bf16[64,1024]{1,0:T(8,128)(2,1)S(1)} %get-tuple-element.98), channel_id=1, source_target_pairs={{0,2},{1,3},{2,0},{3,1},{4,6},{5,7},{6,4},{7,5},{8,10},{9,11},{10,... | collective-permute-start | bytes 393224 | tf_op jit(solution)/shard_map/ppermute | solution.py:40
  102.3 7.9 %collective-permute-start.25 = (bf16[64,1024]{1,0:T(8,128)(2,1)S(1)}, bf16[64,1024]{1,0:T(8,128)(2,1)S(1)}, u32[]{:S(2)}, u32[]{:S(2)}) collective-permute-start(bf16[64,1024]{1,0:T(8,128)(2,1)S(1)} %get-tuple-element.99), channel_id=1, source_target_pairs={{0,3},{1,0},{2,1},{3,2},{4,7},{5,4},{6,5},{7,6},{8,11},{9,8},{10,9... | collective-permute-start | bytes 393224 | tf_op jit(solution)/shard_map/ppermute | solution.py:40
  111.6 7.9 %collective-permute-start.27 = (bf16[64,2048]{1,0:T(8,128)(2,1)S(1)}, bf16[64,2048]{1,0:T(8,128)(2,1)S(1)}, u32[]{:S(2)}, u32[]{:S(2)}) collective-permute-start(bf16[64,2048]{1,0:T(8,128)(2,1)S(1)} %activation.7.refs_0_), channel_id=1, source_target_pairs={{0,2},{1,3},{2,0},{3,1},{4,6},{5,7},{6,4},{7,5},{8,10},{9,11},{10,... | collective-permute-start | bytes 786440 | tf_op jit(solution)/shard_map/ppermute | solution.py:40
  112.8 33.1 %collective-permute-start.33 = (bf16[4,64,1792]{2,1,0:T(8,128)(2,1)S(1)}, bf16[4,64,1792]{2,1,0:T(8,128)(2,1)S(1)}, u32[]{:S(2)}, u32[]{:S(2)}) collective-permute-start(bf16[4,64,1792]{2,1,0:T(8,128)(2,1)S(1)} %second_product.6), channel_id=1, source_target_pairs={{0,28},{4,0},{8,4},{12,8},{16,12},{20,16},{24,20},{28,24},{1,29},{... | collective-permute-start | bytes 2752520 | tf_op jit(solution)/shard_map/ppermute | solution.py:35
  119.6 6.6 %collective-permute-start.26 = (bf16[64,2048]{1,0:T(8,128)(2,1)S(1)}, bf16[64,2048]{1,0:T(8,128)(2,1)S(1)}, u32[]{:S(2)}, u32[]{:S(2)}) collective-permute-start(bf16[64,2048]{1,0:T(8,128)(2,1)S(1)} %activation.7.refs_0_), channel_id=1, source_target_pairs={{0,1},{1,0},{2,3},{3,2},{4,5},{5,4},{6,7},{7,6},{8,9},{9,8},{10,11... | collective-permute-start | bytes 786440 | tf_op jit(solution)/shard_map/ppermute | solution.py:45
  133.3 27.3 %collective-permute-start.32 = (bf16[4,48,1792]{2,1,0:T(8,128)(2,1)S(1)}, bf16[4,48,1792]{2,1,0:T(8,128)(2,1)S(1)}, u32[]{:S(2)}, u32[]{:S(2)}) collective-permute-start(bf16[4,48,1792]{2,1,0:T(8,128)(2,1)S(1)} %get-tuple-element.105), channel_id=1, source_target_pairs={{0,28},{4,0},{8,4},{12,8},{16,12},{20,16},{24,20},{28,24},{1,29},{... | collective-permute-start | bytes 2064392 | tf_op jit(solution)/shard_map/ppermute | solution.py:35
  140.6 21.5 %collective-permute-start.31 = (bf16[4,16,1792]{2,1,0:T(8,128)(2,1)S(1)}, bf16[4,16,1792]{2,1,0:T(8,128)(2,1)S(1)}, u32[]{:S(2)}, u32[]{:S(2)}) collective-permute-start(bf16[4,16,1792]{2,1,0:T(8,128)(2,1)S(1)} %get-tuple-element.102), channel_id=1, source_target_pairs={{4,0},{8,4},{12,8},{16,12},{20,16},{24,20},{28,24},{5,1},{9,5},{13... | collective-permute-start | bytes 688136 | tf_op jit(solution)/shard_map/ppermute | solution.py:342
  141.9 22.5 %collective-permute-start.30 = (bf16[4,16,1792]{2,1,0:T(8,128)(2,1)S(1)}, bf16[4,16,1792]{2,1,0:T(8,128)(2,1)S(1)}, u32[]{:S(2)}, u32[]{:S(2)}) collective-permute-start(bf16[4,16,1792]{2,1,0:T(8,128)(2,1)S(1)} %get-tuple-element.102), channel_id=1, source_target_pairs={{0,28},{1,29},{2,30},{3,31}} | collective-permute-start | bytes 688136 | tf_op jit(solution)/shard_map/ppermute | solution.py:343
  (6 other events, 89.9 us)
